TPU v7x, 32 devices: a whole 2x2x4 slice. The times are simulated.
32 devices in a mesh: narrow: 4 (over z), wide: 8 (over y, x, core).
Axes of the slice: x: 2, y: 2, z: 4, core: 2. Of those that a mesh axis runs over, the one named last changes fastest.
Arguments:
- sources: float32 [16, 16, 32, 256], P(None, 'wide', 'narrow')
- well_columns: int32 [16], replicated, may hold values from 0 to 511
- column_active: int32 [16, 32], P('wide', 'narrow'), may hold values 0 or 1
- perm_root: float32 [16, 32, 256], P('wide', 'narrow'), may hold values from 0.5 to 2
- storage_term: float32 [16, 32, 256], P('wide', 'narrow'), may hold values from 0.2 to 2
- inverse_blocks: bfloat16 [16, 32, 2, 128, 128], P('wide', 'narrow')
Outputs:
- solution: float32 [16, 16, 32, 256], P(None, 'wide', 'narrow')
- residual: float32 [16, 16, 32, 256], P(None, 'wide', 'narrow')
All inputs are finite; a program needn't handle non-finite values. No bound on the sum of `column_active` on one device may be relied on, other than what follows from the above.
Results may differ from a plain program's by a relative error of at most 0.0085.
Values sent between devices are 32-bit elements; how exact they have to be, the bound alone decides.
No kernel may reach another device: no remote copies, remote signals or barrier semaphores. Data moves between devices by JAX's collectives and lax.ppermute only.
A program may use at most 64 MiB of HBM per device.

v0:
```python
import jax
import jax.numpy as jnp
from jax import lax
from jax.sharding import PartitionSpec as P

ITERS = 3


WELL_RATE = 4.0


def with_halo(x, sides, width):
    for axis, dim in sides:
        peers, length = (lax.axis_size(axis), x.shape[dim])
        up = [(i, (i + 1) % peers) for i in range(peers - 1)]
        down = [(j, i) for i, j in up]
        last = lax.slice_in_dim(x, length - width, length, axis=dim)
        first = lax.slice_in_dim(x, 0, width, axis=dim)
        before = lax.ppermute(last, axis, up)
        after = lax.ppermute(first, axis, down)
        x = jnp.concatenate([before, x, after], axis=dim)
    return x


def coupling(padded, coef_pad):
    center = padded[:, 1:-1, 1:-1]
    coef = coef_pad[1:-1, 1:-1]
    total = coef_pad[2:, 1:-1] * (center - padded[:, 2:, 1:-1]) + coef_pad[:-2, 1:-1] * (
        center - padded[:, :-2, 1:-1]
    )
    total = (
        total
        + coef_pad[1:-1, 2:] * (center - padded[:, 1:-1, 2:])
        + coef_pad[1:-1, :-2] * (center - padded[:, 1:-1, :-2])
    )
    zero_layer = jnp.zeros_like(center[..., :1])
    zero_coef = jnp.zeros_like(coef[..., :1])
    upper = jnp.concatenate([center[..., 1:], zero_layer], -1)
    upper_coef = jnp.concatenate([coef[..., 1:], zero_coef], -1)
    lower = jnp.concatenate([zero_layer, center[..., :-1]], -1)
    lower_coef = jnp.concatenate([zero_coef, coef[..., :-1]], -1)
    total = total + upper_coef * (center - upper) + lower_coef * (center - lower)
    return coef * total


def operate(values, diag_term, coef, coef_pad):
    if coef_pad is None:
        stacked = jnp.concatenate([values, coef[None]], 0)
    else:
        stacked = values
    padded = with_halo(stacked, (("narrow", 2), ("wide", 1)), 1)
    if coef_pad is None:
        coef_pad = padded[-1]
        padded = padded[:-1]
    return (diag_term * values + coupling(padded, coef_pad), coef_pad)


def precondition(values, inverse_blocks):
    count, cols_x, cols_y, layers = values.shape
    blocks = inverse_blocks.shape[2]
    shaped = values.astype(jnp.bfloat16).reshape(count, cols_x, cols_y, blocks, layers // blocks)
    output = jnp.einsum(
        "xybij,kxybj->kxybi", inverse_blocks, shaped, preferred_element_type=jnp.float32
    )
    return output.reshape(count, cols_x, cols_y, layers)


def local_gram(left, right):
    return jnp.einsum("kxyz,lxyz->kl", left, right, precision=lax.Precision.HIGHEST)


def combine(values, coefs):
    return jnp.einsum("kxyz,kl->lxyz", values, coefs, precision=lax.Precision.HIGHEST)


def solve_gram(matrix, target):
    sym = 0.5 * (matrix + matrix.T)
    factor = jnp.linalg.cholesky(sym)
    inner = lax.linalg.triangular_solve(factor, target, left_side=True, lower=True)
    return lax.linalg.triangular_solve(factor, inner, left_side=True, lower=True, transpose_a=True)


def joint_sum(stacked):
    return lax.psum(stacked, ("narrow", "wide"))


def on_device(sources, well_columns, column_active, perm_root, storage_term, inverse_blocks):
    cols_x, cols_y = column_active.shape
    grid_y = cols_y * lax.axis_size("narrow")
    first_x = lax.axis_index("wide") * cols_x
    first_y = lax.axis_index("narrow") * cols_y
    column_ids = (
        (first_x + jnp.arange(cols_x, dtype=jnp.int32))[:, None] * grid_y
        + first_y
        + jnp.arange(cols_y, dtype=jnp.int32)[None, :]
    )
    wells = (column_ids[None] == well_columns[:, None, None]).astype(jnp.float32)
    active = column_active.astype(jnp.float32)[..., None]
    coef = perm_root * active
    diag_term = active * storage_term + (1.0 - active)
    residual = sources + WELL_RATE * wells[..., None]
    solution = jnp.zeros_like(residual)
    zset = precondition(residual, inverse_blocks)
    coef_pad = None
    image, coef_pad = operate(zset, diag_term, coef, coef_pad)
    first_grams = jnp.stack(
        [
            local_gram(zset, residual),
            local_gram(zset, image),
            jnp.zeros_like(local_gram(zset, residual)),
        ]
    )
    summed = joint_sum(first_grams)
    res_gram = summed[0]
    curv_gram = summed[1]
    direction = zset
    for iteration in range(ITERS):
        step_size = solve_gram(curv_gram, res_gram)
        solution = solution + combine(direction, step_size)
        residual = residual - combine(image, step_size)
        if iteration + 1 < ITERS:
            zset = precondition(residual, inverse_blocks)
            applied, coef_pad = operate(zset, diag_term, coef, coef_pad)
            summed = joint_sum(
                jnp.stack(
                    [local_gram(zset, residual), local_gram(zset, applied), local_gram(zset, image)]
                )
            )
            new_gram = summed[0]
            conj_coef = solve_gram(res_gram, new_gram)
            cross_gram = summed[2]
            curv_gram = (
                summed[1]
                + jnp.dot(cross_gram, conj_coef, precision=lax.Precision.HIGHEST)
                + jnp.dot(conj_coef.T, cross_gram.T, precision=lax.Precision.HIGHEST)
                + jnp.dot(
                    conj_coef.T,
                    jnp.dot(curv_gram, conj_coef, precision=lax.Precision.HIGHEST),
                    precision=lax.Precision.HIGHEST,
                )
            )
            direction = zset + combine(direction, conj_coef)
            image = applied + combine(image, conj_coef)
            res_gram = new_gram
    return (solution, residual)


def solution(mesh):
    in_specs = (
        P(None, "wide", "narrow", None),
        P(),
        P("wide", "narrow"),
        P("wide", "narrow", None),
        P("wide", "narrow", None),
        P("wide", "narrow", None, None, None),
    )
    out_specs = (P(None, "wide", "narrow", None), P(None, "wide", "narrow", None))
    return jax.shard_map(
        on_device, mesh=mesh, in_specs=in_specs, out_specs=out_specs, check_vma=False
    )
```

profile of v0, /device:TPU:0, one launch (start us, length us, event | category | flops | bytes accessed | tf_op | source)
XLA Modules:
  0.0 226.1 jit_solution(16416065521279987508)
XLA Ops:
  2.2 1.6 convolution_bitcast_fusion.2
  4.9 4.9 %collective-permute-start = (f32[17,2,1,256]{3,0,2,1:T(8,128)S(1)}, f32[17,2,1,256]{3,0,2,1:T(8,128)S(1)}, u32[]{:S(2)}, u32[]{:S(2)}) collective-permute-start(f32[17,2,1,256]{3,0,2,1:T(8,128)S(1)} %get-tuple-element.12), channel_id=1, source_target_pairs={{0,8},{8,16},{16,24},{1,9},{9,17},{17,25},{2,10},{10,18},{18,26},{... | collective-permute-start | bytes 104456 | tf_op jit(solution)/shard_map/ppermute | solution.py:19
  9.8 1.3 collective-permute-start.1
  11.6 4.3 %collective-permute-done.1 = f32[17,2,1,256]{3,0,2,1:T(8,128)S(1)} collective-permute-done((f32[17,2,1,256]{3,0,2,1:T(8,128)S(1)}, f32[17,2,1,256]{3,0,2,1:T(8,128)S(1)}, u32[]{:S(2)}, u32[]{:S(2)}) %collective-permute-start.1) | collective-permute-done | bytes 34848 | tf_op jit(solution)/shard_map/ppermute | solution.py:20
  15.9 1.3 collective-permute-start.2
  17.2 1.3 collective-permute-start.3
  20.5 1.8 collective-permute-done.3
  24.2 44.6 %psum.21 = f32[3,16,16]{2,1,0:T(8,128)S(1)} all-reduce(f32[3,16,16]{2,1,0:T(8,128)S(1)} %maximum_maximum_fusion), channel_id=1, replica_groups=mesh['narrow'=4,'wide'=8] {'narrow','wide'}, use_global_device_ids=true, to_apply=%region_0.0 | all-reduce | flops 768 | bytes 6144 | tf_op jit(solution)/shard_map/psum | solution.py:84
  69.1 1.5 cholesky.89
  76.4 1.5 cholesky.100
  78.5 2.1 collective-permute-start.4
  81.3 1.3 collective-permute-start.5
  83.4 3.7 %collective-permute-done.5 = f32[16,2,1,256]{3,0,2,1:T(8,128)S(1)} collective-permute-done((f32[16,2,1,256]{3,0,2,1:T(8,128)S(1)}, f32[16,2,1,256]{3,0,2,1:T(8,128)S(1)}, u32[]{:S(2)}, u32[]{:S(2)}) %collective-permute-start.5) | collective-permute-done | bytes 32800 | tf_op jit(solution)/shard_map/ppermute | solution.py:20
  88.4 2.0 collective-permute-start.7
  92.8 1.8 custom-call.19
  97.6 43.9 %psum.22 = f32[3,16,16]{2,1,0:T(8,128)S(1)} all-reduce(f32[3,16,16]{2,1,0:T(8,128)S(1)} %pad_maximum_fusion.21), channel_id=1, replica_groups=mesh['narrow'=4,'wide'=8] {'narrow','wide'}, use_global_device_ids=true, to_apply=%region_3.7 | all-reduce | flops 768 | bytes 6144 | tf_op jit(solution)/shard_map/psum | solution.py:84
  145.0 1.5 cholesky.111
  151.5 1.5 cholesky.122
  153.7 2.2 collective-permute-start.8
  158.8 4.0 %collective-permute-done.9 = f32[16,2,1,256]{3,0,2,1:T(8,128)} collective-permute-done((f32[16,2,1,256]{3,0,2,1:T(8,128)S(1)}, f32[16,2,1,256]{3,0,2,1:T(8,128)}, u32[]{:S(2)}, u32[]{:S(2)}) %collective-permute-start.9) | collective-permute-done | bytes 32800 | tf_op jit(solution)/shard_map/ppermute | solution.py:20
  163.6 2.2 collective-permute-start.11
  167.5 1.8 custom-call.23
  172.8 43.8 %psum.23 = f32[3,16,16]{2,1,0:T(8,128)S(1)} all-reduce(f32[3,16,16]{2,1,0:T(8,128)S(1)} %pad_maximum_fusion.22), channel_id=1, replica_groups=mesh['narrow'=4,'wide'=8] {'narrow','wide'}, use_global_device_ids=true, to_apply=%region_4.8 | all-reduce | flops 768 | bytes 6144 | tf_op jit(solution)/shard_map/psum | solution.py:84
  219.2 1.5 cholesky.133
  (204 shorter events, 47.4 us)
Async XLA Ops:
  0.6 1.5 copy-start
  4.8 17.9 %copy-start.11 = (f32[2,8,256]{2,1,0:T(8,128)}, f32[2,8,256]{2,1,0:T(8,128)S(1)}, u32[]{:S(2)}) copy-start(f32[2,8,256]{2,1,0:T(8,128)S(1)} %get-tuple-element.36) | copy-start | bytes 49156
  4.9 6.7 %collective-permute-start = (f32[17,2,1,256]{3,0,2,1:T(8,128)S(1)}, f32[17,2,1,256]{3,0,2,1:T(8,128)S(1)}, u32[]{:S(2)}, u32[]{:S(2)}) collective-permute-start(f32[17,2,1,256]{3,0,2,1:T(8,128)S(1)} %get-tuple-element.12), channel_id=1, source_target_pairs={{0,8},{8,16},{16,24},{1,9},{9,17},{17,25},{2,10},{10,18},{18,26},{... | collective-permute-start | bytes 104456 | tf_op jit(solution)/shard_map/ppermute | solution.py:19
  9.8 6.0 %collective-permute-start.1 = (f32[17,2,1,256]{3,0,2,1:T(8,128)S(1)}, f32[17,2,1,256]{3,0,2,1:T(8,128)S(1)}, u32[]{:S(2)}, u32[]{:S(2)}) collective-permute-start(f32[17,2,1,256]{3,0,2,1:T(8,128)S(1)} %get-tuple-element.11), channel_id=1, source_target_pairs={{8,0},{16,8},{24,16},{9,1},{17,9},{25,17},{10,2},{18,10},{26,18},{... | collective-permute-start | bytes 104456 | tf_op jit(solution)/shard_map/ppermute | solution.py:20
  15.9 4.6 %collective-permute-start.2 = (f32[17,1,10,256]{3,0,2,1:T(8,128)S(1)}, f32[17,1,10,256]{3,0,2,1:T(8,128)S(1)}, u32[]{:S(2)}, u32[]{:S(2)}) collective-permute-start(f32[17,1,10,256]{3,0,2,1:T(8,128)S(1)} %get-tuple-element.10), channel_id=1, source_target_pairs={{0,1},{1,2},{2,3},{3,4},{4,5},{5,6},{6,7},{8,9},{9,10},{10,11},{11... | collective-permute-start | bytes 522248 | tf_op jit(solution)/shard_map/ppermute | solution.py:19
  17.2 5.1 %collective-permute-start.3 = (f32[17,1,10,256]{3,0,2,1:T(8,128)S(1)}, f32[17,1,10,256]{3,0,2,1:T(8,128)S(1)}, u32[]{:S(2)}, u32[]{:S(2)}) collective-permute-start(f32[17,1,10,256]{3,0,2,1:T(8,128)S(1)} %get-tuple-element.9), channel_id=1, source_target_pairs={{1,0},{2,1},{3,2},{4,3},{5,4},{6,5},{7,6},{9,8},{10,9},{11,10},{12... | collective-permute-start | bytes 522248 | tf_op jit(solution)/shard_map/ppermute | solution.py:20
  68.8 7.5 %copy-start.14 = (f32[3,16,16]{2,1,0:T(8,128)}, f32[3,16,16]{2,1,0:T(8,128)S(1)}, u32[]{:S(2)}) copy-start(f32[3,16,16]{2,1,0:T(8,128)S(1)} %psum.21) | copy-start | bytes 9220
  78.5 4.1 %collective-permute-start.4 = (f32[16,2,1,256]{3,0,2,1:T(8,128)S(1)}, f32[16,2,1,256]{3,0,2,1:T(8,128)S(1)}, u32[]{:S(2)}, u32[]{:S(2)}) collective-permute-start(f32[16,2,1,256]{3,0,2,1:T(8,128)S(1)} %get-tuple-element.24), channel_id=1, source_target_pairs={{0,8},{8,16},{16,24},{1,9},{9,17},{17,25},{2,10},{10,18},{18,26},{... | collective-permute-start | bytes 98312 | tf_op jit(solution)/shard_map/ppermute | solution.py:19
  81.3 5.8 %collective-permute-start.5 = (f32[16,2,1,256]{3,0,2,1:T(8,128)S(1)}, f32[16,2,1,256]{3,0,2,1:T(8,128)S(1)}, u32[]{:S(2)}, u32[]{:S(2)}) collective-permute-start(f32[16,2,1,256]{3,0,2,1:T(8,128)S(1)} %get-tuple-element.23), channel_id=1, source_target_pairs={{8,0},{16,8},{24,16},{9,1},{17,9},{25,17},{10,2},{18,10},{26,18},{... | collective-permute-start | bytes 98312 | tf_op jit(solution)/shard_map/ppermute | solution.py:20
  88.4 6.8 %collective-permute-start.7 = (f32[16,1,10,256]{3,0,2,1:T(8,128)}, f32[16,1,10,256]{3,0,2,1:T(8,128)}, u32[]{:S(2)}, u32[]{:S(2)}) collective-permute-start(f32[16,1,10,256]{3,0,2,1:T(8,128)} %get-tuple-element.16), channel_id=1, source_target_pairs={{0,1},{1,2},{2,3},{3,4},{4,5},{5,6},{6,7},{8,9},{9,10},{10,11},{11... | collective-permute-start | bytes 491528 | tf_op jit(solution)/shard_map/ppermute | solution.py:19
  90.4 5.2 %collective-permute-start.6 = (f32[16,1,10,256]{3,0,2,1:T(8,128)S(1)}, f32[16,1,10,256]{3,0,2,1:T(8,128)}, u32[]{:S(2)}, u32[]{:S(2)}) collective-permute-start(f32[16,1,10,256]{3,0,2,1:T(8,128)S(1)} %get-tuple-element.15), channel_id=1, source_target_pairs={{1,0},{2,1},{3,2},{4,3},{5,4},{6,5},{7,6},{9,8},{10,9},{11,10},{12... | collective-permute-start | bytes 491528 | tf_op jit(solution)/shard_map/ppermute | solution.py:20
  94.6 1.0 copy-start.20
  97.6 43.9 %copy-start.25 = (f32[1,16,16]{1,2,0:T(8,128)S(1)}, f32[1,16,16]{1,2,0:T(8,128)}, u32[]{:S(2)}) copy-start(f32[1,16,16]{1,2,0:T(8,128)} %custom-call.19) | copy-start | bytes 3076
  153.7 4.5 %collective-permute-start.8 = (f32[16,2,1,256]{3,0,2,1:T(8,128)S(1)}, f32[16,2,1,256]{3,0,2,1:T(8,128)S(1)}, u32[]{:S(2)}, u32[]{:S(2)}) collective-permute-start(f32[16,2,1,256]{3,0,2,1:T(8,128)S(1)} %get-tuple-element.20), channel_id=1, source_target_pairs={{0,8},{8,16},{16,24},{1,9},{9,17},{17,25},{2,10},{10,18},{18,26},{... | collective-permute-start | bytes 98312 | tf_op jit(solution)/shard_map/ppermute | solution.py:19
  156.9 5.9 %collective-permute-start.9 = (f32[16,2,1,256]{3,0,2,1:T(8,128)S(1)}, f32[16,2,1,256]{3,0,2,1:T(8,128)}, u32[]{:S(2)}, u32[]{:S(2)}) collective-permute-start(f32[16,2,1,256]{3,0,2,1:T(8,128)S(1)} %get-tuple-element.19), channel_id=1, source_target_pairs={{8,0},{16,8},{24,16},{9,1},{17,9},{25,17},{10,2},{18,10},{26,18},{... | collective-permute-start | bytes 98312 | tf_op jit(solution)/shard_map/ppermute | solution.py:20
  163.6 6.2 %collective-permute-start.11 = (f32[16,1,10,256]{3,0,2,1:T(8,128)S(1)}, f32[16,1,10,256]{3,0,2,1:T(8,128)}, u32[]{:S(2)}, u32[]{:S(2)}) collective-permute-start(f32[16,1,10,256]{3,0,2,1:T(8,128)S(1)} %get-tuple-element.14), channel_id=1, source_target_pairs={{0,1},{1,2},{2,3},{3,4},{4,5},{5,6},{6,7},{8,9},{9,10},{10,11},{11... | collective-permute-start | bytes 491528 | tf_op jit(solution)/shard_map/ppermute | solution.py:19
  165.7 5.2 %collective-permute-start.10 = (f32[16,1,10,256]{3,0,2,1:T(8,128)S(1)}, f32[16,1,10,256]{3,0,2,1:T(8,128)}, u32[]{:S(2)}, u32[]{:S(2)}) collective-permute-start(f32[16,1,10,256]{3,0,2,1:T(8,128)S(1)} %get-tuple-element.13), channel_id=1, source_target_pairs={{1,0},{2,1},{3,2},{4,3},{5,4},{6,5},{7,6},{9,8},{10,9},{11,10},{12... | collective-permute-start | bytes 491528 | tf_op jit(solution)/shard_map/ppermute | solution.py:20
  167.0 4.0 %copy-start.7 = (f32[2,8,256]{2,1,0:T(8,128)S(1)}, f32[2,8,256]{2,1,0:T(8,128)}, u32[]{:S(2)}) copy-start(f32[2,8,256]{2,1,0:T(8,128)} %copy-done.5) | copy-start | bytes 49156
  167.0 4.0 %copy-start.10 = (f32[2,8,256]{2,1,0:T(8,128)S(1)}, f32[2,8,256]{2,1,0:T(8,128)}, u32[]{:S(2)}) copy-start(f32[2,8,256]{2,1,0:T(8,128)} %copy-done.8) | copy-start | bytes 49156
  167.0 4.0 %copy-start.13 = (f32[2,8,256]{2,1,0:T(8,128)S(1)}, f32[2,8,256]{2,1,0:T(8,128)}, u32[]{:S(2)}) copy-start(f32[2,8,256]{2,1,0:T(8,128)} %copy-done.11) | copy-start | bytes 49156
  167.1 3.9 %copy-start.18 = (f32[16,2,1,256]{3,0,2,1:T(8,128)S(1)}, f32[16,2,1,256]{3,0,2,1:T(8,128)}, u32[]{:S(2)}) copy-start(f32[16,2,1,256]{3,0,2,1:T(8,128)} %copy-done.17) | copy-start | bytes 98308
  169.4 1.6 copy-start.2
  169.4 1.7 copy-start.3
  172.8 43.9 %copy-start.24 = (f32[1,16,16]{1,2,0:T(8,128)S(1)}, f32[1,16,16]{1,2,0:T(8,128)}, u32[]{:S(2)}) copy-start(f32[1,16,16]{1,2,0:T(8,128)} %custom-call.23) | copy-start | bytes 3076
  (18 other events, 14.1 us)
where the time goes:
time: 227 us; the launch traced here: 226 us
  blocking collectives  132 us (58%)
  other arithmetic  24.5 us (11%)
  starting transfers between devices  22.4 us (10%)
  matrix products  15.8 us (7%)
  waiting for transfers between devices  15.8 us (7%)
  local copies, waits for them, and re-layouts  13.8 us (6%)
    psum x3, blocking collectives, joint_sum(): return lax.psum(stacked, ('narrow', 'wide'))  132 us
    ppermute x6, waiting for transfers between devices, with_halo(): after = lax.ppermute(first, axis, down)  15.4 us
    ppermute x6, starting transfers between devices, with_halo(): before = lax.ppermute(last, axis, up)  14.7 us
    another operation x15, other arithmetic, solve_gram(): factor = jnp.linalg.cholesky(sym)  10.7 us
    another operation x10, other arithmetic, solve_gram(): lax.linalg.triangular_solve(factor, inner, left_side=True, lower=True, tr...  10.6 us
    unnamed x71, local copies, waits for them, and re-layouts  8.66 us
    ppermute x6, starting transfers between devices, with_halo(): after = lax.ppermute(first, axis, down)  7.73 us
    dot_general x8, matrix products, local_gram(): jnp.einsum('kxyz,lxyz->kl', left, right, precision=lax.Precision.HIGHEST)  4.81 us
  transfers between devices with their start and end apart: 12, of which 7 were waited for; matrix products, arithmetic and copies ran while one was open for 4% of the time, Pallas kernels for 0%

commit v1 on v0

v1 whole, which is shorter than its diff:
```python
import functools

import jax
import jax.numpy as jnp
from jax import lax
from jax.experimental import pallas as pl
from jax.experimental.pallas import tpu as pltpu
from jax.sharding import PartitionSpec as P

ITERS = 3
WELL_RATE = 4.0
VMEM_BYTES = 24 * 1024 * 1024
VMEM = pl.BlockSpec(memory_space=pltpu.VMEM)
SMEM = pl.BlockSpec(memory_space=pltpu.SMEM)
HIGHEST = lax.Precision.HIGHEST


def call(kernel, out_shape, in_specs, *args, flops=0, scratch=()):
    shapes = [jax.ShapeDtypeStruct(shape, jnp.float32) for shape in out_shape]
    size = sum(a.size * a.dtype.itemsize for a in args) + sum(s.size * 4 for s in shapes)
    return pl.pallas_call(
        kernel,
        out_shape=shapes,
        in_specs=in_specs,
        out_specs=[VMEM] * len(shapes),
        scratch_shapes=list(scratch),
        compiler_params=pltpu.CompilerParams(vmem_limit_bytes=VMEM_BYTES),
        cost_estimate=pl.CostEstimate(flops=flops, bytes_accessed=size, transcendentals=0),
    )(*args)


def apply_blocks(value, blocks_ref, col):
    count, layers = value.shape
    parts = []
    size = blocks_ref.shape[-1]
    for b in range(layers // size):
        piece = value[:, b * size : (b + 1) * size]
        high = piece.astype(jnp.bfloat16)
        low = (piece - high.astype(jnp.float32)).astype(jnp.bfloat16)
        both = jnp.concatenate([high, low], axis=0)
        out = jnp.dot(both, blocks_ref[col, b], preferred_element_type=jnp.float32)
        parts.append(out[:count] + out[count:])
    return jnp.concatenate(parts, axis=1)


def write_edges(sides_ref, cols, v_ref, coef_ref, edges):
    cols_x, cols_y = cols
    count = v_ref.shape[1]
    odd_wide, odd_narrow = sides_ref[0], sides_ref[1]
    for slot, (ref, odd) in enumerate(zip(edges, (odd_wide, odd_wide, odd_narrow, odd_narrow))):
        at_low = odd if slot % 2 == 0 else 1 - odd
        number = cols_y if slot < 2 else cols_x
        for i in range(number):
            if slot < 2:
                col = jnp.where(at_low == 1, 0, (cols_x - 1) * cols_y) + i
            else:
                col = i * cols_y + jnp.where(at_low == 1, 0, cols_y - 1)
            ref[i * count : (i + 1) * count, :] = v_ref[col]
            if coef_ref is not None:
                ref[number * count + i : number * count + i + 1, :] = coef_ref[pl.ds(col, 1), :]


def start_kernel(cols, sides_ref, r_ref, coef_ref, blocks_ref, v_ref, *edges):
    for col in range(cols[0] * cols[1]):
        v_ref[col] = apply_blocks(r_ref[col], blocks_ref, col)
    write_edges(sides_ref, cols, v_ref, coef_ref, edges)


def neighbours(sides_ref, cols, count, got, got_coefs):
    cols_x, cols_y = cols
    odd_wide, odd_narrow = sides_ref[0] == 1, sides_ref[1] == 1

    def beyond(v_ref, coef_ref, x, y, step_x, step_y):
        nx, ny = x + step_x, y + step_y
        if 0 <= nx < cols_x and 0 <= ny < cols_y:
            col = nx * cols_y + ny
            return v_ref[col], coef_ref[col : col + 1, :]
        if step_x:
            pair, odd, i, number, low = got[0:2], odd_wide, y, cols_y, step_x < 0
            coefs = got_coefs[0:2]
        else:
            pair, odd, i, number, low = got[2:4], odd_narrow, x, cols_x, step_y < 0
            coefs = got_coefs[2:4]
        first, second = (ref[i * count : (i + 1) * count, :] for ref in pair)
        row = number * count + i
        c_first, c_second = (ref[row : row + 1, :] for ref in coefs)
        if low:
            return jnp.where(odd, first, second), jnp.where(odd, c_first, c_second)
        return jnp.where(odd, second, first), jnp.where(odd, c_second, c_first)

    return beyond


def operate(beyond, cols, v_ref, coef_ref, diag_ref, x, y):
    col = x * cols[1] + y
    center = v_ref[col]
    layers = center.shape[-1]
    coef = coef_ref[col : col + 1, :]
    lane = lax.broadcasted_iota(jnp.int32, (1, layers), 1)
    total = jnp.zeros_like(center)
    for step_x, step_y in ((1, 0), (-1, 0), (0, 1), (0, -1)):
        other, other_coef = beyond(v_ref, coef_ref, x, y, step_x, step_y)
        total = total + other_coef * (center - other)
    upper_coef = jnp.where(lane == layers - 1, 0.0, pltpu.roll(coef, layers - 1, 1))
    lower_coef = jnp.where(lane == 0, 0.0, pltpu.roll(coef, 1, 1))
    total = total + upper_coef * (center - pltpu.roll(center, layers - 1, 1))
    total = total + lower_coef * (center - pltpu.roll(center, 1, 1))
    return diag_ref[col : col + 1, :] * center + coef * total


def step_kernel(cols, sides_ref, v_ref, coef_ref, diag_ref, blocks_ref, *refs):
    got, got_coefs, (w_ref, next_ref), edges = refs[:4], refs[4:8], refs[8:10], refs[10:14]
    count = v_ref.shape[1]
    beyond = neighbours(sides_ref, cols, count, got, got_coefs)
    for x in range(cols[0]):
        for y in range(cols[1]):
            col = x * cols[1] + y
            w = operate(beyond, cols, v_ref, coef_ref, diag_ref, x, y)
            w_ref[col] = w
            next_ref[col] = apply_blocks(w, blocks_ref, col)
    write_edges(sides_ref, cols, next_ref, None, edges)


def gram(left, right):
    return lax.dot_general(
        left, right, (((1,), (1,)), ((), ())), precision=HIGHEST, preferred_element_type=jnp.float32
    )


def gram_kernel(pairs, *refs):
    arrays, out_ref = refs[:-1], refs[-1]
    count = arrays[0].shape[1]
    for slot, (left, right) in enumerate(pairs):
        total = jnp.zeros((count, count), jnp.float32)
        for col in range(arrays[0].shape[0]):
            total = total + gram(arrays[left][col], arrays[right][col])
        out_ref[:, slot * count : (slot + 1) * count] = total


def last_kernel(cols, sides_ref, v_ref, coef_ref, diag_ref, early_ref, late_ref, *refs):
    got, got_coefs, (w_ref, out_ref) = refs[:4], refs[4:8], refs[8:10]
    count = v_ref.shape[1]
    beyond = neighbours(sides_ref, cols, count, got, got_coefs)
    total = jnp.zeros((count, count), jnp.float32)
    for x in range(cols[0]):
        for y in range(cols[1]):
            col = x * cols[1] + y
            w = operate(beyond, cols, v_ref, coef_ref, diag_ref, x, y)
            w_ref[col] = w
            total = total + gram(v_ref[col], w)
    grams = [early_ref[...], late_ref[...], total]
    used = sum(g.shape[1] for g in grams)
    lanes = out_ref.shape[2]
    grams.append(jnp.zeros((count, lanes - used), jnp.float32))
    joint = jnp.concatenate(grams, axis=1)
    for peer in range(out_ref.shape[0]):
        out_ref[peer] = joint


def symmetric(matrix):
    return 0.5 * (matrix + matrix.T)


def solve_spd(matrix, target):
    size = matrix.shape[0]
    rows = lax.broadcasted_iota(jnp.int32, (size, size), 0)
    lanes = lax.broadcasted_iota(jnp.int32, (size, size), 1)
    eye = rows == lanes
    down = lax.rsqrt(jnp.sum(jnp.where(eye, matrix, 0.0), axis=1, keepdims=True))
    across = lax.rsqrt(jnp.sum(jnp.where(eye, matrix, 0.0), axis=0, keepdims=True))
    work = jnp.concatenate([down * matrix * across, down * target], axis=1)
    width = work.shape[1]
    row_ids = lax.broadcasted_iota(jnp.int32, (size, 1), 0)
    for p in range(size):
        pivot_row = work[p : p + 1, :]
        scaled = pivot_row / pivot_row[:, p : p + 1]
        column = work[:, p : p + 1]
        work = jnp.where(row_ids == p, scaled, work - column * scaled)
    return down * work[:, size:width]


def finish_kernel(blocks, sums_ref, r_ref, *refs):
    v_refs, w_refs, (x_ref, out_ref) = refs[:blocks], refs[blocks : 2 * blocks], refs[2 * blocks :]
    count = r_ref.shape[1]
    joint = sums_ref[0]
    for peer in range(1, sums_ref.shape[0]):
        joint = joint + sums_ref[peer]
    moments = [
        symmetric(joint[:, i * count : (i + 1) * count]) for i in range(2 * blocks)
    ]
    matrix = jnp.concatenate(
        [
            jnp.concatenate([moments[1 + i + j] for j in range(blocks)], axis=1)
            for i in range(blocks)
        ],
        axis=0,
    )
    target = jnp.concatenate(moments[:blocks], axis=0)
    coefs = solve_spd(matrix, target).T
    for col in range(r_ref.shape[0]):
        v = jnp.concatenate([ref[col] for ref in v_refs], axis=0)
        w = jnp.concatenate([ref[col] for ref in w_refs], axis=0)
        x_ref[col] = jnp.dot(coefs, v, precision=HIGHEST, preferred_element_type=jnp.float32)
        out_ref[col] = r_ref[col] - jnp.dot(
            coefs, w, precision=HIGHEST, preferred_element_type=jnp.float32
        )


def exchange(edges):
    out = []
    for slot, edge in enumerate(edges):
        axis = "wide" if slot < 2 else "narrow"
        peers = lax.axis_size(axis)
        pairs = [(i, i + 1) for i in range(slot % 2, peers - 1, 2)]
        out.append(lax.ppermute(edge, axis, pairs + [(j, i) for i, j in pairs]))
    return out


def on_device(sources, well_columns, column_active, perm_root, storage_term, inverse_blocks):
    count, cols_x, cols_y, layers = sources.shape
    cols = (cols_x, cols_y)
    number = cols_x * cols_y
    wide, narrow = lax.axis_index("wide"), lax.axis_index("narrow")
    devices = lax.axis_size("narrow") * lax.axis_size("wide")
    grid_y = cols_y * lax.axis_size("narrow")
    column_ids = (
        (wide * cols_x + jnp.arange(cols_x, dtype=jnp.int32))[:, None] * grid_y
        + narrow * cols_y
        + jnp.arange(cols_y, dtype=jnp.int32)[None, :]
    )
    wells = (column_ids.reshape(-1, 1) == well_columns[None]).astype(jnp.float32)
    active = column_active.astype(jnp.float32)[..., None]
    coef = (perm_root * active).reshape(number, layers)
    diag_term = (active * storage_term + (1.0 - active)).reshape(number, layers)
    rhs = jnp.transpose(sources, (1, 2, 0, 3)).reshape(number, count, layers)
    rhs = rhs + WELL_RATE * wells[..., None]
    blocks = inverse_blocks.reshape((number,) + inverse_blocks.shape[2:])
    sides = jnp.stack([wide % 2, narrow % 2]).astype(jnp.int32)
    state = (number, count, layers)
    apply_flops = 4 * count * number * layers * inverse_blocks.shape[-1]
    gram_flops = 12 * count * count * number * layers

    numbers = (cols_y, cols_y, cols_x, cols_x)
    first_edges = [(n * (count + 1), layers) for n in numbers]
    later_edges = [(n * count, layers) for n in numbers]
    v, *edges = call(
        functools.partial(start_kernel, cols),
        [state] + first_edges,
        [SMEM] + [VMEM] * 3,
        sides, rhs, coef, blocks,
        flops=apply_flops,
    )
    vs, ws, grams = [v], [], []
    got_coefs = got = exchange(edges)
    for j in range(1, ITERS):
        w, v, *edges = call(
            functools.partial(step_kernel, cols),
            [state, state] + later_edges,
            [SMEM] + [VMEM] * 12,
            sides, vs[-1], coef, diag_term, blocks, *got, *got_coefs,
            flops=apply_flops,
        )
        vs.append(v)
        ws.append(w)
        got = exchange(edges)
        arrays = [vs[-2], v, w] + ([rhs] if j == 1 else [])
        pairs = ([(0, 3)] if j == 1 else []) + [(0, 2), (1, 2)]
        grams += call(
            functools.partial(gram_kernel, pairs),
            [(count, len(pairs) * count)],
            [VMEM] * len(arrays),
            *arrays,
            flops=len(pairs) * gram_flops,
        )
    lanes = 128
    w, joint = call(
        functools.partial(last_kernel, cols),
        [state, (devices, count, lanes)],
        [SMEM] + [VMEM] * 13,
        sides, vs[-1], coef, diag_term, *grams, *got, *got_coefs,
        flops=gram_flops,
    )
    ws.append(w)
    joint = lax.all_to_all(joint, ("narrow", "wide"), 0, 0)
    outs = call(
        functools.partial(finish_kernel, ITERS),
        [state, state],
        [VMEM] * (2 + 2 * ITERS),
        joint, rhs, *vs, *ws,
        flops=24 * ITERS * count * count * number * layers,
    )
    return tuple(
        jnp.transpose(o.reshape(cols_x, cols_y, count, layers), (2, 0, 1, 3)) for o in outs
    )


def solution(mesh):
    in_specs = (
        P(None, "wide", "narrow", None),
        P(),
        P("wide", "narrow"),
        P("wide", "narrow", None),
        P("wide", "narrow", None),
        P("wide", "narrow", None, None, None),
    )
    out_specs = (P(None, "wide", "narrow", None), P(None, "wide", "narrow", None))
    return jax.shard_map(
        on_device, mesh=mesh, in_specs=in_specs, out_specs=out_specs, check_vma=False
    )
```

time: 227 us -> 61.4 us (0.27)
  blocking collectives: 132 us -> 19.8 us
  other arithmetic: 24.5 us -> 2.5 us
  matrix products: 15.8 us -> 0 us
  waiting for transfers between devices: 15.8 us -> 2.6 us
  Pallas kernels: 0 us -> 12 us
  local copies, waits for them, and re-layouts: 13.8 us -> 2.92 us
    psum x3 -> x0, blocking collectives: 132 us -> none  [joint_sum(): return lax.psum(stacked, ('narrow', 'wide'))]
    another operation x28 -> x1, other arithmetic: 21.4 us -> 0.08 us  [on_device(): sides = jnp.stack([wide % 2, narrow % 2]).astype(jnp.int32)]
    all_to_all x0 -> x1, blocking collectives: none -> 19.8 us  [on_device(): joint = lax.all_to_all(joint, ('narrow', 'wide'), 0, 0)]
    dot_general x29 -> x0, matrix products: 13.9 us -> none  [the longest x8 4.81 us: local_gram(): jnp.einsum('kxyz,lxyz->kl', left, right, precision=lax.Precision.HIGHEST)]
    ppermute x12, waiting for transfers between devices: 15.8 us -> 2.6 us  [exchange(): out.append(lax.ppermute(edge, axis, pairs + [(j, i) for i, j in pairs]))]
    pallas_call x0 -> x7, Pallas kernels: none -> 12 us  [call(): pl.pallas_call(kernel, out_shape=shapes, in_specs=in_specs, out_specs=[VM...]
    unnamed x71 -> x6, local copies, waits for them, and re-layouts: 8.66 us -> 0.63 us
    add x6 -> x3, other arithmetic: 2.92 us -> 0.17 us  [the longest x1 0.1 us: on_device(): rhs = rhs + WELL_RATE * wells[..., None]]
  transfers between devices with their start and end apart: 12 -> 12, of which waited for: 7 -> 2; matrix products, arithmetic and copies ran while one was open for 4% -> 0% of each run, Pallas kernels for 0% -> 3%
where the time goes in v1:
time: 61.4 us; the launch traced here: 61 us
  starting transfers between devices  20.4 us (33%)
  blocking collectives  19.8 us (32%)
  Pallas kernels  12 us (20%)
  local copies, waits for them, and re-layouts  2.92 us (5%)
  waiting for transfers between devices  2.6 us (4%)
  other arithmetic  2.5 us (4%)
  between operations  0.79 us (1%)
    ppermute x12, starting transfers between devices, exchange(): out.append(lax.ppermute(edge, axis, pairs + [(j, i) for i, j in pairs]))  20.4 us
    all_to_all x1, blocking collectives, on_device(): joint = lax.all_to_all(joint, ('narrow', 'wide'), 0, 0)  19.8 us
    pallas_call x7, Pallas kernels, call(): pl.pallas_call(kernel, out_shape=shapes, in_specs=in_specs, out_specs=[VM...  12 us
    ppermute x12, waiting for transfers between devices, exchange(): out.append(lax.ppermute(edge, axis, pairs + [(j, i) for i, j in pairs]))  2.6 us
  transfers between devices with their start and end apart: 12, of which 2 were waited for; matrix products, arithmetic and copies ran while one was open for 0% of the time, Pallas kernels for 3%

profile of v1, /device:TPU:0, one launch (start us, length us, event | category | flops | bytes accessed | tf_op | source)
XLA Modules:
  0.0 61.0 jit_solution(1663955096399441884)
XLA Ops:
  0.7 0.8 %broadcast_subtract_fusion = f32[2,8]{1,0:T(2,128)S(1)} fusion(s32[2,8]{1,0:T(2,128)} %param.8), kind=kLoop, calls=%fused_computation.8 | loop fusion | flops 32 | bytes 128 | tf_op jit(solution)/shard_map/sub | solution.py:234
  1.4 0.7 %convert_element_type.5 = f32[2,8]{1,0:T(2,128)S(1)} convert(s32[2,8]{1,0:T(2,128)} %param.8) | non-fusion elementwise | flops 16 | bytes 128 | tf_op jit(solution)/shard_map/convert_element_type | solution.py:232
  2.3 1.1 %copy.8 = f32[2,8,16,256]{3,2,1,0:T(8,128)S(1)} copy(f32[2,8,16,256]{3,1,0,2:T(8,128)} %bitcast.21) | data formatting | bytes 524288 | tf_op jit(solution)/shard_map/transpose | solution.py:235
  3.5 0.7 %compare_select_fusion = f32[16,16]{1,0:T(8,128)S(1)} fusion(s32[16]{0:T(128)} %param.7, s32[16]{0:T(128)S(1)} %add.73), kind=kLoop, calls=%fused_computation.5 | loop fusion | flops 512 | bytes 1152 | tf_op jit(solution)/shard_map/mul | solution.py:236
  5.0 0.9 %shard_map.77 = (f32[16,16,256]{2,1,0:T(8,128)S(1)}, f32[136,256]{1,0:T(8,128)S(1)}, f32[136,256]{1,0:T(8,128)S(1)}, f32[34,256]{1,0:T(8,128)S(1)}, f32[34,256]{1,0:T(8,128)S(1)}) custom-call(s32[2]{0:T(128)S(1)} %pad_add_fusion.sides_ref, f32[16,16,256]{2,1,0:T(8,128)S(1)} %bitcast_add_fusion.r_ref.refs_3_, f32[16,256]{1,0:T(8,128)S(1)} %get-tuple-element.45.coef_ref, ...), custom_call_target="tpu_custom_call" | custom-call | flops 33554432 | bytes 1937416 | tf_op jit(solution)/shard_map/pallas_call | solution.py:21
  6.5 0.7 %collective-permute-start.1 = (f32[136,256]{1,0:T(8,128)S(1)}, f32[136,256]{1,0:T(8,128)S(1)}, u32[]{:S(2)}, u32[]{:S(2)}) collective-permute-start(f32[136,256]{1,0:T(8,128)S(1)} %get-tuple-element.25), channel_id=1, source_target_pairs={{1,2},{3,4},{5,6},{2,1},{4,3},{6,5},{9,10},{11,12},{13,14},{10,9},... | collective-permute-start | bytes 417800 | tf_op jit(solution)/shard_map/ppermute | solution.py:215
  7.1 2.7 %collective-permute-start.2 = (f32[34,256]{1,0:T(8,128)S(1)}, f32[34,256]{1,0:T(8,128)S(1)}, u32[]{:S(2)}, u32[]{:S(2)}) collective-permute-start(f32[34,256]{1,0:T(8,128)S(1)} %get-tuple-element.26), channel_id=1, source_target_pairs={{0,8},{16,24},{8,0},{24,16},{1,9},{17,25},{9,1},{25,17},{2,10},{18... | collective-permute-start | bytes 104456 | tf_op jit(solution)/shard_map/ppermute | solution.py:215
  9.8 0.7 %collective-permute-start.3 = (f32[34,256]{1,0:T(8,128)S(1)}, f32[34,256]{1,0:T(8,128)S(1)}, u32[]{:S(2)}, u32[]{:S(2)}) collective-permute-start(f32[34,256]{1,0:T(8,128)S(1)} %get-tuple-element.27), channel_id=1, source_target_pairs={{8,16},{16,8},{9,17},{17,9},{10,18},{18,10},{11,19},{19,11},{12,20... | collective-permute-start | bytes 104456 | tf_op jit(solution)/shard_map/ppermute | solution.py:215
  10.4 1.3 %collective-permute-done.2.refs_2_.refs_6_ = f32[34,256]{1,0:T(8,128)S(1)} collective-permute-done((f32[34,256]{1,0:T(8,128)S(1)}, f32[34,256]{1,0:T(8,128)S(1)}, u32[]{:S(2)}, u32[]{:S(2)}) %collective-permute-start.2) | collective-permute-done | bytes 34848 | tf_op jit(solution)/shard_map/ppermute | solution.py:215
  11.8 1.1 %shard_map.78 = (f32[16,16,256]{2,1,0:T(8,128)S(1)}, f32[16,16,256]{2,1,0:T(8,128)S(1)}, f32[128,256]{1,0:T(8,128)S(1)}, f32[128,256]{1,0:T(8,128)S(1)}, f32[32,256]{1,0:T(8,128)S(1)}, /*index=5*/f32[32,256]{1,0:T(8,128)S(1)}) custom-call(s32[2]{0:T(128)S(1)} %pad_add_fusion.sides_ref, f32[16,16,256]{2,1,0:T(8,128)S(1)} %get-tuple-element.23.v_ref.refs_0_, ...), custom_call_target="tpu_custom_call" | custom-call | flops 33554432 | bytes 2891784 | tf_op jit(solution)/shard_map/pallas_call | solution.py:21
  12.8 2.6 %collective-permute-start.4 = (f32[128,256]{1,0:T(8,128)S(1)}, f32[128,256]{1,0:T(8,128)S(1)}, u32[]{:S(2)}, u32[]{:S(2)}) collective-permute-start(f32[128,256]{1,0:T(8,128)S(1)} %get-tuple-element.29), channel_id=1, source_target_pairs={{0,1},{2,3},{4,5},{6,7},{1,0},{3,2},{5,4},{7,6},{8,9},{10,11},{12,... | collective-permute-start | bytes 393224 | tf_op jit(solution)/shard_map/ppermute | solution.py:215
  15.4 0.7 %collective-permute-start.5 = (f32[128,256]{1,0:T(8,128)S(1)}, f32[128,256]{1,0:T(8,128)S(1)}, u32[]{:S(2)}, u32[]{:S(2)}) collective-permute-start(f32[128,256]{1,0:T(8,128)S(1)} %get-tuple-element.30), channel_id=1, source_target_pairs={{1,2},{3,4},{5,6},{2,1},{4,3},{6,5},{9,10},{11,12},{13,14},{10,9},... | collective-permute-start | bytes 393224 | tf_op jit(solution)/shard_map/ppermute | solution.py:215
  16.1 4.3 %collective-permute-start.6 = (f32[32,256]{1,0:T(8,128)S(1)}, f32[32,256]{1,0:T(8,128)S(1)}, u32[]{:S(2)}, u32[]{:S(2)}) collective-permute-start(f32[32,256]{1,0:T(8,128)S(1)} %get-tuple-element.31), channel_id=1, source_target_pairs={{0,8},{16,24},{8,0},{24,16},{1,9},{17,25},{9,1},{25,17},{2,10},{18... | collective-permute-start | bytes 98312 | tf_op jit(solution)/shard_map/ppermute | solution.py:215
  21.0 1.2 %collective-permute-done.6.refs_2_ = f32[32,256]{1,0:T(8,128)S(1)} collective-permute-done((f32[32,256]{1,0:T(8,128)S(1)}, f32[32,256]{1,0:T(8,128)S(1)}, u32[]{:S(2)}, u32[]{:S(2)}) %collective-permute-start.6) | collective-permute-done | bytes 32800 | tf_op jit(solution)/shard_map/ppermute | solution.py:215
  22.3 1.1 %shard_map.79 = (f32[16,16,256]{2,1,0:T(8,128)S(1)}, f32[16,16,256]{2,1,0:T(8,128)S(1)}, f32[128,256]{1,0:T(8,128)S(1)}, f32[128,256]{1,0:T(8,128)S(1)}, f32[32,256]{1,0:T(8,128)S(1)}, /*index=5*/f32[32,256]{1,0:T(8,128)S(1)}) custom-call(s32[2]{0:T(128)S(1)} %pad_add_fusion.sides_ref, f32[16,16,256]{2,1,0:T(8,128)S(1)} %get-tuple-element.28.v_ref.refs_1_.refs_0_, ...), custom_call_target="tpu_custom_call" | custom-call | flops 33554432 | bytes 2871304 | tf_op jit(solution)/shard_map/pallas_call | solution.py:21
  23.3 2.7 %collective-permute-start.8 = (f32[128,256]{1,0:T(8,128)S(1)}, f32[128,256]{1,0:T(8,128)S(1)}, u32[]{:S(2)}, u32[]{:S(2)}) collective-permute-start(f32[128,256]{1,0:T(8,128)S(1)} %get-tuple-element.36), channel_id=1, source_target_pairs={{0,1},{2,3},{4,5},{6,7},{1,0},{3,2},{5,4},{7,6},{8,9},{10,11},{12,... | collective-permute-start | bytes 393224 | tf_op jit(solution)/shard_map/ppermute | solution.py:215
  26.1 0.7 %collective-permute-start.9 = (f32[128,256]{1,0:T(8,128)S(1)}, f32[128,256]{1,0:T(8,128)S(1)}, u32[]{:S(2)}, u32[]{:S(2)}) collective-permute-start(f32[128,256]{1,0:T(8,128)S(1)} %get-tuple-element.37), channel_id=1, source_target_pairs={{1,2},{3,4},{5,6},{2,1},{4,3},{6,5},{9,10},{11,12},{13,14},{10,9},... | collective-permute-start | bytes 393224 | tf_op jit(solution)/shard_map/ppermute | solution.py:215
  26.7 3.7 %collective-permute-start.10 = (f32[32,256]{1,0:T(8,128)S(1)}, f32[32,256]{1,0:T(8,128)S(1)}, u32[]{:S(2)}, u32[]{:S(2)}) collective-permute-start(f32[32,256]{1,0:T(8,128)S(1)} %get-tuple-element.38), channel_id=1, source_target_pairs={{0,8},{16,24},{8,0},{24,16},{1,9},{17,25},{9,1},{25,17},{2,10},{18... | collective-permute-start | bytes 98312 | tf_op jit(solution)/shard_map/ppermute | solution.py:215
  31.1 1.2 %shard_map.80.early_ref = f32[16,48]{1,0:T(8,128)S(1)} custom-call(f32[16,16,256]{2,1,0:T(8,128)S(1)} %get-tuple-element.23.v_ref.refs_0_, f32[16,16,256]{2,1,0:T(8,128)S(1)} %get-tuple-element.28.v_ref.refs_1_.refs_0_, f32[16,16,256]{2,1,0:T(8,128)S(1)} %get-tuple-element.34.refs_2_.refs_3_, f32[16,16,256]{2,1,0:T(8,128)S(1)} %bitcast_add_fusion.r_ref.refs_3_), custom_call_target="tpu_custom_call" | custom-call | flops 37748736 | bytes 1051648 | tf_op jit(solution)/shard_map/pallas_call | solution.py:21
  32.3 0.8 %shard_map.81.late_ref = f32[16,32]{1,0:T(8,128)S(1)} custom-call(f32[16,16,256]{2,1,0:T(8,128)S(1)} %get-tuple-element.28.v_ref.refs_1_.refs_0_, f32[16,16,256]{2,1,0:T(8,128)S(1)} %get-tuple-element.33.refs_1_.v_ref.refs_2_, f32[16,16,256]{2,1,0:T(8,128)S(1)} %get-tuple-element.35.refs_2_.refs_4_), custom_call_target="tpu_custom_call" | custom-call | flops 25165824 | bytes 788480 | tf_op jit(solution)/shard_map/pallas_call | solution.py:21
  33.2 1.3 %shard_map.82 = (f32[16,16,256]{2,1,0:T(8,128)S(1)}, f32[32,16,128]{2,1,0:T(8,128)S(1)}) custom-call(s32[2]{0:T(128)S(1)} %pad_add_fusion.sides_ref, f32[16,16,256]{2,1,0:T(8,128)S(1)} %get-tuple-element.33.refs_1_.v_ref.refs_2_, f32[16,256]{1,0:T(8,128)S(1)} %get-tuple-element.45.coef_ref, f32[16,256]{1,0:T(8,128)S(1)} %get-tuple-element.44.diag_ref, ...), custom_call_target="tpu_custom_call" | custom-call | flops 12582912 | bytes 1500168 | tf_op jit(solution)/shard_map/pallas_call | solution.py:21
  34.5 19.8 %all_to_all.5.sums_ref = f32[32,16,128]{2,1,0:T(8,128)S(1)} all-to-all(f32[32,16,128]{2,1,0:T(8,128)S(1)} %get-tuple-element.40), channel_id=1, replica_groups=mesh['narrow'=4,'wide'=8] {'narrow','wide'}, dimensions={0} | all-to-all | bytes 524288 | tf_op jit(solution)/shard_map/all_to_all | solution.py:284
  54.3 5.6 %shard_map.83 = (f32[16,16,256]{2,1,0:T(8,128)S(1)}, f32[16,16,256]{2,1,0:T(8,128)S(1)}) custom-call(f32[32,16,128]{2,1,0:T(8,128)S(1)} %all_to_all.5.sums_ref, f32[16,16,256]{2,1,0:T(8,128)S(1)} %bitcast_add_fusion.r_ref.refs_3_, f32[16,16,256]{2,1,0:T(8,128)S(1)} %get-tuple-element.23.v_ref.refs_0_, ...), custom_call_target="tpu_custom_call" | custom-call | flops 75497472 | bytes 2621440 | tf_op jit(solution)/shard_map/pallas_call | solution.py:21
  59.9 1.1 %copy_bitcast_fusion = (f32[16,2,8,256]{3,2,1,0:T(8,128)}, f32[16,2,8,256]{3,2,1,0:T(8,128)}) fusion(f32[2,8,16,256]{3,2,1,0:T(8,128)S(1)} %bitcast.20, f32[2,8,16,256]{3,2,1,0:T(8,128)S(1)} %bitcast.19), kind=kLoop, calls=%fused_computation.1 | loop fusion | bytes 1048576 | tf_op jit(solution)/shard_map/transpose | solution.py:293
  (25 shorter events, 2.9 us)
Async XLA Ops:
  0.6 4.4 %copy-start = (bf16[2,8,2,128,128]{4,3,2,1,0:T(8,128)(2,1)S(1)}, bf16[2,8,2,128,128]{4,3,2,1,0:T(8,128)(2,1)}, u32[]{:S(2)}) copy-start(bf16[2,8,2,128,128]{4,3,2,1,0:T(8,128)(2,1)} %param.11) | copy-start | bytes 3145732
  4.2 0.7 %copy-start.1 = (f32[2,8,256]{2,1,0:T(8,128)S(1)}, f32[2,8,256]{2,1,0:T(8,128)}, u32[]{:S(2)}) copy-start(f32[2,8,256]{2,1,0:T(8,128)} %param.10) | copy-start | bytes 49156
  4.2 0.7 %copy-start.2 = (f32[2,8,256]{2,1,0:T(8,128)S(1)}, f32[2,8,256]{2,1,0:T(8,128)}, u32[]{:S(2)}) copy-start(f32[2,8,256]{2,1,0:T(8,128)} %param.9) | copy-start | bytes 49156
  5.9 5.8 %collective-permute-start = (f32[136,256]{1,0:T(8,128)S(1)}, f32[136,256]{1,0:T(8,128)S(1)}, u32[]{:S(2)}, u32[]{:S(2)}) collective-permute-start(f32[136,256]{1,0:T(8,128)S(1)} %get-tuple-element.24), channel_id=1, source_target_pairs={{0,1},{2,3},{4,5},{6,7},{1,0},{3,2},{5,4},{7,6},{8,9},{10,11},{12,... | collective-permute-start | bytes 417800 | tf_op jit(solution)/shard_map/ppermute | solution.py:215
  6.5 5.3 %collective-permute-start.1 = (f32[136,256]{1,0:T(8,128)S(1)}, f32[136,256]{1,0:T(8,128)S(1)}, u32[]{:S(2)}, u32[]{:S(2)}) collective-permute-start(f32[136,256]{1,0:T(8,128)S(1)} %get-tuple-element.25), channel_id=1, source_target_pairs={{1,2},{3,4},{5,6},{2,1},{4,3},{6,5},{9,10},{11,12},{13,14},{10,9},... | collective-permute-start | bytes 417800 | tf_op jit(solution)/shard_map/ppermute | solution.py:215
  7.1 4.6 %collective-permute-start.2 = (f32[34,256]{1,0:T(8,128)S(1)}, f32[34,256]{1,0:T(8,128)S(1)}, u32[]{:S(2)}, u32[]{:S(2)}) collective-permute-start(f32[34,256]{1,0:T(8,128)S(1)} %get-tuple-element.26), channel_id=1, source_target_pairs={{0,8},{16,24},{8,0},{24,16},{1,9},{17,25},{9,1},{25,17},{2,10},{18... | collective-permute-start | bytes 104456 | tf_op jit(solution)/shard_map/ppermute | solution.py:215
  9.8 2.0 %collective-permute-start.3 = (f32[34,256]{1,0:T(8,128)S(1)}, f32[34,256]{1,0:T(8,128)S(1)}, u32[]{:S(2)}, u32[]{:S(2)}) collective-permute-start(f32[34,256]{1,0:T(8,128)S(1)} %get-tuple-element.27), channel_id=1, source_target_pairs={{8,16},{16,8},{9,17},{17,9},{10,18},{18,10},{11,19},{19,11},{12,20... | collective-permute-start | bytes 104456 | tf_op jit(solution)/shard_map/ppermute | solution.py:215
  12.8 9.4 %collective-permute-start.4 = (f32[128,256]{1,0:T(8,128)S(1)}, f32[128,256]{1,0:T(8,128)S(1)}, u32[]{:S(2)}, u32[]{:S(2)}) collective-permute-start(f32[128,256]{1,0:T(8,128)S(1)} %get-tuple-element.29), channel_id=1, source_target_pairs={{0,1},{2,3},{4,5},{6,7},{1,0},{3,2},{5,4},{7,6},{8,9},{10,11},{12,... | collective-permute-start | bytes 393224 | tf_op jit(solution)/shard_map/ppermute | solution.py:215
  15.4 6.8 %collective-permute-start.5 = (f32[128,256]{1,0:T(8,128)S(1)}, f32[128,256]{1,0:T(8,128)S(1)}, u32[]{:S(2)}, u32[]{:S(2)}) collective-permute-start(f32[128,256]{1,0:T(8,128)S(1)} %get-tuple-element.30), channel_id=1, source_target_pairs={{1,2},{3,4},{5,6},{2,1},{4,3},{6,5},{9,10},{11,12},{13,14},{10,9},... | collective-permute-start | bytes 393224 | tf_op jit(solution)/shard_map/ppermute | solution.py:215
  16.1 6.2 %collective-permute-start.6 = (f32[32,256]{1,0:T(8,128)S(1)}, f32[32,256]{1,0:T(8,128)S(1)}, u32[]{:S(2)}, u32[]{:S(2)}) collective-permute-start(f32[32,256]{1,0:T(8,128)S(1)} %get-tuple-element.31), channel_id=1, source_target_pairs={{0,8},{16,24},{8,0},{24,16},{1,9},{17,25},{9,1},{25,17},{2,10},{18... | collective-permute-start | bytes 98312 | tf_op jit(solution)/shard_map/ppermute | solution.py:215
  20.4 1.9 %collective-permute-start.7 = (f32[32,256]{1,0:T(8,128)S(1)}, f32[32,256]{1,0:T(8,128)S(1)}, u32[]{:S(2)}, u32[]{:S(2)}) collective-permute-start(f32[32,256]{1,0:T(8,128)S(1)} %get-tuple-element.32), channel_id=1, source_target_pairs={{8,16},{16,8},{9,17},{17,9},{10,18},{18,10},{11,19},{19,11},{12,20... | collective-permute-start | bytes 98312 | tf_op jit(solution)/shard_map/ppermute | solution.py:215
  23.3 9.8 %collective-permute-start.8 = (f32[128,256]{1,0:T(8,128)S(1)}, f32[128,256]{1,0:T(8,128)S(1)}, u32[]{:S(2)}, u32[]{:S(2)}) collective-permute-start(f32[128,256]{1,0:T(8,128)S(1)} %get-tuple-element.36), channel_id=1, source_target_pairs={{0,1},{2,3},{4,5},{6,7},{1,0},{3,2},{5,4},{7,6},{8,9},{10,11},{12,... | collective-permute-start | bytes 393224 | tf_op jit(solution)/shard_map/ppermute | solution.py:215
  26.1 7.1 %collective-permute-start.9 = (f32[128,256]{1,0:T(8,128)S(1)}, f32[128,256]{1,0:T(8,128)S(1)}, u32[]{:S(2)}, u32[]{:S(2)}) collective-permute-start(f32[128,256]{1,0:T(8,128)S(1)} %get-tuple-element.37), channel_id=1, source_target_pairs={{1,2},{3,4},{5,6},{2,1},{4,3},{6,5},{9,10},{11,12},{13,14},{10,9},... | collective-permute-start | bytes 393224 | tf_op jit(solution)/shard_map/ppermute | solution.py:215
  26.7 6.4 %collective-permute-start.10 = (f32[32,256]{1,0:T(8,128)S(1)}, f32[32,256]{1,0:T(8,128)S(1)}, u32[]{:S(2)}, u32[]{:S(2)}) collective-permute-start(f32[32,256]{1,0:T(8,128)S(1)} %get-tuple-element.38), channel_id=1, source_target_pairs={{0,8},{16,24},{8,0},{24,16},{1,9},{17,25},{9,1},{25,17},{2,10},{18... | collective-permute-start | bytes 98312 | tf_op jit(solution)/shard_map/ppermute | solution.py:215
  30.4 2.7 %collective-permute-start.11 = (f32[32,256]{1,0:T(8,128)S(1)}, f32[32,256]{1,0:T(8,128)S(1)}, u32[]{:S(2)}, u32[]{:S(2)}) collective-permute-start(f32[32,256]{1,0:T(8,128)S(1)} %get-tuple-element.39), channel_id=1, source_target_pairs={{8,16},{16,8},{9,17},{17,9},{10,18},{18,10},{11,19},{19,11},{12,20... | collective-permute-start | bytes 98312 | tf_op jit(solution)/shard_map/ppermute | solution.py:215

commit v2 on v1

--- a/solution.py
+++ b/solution.py
@@ -12,7 +12,6 @@
 VMEM_BYTES = 24 * 1024 * 1024
 VMEM = pl.BlockSpec(memory_space=pltpu.VMEM)
 SMEM = pl.BlockSpec(memory_space=pltpu.SMEM)
-HIGHEST = lax.Precision.HIGHEST
 
 
 def call(kernel, out_shape, in_specs, *args, flops=0, scratch=()):
@@ -29,15 +28,17 @@
     )(*args)
 
 
+def split(value):
+    high = value.astype(jnp.bfloat16)
+    return high, (value - high.astype(jnp.float32)).astype(jnp.bfloat16)
+
+
 def apply_blocks(value, blocks_ref, col):
     count, layers = value.shape
     parts = []
     size = blocks_ref.shape[-1]
     for b in range(layers // size):
-        piece = value[:, b * size : (b + 1) * size]
-        high = piece.astype(jnp.bfloat16)
-        low = (piece - high.astype(jnp.float32)).astype(jnp.bfloat16)
-        both = jnp.concatenate([high, low], axis=0)
+        both = jnp.concatenate(split(value[:, b * size : (b + 1) * size]), axis=0)
         out = jnp.dot(both, blocks_ref[col, b], preferred_element_type=jnp.float32)
         parts.append(out[:count] + out[count:])
     return jnp.concatenate(parts, axis=1)
@@ -46,8 +47,8 @@
 def write_edges(sides_ref, cols, v_ref, coef_ref, edges):
     cols_x, cols_y = cols
     count = v_ref.shape[1]
-    odd_wide, odd_narrow = sides_ref[0], sides_ref[1]
-    for slot, (ref, odd) in enumerate(zip(edges, (odd_wide, odd_wide, odd_narrow, odd_narrow))):
+    for slot, ref in enumerate(edges):
+        odd = sides_ref[slot // 2]
         at_low = odd if slot % 2 == 0 else 1 - odd
         number = cols_y if slot < 2 else cols_x
         for i in range(number):
@@ -60,15 +61,32 @@
                 ref[number * count + i : number * count + i + 1, :] = coef_ref[pl.ds(col, 1), :]
 
 
-def start_kernel(cols, sides_ref, r_ref, coef_ref, blocks_ref, v_ref, *edges):
-    for col in range(cols[0] * cols[1]):
-        v_ref[col] = apply_blocks(r_ref[col], blocks_ref, col)
+def start_kernel(
+    cols, sides_ref, wells_ref, active_ref, sources_ref, perm_ref, storage_ref, blocks_ref,
+    r_ref, v_ref, coef_ref, diag_ref, *edges,
+):
+    cols_x, cols_y = cols
+    _, count, layers = r_ref.shape
+    row = lax.broadcasted_iota(jnp.int32, (count, layers), 0)
+    wells = jnp.zeros((count, layers), jnp.int32)
+    for k in range(count):
+        wells = jnp.where(row == k, wells_ref[k], wells)
+    for x in range(cols_x):
+        across = jnp.transpose(sources_ref[:, x], (1, 0, 2))
+        for y in range(cols_y):
+            col = x * cols_y + y
+            active = active_ref[x, y].astype(jnp.float32)
+            coef_ref[col : col + 1, :] = active * perm_ref[col : col + 1, :]
+            diag_ref[col : col + 1, :] = active * storage_ref[col : col + 1, :] + (1.0 - active)
+            column_id = sides_ref[6] + x * sides_ref[7] + y
+            r = across[y] + jnp.where(wells == column_id, WELL_RATE, 0.0)
+            r_ref[col] = r
+            v_ref[col] = apply_blocks(r, blocks_ref, col)
     write_edges(sides_ref, cols, v_ref, coef_ref, edges)
 
 
 def neighbours(sides_ref, cols, count, got, got_coefs):
     cols_x, cols_y = cols
-    odd_wide, odd_narrow = sides_ref[0] == 1, sides_ref[1] == 1
 
     def beyond(v_ref, coef_ref, x, y, step_x, step_y):
         nx, ny = x + step_x, y + step_y
@@ -76,17 +94,21 @@
             col = nx * cols_y + ny
             return v_ref[col], coef_ref[col : col + 1, :]
         if step_x:
-            pair, odd, i, number, low = got[0:2], odd_wide, y, cols_y, step_x < 0
-            coefs = got_coefs[0:2]
+            axis, i, number, low = 0, y, cols_y, step_x < 0
         else:
-            pair, odd, i, number, low = got[2:4], odd_narrow, x, cols_x, step_y < 0
-            coefs = got_coefs[2:4]
-        first, second = (ref[i * count : (i + 1) * count, :] for ref in pair)
+            axis, i, number, low = 1, x, cols_x, step_y < 0
+        odd = sides_ref[axis] == 1
+        inside = sides_ref[2 + 2 * axis + (0 if low else 1)].astype(jnp.float32)
+        first, second = (
+            ref[i * count : (i + 1) * count, :] for ref in got[2 * axis : 2 * axis + 2]
+        )
         row = number * count + i
-        c_first, c_second = (ref[row : row + 1, :] for ref in coefs)
+        c_first, c_second = (ref[row : row + 1, :] for ref in got_coefs[2 * axis : 2 * axis + 2])
         if low:
-            return jnp.where(odd, first, second), jnp.where(odd, c_first, c_second)
-        return jnp.where(odd, second, first), jnp.where(odd, c_second, c_first)
+            value, coef = jnp.where(odd, first, second), jnp.where(odd, c_first, c_second)
+        else:
+            value, coef = jnp.where(odd, second, first), jnp.where(odd, c_second, c_first)
+        return value, coef * inside
 
     return beyond
 
@@ -121,44 +143,86 @@
     write_edges(sides_ref, cols, next_ref, None, edges)
 
 
-def gram(left, right):
+def split_gram(left, right):
     return lax.dot_general(
-        left, right, (((1,), (1,)), ((), ())), precision=HIGHEST, preferred_element_type=jnp.float32
-    )
+        jnp.concatenate(split(left), axis=0),
+        jnp.concatenate(split(right), axis=0),
+        (((1,), (1,)), ((), ())),
+        preferred_element_type=jnp.float32,
+    )
+
+
+def fold(total):
+    count = total.shape[0] // 2
+    total = total[:count] + total[count:]
+    total = total[:, :count] + total[:, count:]
+    return 0.5 * (total + total.T)
 
 
 def gram_kernel(pairs, *refs):
     arrays, out_ref = refs[:-1], refs[-1]
     count = arrays[0].shape[1]
     for slot, (left, right) in enumerate(pairs):
-        total = jnp.zeros((count, count), jnp.float32)
+        total = jnp.zeros((2 * count, 2 * count), jnp.float32)
         for col in range(arrays[0].shape[0]):
-            total = total + gram(arrays[left][col], arrays[right][col])
-        out_ref[:, slot * count : (slot + 1) * count] = total
+            total = total + split_gram(arrays[left][col], arrays[right][col])
+        out_ref[:, slot * count : (slot + 1) * count] = fold(total)
+
+
+def pack(squares):
+    count = squares[0].shape[0]
+    row = lax.broadcasted_iota(jnp.int32, (count, count), 0)
+    lane = lax.broadcasted_iota(jnp.int32, (count, count), 1)
+    halves = [
+        jnp.where(row >= lane, first, second)
+        for first, second in zip(squares[0::2], squares[1::2])
+    ]
+    diagonals = [
+        jnp.sum(jnp.where(row == lane, second, 0.0), axis=1, keepdims=True)
+        for second in squares[1::2]
+    ]
+    used = len(halves) * (count + 1)
+    packed = jnp.concatenate(
+        halves + diagonals + [jnp.zeros((count, 64 - used), jnp.float32)], axis=1
+    )
+    return jnp.concatenate([packed[: count // 2], packed[count // 2 :]], axis=1)
+
+
+def unpack(packed, number):
+    count = 2 * packed.shape[0]
+    packed = jnp.concatenate([packed[:, :64], packed[:, 64:]], axis=0)
+    row = lax.broadcasted_iota(jnp.int32, (count, count), 0)
+    lane = lax.broadcasted_iota(jnp.int32, (count, count), 1)
+    squares = []
+    for i in range(number // 2):
+        half = packed[:, i * count : (i + 1) * count]
+        place = number // 2 * count + i
+        turned = half.T
+        squares.append(jnp.where(row >= lane, half, turned))
+        second = jnp.where(row <= lane, half, turned)
+        squares.append(jnp.where(row == lane, packed[:, place : place + 1], second))
+    return squares
 
 
 def last_kernel(cols, sides_ref, v_ref, coef_ref, diag_ref, early_ref, late_ref, *refs):
     got, got_coefs, (w_ref, out_ref) = refs[:4], refs[4:8], refs[8:10]
     count = v_ref.shape[1]
     beyond = neighbours(sides_ref, cols, count, got, got_coefs)
-    total = jnp.zeros((count, count), jnp.float32)
+    total = jnp.zeros((2 * count, 2 * count), jnp.float32)
     for x in range(cols[0]):
         for y in range(cols[1]):
             col = x * cols[1] + y
             w = operate(beyond, cols, v_ref, coef_ref, diag_ref, x, y)
             w_ref[col] = w
-            total = total + gram(v_ref[col], w)
-    grams = [early_ref[...], late_ref[...], total]
-    used = sum(g.shape[1] for g in grams)
-    lanes = out_ref.shape[2]
-    grams.append(jnp.zeros((count, lanes - used), jnp.float32))
-    joint = jnp.concatenate(grams, axis=1)
+            total = total + split_gram(v_ref[col], w)
+    squares = [
+        ref[:, i * count : (i + 1) * count]
+        for ref in (early_ref, late_ref)
+        for i in range(ref.shape[1] // count)
+    ]
+    packed = pack(squares + [fold(total)])
     for peer in range(out_ref.shape[0]):
-        out_ref[peer] = joint
-
-
-def symmetric(matrix):
-    return 0.5 * (matrix + matrix.T)
+        out_ref[peer] = packed
 
 
 def solve_spd(matrix, target):
@@ -181,13 +245,11 @@
 
 def finish_kernel(blocks, sums_ref, r_ref, *refs):
     v_refs, w_refs, (x_ref, out_ref) = refs[:blocks], refs[blocks : 2 * blocks], refs[2 * blocks :]
-    count = r_ref.shape[1]
+    cols_x, cols_y = x_ref.shape[1:3]
     joint = sums_ref[0]
     for peer in range(1, sums_ref.shape[0]):
         joint = joint + sums_ref[peer]
-    moments = [
-        symmetric(joint[:, i * count : (i + 1) * count]) for i in range(2 * blocks)
-    ]
+    moments = unpack(joint, 2 * blocks)
     matrix = jnp.concatenate(
         [
             jnp.concatenate([moments[1 + i + j] for j in range(blocks)], axis=1)
@@ -197,12 +259,22 @@
     )
     target = jnp.concatenate(moments[:blocks], axis=0)
     coefs = solve_spd(matrix, target).T
-    for col in range(r_ref.shape[0]):
-        v = jnp.concatenate([ref[col] for ref in v_refs], axis=0)
-        w = jnp.concatenate([ref[col] for ref in w_refs], axis=0)
-        x_ref[col] = jnp.dot(coefs, v, precision=HIGHEST, preferred_element_type=jnp.float32)
-        out_ref[col] = r_ref[col] - jnp.dot(
-            coefs, w, precision=HIGHEST, preferred_element_type=jnp.float32
+    high, rest = coefs.astype(jnp.bfloat16), coefs - coefs.astype(jnp.bfloat16).astype(jnp.float32)
+    middle, low = split(rest)
+    left = jnp.concatenate([high, high, middle, middle, low], axis=1)
+
+    def combine(values, col):
+        highs, lows = zip(*(split(ref[col]) for ref in values))
+        right = jnp.concatenate(highs + lows + highs + lows + highs, axis=0)
+        return jnp.dot(left, right, preferred_element_type=jnp.float32)
+
+    for x in range(cols_x):
+        columns = range(x * cols_y, (x + 1) * cols_y)
+        x_ref[:, x] = jnp.transpose(
+            jnp.stack([combine(v_refs, col) for col in columns]), (1, 0, 2)
+        )
+        out_ref[:, x] = jnp.transpose(
+            jnp.stack([r_ref[col] - combine(w_refs, col) for col in columns]), (1, 0, 2)
         )
 
 
@@ -211,7 +283,7 @@
     for slot, edge in enumerate(edges):
         axis = "wide" if slot < 2 else "narrow"
         peers = lax.axis_size(axis)
-        pairs = [(i, i + 1) for i in range(slot % 2, peers - 1, 2)]
+        pairs = [(i, (i + 1) % peers) for i in range(slot % 2, peers, 2)]
         out.append(lax.ppermute(edge, axis, pairs + [(j, i) for i, j in pairs]))
     return out
 
@@ -221,33 +293,39 @@
     cols = (cols_x, cols_y)
     number = cols_x * cols_y
     wide, narrow = lax.axis_index("wide"), lax.axis_index("narrow")
-    devices = lax.axis_size("narrow") * lax.axis_size("wide")
-    grid_y = cols_y * lax.axis_size("narrow")
-    column_ids = (
-        (wide * cols_x + jnp.arange(cols_x, dtype=jnp.int32))[:, None] * grid_y
-        + narrow * cols_y
-        + jnp.arange(cols_y, dtype=jnp.int32)[None, :]
-    )
-    wells = (column_ids.reshape(-1, 1) == well_columns[None]).astype(jnp.float32)
-    active = column_active.astype(jnp.float32)[..., None]
-    coef = (perm_root * active).reshape(number, layers)
-    diag_term = (active * storage_term + (1.0 - active)).reshape(number, layers)
-    rhs = jnp.transpose(sources, (1, 2, 0, 3)).reshape(number, count, layers)
-    rhs = rhs + WELL_RATE * wells[..., None]
+    peers_x, peers_y = lax.axis_size("wide"), lax.axis_size("narrow")
+    grid_y = cols_y * peers_y
+    sides = jnp.stack(
+        [
+            wide % 2,
+            narrow % 2,
+            (wide > 0).astype(jnp.int32),
+            (wide < peers_x - 1).astype(jnp.int32),
+            (narrow > 0).astype(jnp.int32),
+            (narrow < peers_y - 1).astype(jnp.int32),
+            wide * cols_x * grid_y + narrow * cols_y,
+            jnp.full((), grid_y, jnp.int32),
+        ]
+    ).astype(jnp.int32)
     blocks = inverse_blocks.reshape((number,) + inverse_blocks.shape[2:])
-    sides = jnp.stack([wide % 2, narrow % 2]).astype(jnp.int32)
-    state = (number, count, layers)
+    state, rows = (number, count, layers), (number, layers)
     apply_flops = 4 * count * number * layers * inverse_blocks.shape[-1]
-    gram_flops = 12 * count * count * number * layers
+    gram_flops = 8 * count * count * number * layers
 
     numbers = (cols_y, cols_y, cols_x, cols_x)
     first_edges = [(n * (count + 1), layers) for n in numbers]
     later_edges = [(n * count, layers) for n in numbers]
-    v, *edges = call(
+    rhs, v, coef, diag_term, *edges = call(
         functools.partial(start_kernel, cols),
-        [state] + first_edges,
-        [SMEM] + [VMEM] * 3,
-        sides, rhs, coef, blocks,
+        [state, state, rows, rows] + first_edges,
+        [SMEM] * 3 + [VMEM] * 4,
+        sides,
+        well_columns,
+        column_active,
+        sources,
+        perm_root.reshape(rows),
+        storage_term.reshape(rows),
+        blocks,
         flops=apply_flops,
     )
     vs, ws, grams = [v], [], []
@@ -272,10 +350,9 @@
             *arrays,
             flops=len(pairs) * gram_flops,
         )
-    lanes = 128
     w, joint = call(
         functools.partial(last_kernel, cols),
-        [state, (devices, count, lanes)],
+        [state, (peers_x * peers_y, count // 2, 128)],
         [SMEM] + [VMEM] * 13,
         sides, vs[-1], coef, diag_term, *grams, *got, *got_coefs,
         flops=gram_flops,
@@ -284,14 +361,12 @@
     joint = lax.all_to_all(joint, ("narrow", "wide"), 0, 0)
     outs = call(
         functools.partial(finish_kernel, ITERS),
-        [state, state],
+        [sources.shape] * 2,
         [VMEM] * (2 + 2 * ITERS),
         joint, rhs, *vs, *ws,
         flops=24 * ITERS * count * count * number * layers,
     )
-    return tuple(
-        jnp.transpose(o.reshape(cols_x, cols_y, count, layers), (2, 0, 1, 3)) for o in outs
-    )
+    return tuple(outs)
 
 
 def solution(mesh):

time: 61.4 us -> 51.7 us (0.84)
  blocking collectives: 19.8 us -> 11 us
  waiting for transfers between devices: 2.6 us -> 8.65 us
  starting transfers between devices: 20.4 us -> 16.4 us
  other arithmetic: 2.5 us -> 0 us
    all_to_all x1, blocking collectives: 19.8 us -> 11 us  [on_device(): joint = lax.all_to_all(joint, ('narrow', 'wide'), 0, 0)]
    ppermute x12, waiting for transfers between devices: 2.6 us -> 8.65 us  [exchange(): out.append(lax.ppermute(edge, axis, pairs + [(j, i) for i, j in pairs]))]
    ppermute x12, starting transfers between devices: 20.4 us -> 16.4 us  [exchange(): out.append(lax.ppermute(edge, axis, pairs + [(j, i) for i, j in pairs]))]
    unnamed x6 -> x14, local copies, waits for them, and re-layouts: 0.63 us -> 2.87 us
    transpose x2 -> x0, local copies, waits for them, and re-layouts: 2.2 us -> none  [the longest x1 1.11 us: on_device(): rhs = jnp.transpose(sources, (1, 2, 0, 3)).reshape(number, count, layers)]
    sub x1 -> x0, other arithmetic: 0.77 us -> none  [on_device(): diag_term = (active * storage_term + (1.0 - active)).reshape(number, layers)]
    mul x1 -> x0, other arithmetic: 0.73 us -> none  [on_device(): rhs = rhs + WELL_RATE * wells[..., None]]
    convert_element_type x1 -> x0, other arithmetic: 0.68 us -> none  [on_device(): active = column_active.astype(jnp.float32)[..., None]]
  transfers between devices with their start and end apart: 12 -> 12, of which waited for: 2 -> 4; matrix products, arithmetic and copies ran while one was open for 0% -> 0% of each run, Pallas kernels for 3% -> 2%
where the time goes in v2:
time: 51.7 us; the launch traced here: 51.4 us
  starting transfers between devices  16.4 us (32%)
  Pallas kernels  11.7 us (23%)
  blocking collectives  11 us (21%)
  waiting for transfers between devices  8.65 us (17%)
  local copies, waits for them, and re-layouts  2.95 us (6%)
  between operations  0.75 us (1%)
    ppermute x12, starting transfers between devices, exchange(): out.append(lax.ppermute(edge, axis, pairs + [(j, i) for i, j in pairs]))  16.4 us
    pallas_call x7, Pallas kernels, call(): pl.pallas_call(kernel, out_shape=shapes, in_specs=in_specs, out_specs=[VM...  11.7 us
    all_to_all x1, blocking collectives, on_device(): joint = lax.all_to_all(joint, ('narrow', 'wide'), 0, 0)  11 us
    ppermute x12, waiting for transfers between devices, exchange(): out.append(lax.ppermute(edge, axis, pairs + [(j, i) for i, j in pairs]))  8.65 us
    unnamed x14, local copies, waits for them, and re-layouts  2.87 us
  transfers between devices with their start and end apart: 12, of which 4 were waited for; matrix products, arithmetic and copies ran while one was open for 0% of the time, Pallas kernels for 2%

profile of v2, /device:TPU:0, one launch (start us, length us, event | category | flops | bytes accessed | tf_op | source)
XLA Modules:
  0.0 51.4 jit_solution(12109555731154341516)
XLA Ops:
  0.8 0.5 %copy-done.6 = s32[16]{0:T(128)S(1)} copy-done((s32[16]{0:T(128)S(1)}, s32[16]{0:T(128)}, u32[]{:S(2)}) %copy-start.6) | copy-done | bytes 88
  1.5 1.2 %copy-done = bf16[2,8,2,128,128]{4,3,2,1,0:T(8,128)(2,1)S(1)} copy-done((bf16[2,8,2,128,128]{4,3,2,1,0:T(8,128)(2,1)S(1)}, bf16[2,8,2,128,128]{4,3,2,1,0:T(8,128)(2,1)}, u32[]{:S(2)}) %copy-start) | copy-done | bytes 1048600
  2.7 0.9 %copy-done.2 = f32[16,2,8,256]{3,2,1,0:T(8,128)S(1)} copy-done((f32[16,2,8,256]{3,2,1,0:T(8,128)S(1)}, f32[16,2,8,256]{3,2,1,0:T(8,128)}, u32[]{:S(2)}) %copy-start.2) | copy-done | bytes 262168
  3.6 1.0 %shard_map.77 = (f32[16,16,256]{2,1,0:T(8,128)S(1)}, f32[16,16,256]{2,1,0:T(8,128)S(1)}, f32[16,256]{1,0:T(8,128)S(1)}, f32[16,256]{1,0:T(8,128)S(1)}, f32[136,2...) custom-call(s32[8]{0:T(128)S(1)} %stack.47.sides_ref, ...), custom_call_target="tpu_custom_call" | custom-call | flops 33554432 | bytes 2248864 | tf_op jit(solution)/shard_map/pallas_call | solution.py:20
  4.6 0.5 collective-permute-start
  5.1 3.6 %collective-permute-start.1 = (f32[136,256]{1,0:T(8,128)S(1)}, f32[136,256]{1,0:T(8,128)S(1)}, u32[]{:S(2)}, u32[]{:S(2)}) collective-permute-start(f32[136,256]{1,0:T(8,128)S(1)} %get-tuple-element.28), channel_id=1, source_target_pairs={{1,2},{3,4},{5,6},{7,0},{2,1},{4,3},{6,5},{0,7},{9,10},{11,12},{13... | collective-permute-start | bytes 417800 | tf_op jit(solution)/shard_map/ppermute | solution.py:287
  8.7 1.6 %collective-permute-start.2 = (f32[34,256]{1,0:T(8,128)S(1)}, f32[34,256]{1,0:T(8,128)S(1)}, u32[]{:S(2)}, u32[]{:S(2)}) collective-permute-start(f32[34,256]{1,0:T(8,128)S(1)} %get-tuple-element.29), channel_id=1, source_target_pairs={{0,8},{16,24},{8,0},{24,16},{1,9},{17,25},{9,1},{25,17},{2,10},{18... | collective-permute-start | bytes 104456 | tf_op jit(solution)/shard_map/ppermute | solution.py:287
  10.3 2.5 %collective-permute-start.3 = (f32[34,256]{1,0:T(8,128)S(1)}, f32[34,256]{1,0:T(8,128)S(1)}, u32[]{:S(2)}, u32[]{:S(2)}) collective-permute-start(f32[34,256]{1,0:T(8,128)S(1)} %get-tuple-element.30), channel_id=1, source_target_pairs={{8,16},{24,0},{16,8},{0,24},{9,17},{25,1},{17,9},{1,25},{10,18},{2... | collective-permute-start | bytes 104456 | tf_op jit(solution)/shard_map/ppermute | solution.py:287
  12.8 3.3 %collective-permute-done.3.refs_3_.refs_7_ = f32[34,256]{1,0:T(8,128)S(1)} collective-permute-done((f32[34,256]{1,0:T(8,128)S(1)}, f32[34,256]{1,0:T(8,128)S(1)}, u32[]{:S(2)}, u32[]{:S(2)}) %collective-permute-start.3) | collective-permute-done | bytes 34848 | tf_op jit(solution)/shard_map/ppermute | solution.py:287
  16.1 1.0 %shard_map.78 = (f32[16,16,256]{2,1,0:T(8,128)S(1)}, f32[16,16,256]{2,1,0:T(8,128)S(1)}, f32[128,256]{1,0:T(8,128)S(1)}, f32[128,256]{1,0:T(8,128)S(1)}, f32[32,256]{1,0:T(8,128)S(1)}, /*index=5*/f32[32,256]{1,0:T(8,128)S(1)}) custom-call(s32[8]{0:T(128)S(1)} %stack.47.sides_ref, f32[16,16,256]{2,1,0:T(8,128)S(1)} %get-tuple-element.24.v_ref.refs_0_, ...), custom_call_target="tpu_custom_call" | custom-call | flops 33554432 | bytes 2891808 | tf_op jit(solution)/shard_map/pallas_call | solution.py:20
  17.2 0.6 %collective-permute-start.5 = (f32[128,256]{1,0:T(8,128)S(1)}, f32[128,256]{1,0:T(8,128)S(1)}, u32[]{:S(2)}, u32[]{:S(2)}) collective-permute-start(f32[128,256]{1,0:T(8,128)S(1)} %get-tuple-element.33), channel_id=1, source_target_pairs={{1,2},{3,4},{5,6},{7,0},{2,1},{4,3},{6,5},{0,7},{9,10},{11,12},{13... | collective-permute-start | bytes 393224 | tf_op jit(solution)/shard_map/ppermute | solution.py:287
  17.8 2.5 %collective-permute-start.7 = (f32[32,256]{1,0:T(8,128)S(1)}, f32[32,256]{1,0:T(8,128)S(1)}, u32[]{:S(2)}, u32[]{:S(2)}) collective-permute-start(f32[32,256]{1,0:T(8,128)S(1)} %get-tuple-element.35), channel_id=1, source_target_pairs={{8,16},{24,0},{16,8},{0,24},{9,17},{25,1},{17,9},{1,25},{10,18},{2... | collective-permute-start | bytes 98312 | tf_op jit(solution)/shard_map/ppermute | solution.py:287
  20.3 1.4 %collective-permute-done.6.refs_2_ = f32[32,256]{1,0:T(8,128)S(1)} collective-permute-done((f32[32,256]{1,0:T(8,128)S(1)}, f32[32,256]{1,0:T(8,128)S(1)}, u32[]{:S(2)}, u32[]{:S(2)}) %collective-permute-start.6) | collective-permute-done | bytes 32800 | tf_op jit(solution)/shard_map/ppermute | solution.py:287
  21.8 1.8 %collective-permute-done.7.refs_3_ = f32[32,256]{1,0:T(8,128)S(1)} collective-permute-done((f32[32,256]{1,0:T(8,128)S(1)}, f32[32,256]{1,0:T(8,128)S(1)}, u32[]{:S(2)}, u32[]{:S(2)}) %collective-permute-start.7) | collective-permute-done | bytes 32800 | tf_op jit(solution)/shard_map/ppermute | solution.py:287
  23.6 1.0 %shard_map.79 = (f32[16,16,256]{2,1,0:T(8,128)S(1)}, f32[16,16,256]{2,1,0:T(8,128)S(1)}, f32[128,256]{1,0:T(8,128)S(1)}, f32[128,256]{1,0:T(8,128)S(1)}, f32[32,256]{1,0:T(8,128)S(1)}, /*index=5*/f32[32,256]{1,0:T(8,128)S(1)}) custom-call(s32[8]{0:T(128)S(1)} %stack.47.sides_ref, f32[16,16,256]{2,1,0:T(8,128)S(1)} %get-tuple-element.31.v_ref.refs_1_.refs_0_, ...), custom_call_target="tpu_custom_call" | custom-call | flops 33554432 | bytes 2871328 | tf_op jit(solution)/shard_map/pallas_call | solution.py:20
  24.7 1.9 %collective-permute-start.9 = (f32[128,256]{1,0:T(8,128)S(1)}, f32[128,256]{1,0:T(8,128)S(1)}, u32[]{:S(2)}, u32[]{:S(2)}) collective-permute-start(f32[128,256]{1,0:T(8,128)S(1)} %get-tuple-element.41), channel_id=1, source_target_pairs={{1,2},{3,4},{5,6},{7,0},{2,1},{4,3},{6,5},{0,7},{9,10},{11,12},{13... | collective-permute-start | bytes 393224 | tf_op jit(solution)/shard_map/ppermute | solution.py:287
  26.6 0.7 %collective-permute-start.10 = (f32[32,256]{1,0:T(8,128)S(1)}, f32[32,256]{1,0:T(8,128)S(1)}, u32[]{:S(2)}, u32[]{:S(2)}) collective-permute-start(f32[32,256]{1,0:T(8,128)S(1)} %get-tuple-element.42), channel_id=1, source_target_pairs={{0,8},{16,24},{8,0},{24,16},{1,9},{17,25},{9,1},{25,17},{2,10},{18... | collective-permute-start | bytes 98312 | tf_op jit(solution)/shard_map/ppermute | solution.py:287
  27.3 2.5 %collective-permute-start.11 = (f32[32,256]{1,0:T(8,128)S(1)}, f32[32,256]{1,0:T(8,128)S(1)}, u32[]{:S(2)}, u32[]{:S(2)}) collective-permute-start(f32[32,256]{1,0:T(8,128)S(1)} %get-tuple-element.43), channel_id=1, source_target_pairs={{8,16},{24,0},{16,8},{0,24},{9,17},{25,1},{17,9},{1,25},{10,18},{2... | collective-permute-start | bytes 98312 | tf_op jit(solution)/shard_map/ppermute | solution.py:287
  29.8 0.7 %shard_map.80.early_ref = f32[16,48]{1,0:T(8,128)S(1)} custom-call(f32[16,16,256]{2,1,0:T(8,128)S(1)} %get-tuple-element.24.v_ref.refs_0_, f32[16,16,256]{2,1,0:T(8,128)S(1)} %get-tuple-element.31.v_ref.refs_1_.refs_0_, f32[16,16,256]{2,1,0:T(8,128)S(1)} %get-tuple-element.37.refs_2_.refs_3_, f32[16,16,256]{2,1,0:T(8,128)S(1)} %get-tuple-element.38.refs_3_.r_ref), custom_call_target="tpu_custom_call" | custom-call | flops 25165824 | bytes 1051648 | tf_op jit(solution)/shard_map/pallas_call | solution.py:20
  30.5 0.5 %shard_map.81.late_ref = f32[16,32]{1,0:T(8,128)S(1)} custom-call(f32[16,16,256]{2,1,0:T(8,128)S(1)} %get-tuple-element.31.v_ref.refs_1_.refs_0_, f32[16,16,256]{2,1,0:T(8,128)S(1)} %get-tuple-element.36.refs_1_.v_ref.refs_2_, f32[16,16,256]{2,1,0:T(8,128)S(1)} %get-tuple-element.39.refs_2_.refs_4_), custom_call_target="tpu_custom_call" | custom-call | flops 16777216 | bytes 788480 | tf_op jit(solution)/shard_map/pallas_call | solution.py:20
  31.0 2.0 %collective-permute-done.11.refs_3_ = f32[32,256]{1,0:T(8,128)S(1)} collective-permute-done((f32[32,256]{1,0:T(8,128)S(1)}, f32[32,256]{1,0:T(8,128)S(1)}, u32[]{:S(2)}, u32[]{:S(2)}) %collective-permute-start.11) | collective-permute-done | bytes 32800 | tf_op jit(solution)/shard_map/ppermute | solution.py:287
  33.0 1.3 %shard_map.82 = (f32[16,16,256]{2,1,0:T(8,128)S(1)}, f32[32,8,128]{2,1,0:T(8,128)S(1)}) custom-call(s32[8]{0:T(128)S(1)} %stack.47.sides_ref, f32[16,16,256]{2,1,0:T(8,128)S(1)} %get-tuple-element.36.refs_1_.v_ref.refs_2_, f32[16,256]{1,0:T(8,128)S(1)} %get-tuple-element.25.coef_ref, f32[16,256]{1,0:T(8,128)S(1)} %get-tuple-element.26.diag_ref, ...), custom_call_target="tpu_custom_call" | custom-call | flops 8388608 | bytes 1369120 | tf_op jit(solution)/shard_map/pallas_call | solution.py:20
  34.3 11.0 %all_to_all.5.sums_ref = f32[32,8,128]{2,1,0:T(8,128)S(1)} all-to-all(f32[32,8,128]{2,1,0:T(8,128)S(1)} %get-tuple-element.44), channel_id=1, replica_groups=mesh['narrow'=4,'wide'=8] {'narrow','wide'}, dimensions={0} | all-to-all | bytes 262144 | tf_op jit(solution)/shard_map/all_to_all | solution.py:361
  45.3 6.1 %shard_map.83 = (f32[16,2,8,256]{3,2,1,0:T(8,128)}, f32[16,2,8,256]{3,2,1,0:T(8,128)}) custom-call(f32[32,8,128]{2,1,0:T(8,128)S(1)} %all_to_all.5.sums_ref, f32[16,16,256]{2,1,0:T(8,128)S(1)} %get-tuple-element.38.refs_3_.r_ref, f32[16,16,256]{2,1,0:T(8,128)S(1)} %get-tuple-element.24.v_ref.refs_0_, ...), custom_call_target="tpu_custom_call" | custom-call | flops 75497472 | bytes 2490368 | tf_op jit(solution)/shard_map/pallas_call | solution.py:20
  (23 shorter events, 0.5 us)
Async XLA Ops:
  0.6 0.7 %copy-start.6 = (s32[16]{0:T(128)S(1)}, s32[16]{0:T(128)}, u32[]{:S(2)}) copy-start(s32[16]{0:T(128)} %wells_ref.1) | copy-start | bytes 196
  0.7 0.7 %copy-start.4 = (f32[2,8,256]{2,1,0:T(8,128)S(1)}, f32[2,8,256]{2,1,0:T(8,128)}, u32[]{:S(2)}) copy-start(f32[2,8,256]{2,1,0:T(8,128)} %param.10) | copy-start | bytes 49156
  0.7 0.7 %copy-start.3 = (f32[2,8,256]{2,1,0:T(8,128)S(1)}, f32[2,8,256]{2,1,0:T(8,128)}, u32[]{:S(2)}) copy-start(f32[2,8,256]{2,1,0:T(8,128)} %param.9) | copy-start | bytes 49156
  0.8 0.7 %copy-start.5 = (s32[2,8]{1,0:T(2,128)S(1)}, s32[2,8]{1,0:T(2,128)}, u32[]{:S(2)}) copy-start(s32[2,8]{1,0:T(2,128)} %active_ref.1) | copy-start | bytes 196
  1.5 1.2 %copy-start = (bf16[2,8,2,128,128]{4,3,2,1,0:T(8,128)(2,1)S(1)}, bf16[2,8,2,128,128]{4,3,2,1,0:T(8,128)(2,1)}, u32[]{:S(2)}) copy-start(bf16[2,8,2,128,128]{4,3,2,1,0:T(8,128)(2,1)} %param.11) | copy-start | bytes 3145732
  2.7 0.9 %copy-start.2 = (f32[16,2,8,256]{3,2,1,0:T(8,128)S(1)}, f32[16,2,8,256]{3,2,1,0:T(8,128)}, u32[]{:S(2)}) copy-start(f32[16,2,8,256]{3,2,1,0:T(8,128)} %sources_ref.1) | copy-start | bytes 786436
  3.6 12.5 %copy-start.1 = (bf16[2,8,2,128,128]{4,3,2,1,0:T(8,128)(2,1)S(1)}, bf16[2,8,2,128,128]{4,3,2,1,0:T(8,128)(2,1)}, u32[]{:S(2)}) copy-start(bf16[2,8,2,128,128]{4,3,2,1,0:T(8,128)(2,1)} %param.11) | copy-start | bytes 3145732
  4.6 11.5 %collective-permute-start = (f32[136,256]{1,0:T(8,128)S(1)}, f32[136,256]{1,0:T(8,128)S(1)}, u32[]{:S(2)}, u32[]{:S(2)}) collective-permute-start(f32[136,256]{1,0:T(8,128)S(1)} %get-tuple-element.27), channel_id=1, source_target_pairs={{0,1},{2,3},{4,5},{6,7},{1,0},{3,2},{5,4},{7,6},{8,9},{10,11},{12,... | collective-permute-start | bytes 417800 | tf_op jit(solution)/shard_map/ppermute | solution.py:287
  5.1 10.9 %collective-permute-start.1 = (f32[136,256]{1,0:T(8,128)S(1)}, f32[136,256]{1,0:T(8,128)S(1)}, u32[]{:S(2)}, u32[]{:S(2)}) collective-permute-start(f32[136,256]{1,0:T(8,128)S(1)} %get-tuple-element.28), channel_id=1, source_target_pairs={{1,2},{3,4},{5,6},{7,0},{2,1},{4,3},{6,5},{0,7},{9,10},{11,12},{13... | collective-permute-start | bytes 417800 | tf_op jit(solution)/shard_map/ppermute | solution.py:287
  8.7 4.1 %collective-permute-start.2 = (f32[34,256]{1,0:T(8,128)S(1)}, f32[34,256]{1,0:T(8,128)S(1)}, u32[]{:S(2)}, u32[]{:S(2)}) collective-permute-start(f32[34,256]{1,0:T(8,128)S(1)} %get-tuple-element.29), channel_id=1, source_target_pairs={{0,8},{16,24},{8,0},{24,16},{1,9},{17,25},{9,1},{25,17},{2,10},{18... | collective-permute-start | bytes 104456 | tf_op jit(solution)/shard_map/ppermute | solution.py:287
  10.3 5.8 %collective-permute-start.3 = (f32[34,256]{1,0:T(8,128)S(1)}, f32[34,256]{1,0:T(8,128)S(1)}, u32[]{:S(2)}, u32[]{:S(2)}) collective-permute-start(f32[34,256]{1,0:T(8,128)S(1)} %get-tuple-element.30), channel_id=1, source_target_pairs={{8,16},{24,0},{16,8},{0,24},{9,17},{25,1},{17,9},{1,25},{10,18},{2... | collective-permute-start | bytes 104456 | tf_op jit(solution)/shard_map/ppermute | solution.py:287
  17.1 6.4 %collective-permute-start.4 = (f32[128,256]{1,0:T(8,128)S(1)}, f32[128,256]{1,0:T(8,128)S(1)}, u32[]{:S(2)}, u32[]{:S(2)}) collective-permute-start(f32[128,256]{1,0:T(8,128)S(1)} %get-tuple-element.32), channel_id=1, source_target_pairs={{0,1},{2,3},{4,5},{6,7},{1,0},{3,2},{5,4},{7,6},{8,9},{10,11},{12,... | collective-permute-start | bytes 393224 | tf_op jit(solution)/shard_map/ppermute | solution.py:287
  17.2 6.4 %collective-permute-start.5 = (f32[128,256]{1,0:T(8,128)S(1)}, f32[128,256]{1,0:T(8,128)S(1)}, u32[]{:S(2)}, u32[]{:S(2)}) collective-permute-start(f32[128,256]{1,0:T(8,128)S(1)} %get-tuple-element.33), channel_id=1, source_target_pairs={{1,2},{3,4},{5,6},{7,0},{2,1},{4,3},{6,5},{0,7},{9,10},{11,12},{13... | collective-permute-start | bytes 393224 | tf_op jit(solution)/shard_map/ppermute | solution.py:287
  17.8 3.9 %collective-permute-start.6 = (f32[32,256]{1,0:T(8,128)S(1)}, f32[32,256]{1,0:T(8,128)S(1)}, u32[]{:S(2)}, u32[]{:S(2)}) collective-permute-start(f32[32,256]{1,0:T(8,128)S(1)} %get-tuple-element.34), channel_id=1, source_target_pairs={{0,8},{16,24},{8,0},{24,16},{1,9},{17,25},{9,1},{25,17},{2,10},{18... | collective-permute-start | bytes 98312 | tf_op jit(solution)/shard_map/ppermute | solution.py:287
  17.8 5.7 %collective-permute-start.7 = (f32[32,256]{1,0:T(8,128)S(1)}, f32[32,256]{1,0:T(8,128)S(1)}, u32[]{:S(2)}, u32[]{:S(2)}) collective-permute-start(f32[32,256]{1,0:T(8,128)S(1)} %get-tuple-element.35), channel_id=1, source_target_pairs={{8,16},{24,0},{16,8},{0,24},{9,17},{25,1},{17,9},{1,25},{10,18},{2... | collective-permute-start | bytes 98312 | tf_op jit(solution)/shard_map/ppermute | solution.py:287
  24.7 8.3 %collective-permute-start.8 = (f32[128,256]{1,0:T(8,128)S(1)}, f32[128,256]{1,0:T(8,128)S(1)}, u32[]{:S(2)}, u32[]{:S(2)}) collective-permute-start(f32[128,256]{1,0:T(8,128)S(1)} %get-tuple-element.40), channel_id=1, source_target_pairs={{0,1},{2,3},{4,5},{6,7},{1,0},{3,2},{5,4},{7,6},{8,9},{10,11},{12,... | collective-permute-start | bytes 393224 | tf_op jit(solution)/shard_map/ppermute | solution.py:287
  24.7 8.3 %collective-permute-start.9 = (f32[128,256]{1,0:T(8,128)S(1)}, f32[128,256]{1,0:T(8,128)S(1)}, u32[]{:S(2)}, u32[]{:S(2)}) collective-permute-start(f32[128,256]{1,0:T(8,128)S(1)} %get-tuple-element.41), channel_id=1, source_target_pairs={{1,2},{3,4},{5,6},{7,0},{2,1},{4,3},{6,5},{0,7},{9,10},{11,12},{13... | collective-permute-start | bytes 393224 | tf_op jit(solution)/shard_map/ppermute | solution.py:287
  26.6 4.4 %collective-permute-start.10 = (f32[32,256]{1,0:T(8,128)S(1)}, f32[32,256]{1,0:T(8,128)S(1)}, u32[]{:S(2)}, u32[]{:S(2)}) collective-permute-start(f32[32,256]{1,0:T(8,128)S(1)} %get-tuple-element.42), channel_id=1, source_target_pairs={{0,8},{16,24},{8,0},{24,16},{1,9},{17,25},{9,1},{25,17},{2,10},{18... | collective-permute-start | bytes 98312 | tf_op jit(solution)/shard_map/ppermute | solution.py:287
  27.3 5.7 %collective-permute-start.11 = (f32[32,256]{1,0:T(8,128)S(1)}, f32[32,256]{1,0:T(8,128)S(1)}, u32[]{:S(2)}, u32[]{:S(2)}) collective-permute-start(f32[32,256]{1,0:T(8,128)S(1)} %get-tuple-element.43), channel_id=1, source_target_pairs={{8,16},{24,0},{16,8},{0,24},{9,17},{25,1},{17,9},{1,25},{10,18},{2... | collective-permute-start | bytes 98312 | tf_op jit(solution)/shard_map/ppermute | solution.py:287

commit v3 on v2

--- a/solution.py
+++ b/solution.py
@@ -12,16 +12,22 @@
 VMEM_BYTES = 24 * 1024 * 1024
 VMEM = pl.BlockSpec(memory_space=pltpu.VMEM)
 SMEM = pl.BlockSpec(memory_space=pltpu.SMEM)
-
-
-def call(kernel, out_shape, in_specs, *args, flops=0, scratch=()):
-    shapes = [jax.ShapeDtypeStruct(shape, jnp.float32) for shape in out_shape]
+HBM = pl.BlockSpec(memory_space=pltpu.HBM)
+SCALE = 64.0
+AHEAD = 6
+
+
+def call(kernel, out_shape, in_specs, *args, flops=0, out_specs=None, scratch=()):
+    shapes = [
+        s if isinstance(s, jax.ShapeDtypeStruct) else jax.ShapeDtypeStruct(s, jnp.float32)
+        for s in out_shape
+    ]
     size = sum(a.size * a.dtype.itemsize for a in args) + sum(s.size * 4 for s in shapes)
     return pl.pallas_call(
         kernel,
         out_shape=shapes,
         in_specs=in_specs,
-        out_specs=[VMEM] * len(shapes),
+        out_specs=out_specs or [VMEM] * len(shapes),
         scratch_shapes=list(scratch),
         compiler_params=pltpu.CompilerParams(vmem_limit_bytes=VMEM_BYTES),
         cost_estimate=pl.CostEstimate(flops=flops, bytes_accessed=size, transcendentals=0),
@@ -62,22 +68,59 @@
 
 
 def start_kernel(
-    cols, sides_ref, wells_ref, active_ref, sources_ref, perm_ref, storage_ref, blocks_ref,
-    r_ref, v_ref, coef_ref, diag_ref, *edges,
+    cols, sides_ref, wells_hbm, active_hbm, sources_hbm, perm_hbm, storage_hbm, blocks_hbm,
+    r_ref, v_ref, coef_ref, diag_ref, blocks_ref, *refs,
 ):
+    edges = refs[:4]
+    wells_ref, active_ref, sources_ref, perm_ref, storage_ref, small_sem, big_sem, block_sem = refs[4:]
     cols_x, cols_y = cols
     _, count, layers = r_ref.shape
+    small = [
+        pltpu.make_async_copy(source, target, small_sem.at[i])
+        for i, (source, target) in enumerate(
+            (
+                (wells_hbm, wells_ref),
+                (active_hbm, active_ref),
+                (perm_hbm, perm_ref),
+                (storage_hbm, storage_ref),
+            )
+        )
+    ]
+    sources = [
+        pltpu.make_async_copy(sources_hbm.at[:, x], sources_ref.at[:, x], big_sem.at[x])
+        for x in range(cols_x)
+    ]
+    blocks = [
+        pltpu.make_async_copy(
+            blocks_hbm.at[pl.ds(x * cols_y, cols_y)],
+            blocks_ref.at[pl.ds(x * cols_y, cols_y)],
+            block_sem.at[x],
+        )
+        for x in range(cols_x)
+    ]
+    for copy in small:
+        copy.start()
+    for pair in zip(sources, blocks):
+        for copy in pair:
+            copy.start()
+    for copy in small:
+        copy.wait()
     row = lax.broadcasted_iota(jnp.int32, (count, layers), 0)
     wells = jnp.zeros((count, layers), jnp.int32)
     for k in range(count):
         wells = jnp.where(row == k, wells_ref[k], wells)
     for x in range(cols_x):
-        across = jnp.transpose(sources_ref[:, x], (1, 0, 2))
         for y in range(cols_y):
             col = x * cols_y + y
             active = active_ref[x, y].astype(jnp.float32)
             coef_ref[col : col + 1, :] = active * perm_ref[col : col + 1, :]
             diag_ref[col : col + 1, :] = active * storage_ref[col : col + 1, :] + (1.0 - active)
+    for x in range(cols_x):
+        sources[x].wait()
+        across = jnp.transpose(sources_ref[:, x], (1, 0, 2))
+        blocks[x].wait()
+        for y in range(cols_y):
+            col = x * cols_y + y
             column_id = sides_ref[6] + x * sides_ref[7] + y
             r = across[y] + jnp.where(wells == column_id, WELL_RATE, 0.0)
             r_ref[col] = r
@@ -127,7 +170,7 @@
     lower_coef = jnp.where(lane == 0, 0.0, pltpu.roll(coef, 1, 1))
     total = total + upper_coef * (center - pltpu.roll(center, layers - 1, 1))
     total = total + lower_coef * (center - pltpu.roll(center, 1, 1))
-    return diag_ref[col : col + 1, :] * center + coef * total
+    return (diag_ref[col : col + 1, :] * center + coef * total) * (1.0 / SCALE)
 
 
 def step_kernel(cols, sides_ref, v_ref, coef_ref, diag_ref, blocks_ref, *refs):
@@ -226,25 +269,37 @@
 
 
 def solve_spd(matrix, target):
-    size = matrix.shape[0]
-    rows = lax.broadcasted_iota(jnp.int32, (size, size), 0)
-    lanes = lax.broadcasted_iota(jnp.int32, (size, size), 1)
-    eye = rows == lanes
-    down = lax.rsqrt(jnp.sum(jnp.where(eye, matrix, 0.0), axis=1, keepdims=True))
-    across = lax.rsqrt(jnp.sum(jnp.where(eye, matrix, 0.0), axis=0, keepdims=True))
-    work = jnp.concatenate([down * matrix * across, down * target], axis=1)
-    width = work.shape[1]
-    row_ids = lax.broadcasted_iota(jnp.int32, (size, 1), 0)
+    size, width = matrix.shape[0], matrix.shape[1] + target.shape[1]
+    lanes = 128
+    work = jnp.concatenate(
+        [matrix, target, jnp.zeros((size, lanes - width), jnp.float32)], axis=1
+    )
+    row = lax.broadcasted_iota(jnp.int32, (size, lanes), 0)
+
+    def spread(p):
+        return jnp.broadcast_to(work[:, p : p + 1], (size, lanes))
+
+    ahead = {p: spread(p) for p in range(AHEAD)}
+    inverses = jnp.zeros((size, lanes), jnp.float32)
     for p in range(size):
-        pivot_row = work[p : p + 1, :]
-        scaled = pivot_row / pivot_row[:, p : p + 1]
-        column = work[:, p : p + 1]
-        work = jnp.where(row_ids == p, scaled, work - column * scaled)
-    return down * work[:, size:width]
+        column = ahead.pop(p)
+        if p + AHEAD < size:
+            ahead[p + AHEAD] = spread(p + AHEAD)
+        inverse = 1.0 / column[p : p + 1, :]
+        inverses = jnp.where(row == p, inverse, inverses)
+        factor = jnp.where(row == p, 0.0, column)
+
+        def eliminate(value):
+            return value - factor * jnp.broadcast_to(value[p : p + 1, :] * inverse, value.shape)
+
+        ahead = {q: eliminate(value) for q, value in ahead.items()}
+        work = eliminate(work)
+    return work[:, size:width] * inverses[:, size:width]
 
 
 def finish_kernel(blocks, sums_ref, r_ref, *refs):
-    v_refs, w_refs, (x_ref, out_ref) = refs[:blocks], refs[blocks : 2 * blocks], refs[2 * blocks :]
+    v_refs, w_refs, (x_hbm, out_hbm) = refs[:blocks], refs[blocks : 2 * blocks], refs[2 * blocks : 2 * blocks + 2]
+    x_ref, out_ref, sem = refs[2 * blocks + 2 :]
     cols_x, cols_y = x_ref.shape[1:3]
     joint = sums_ref[0]
     for peer in range(1, sums_ref.shape[0]):
@@ -259,8 +314,8 @@
     )
     target = jnp.concatenate(moments[:blocks], axis=0)
     coefs = solve_spd(matrix, target).T
-    high, rest = coefs.astype(jnp.bfloat16), coefs - coefs.astype(jnp.bfloat16).astype(jnp.float32)
-    middle, low = split(rest)
+    high = coefs.astype(jnp.bfloat16)
+    middle, low = split(coefs - high.astype(jnp.float32))
     left = jnp.concatenate([high, high, middle, middle, low], axis=1)
 
     def combine(values, col):
@@ -268,14 +323,25 @@
         right = jnp.concatenate(highs + lows + highs + lows + highs, axis=0)
         return jnp.dot(left, right, preferred_element_type=jnp.float32)
 
+    copies = []
     for x in range(cols_x):
         columns = range(x * cols_y, (x + 1) * cols_y)
-        x_ref[:, x] = jnp.transpose(
-            jnp.stack([combine(v_refs, col) for col in columns]), (1, 0, 2)
-        )
         out_ref[:, x] = jnp.transpose(
             jnp.stack([r_ref[col] - combine(w_refs, col) for col in columns]), (1, 0, 2)
         )
+        copies.append(
+            pltpu.make_async_copy(out_ref.at[:, x], out_hbm.at[:, x], sem.at[2 * x])
+        )
+        copies[-1].start()
+        x_ref[:, x] = jnp.transpose(
+            jnp.stack([combine(v_refs, col) * (1.0 / SCALE) for col in columns]), (1, 0, 2)
+        )
+        copies.append(
+            pltpu.make_async_copy(x_ref.at[:, x], x_hbm.at[:, x], sem.at[2 * x + 1])
+        )
+        copies[-1].start()
+    for copy in copies:
+        copy.wait()
 
 
 def exchange(edges):
@@ -315,10 +381,11 @@
     numbers = (cols_y, cols_y, cols_x, cols_x)
     first_edges = [(n * (count + 1), layers) for n in numbers]
     later_edges = [(n * count, layers) for n in numbers]
-    rhs, v, coef, diag_term, *edges = call(
+    rhs, v, coef, diag_term, blocks, *edges = call(
         functools.partial(start_kernel, cols),
-        [state, state, rows, rows] + first_edges,
-        [SMEM] * 3 + [VMEM] * 4,
+        [state, state, rows, rows, jax.ShapeDtypeStruct(blocks.shape, blocks.dtype)]
+        + first_edges,
+        [SMEM] + [HBM] * 6,
         sides,
         well_columns,
         column_active,
@@ -327,6 +394,16 @@
         storage_term.reshape(rows),
         blocks,
         flops=apply_flops,
+        scratch=[
+            pltpu.SMEM(well_columns.shape, jnp.int32),
+            pltpu.SMEM(column_active.shape, jnp.int32),
+            pltpu.VMEM(sources.shape, jnp.float32),
+            pltpu.VMEM(rows, jnp.float32),
+            pltpu.VMEM(rows, jnp.float32),
+            pltpu.SemaphoreType.DMA((4,)),
+            pltpu.SemaphoreType.DMA((cols_x,)),
+            pltpu.SemaphoreType.DMA((cols_x,)),
+        ],
     )
     vs, ws, grams = [v], [], []
     got_coefs = got = exchange(edges)
@@ -365,6 +442,12 @@
         [VMEM] * (2 + 2 * ITERS),
         joint, rhs, *vs, *ws,
         flops=24 * ITERS * count * count * number * layers,
+        out_specs=[HBM, HBM],
+        scratch=[
+            pltpu.VMEM(sources.shape, jnp.float32),
+            pltpu.VMEM(sources.shape, jnp.float32),
+            pltpu.SemaphoreType.DMA((2 * cols_x,)),
+        ],
     )
     return tuple(outs)
 

time: 51.7 us -> 49.3 us (0.954)
  Pallas kernels: 11.7 us -> 9.27 us
    pallas_call x7, Pallas kernels: 11.7 us -> 9.27 us  [call(): pl.pallas_call(kernel, out_shape=shapes, in_specs=in_specs, out_specs=out...]
    unnamed x14 -> x12, local copies, waits for them, and re-layouts: 2.87 us -> 2.86 us
where the time goes in v3:
time: 49.3 us; the launch traced here: 49 us
  starting transfers between devices  16.4 us (33%)
  blocking collectives  11 us (22%)
  Pallas kernels  9.27 us (19%)
  waiting for transfers between devices  8.65 us (18%)
  local copies, waits for them, and re-layouts  2.95 us (6%)
  between operations  0.76 us (2%)
    ppermute x12, starting transfers between devices, exchange(): out.append(lax.ppermute(edge, axis, pairs + [(j, i) for i, j in pairs]))  16.4 us
    all_to_all x1, blocking collectives, on_device(): joint = lax.all_to_all(joint, ('narrow', 'wide'), 0, 0)  11 us
    pallas_call x7, Pallas kernels, call(): pl.pallas_call(kernel, out_shape=shapes, in_specs=in_specs, out_specs=out...  9.27 us
    ppermute x12, waiting for transfers between devices, exchange(): out.append(lax.ppermute(edge, axis, pairs + [(j, i) for i, j in pairs]))  8.65 us
    unnamed x12, local copies, waits for them, and re-layouts  2.86 us
  transfers between devices with their start and end apart: 12, of which 4 were waited for; matrix products, arithmetic and copies ran while one was open for 0% of the time, Pallas kernels for 2%

profile of v3, /device:TPU:0, one launch (start us, length us, event | category | flops | bytes accessed | tf_op | source)
XLA Modules:
  0.0 49.0 jit_solution(13722172208358327520)
XLA Ops:
  0.8 0.5 %copy-done.5 = s32[16]{0:T(128)S(1)} copy-done((s32[16]{0:T(128)S(1)}, s32[16]{0:T(128)}, u32[]{:S(2)}) %copy-start.5) | copy-done | bytes 88
  1.5 1.2 %copy-done = bf16[2,8,2,128,128]{4,3,2,1,0:T(8,128)(2,1)S(1)} copy-done((bf16[2,8,2,128,128]{4,3,2,1,0:T(8,128)(2,1)S(1)}, bf16[2,8,2,128,128]{4,3,2,1,0:T(8,128)(2,1)}, u32[]{:S(2)}) %copy-start) | copy-done | bytes 1048600
  2.7 0.9 %copy-done.1 = f32[16,2,8,256]{3,2,1,0:T(8,128)S(1)} copy-done((f32[16,2,8,256]{3,2,1,0:T(8,128)S(1)}, f32[16,2,8,256]{3,2,1,0:T(8,128)}, u32[]{:S(2)}) %copy-start.1) | copy-done | bytes 262168
  3.6 1.8 %shard_map.77 = (f32[16,16,256]{2,1,0:T(8,128)S(1)}, f32[16,16,256]{2,1,0:T(8,128)S(1)}, f32[16,256]{1,0:T(8,128)S(1)}, f32[16,256]{1,0:T(8,128)S(1)}, bf16[16,2...) custom-call(s32[8]{0:T(128)S(1)} %stack.47.sides_ref, ...), custom_call_target="tpu_custom_call" | custom-call | flops 33554432 | bytes 4346016 | tf_op jit(solution)/shard_map/pallas_call | solution.py:26
  5.4 0.5 %collective-permute-start = (f32[136,256]{1,0:T(8,128)S(1)}, f32[136,256]{1,0:T(8,128)S(1)}, u32[]{:S(2)}, u32[]{:S(2)}) collective-permute-start(f32[136,256]{1,0:T(8,128)S(1)} %get-tuple-element.29), channel_id=1, source_target_pairs={{0,1},{2,3},{4,5},{6,7},{1,0},{3,2},{5,4},{7,6},{8,9},{10,11},{12,... | collective-permute-start | bytes 417800 | tf_op jit(solution)/shard_map/ppermute | solution.py:353
  5.9 3.6 %collective-permute-start.1 = (f32[136,256]{1,0:T(8,128)S(1)}, f32[136,256]{1,0:T(8,128)S(1)}, u32[]{:S(2)}, u32[]{:S(2)}) collective-permute-start(f32[136,256]{1,0:T(8,128)S(1)} %get-tuple-element.30), channel_id=1, source_target_pairs={{1,2},{3,4},{5,6},{7,0},{2,1},{4,3},{6,5},{0,7},{9,10},{11,12},{13... | collective-permute-start | bytes 417800 | tf_op jit(solution)/shard_map/ppermute | solution.py:353
  9.5 1.6 %collective-permute-start.2 = (f32[34,256]{1,0:T(8,128)S(1)}, f32[34,256]{1,0:T(8,128)S(1)}, u32[]{:S(2)}, u32[]{:S(2)}) collective-permute-start(f32[34,256]{1,0:T(8,128)S(1)} %get-tuple-element.31), channel_id=1, source_target_pairs={{0,8},{16,24},{8,0},{24,16},{1,9},{17,25},{9,1},{25,17},{2,10},{18... | collective-permute-start | bytes 104456 | tf_op jit(solution)/shard_map/ppermute | solution.py:353
  11.1 2.5 %collective-permute-start.3 = (f32[34,256]{1,0:T(8,128)S(1)}, f32[34,256]{1,0:T(8,128)S(1)}, u32[]{:S(2)}, u32[]{:S(2)}) collective-permute-start(f32[34,256]{1,0:T(8,128)S(1)} %get-tuple-element.32), channel_id=1, source_target_pairs={{8,16},{24,0},{16,8},{0,24},{9,17},{25,1},{17,9},{1,25},{10,18},{2... | collective-permute-start | bytes 104456 | tf_op jit(solution)/shard_map/ppermute | solution.py:353
  13.5 3.3 %collective-permute-done.3.refs_3_.refs_7_ = f32[34,256]{1,0:T(8,128)S(1)} collective-permute-done((f32[34,256]{1,0:T(8,128)S(1)}, f32[34,256]{1,0:T(8,128)S(1)}, u32[]{:S(2)}, u32[]{:S(2)}) %collective-permute-start.3) | collective-permute-done | bytes 34848 | tf_op jit(solution)/shard_map/ppermute | solution.py:353
  16.9 1.1 %shard_map.78 = (f32[16,16,256]{2,1,0:T(8,128)S(1)}, f32[16,16,256]{2,1,0:T(8,128)S(1)}, f32[128,256]{1,0:T(8,128)S(1)}, f32[128,256]{1,0:T(8,128)S(1)}, f32[32,256]{1,0:T(8,128)S(1)}, /*index=5*/f32[32,256]{1,0:T(8,128)S(1)}) custom-call(s32[8]{0:T(128)S(1)} %stack.47.sides_ref, f32[16,16,256]{2,1,0:T(8,128)S(1)} %get-tuple-element.25.v_ref.refs_0_, ...), custom_call_target="tpu_custom_call" | custom-call | flops 33554432 | bytes 2891808 | tf_op jit(solution)/shard_map/pallas_call | solution.py:26
  18.0 0.6 %collective-permute-start.5 = (f32[128,256]{1,0:T(8,128)S(1)}, f32[128,256]{1,0:T(8,128)S(1)}, u32[]{:S(2)}, u32[]{:S(2)}) collective-permute-start(f32[128,256]{1,0:T(8,128)S(1)} %get-tuple-element.35), channel_id=1, source_target_pairs={{1,2},{3,4},{5,6},{7,0},{2,1},{4,3},{6,5},{0,7},{9,10},{11,12},{13... | collective-permute-start | bytes 393224 | tf_op jit(solution)/shard_map/ppermute | solution.py:353
  18.6 2.5 %collective-permute-start.7 = (f32[32,256]{1,0:T(8,128)S(1)}, f32[32,256]{1,0:T(8,128)S(1)}, u32[]{:S(2)}, u32[]{:S(2)}) collective-permute-start(f32[32,256]{1,0:T(8,128)S(1)} %get-tuple-element.37), channel_id=1, source_target_pairs={{8,16},{24,0},{16,8},{0,24},{9,17},{25,1},{17,9},{1,25},{10,18},{2... | collective-permute-start | bytes 98312 | tf_op jit(solution)/shard_map/ppermute | solution.py:353
  21.1 1.4 %collective-permute-done.6.refs_2_ = f32[32,256]{1,0:T(8,128)S(1)} collective-permute-done((f32[32,256]{1,0:T(8,128)S(1)}, f32[32,256]{1,0:T(8,128)S(1)}, u32[]{:S(2)}, u32[]{:S(2)}) %collective-permute-start.6) | collective-permute-done | bytes 32800 | tf_op jit(solution)/shard_map/ppermute | solution.py:353
  22.6 1.8 %collective-permute-done.7.refs_3_ = f32[32,256]{1,0:T(8,128)S(1)} collective-permute-done((f32[32,256]{1,0:T(8,128)S(1)}, f32[32,256]{1,0:T(8,128)S(1)}, u32[]{:S(2)}, u32[]{:S(2)}) %collective-permute-start.7) | collective-permute-done | bytes 32800 | tf_op jit(solution)/shard_map/ppermute | solution.py:353
  24.4 1.1 %shard_map.79 = (f32[16,16,256]{2,1,0:T(8,128)S(1)}, f32[16,16,256]{2,1,0:T(8,128)S(1)}, f32[128,256]{1,0:T(8,128)S(1)}, f32[128,256]{1,0:T(8,128)S(1)}, f32[32,256]{1,0:T(8,128)S(1)}, /*index=5*/f32[32,256]{1,0:T(8,128)S(1)}) custom-call(s32[8]{0:T(128)S(1)} %stack.47.sides_ref, f32[16,16,256]{2,1,0:T(8,128)S(1)} %get-tuple-element.33.v_ref.refs_1_.refs_0_, ...), custom_call_target="tpu_custom_call" | custom-call | flops 33554432 | bytes 2871328 | tf_op jit(solution)/shard_map/pallas_call | solution.py:26
  25.6 1.9 %collective-permute-start.9 = (f32[128,256]{1,0:T(8,128)S(1)}, f32[128,256]{1,0:T(8,128)S(1)}, u32[]{:S(2)}, u32[]{:S(2)}) collective-permute-start(f32[128,256]{1,0:T(8,128)S(1)} %get-tuple-element.43), channel_id=1, source_target_pairs={{1,2},{3,4},{5,6},{7,0},{2,1},{4,3},{6,5},{0,7},{9,10},{11,12},{13... | collective-permute-start | bytes 393224 | tf_op jit(solution)/shard_map/ppermute | solution.py:353
  27.4 0.7 %collective-permute-start.10 = (f32[32,256]{1,0:T(8,128)S(1)}, f32[32,256]{1,0:T(8,128)S(1)}, u32[]{:S(2)}, u32[]{:S(2)}) collective-permute-start(f32[32,256]{1,0:T(8,128)S(1)} %get-tuple-element.44), channel_id=1, source_target_pairs={{0,8},{16,24},{8,0},{24,16},{1,9},{17,25},{9,1},{25,17},{2,10},{18... | collective-permute-start | bytes 98312 | tf_op jit(solution)/shard_map/ppermute | solution.py:353
  28.1 2.5 %collective-permute-start.11 = (f32[32,256]{1,0:T(8,128)S(1)}, f32[32,256]{1,0:T(8,128)S(1)}, u32[]{:S(2)}, u32[]{:S(2)}) collective-permute-start(f32[32,256]{1,0:T(8,128)S(1)} %get-tuple-element.45), channel_id=1, source_target_pairs={{8,16},{24,0},{16,8},{0,24},{9,17},{25,1},{17,9},{1,25},{10,18},{2... | collective-permute-start | bytes 98312 | tf_op jit(solution)/shard_map/ppermute | solution.py:353
  30.6 0.7 %shard_map.80.early_ref = f32[16,48]{1,0:T(8,128)S(1)} custom-call(f32[16,16,256]{2,1,0:T(8,128)S(1)} %get-tuple-element.25.v_ref.refs_0_, f32[16,16,256]{2,1,0:T(8,128)S(1)} %get-tuple-element.33.v_ref.refs_1_.refs_0_, f32[16,16,256]{2,1,0:T(8,128)S(1)} %get-tuple-element.39.refs_2_.refs_3_, f32[16,16,256]{2,1,0:T(8,128)S(1)} %get-tuple-element.40.refs_3_.r_ref), custom_call_target="tpu_custom_call" | custom-call | flops 25165824 | bytes 1051648 | tf_op jit(solution)/shard_map/pallas_call | solution.py:26
  31.3 0.5 %shard_map.81.late_ref = f32[16,32]{1,0:T(8,128)S(1)} custom-call(f32[16,16,256]{2,1,0:T(8,128)S(1)} %get-tuple-element.33.v_ref.refs_1_.refs_0_, f32[16,16,256]{2,1,0:T(8,128)S(1)} %get-tuple-element.38.refs_1_.v_ref.refs_2_, f32[16,16,256]{2,1,0:T(8,128)S(1)} %get-tuple-element.41.refs_2_.refs_4_), custom_call_target="tpu_custom_call" | custom-call | flops 16777216 | bytes 788480 | tf_op jit(solution)/shard_map/pallas_call | solution.py:26
  31.8 2.0 %collective-permute-done.11.refs_3_ = f32[32,256]{1,0:T(8,128)S(1)} collective-permute-done((f32[32,256]{1,0:T(8,128)S(1)}, f32[32,256]{1,0:T(8,128)S(1)}, u32[]{:S(2)}, u32[]{:S(2)}) %collective-permute-start.11) | collective-permute-done | bytes 32800 | tf_op jit(solution)/shard_map/ppermute | solution.py:353
  33.8 1.3 %shard_map.82 = (f32[16,16,256]{2,1,0:T(8,128)S(1)}, f32[32,8,128]{2,1,0:T(8,128)S(1)}) custom-call(s32[8]{0:T(128)S(1)} %stack.47.sides_ref, f32[16,16,256]{2,1,0:T(8,128)S(1)} %get-tuple-element.38.refs_1_.v_ref.refs_2_, f32[16,256]{1,0:T(8,128)S(1)} %get-tuple-element.26.coef_ref, f32[16,256]{1,0:T(8,128)S(1)} %get-tuple-element.27.diag_ref, ...), custom_call_target="tpu_custom_call" | custom-call | flops 8388608 | bytes 1369120 | tf_op jit(solution)/shard_map/pallas_call | solution.py:26
  35.2 11.0 %all_to_all.5.sums_ref = f32[32,8,128]{2,1,0:T(8,128)S(1)} all-to-all(f32[32,8,128]{2,1,0:T(8,128)S(1)} %get-tuple-element.46), channel_id=1, replica_groups=mesh['narrow'=4,'wide'=8] {'narrow','wide'}, dimensions={0} | all-to-all | bytes 262144 | tf_op jit(solution)/shard_map/all_to_all | solution.py:438
  46.2 2.9 %shard_map.83 = (f32[16,2,8,256]{3,2,1,0:T(8,128)}, f32[16,2,8,256]{3,2,1,0:T(8,128)}) custom-call(f32[32,8,128]{2,1,0:T(8,128)S(1)} %all_to_all.5.sums_ref, f32[16,16,256]{2,1,0:T(8,128)S(1)} %get-tuple-element.40.refs_3_.r_ref, f32[16,16,256]{2,1,0:T(8,128)S(1)} %get-tuple-element.25.v_ref.refs_0_, ...), custom_call_target="tpu_custom_call" | custom-call | flops 75497472 | bytes 2490368 | tf_op jit(solution)/shard_map/pallas_call | solution.py:26
  (21 shorter events, 0.5 us)
Async XLA Ops:
  0.7 0.7 %copy-start.5 = (s32[16]{0:T(128)S(1)}, s32[16]{0:T(128)}, u32[]{:S(2)}) copy-start(s32[16]{0:T(128)} %wells_hbm.1) | copy-start | bytes 196
  0.7 0.7 %copy-start.3 = (f32[2,8,256]{2,1,0:T(8,128)S(1)}, f32[2,8,256]{2,1,0:T(8,128)}, u32[]{:S(2)}) copy-start(f32[2,8,256]{2,1,0:T(8,128)} %param.10) | copy-start | bytes 49156
  0.7 0.7 %copy-start.2 = (f32[2,8,256]{2,1,0:T(8,128)S(1)}, f32[2,8,256]{2,1,0:T(8,128)}, u32[]{:S(2)}) copy-start(f32[2,8,256]{2,1,0:T(8,128)} %param.9) | copy-start | bytes 49156
  0.8 0.7 %copy-start.4 = (s32[2,8]{1,0:T(2,128)S(1)}, s32[2,8]{1,0:T(2,128)}, u32[]{:S(2)}) copy-start(s32[2,8]{1,0:T(2,128)} %active_hbm.1) | copy-start | bytes 196
  1.5 1.2 %copy-start = (bf16[2,8,2,128,128]{4,3,2,1,0:T(8,128)(2,1)S(1)}, bf16[2,8,2,128,128]{4,3,2,1,0:T(8,128)(2,1)}, u32[]{:S(2)}) copy-start(bf16[2,8,2,128,128]{4,3,2,1,0:T(8,128)(2,1)} %param.11) | copy-start | bytes 3145732
  2.7 0.9 %copy-start.1 = (f32[16,2,8,256]{3,2,1,0:T(8,128)S(1)}, f32[16,2,8,256]{3,2,1,0:T(8,128)}, u32[]{:S(2)}) copy-start(f32[16,2,8,256]{3,2,1,0:T(8,128)} %sources_hbm.1) | copy-start | bytes 786436
  5.4 11.5 %collective-permute-start = (f32[136,256]{1,0:T(8,128)S(1)}, f32[136,256]{1,0:T(8,128)S(1)}, u32[]{:S(2)}, u32[]{:S(2)}) collective-permute-start(f32[136,256]{1,0:T(8,128)S(1)} %get-tuple-element.29), channel_id=1, source_target_pairs={{0,1},{2,3},{4,5},{6,7},{1,0},{3,2},{5,4},{7,6},{8,9},{10,11},{12,... | collective-permute-start | bytes 417800 | tf_op jit(solution)/shard_map/ppermute | solution.py:353
  5.9 10.9 %collective-permute-start.1 = (f32[136,256]{1,0:T(8,128)S(1)}, f32[136,256]{1,0:T(8,128)S(1)}, u32[]{:S(2)}, u32[]{:S(2)}) collective-permute-start(f32[136,256]{1,0:T(8,128)S(1)} %get-tuple-element.30), channel_id=1, source_target_pairs={{1,2},{3,4},{5,6},{7,0},{2,1},{4,3},{6,5},{0,7},{9,10},{11,12},{13... | collective-permute-start | bytes 417800 | tf_op jit(solution)/shard_map/ppermute | solution.py:353
  9.5 4.1 %collective-permute-start.2 = (f32[34,256]{1,0:T(8,128)S(1)}, f32[34,256]{1,0:T(8,128)S(1)}, u32[]{:S(2)}, u32[]{:S(2)}) collective-permute-start(f32[34,256]{1,0:T(8,128)S(1)} %get-tuple-element.31), channel_id=1, source_target_pairs={{0,8},{16,24},{8,0},{24,16},{1,9},{17,25},{9,1},{25,17},{2,10},{18... | collective-permute-start | bytes 104456 | tf_op jit(solution)/shard_map/ppermute | solution.py:353
  11.1 5.8 %collective-permute-start.3 = (f32[34,256]{1,0:T(8,128)S(1)}, f32[34,256]{1,0:T(8,128)S(1)}, u32[]{:S(2)}, u32[]{:S(2)}) collective-permute-start(f32[34,256]{1,0:T(8,128)S(1)} %get-tuple-element.32), channel_id=1, source_target_pairs={{8,16},{24,0},{16,8},{0,24},{9,17},{25,1},{17,9},{1,25},{10,18},{2... | collective-permute-start | bytes 104456 | tf_op jit(solution)/shard_map/ppermute | solution.py:353
  17.9 6.4 %collective-permute-start.4 = (f32[128,256]{1,0:T(8,128)S(1)}, f32[128,256]{1,0:T(8,128)S(1)}, u32[]{:S(2)}, u32[]{:S(2)}) collective-permute-start(f32[128,256]{1,0:T(8,128)S(1)} %get-tuple-element.34), channel_id=1, source_target_pairs={{0,1},{2,3},{4,5},{6,7},{1,0},{3,2},{5,4},{7,6},{8,9},{10,11},{12,... | collective-permute-start | bytes 393224 | tf_op jit(solution)/shard_map/ppermute | solution.py:353
  18.0 6.4 %collective-permute-start.5 = (f32[128,256]{1,0:T(8,128)S(1)}, f32[128,256]{1,0:T(8,128)S(1)}, u32[]{:S(2)}, u32[]{:S(2)}) collective-permute-start(f32[128,256]{1,0:T(8,128)S(1)} %get-tuple-element.35), channel_id=1, source_target_pairs={{1,2},{3,4},{5,6},{7,0},{2,1},{4,3},{6,5},{0,7},{9,10},{11,12},{13... | collective-permute-start | bytes 393224 | tf_op jit(solution)/shard_map/ppermute | solution.py:353
  18.6 3.9 %collective-permute-start.6 = (f32[32,256]{1,0:T(8,128)S(1)}, f32[32,256]{1,0:T(8,128)S(1)}, u32[]{:S(2)}, u32[]{:S(2)}) collective-permute-start(f32[32,256]{1,0:T(8,128)S(1)} %get-tuple-element.36), channel_id=1, source_target_pairs={{0,8},{16,24},{8,0},{24,16},{1,9},{17,25},{9,1},{25,17},{2,10},{18... | collective-permute-start | bytes 98312 | tf_op jit(solution)/shard_map/ppermute | solution.py:353
  18.6 5.7 %collective-permute-start.7 = (f32[32,256]{1,0:T(8,128)S(1)}, f32[32,256]{1,0:T(8,128)S(1)}, u32[]{:S(2)}, u32[]{:S(2)}) collective-permute-start(f32[32,256]{1,0:T(8,128)S(1)} %get-tuple-element.37), channel_id=1, source_target_pairs={{8,16},{24,0},{16,8},{0,24},{9,17},{25,1},{17,9},{1,25},{10,18},{2... | collective-permute-start | bytes 98312 | tf_op jit(solution)/shard_map/ppermute | solution.py:353
  25.5 8.3 %collective-permute-start.8 = (f32[128,256]{1,0:T(8,128)S(1)}, f32[128,256]{1,0:T(8,128)S(1)}, u32[]{:S(2)}, u32[]{:S(2)}) collective-permute-start(f32[128,256]{1,0:T(8,128)S(1)} %get-tuple-element.42), channel_id=1, source_target_pairs={{0,1},{2,3},{4,5},{6,7},{1,0},{3,2},{5,4},{7,6},{8,9},{10,11},{12,... | collective-permute-start | bytes 393224 | tf_op jit(solution)/shard_map/ppermute | solution.py:353
  25.6 8.3 %collective-permute-start.9 = (f32[128,256]{1,0:T(8,128)S(1)}, f32[128,256]{1,0:T(8,128)S(1)}, u32[]{:S(2)}, u32[]{:S(2)}) collective-permute-start(f32[128,256]{1,0:T(8,128)S(1)} %get-tuple-element.43), channel_id=1, source_target_pairs={{1,2},{3,4},{5,6},{7,0},{2,1},{4,3},{6,5},{0,7},{9,10},{11,12},{13... | collective-permute-start | bytes 393224 | tf_op jit(solution)/shard_map/ppermute | solution.py:353
  27.4 4.4 %collective-permute-start.10 = (f32[32,256]{1,0:T(8,128)S(1)}, f32[32,256]{1,0:T(8,128)S(1)}, u32[]{:S(2)}, u32[]{:S(2)}) collective-permute-start(f32[32,256]{1,0:T(8,128)S(1)} %get-tuple-element.44), channel_id=1, source_target_pairs={{0,8},{16,24},{8,0},{24,16},{1,9},{17,25},{9,1},{25,17},{2,10},{18... | collective-permute-start | bytes 98312 | tf_op jit(solution)/shard_map/ppermute | solution.py:353
  28.1 5.7 %collective-permute-start.11 = (f32[32,256]{1,0:T(8,128)S(1)}, f32[32,256]{1,0:T(8,128)S(1)}, u32[]{:S(2)}, u32[]{:S(2)}) collective-permute-start(f32[32,256]{1,0:T(8,128)S(1)} %get-tuple-element.45), channel_id=1, source_target_pairs={{8,16},{24,0},{16,8},{0,24},{9,17},{25,1},{17,9},{1,25},{10,18},{2... | collective-permute-start | bytes 98312 | tf_op jit(solution)/shard_map/ppermute | solution.py:353

commit v4 on v3

--- a/solution.py
+++ b/solution.py
@@ -387,12 +387,17 @@
         + first_edges,
         [SMEM] + [HBM] * 6,
         sides,
-        well_columns,
-        column_active,
-        sources,
-        perm_root.reshape(rows),
-        storage_term.reshape(rows),
-        blocks,
+        *(
+            pltpu.with_memory_space_constraint(a, pltpu.HBM)
+            for a in (
+                well_columns,
+                column_active,
+                sources,
+                perm_root.reshape(rows),
+                storage_term.reshape(rows),
+                blocks,
+            )
+        ),
         flops=apply_flops,
         scratch=[
             pltpu.SMEM(well_columns.shape, jnp.int32),

time: 49.3 us -> 46.8 us (0.949)
  local copies, waits for them, and re-layouts: 2.95 us -> 0.09 us
    unnamed x12 -> x0, local copies, waits for them, and re-layouts: 2.86 us -> none
  transfers between devices with their start and end apart: 12 -> 12, of which waited for: 4 -> 4; matrix products, arithmetic and copies ran while one was open for 0% -> 0% of each run, Pallas kernels for 2% -> 3%
where the time goes in v4:
time: 46.8 us; the launch traced here: 46.6 us
  starting transfers between devices  16.4 us (35%)
  blocking collectives  11 us (24%)
  Pallas kernels  9.74 us (21%)
  waiting for transfers between devices  8.65 us (18%)
  between operations  0.73 us (2%)
    ppermute x12, starting transfers between devices, exchange(): out.append(lax.ppermute(edge, axis, pairs + [(j, i) for i, j in pairs]))  16.4 us
    all_to_all x1, blocking collectives, on_device(): joint = lax.all_to_all(joint, ('narrow', 'wide'), 0, 0)  11 us
    pallas_call x7, Pallas kernels, call(): pl.pallas_call(kernel, out_shape=shapes, in_specs=in_specs, out_specs=out...  9.74 us
    ppermute x12, waiting for transfers between devices, exchange(): out.append(lax.ppermute(edge, axis, pairs + [(j, i) for i, j in pairs]))  8.65 us
  transfers between devices with their start and end apart: 12, of which 4 were waited for; matrix products, arithmetic and copies ran while one was open for 0% of the time, Pallas kernels for 3%

profile of v4, /device:TPU:0, one launch (start us, length us, event | category | flops | bytes accessed | tf_op | source)
XLA Modules:
  0.0 46.6 jit_solution(872155192065197674)
XLA Ops:
  0.7 0.1 stack.47.sides_ref
  0.7 2.3 %shard_map.77 = (f32[16,16,256]{2,1,0:T(8,128)S(1)}, f32[16,16,256]{2,1,0:T(8,128)S(1)}, f32[16,256]{1,0:T(8,128)S(1)}, f32[16,256]{1,0:T(8,128)S(1)}, bf16[16,2...) custom-call(s32[8]{0:T(128)S(1)} %stack.47.sides_ref, ...), custom_call_target="tpu_custom_call" | custom-call | flops 33554432 | bytes 4346016 | tf_op jit(solution)/shard_map/pallas_call | solution.py:26
  3.0 0.5 %collective-permute-start = (f32[136,256]{1,0:T(8,128)S(1)}, f32[136,256]{1,0:T(8,128)S(1)}, u32[]{:S(2)}, u32[]{:S(2)}) collective-permute-start(f32[136,256]{1,0:T(8,128)S(1)} %get-tuple-element.29), channel_id=1, source_target_pairs={{0,1},{2,3},{4,5},{6,7},{1,0},{3,2},{5,4},{7,6},{8,9},{10,11},{12,... | collective-permute-start | bytes 417800 | tf_op jit(solution)/shard_map/ppermute | solution.py:353
  3.6 3.6 %collective-permute-start.1 = (f32[136,256]{1,0:T(8,128)S(1)}, f32[136,256]{1,0:T(8,128)S(1)}, u32[]{:S(2)}, u32[]{:S(2)}) collective-permute-start(f32[136,256]{1,0:T(8,128)S(1)} %get-tuple-element.30), channel_id=1, source_target_pairs={{1,2},{3,4},{5,6},{7,0},{2,1},{4,3},{6,5},{0,7},{9,10},{11,12},{13... | collective-permute-start | bytes 417800 | tf_op jit(solution)/shard_map/ppermute | solution.py:353
  7.1 1.6 %collective-permute-start.2 = (f32[34,256]{1,0:T(8,128)S(1)}, f32[34,256]{1,0:T(8,128)S(1)}, u32[]{:S(2)}, u32[]{:S(2)}) collective-permute-start(f32[34,256]{1,0:T(8,128)S(1)} %get-tuple-element.31), channel_id=1, source_target_pairs={{0,8},{16,24},{8,0},{24,16},{1,9},{17,25},{9,1},{25,17},{2,10},{18... | collective-permute-start | bytes 104456 | tf_op jit(solution)/shard_map/ppermute | solution.py:353
  8.7 2.5 %collective-permute-start.3 = (f32[34,256]{1,0:T(8,128)S(1)}, f32[34,256]{1,0:T(8,128)S(1)}, u32[]{:S(2)}, u32[]{:S(2)}) collective-permute-start(f32[34,256]{1,0:T(8,128)S(1)} %get-tuple-element.32), channel_id=1, source_target_pairs={{8,16},{24,0},{16,8},{0,24},{9,17},{25,1},{17,9},{1,25},{10,18},{2... | collective-permute-start | bytes 104456 | tf_op jit(solution)/shard_map/ppermute | solution.py:353
  11.2 3.3 %collective-permute-done.3.refs_3_.refs_7_ = f32[34,256]{1,0:T(8,128)S(1)} collective-permute-done((f32[34,256]{1,0:T(8,128)S(1)}, f32[34,256]{1,0:T(8,128)S(1)}, u32[]{:S(2)}, u32[]{:S(2)}) %collective-permute-start.3) | collective-permute-done | bytes 34848 | tf_op jit(solution)/shard_map/ppermute | solution.py:353
  14.5 1.0 %shard_map.78 = (f32[16,16,256]{2,1,0:T(8,128)S(1)}, f32[16,16,256]{2,1,0:T(8,128)S(1)}, f32[128,256]{1,0:T(8,128)S(1)}, f32[128,256]{1,0:T(8,128)S(1)}, f32[32,256]{1,0:T(8,128)S(1)}, /*index=5*/f32[32,256]{1,0:T(8,128)S(1)}) custom-call(s32[8]{0:T(128)S(1)} %stack.47.sides_ref, f32[16,16,256]{2,1,0:T(8,128)S(1)} %get-tuple-element.25.v_ref.refs_0_, ...), custom_call_target="tpu_custom_call" | custom-call | flops 33554432 | bytes 2891808 | tf_op jit(solution)/shard_map/pallas_call | solution.py:26
  15.5 0.1 collective-permute-start.4
  15.6 0.6 %collective-permute-start.5 = (f32[128,256]{1,0:T(8,128)S(1)}, f32[128,256]{1,0:T(8,128)S(1)}, u32[]{:S(2)}, u32[]{:S(2)}) collective-permute-start(f32[128,256]{1,0:T(8,128)S(1)} %get-tuple-element.35), channel_id=1, source_target_pairs={{1,2},{3,4},{5,6},{7,0},{2,1},{4,3},{6,5},{0,7},{9,10},{11,12},{13... | collective-permute-start | bytes 393224 | tf_op jit(solution)/shard_map/ppermute | solution.py:353
  16.3 2.5 %collective-permute-start.7 = (f32[32,256]{1,0:T(8,128)S(1)}, f32[32,256]{1,0:T(8,128)S(1)}, u32[]{:S(2)}, u32[]{:S(2)}) collective-permute-start(f32[32,256]{1,0:T(8,128)S(1)} %get-tuple-element.37), channel_id=1, source_target_pairs={{8,16},{24,0},{16,8},{0,24},{9,17},{25,1},{17,9},{1,25},{10,18},{2... | collective-permute-start | bytes 98312 | tf_op jit(solution)/shard_map/ppermute | solution.py:353
  18.7 1.4 %collective-permute-done.6.refs_2_ = f32[32,256]{1,0:T(8,128)S(1)} collective-permute-done((f32[32,256]{1,0:T(8,128)S(1)}, f32[32,256]{1,0:T(8,128)S(1)}, u32[]{:S(2)}, u32[]{:S(2)}) %collective-permute-start.6) | collective-permute-done | bytes 32800 | tf_op jit(solution)/shard_map/ppermute | solution.py:353
  20.2 1.8 %collective-permute-done.7.refs_3_ = f32[32,256]{1,0:T(8,128)S(1)} collective-permute-done((f32[32,256]{1,0:T(8,128)S(1)}, f32[32,256]{1,0:T(8,128)S(1)}, u32[]{:S(2)}, u32[]{:S(2)}) %collective-permute-start.7) | collective-permute-done | bytes 32800 | tf_op jit(solution)/shard_map/ppermute | solution.py:353
  22.0 1.0 %shard_map.79 = (f32[16,16,256]{2,1,0:T(8,128)S(1)}, f32[16,16,256]{2,1,0:T(8,128)S(1)}, f32[128,256]{1,0:T(8,128)S(1)}, f32[128,256]{1,0:T(8,128)S(1)}, f32[32,256]{1,0:T(8,128)S(1)}, /*index=5*/f32[32,256]{1,0:T(8,128)S(1)}) custom-call(s32[8]{0:T(128)S(1)} %stack.47.sides_ref, f32[16,16,256]{2,1,0:T(8,128)S(1)} %get-tuple-element.33.v_ref.refs_1_.refs_0_, ...), custom_call_target="tpu_custom_call" | custom-call | flops 33554432 | bytes 2871328 | tf_op jit(solution)/shard_map/pallas_call | solution.py:26
  23.1 0.1 collective-permute-start.8
  23.1 1.9 %collective-permute-start.9 = (f32[128,256]{1,0:T(8,128)S(1)}, f32[128,256]{1,0:T(8,128)S(1)}, u32[]{:S(2)}, u32[]{:S(2)}) collective-permute-start(f32[128,256]{1,0:T(8,128)S(1)} %get-tuple-element.43), channel_id=1, source_target_pairs={{1,2},{3,4},{5,6},{7,0},{2,1},{4,3},{6,5},{0,7},{9,10},{11,12},{13... | collective-permute-start | bytes 393224 | tf_op jit(solution)/shard_map/ppermute | solution.py:353
  25.0 0.7 %collective-permute-start.10 = (f32[32,256]{1,0:T(8,128)S(1)}, f32[32,256]{1,0:T(8,128)S(1)}, u32[]{:S(2)}, u32[]{:S(2)}) collective-permute-start(f32[32,256]{1,0:T(8,128)S(1)} %get-tuple-element.44), channel_id=1, source_target_pairs={{0,8},{16,24},{8,0},{24,16},{1,9},{17,25},{9,1},{25,17},{2,10},{18... | collective-permute-start | bytes 98312 | tf_op jit(solution)/shard_map/ppermute | solution.py:353
  25.7 2.5 %collective-permute-start.11 = (f32[32,256]{1,0:T(8,128)S(1)}, f32[32,256]{1,0:T(8,128)S(1)}, u32[]{:S(2)}, u32[]{:S(2)}) collective-permute-start(f32[32,256]{1,0:T(8,128)S(1)} %get-tuple-element.45), channel_id=1, source_target_pairs={{8,16},{24,0},{16,8},{0,24},{9,17},{25,1},{17,9},{1,25},{10,18},{2... | collective-permute-start | bytes 98312 | tf_op jit(solution)/shard_map/ppermute | solution.py:353
  28.2 0.7 %shard_map.80.early_ref = f32[16,48]{1,0:T(8,128)S(1)} custom-call(f32[16,16,256]{2,1,0:T(8,128)S(1)} %get-tuple-element.25.v_ref.refs_0_, f32[16,16,256]{2,1,0:T(8,128)S(1)} %get-tuple-element.33.v_ref.refs_1_.refs_0_, f32[16,16,256]{2,1,0:T(8,128)S(1)} %get-tuple-element.39.refs_2_.refs_3_, f32[16,16,256]{2,1,0:T(8,128)S(1)} %get-tuple-element.40.refs_3_.r_ref), custom_call_target="tpu_custom_call" | custom-call | flops 25165824 | bytes 1051648 | tf_op jit(solution)/shard_map/pallas_call | solution.py:26
  28.9 0.5 %shard_map.81.late_ref = f32[16,32]{1,0:T(8,128)S(1)} custom-call(f32[16,16,256]{2,1,0:T(8,128)S(1)} %get-tuple-element.33.v_ref.refs_1_.refs_0_, f32[16,16,256]{2,1,0:T(8,128)S(1)} %get-tuple-element.38.refs_1_.v_ref.refs_2_, f32[16,16,256]{2,1,0:T(8,128)S(1)} %get-tuple-element.41.refs_2_.refs_4_), custom_call_target="tpu_custom_call" | custom-call | flops 16777216 | bytes 788480 | tf_op jit(solution)/shard_map/pallas_call | solution.py:26
  29.4 2.0 %collective-permute-done.11.refs_3_ = f32[32,256]{1,0:T(8,128)S(1)} collective-permute-done((f32[32,256]{1,0:T(8,128)S(1)}, f32[32,256]{1,0:T(8,128)S(1)}, u32[]{:S(2)}, u32[]{:S(2)}) %collective-permute-start.11) | collective-permute-done | bytes 32800 | tf_op jit(solution)/shard_map/ppermute | solution.py:353
  31.4 1.3 %shard_map.82 = (f32[16,16,256]{2,1,0:T(8,128)S(1)}, f32[32,8,128]{2,1,0:T(8,128)S(1)}) custom-call(s32[8]{0:T(128)S(1)} %stack.47.sides_ref, f32[16,16,256]{2,1,0:T(8,128)S(1)} %get-tuple-element.38.refs_1_.v_ref.refs_2_, f32[16,256]{1,0:T(8,128)S(1)} %get-tuple-element.26.coef_ref, f32[16,256]{1,0:T(8,128)S(1)} %get-tuple-element.27.diag_ref, ...), custom_call_target="tpu_custom_call" | custom-call | flops 8388608 | bytes 1369120 | tf_op jit(solution)/shard_map/pallas_call | solution.py:26
  32.8 11.0 %all_to_all.5.sums_ref = f32[32,8,128]{2,1,0:T(8,128)S(1)} all-to-all(f32[32,8,128]{2,1,0:T(8,128)S(1)} %get-tuple-element.46), channel_id=1, replica_groups=mesh['narrow'=4,'wide'=8] {'narrow','wide'}, dimensions={0} | all-to-all | bytes 262144 | tf_op jit(solution)/shard_map/all_to_all | solution.py:443
  43.8 2.9 %shard_map.83 = (f32[16,2,8,256]{3,2,1,0:T(8,128)}, f32[16,2,8,256]{3,2,1,0:T(8,128)}) custom-call(f32[32,8,128]{2,1,0:T(8,128)S(1)} %all_to_all.5.sums_ref, f32[16,16,256]{2,1,0:T(8,128)S(1)} %get-tuple-element.40.refs_3_.r_ref, f32[16,16,256]{2,1,0:T(8,128)S(1)} %get-tuple-element.25.v_ref.refs_0_, ...), custom_call_target="tpu_custom_call" | custom-call | flops 75497472 | bytes 2490368 | tf_op jit(solution)/shard_map/pallas_call | solution.py:26
  (9 shorter events, 0.1 us)
Async XLA Ops:
  3.0 11.5 %collective-permute-start = (f32[136,256]{1,0:T(8,128)S(1)}, f32[136,256]{1,0:T(8,128)S(1)}, u32[]{:S(2)}, u32[]{:S(2)}) collective-permute-start(f32[136,256]{1,0:T(8,128)S(1)} %get-tuple-element.29), channel_id=1, source_target_pairs={{0,1},{2,3},{4,5},{6,7},{1,0},{3,2},{5,4},{7,6},{8,9},{10,11},{12,... | collective-permute-start | bytes 417800 | tf_op jit(solution)/shard_map/ppermute | solution.py:353
  3.6 10.9 %collective-permute-start.1 = (f32[136,256]{1,0:T(8,128)S(1)}, f32[136,256]{1,0:T(8,128)S(1)}, u32[]{:S(2)}, u32[]{:S(2)}) collective-permute-start(f32[136,256]{1,0:T(8,128)S(1)} %get-tuple-element.30), channel_id=1, source_target_pairs={{1,2},{3,4},{5,6},{7,0},{2,1},{4,3},{6,5},{0,7},{9,10},{11,12},{13... | collective-permute-start | bytes 417800 | tf_op jit(solution)/shard_map/ppermute | solution.py:353
  7.1 4.1 %collective-permute-start.2 = (f32[34,256]{1,0:T(8,128)S(1)}, f32[34,256]{1,0:T(8,128)S(1)}, u32[]{:S(2)}, u32[]{:S(2)}) collective-permute-start(f32[34,256]{1,0:T(8,128)S(1)} %get-tuple-element.31), channel_id=1, source_target_pairs={{0,8},{16,24},{8,0},{24,16},{1,9},{17,25},{9,1},{25,17},{2,10},{18... | collective-permute-start | bytes 104456 | tf_op jit(solution)/shard_map/ppermute | solution.py:353
  8.7 5.8 %collective-permute-start.3 = (f32[34,256]{1,0:T(8,128)S(1)}, f32[34,256]{1,0:T(8,128)S(1)}, u32[]{:S(2)}, u32[]{:S(2)}) collective-permute-start(f32[34,256]{1,0:T(8,128)S(1)} %get-tuple-element.32), channel_id=1, source_target_pairs={{8,16},{24,0},{16,8},{0,24},{9,17},{25,1},{17,9},{1,25},{10,18},{2... | collective-permute-start | bytes 104456 | tf_op jit(solution)/shard_map/ppermute | solution.py:353
  15.5 6.4 %collective-permute-start.4 = (f32[128,256]{1,0:T(8,128)S(1)}, f32[128,256]{1,0:T(8,128)S(1)}, u32[]{:S(2)}, u32[]{:S(2)}) collective-permute-start(f32[128,256]{1,0:T(8,128)S(1)} %get-tuple-element.34), channel_id=1, source_target_pairs={{0,1},{2,3},{4,5},{6,7},{1,0},{3,2},{5,4},{7,6},{8,9},{10,11},{12,... | collective-permute-start | bytes 393224 | tf_op jit(solution)/shard_map/ppermute | solution.py:353
  15.6 6.4 %collective-permute-start.5 = (f32[128,256]{1,0:T(8,128)S(1)}, f32[128,256]{1,0:T(8,128)S(1)}, u32[]{:S(2)}, u32[]{:S(2)}) collective-permute-start(f32[128,256]{1,0:T(8,128)S(1)} %get-tuple-element.35), channel_id=1, source_target_pairs={{1,2},{3,4},{5,6},{7,0},{2,1},{4,3},{6,5},{0,7},{9,10},{11,12},{13... | collective-permute-start | bytes 393224 | tf_op jit(solution)/shard_map/ppermute | solution.py:353
  16.2 3.9 %collective-permute-start.6 = (f32[32,256]{1,0:T(8,128)S(1)}, f32[32,256]{1,0:T(8,128)S(1)}, u32[]{:S(2)}, u32[]{:S(2)}) collective-permute-start(f32[32,256]{1,0:T(8,128)S(1)} %get-tuple-element.36), channel_id=1, source_target_pairs={{0,8},{16,24},{8,0},{24,16},{1,9},{17,25},{9,1},{25,17},{2,10},{18... | collective-permute-start | bytes 98312 | tf_op jit(solution)/shard_map/ppermute | solution.py:353
  16.3 5.7 %collective-permute-start.7 = (f32[32,256]{1,0:T(8,128)S(1)}, f32[32,256]{1,0:T(8,128)S(1)}, u32[]{:S(2)}, u32[]{:S(2)}) collective-permute-start(f32[32,256]{1,0:T(8,128)S(1)} %get-tuple-element.37), channel_id=1, source_target_pairs={{8,16},{24,0},{16,8},{0,24},{9,17},{25,1},{17,9},{1,25},{10,18},{2... | collective-permute-start | bytes 98312 | tf_op jit(solution)/shard_map/ppermute | solution.py:353
  23.1 8.3 %collective-permute-start.8 = (f32[128,256]{1,0:T(8,128)S(1)}, f32[128,256]{1,0:T(8,128)S(1)}, u32[]{:S(2)}, u32[]{:S(2)}) collective-permute-start(f32[128,256]{1,0:T(8,128)S(1)} %get-tuple-element.42), channel_id=1, source_target_pairs={{0,1},{2,3},{4,5},{6,7},{1,0},{3,2},{5,4},{7,6},{8,9},{10,11},{12,... | collective-permute-start | bytes 393224 | tf_op jit(solution)/shard_map/ppermute | solution.py:353
  23.1 8.3 %collective-permute-start.9 = (f32[128,256]{1,0:T(8,128)S(1)}, f32[128,256]{1,0:T(8,128)S(1)}, u32[]{:S(2)}, u32[]{:S(2)}) collective-permute-start(f32[128,256]{1,0:T(8,128)S(1)} %get-tuple-element.43), channel_id=1, source_target_pairs={{1,2},{3,4},{5,6},{7,0},{2,1},{4,3},{6,5},{0,7},{9,10},{11,12},{13... | collective-permute-start | bytes 393224 | tf_op jit(solution)/shard_map/ppermute | solution.py:353
  25.0 4.4 %collective-permute-start.10 = (f32[32,256]{1,0:T(8,128)S(1)}, f32[32,256]{1,0:T(8,128)S(1)}, u32[]{:S(2)}, u32[]{:S(2)}) collective-permute-start(f32[32,256]{1,0:T(8,128)S(1)} %get-tuple-element.44), channel_id=1, source_target_pairs={{0,8},{16,24},{8,0},{24,16},{1,9},{17,25},{9,1},{25,17},{2,10},{18... | collective-permute-start | bytes 98312 | tf_op jit(solution)/shard_map/ppermute | solution.py:353
  25.7 5.7 %collective-permute-start.11 = (f32[32,256]{1,0:T(8,128)S(1)}, f32[32,256]{1,0:T(8,128)S(1)}, u32[]{:S(2)}, u32[]{:S(2)}) collective-permute-start(f32[32,256]{1,0:T(8,128)S(1)} %get-tuple-element.45), channel_id=1, source_target_pairs={{8,16},{24,0},{16,8},{0,24},{9,17},{25,1},{17,9},{1,25},{10,18},{2... | collective-permute-start | bytes 98312 | tf_op jit(solution)/shard_map/ppermute | solution.py:353

commit v5 on v4

--- a/solution.py
+++ b/solution.py
@@ -2,6 +2,7 @@
 
 import jax
 import jax.numpy as jnp
+import numpy as np
 from jax import lax
 from jax.experimental import pallas as pl
 from jax.experimental.pallas import tpu as pltpu
@@ -344,13 +345,26 @@
         copy.wait()
 
 
+def pairing(sizes, axis, phase):
+    transfers = []
+    for place in np.ndindex(*sizes):
+        partner = list(place)
+        partner[axis] += 1 if place[axis] % 2 == phase else -1
+        if not 0 <= partner[axis] < sizes[axis]:
+            partner = list(place)
+            partner[1 - axis] ^= 1
+            if partner[1 - axis] >= sizes[1 - axis]:
+                continue
+        transfers.append(tuple(int(np.ravel_multi_index(p, sizes)) for p in (place, partner)))
+    return transfers
+
+
 def exchange(edges):
-    out = []
-    for slot, edge in enumerate(edges):
-        axis = "wide" if slot < 2 else "narrow"
-        peers = lax.axis_size(axis)
-        pairs = [(i, (i + 1) % peers) for i in range(slot % 2, peers, 2)]
-        out.append(lax.ppermute(edge, axis, pairs + [(j, i) for i, j in pairs]))
+    axes = ("narrow", "wide")
+    sizes = tuple(lax.axis_size(axis) for axis in axes)
+    out = [None] * len(edges)
+    for slot in (1, 3, 2, 0):
+        out[slot] = lax.ppermute(edges[slot], axes, pairing(sizes, 1 - slot // 2, slot % 2))
     return out
 
 

time: 46.8 us -> 42.8 us (0.915)
  starting transfers between devices: 16.4 us -> 12.1 us
  blocking collectives: 11 us -> 13.5 us
  waiting for transfers between devices: 8.65 us -> 6.44 us
    ppermute x12, starting transfers between devices: 16.4 us -> 12.1 us  [exchange(): lax.ppermute(edges[slot], axes, pairing(sizes, 1 - slot // 2, slot % 2))]
    all_to_all x1, blocking collectives: 11 us -> 13.5 us  [on_device(): joint = lax.all_to_all(joint, ('narrow', 'wide'), 0, 0)]
    ppermute x12, waiting for transfers between devices: 8.65 us -> 6.44 us  [exchange(): lax.ppermute(edges[slot], axes, pairing(sizes, 1 - slot // 2, slot % 2))]
  transfers between devices with their start and end apart: 12 -> 12, of which waited for: 4 -> 3; matrix products, arithmetic and copies ran while one was open for 0% -> 0% of each run, Pallas kernels for 3% -> 3%
where the time goes in v5:
time: 42.8 us; the launch traced here: 42.6 us
  blocking collectives  13.5 us (32%)
  starting transfers between devices  12.1 us (28%)
  Pallas kernels  9.76 us (23%)
  waiting for transfers between devices  6.44 us (15%)
  between operations  0.72 us (2%)
    all_to_all x1, blocking collectives, on_device(): joint = lax.all_to_all(joint, ('narrow', 'wide'), 0, 0)  13.5 us
    ppermute x12, starting transfers between devices, exchange(): lax.ppermute(edges[slot], axes, pairing(sizes, 1 - slot // 2, slot % 2))  12.1 us
    pallas_call x7, Pallas kernels, call(): pl.pallas_call(kernel, out_shape=shapes, in_specs=in_specs, out_specs=out...  9.76 us
    ppermute x12, waiting for transfers between devices, exchange(): lax.ppermute(edges[slot], axes, pairing(sizes, 1 - slot // 2, slot % 2))  6.44 us
  transfers between devices with their start and end apart: 12, of which 3 were waited for; matrix products, arithmetic and copies ran while one was open for 0% of the time, Pallas kernels for 3%

profile of v5, /device:TPU:0, one launch (start us, length us, event | category | flops | bytes accessed | tf_op | source)
XLA Modules:
  0.0 42.6 jit_solution(4966208707346692791)
XLA Ops:
  0.7 0.1 stack.47.sides_ref
  0.7 2.3 %shard_map.77 = (f32[16,16,256]{2,1,0:T(8,128)S(1)}, f32[16,16,256]{2,1,0:T(8,128)S(1)}, f32[16,256]{1,0:T(8,128)S(1)}, f32[16,256]{1,0:T(8,128)S(1)}, bf16[16,2...) custom-call(s32[8]{0:T(128)S(1)} %stack.47.sides_ref, ...), custom_call_target="tpu_custom_call" | custom-call | flops 33554432 | bytes 4346016 | tf_op jit(solution)/shard_map/pallas_call | solution.py:27
  3.0 0.5 %collective-permute-start = (f32[136,256]{1,0:T(8,128)S(1)}, f32[136,256]{1,0:T(8,128)S(1)}, u32[]{:S(2)}, u32[]{:S(2)}) collective-permute-start(f32[136,256]{1,0:T(8,128)S(1)} %get-tuple-element.29), channel_id=1, source_target_pairs={{0,1},{1,0},{2,3},{3,2},{4,5},{5,4},{6,7},{7,6},{8,9},{9,8},{10,11... | collective-permute-start | bytes 417800 | tf_op jit(solution)/shard_map/ppermute | solution.py:367
  3.6 2.7 %collective-permute-start.1 = (f32[136,256]{1,0:T(8,128)S(1)}, f32[136,256]{1,0:T(8,128)S(1)}, u32[]{:S(2)}, u32[]{:S(2)}) collective-permute-start(f32[136,256]{1,0:T(8,128)S(1)} %get-tuple-element.30), channel_id=1, source_target_pairs={{0,8},{1,2},{2,1},{3,4},{4,3},{5,6},{6,5},{7,15},{8,0},{9,10},{10,... | collective-permute-start | bytes 417800 | tf_op jit(solution)/shard_map/ppermute | solution.py:367
  6.2 0.1 collective-permute-start.2
  6.3 1.2 %collective-permute-start.3 = (f32[34,256]{1,0:T(8,128)S(1)}, f32[34,256]{1,0:T(8,128)S(1)}, u32[]{:S(2)}, u32[]{:S(2)}) collective-permute-start(f32[34,256]{1,0:T(8,128)S(1)} %get-tuple-element.32), channel_id=1, source_target_pairs={{0,1},{1,0},{2,3},{3,2},{4,5},{5,4},{6,7},{7,6},{8,16},{9,17},{10,... | collective-permute-start | bytes 104456 | tf_op jit(solution)/shard_map/ppermute | solution.py:367
  7.5 2.7 %collective-permute-done.2.refs_2_.refs_6_ = f32[34,256]{1,0:T(8,128)S(1)} collective-permute-done((f32[34,256]{1,0:T(8,128)S(1)}, f32[34,256]{1,0:T(8,128)S(1)}, u32[]{:S(2)}, u32[]{:S(2)}) %collective-permute-start.2) | collective-permute-done | bytes 34848 | tf_op jit(solution)/shard_map/ppermute | solution.py:367
  10.2 1.0 %shard_map.78 = (f32[16,16,256]{2,1,0:T(8,128)S(1)}, f32[16,16,256]{2,1,0:T(8,128)S(1)}, f32[128,256]{1,0:T(8,128)S(1)}, f32[128,256]{1,0:T(8,128)S(1)}, f32[32,256]{1,0:T(8,128)S(1)}, /*index=5*/f32[32,256]{1,0:T(8,128)S(1)}) custom-call(s32[8]{0:T(128)S(1)} %stack.47.sides_ref, f32[16,16,256]{2,1,0:T(8,128)S(1)} %get-tuple-element.25.v_ref.refs_0_, ...), custom_call_target="tpu_custom_call" | custom-call | flops 33554432 | bytes 2891808 | tf_op jit(solution)/shard_map/pallas_call | solution.py:27
  11.3 0.1 collective-permute-start.4
  11.3 2.3 %collective-permute-start.5 = (f32[128,256]{1,0:T(8,128)S(1)}, f32[128,256]{1,0:T(8,128)S(1)}, u32[]{:S(2)}, u32[]{:S(2)}) collective-permute-start(f32[128,256]{1,0:T(8,128)S(1)} %get-tuple-element.35), channel_id=1, source_target_pairs={{0,8},{1,2},{2,1},{3,4},{4,3},{5,6},{6,5},{7,15},{8,0},{9,10},{10,... | collective-permute-start | bytes 393224 | tf_op jit(solution)/shard_map/ppermute | solution.py:367
  13.6 0.1 collective-permute-start.6
  13.7 1.7 %collective-permute-start.7 = (f32[32,256]{1,0:T(8,128)S(1)}, f32[32,256]{1,0:T(8,128)S(1)}, u32[]{:S(2)}, u32[]{:S(2)}) collective-permute-start(f32[32,256]{1,0:T(8,128)S(1)} %get-tuple-element.37), channel_id=1, source_target_pairs={{0,1},{1,0},{2,3},{3,2},{4,5},{5,4},{6,7},{7,6},{8,16},{9,17},{10,... | collective-permute-start | bytes 98312 | tf_op jit(solution)/shard_map/ppermute | solution.py:367
  15.4 2.2 %collective-permute-done.6.refs_2_ = f32[32,256]{1,0:T(8,128)S(1)} collective-permute-done((f32[32,256]{1,0:T(8,128)S(1)}, f32[32,256]{1,0:T(8,128)S(1)}, u32[]{:S(2)}, u32[]{:S(2)}) %collective-permute-start.6) | collective-permute-done | bytes 32800 | tf_op jit(solution)/shard_map/ppermute | solution.py:367
  17.6 1.0 %shard_map.79 = (f32[16,16,256]{2,1,0:T(8,128)S(1)}, f32[16,16,256]{2,1,0:T(8,128)S(1)}, f32[128,256]{1,0:T(8,128)S(1)}, f32[128,256]{1,0:T(8,128)S(1)}, f32[32,256]{1,0:T(8,128)S(1)}, /*index=5*/f32[32,256]{1,0:T(8,128)S(1)}) custom-call(s32[8]{0:T(128)S(1)} %stack.47.sides_ref, f32[16,16,256]{2,1,0:T(8,128)S(1)} %get-tuple-element.33.v_ref.refs_1_.refs_0_, ...), custom_call_target="tpu_custom_call" | custom-call | flops 33554432 | bytes 2871328 | tf_op jit(solution)/shard_map/pallas_call | solution.py:27
  18.6 0.4 %collective-permute-start.8 = (f32[128,256]{1,0:T(8,128)S(1)}, f32[128,256]{1,0:T(8,128)S(1)}, u32[]{:S(2)}, u32[]{:S(2)}) collective-permute-start(f32[128,256]{1,0:T(8,128)S(1)} %get-tuple-element.42), channel_id=1, source_target_pairs={{0,1},{1,0},{2,3},{3,2},{4,5},{5,4},{6,7},{7,6},{8,9},{9,8},{10,11... | collective-permute-start | bytes 393224 | tf_op jit(solution)/shard_map/ppermute | solution.py:367
  19.0 1.9 %collective-permute-start.9 = (f32[128,256]{1,0:T(8,128)S(1)}, f32[128,256]{1,0:T(8,128)S(1)}, u32[]{:S(2)}, u32[]{:S(2)}) collective-permute-start(f32[128,256]{1,0:T(8,128)S(1)} %get-tuple-element.43), channel_id=1, source_target_pairs={{0,8},{1,2},{2,1},{3,4},{4,3},{5,6},{6,5},{7,15},{8,0},{9,10},{10,... | collective-permute-start | bytes 393224 | tf_op jit(solution)/shard_map/ppermute | solution.py:367
  21.0 0.1 collective-permute-start.10
  21.1 1.0 %collective-permute-start.11 = (f32[32,256]{1,0:T(8,128)S(1)}, f32[32,256]{1,0:T(8,128)S(1)}, u32[]{:S(2)}, u32[]{:S(2)}) collective-permute-start(f32[32,256]{1,0:T(8,128)S(1)} %get-tuple-element.45), channel_id=1, source_target_pairs={{0,1},{1,0},{2,3},{3,2},{4,5},{5,4},{6,7},{7,6},{8,16},{9,17},{10,... | collective-permute-start | bytes 98312 | tf_op jit(solution)/shard_map/ppermute | solution.py:367
  22.1 0.7 %shard_map.80.early_ref = f32[16,48]{1,0:T(8,128)S(1)} custom-call(f32[16,16,256]{2,1,0:T(8,128)S(1)} %get-tuple-element.25.v_ref.refs_0_, f32[16,16,256]{2,1,0:T(8,128)S(1)} %get-tuple-element.33.v_ref.refs_1_.refs_0_, f32[16,16,256]{2,1,0:T(8,128)S(1)} %get-tuple-element.39.refs_2_.refs_3_, f32[16,16,256]{2,1,0:T(8,128)S(1)} %get-tuple-element.40.refs_3_.r_ref), custom_call_target="tpu_custom_call" | custom-call | flops 25165824 | bytes 1051648 | tf_op jit(solution)/shard_map/pallas_call | solution.py:27
  22.8 0.5 %shard_map.81.late_ref = f32[16,32]{1,0:T(8,128)S(1)} custom-call(f32[16,16,256]{2,1,0:T(8,128)S(1)} %get-tuple-element.33.v_ref.refs_1_.refs_0_, f32[16,16,256]{2,1,0:T(8,128)S(1)} %get-tuple-element.38.refs_1_.v_ref.refs_2_, f32[16,16,256]{2,1,0:T(8,128)S(1)} %get-tuple-element.41.refs_2_.refs_4_), custom_call_target="tpu_custom_call" | custom-call | flops 16777216 | bytes 788480 | tf_op jit(solution)/shard_map/pallas_call | solution.py:27
  23.3 1.6 %collective-permute-done.10.refs_2_ = f32[32,256]{1,0:T(8,128)S(1)} collective-permute-done((f32[32,256]{1,0:T(8,128)S(1)}, f32[32,256]{1,0:T(8,128)S(1)}, u32[]{:S(2)}, u32[]{:S(2)}) %collective-permute-start.10) | collective-permute-done | bytes 32800 | tf_op jit(solution)/shard_map/ppermute | solution.py:367
  24.9 1.3 %shard_map.82 = (f32[16,16,256]{2,1,0:T(8,128)S(1)}, f32[32,8,128]{2,1,0:T(8,128)S(1)}) custom-call(s32[8]{0:T(128)S(1)} %stack.47.sides_ref, f32[16,16,256]{2,1,0:T(8,128)S(1)} %get-tuple-element.38.refs_1_.v_ref.refs_2_, f32[16,256]{1,0:T(8,128)S(1)} %get-tuple-element.26.coef_ref, f32[16,256]{1,0:T(8,128)S(1)} %get-tuple-element.27.diag_ref, ...), custom_call_target="tpu_custom_call" | custom-call | flops 8388608 | bytes 1369120 | tf_op jit(solution)/shard_map/pallas_call | solution.py:27
  26.3 13.5 %all_to_all.5.sums_ref = f32[32,8,128]{2,1,0:T(8,128)S(1)} all-to-all(f32[32,8,128]{2,1,0:T(8,128)S(1)} %get-tuple-element.46), channel_id=1, replica_groups=mesh['narrow'=4,'wide'=8] {'narrow','wide'}, dimensions={0} | all-to-all | bytes 262144 | tf_op jit(solution)/shard_map/all_to_all | solution.py:457
  39.7 2.9 %shard_map.83 = (f32[16,2,8,256]{3,2,1,0:T(8,128)}, f32[16,2,8,256]{3,2,1,0:T(8,128)}) custom-call(f32[32,8,128]{2,1,0:T(8,128)S(1)} %all_to_all.5.sums_ref, f32[16,16,256]{2,1,0:T(8,128)S(1)} %get-tuple-element.40.refs_3_.r_ref, f32[16,16,256]{2,1,0:T(8,128)S(1)} %get-tuple-element.25.v_ref.refs_0_, ...), custom_call_target="tpu_custom_call" | custom-call | flops 75497472 | bytes 2490368 | tf_op jit(solution)/shard_map/pallas_call | solution.py:27
  (9 shorter events, 0.0 us)
Async XLA Ops:
  3.0 7.2 %collective-permute-start = (f32[136,256]{1,0:T(8,128)S(1)}, f32[136,256]{1,0:T(8,128)S(1)}, u32[]{:S(2)}, u32[]{:S(2)}) collective-permute-start(f32[136,256]{1,0:T(8,128)S(1)} %get-tuple-element.29), channel_id=1, source_target_pairs={{0,1},{1,0},{2,3},{3,2},{4,5},{5,4},{6,7},{7,6},{8,9},{9,8},{10,11... | collective-permute-start | bytes 417800 | tf_op jit(solution)/shard_map/ppermute | solution.py:367
  3.6 6.7 %collective-permute-start.1 = (f32[136,256]{1,0:T(8,128)S(1)}, f32[136,256]{1,0:T(8,128)S(1)}, u32[]{:S(2)}, u32[]{:S(2)}) collective-permute-start(f32[136,256]{1,0:T(8,128)S(1)} %get-tuple-element.30), channel_id=1, source_target_pairs={{0,8},{1,2},{2,1},{3,4},{4,3},{5,6},{6,5},{7,15},{8,0},{9,10},{10,... | collective-permute-start | bytes 417800 | tf_op jit(solution)/shard_map/ppermute | solution.py:367
  6.2 4.0 %collective-permute-start.2 = (f32[34,256]{1,0:T(8,128)S(1)}, f32[34,256]{1,0:T(8,128)S(1)}, u32[]{:S(2)}, u32[]{:S(2)}) collective-permute-start(f32[34,256]{1,0:T(8,128)S(1)} %get-tuple-element.31), channel_id=1, source_target_pairs={{0,8},{1,9},{2,10},{3,11},{4,12},{5,13},{6,14},{7,15},{8,0},{9,1},... | collective-permute-start | bytes 104456 | tf_op jit(solution)/shard_map/ppermute | solution.py:367
  6.3 3.9 %collective-permute-start.3 = (f32[34,256]{1,0:T(8,128)S(1)}, f32[34,256]{1,0:T(8,128)S(1)}, u32[]{:S(2)}, u32[]{:S(2)}) collective-permute-start(f32[34,256]{1,0:T(8,128)S(1)} %get-tuple-element.32), channel_id=1, source_target_pairs={{0,1},{1,0},{2,3},{3,2},{4,5},{5,4},{6,7},{7,6},{8,16},{9,17},{10,... | collective-permute-start | bytes 104456 | tf_op jit(solution)/shard_map/ppermute | solution.py:367
  11.3 6.3 %collective-permute-start.4 = (f32[128,256]{1,0:T(8,128)S(1)}, f32[128,256]{1,0:T(8,128)S(1)}, u32[]{:S(2)}, u32[]{:S(2)}) collective-permute-start(f32[128,256]{1,0:T(8,128)S(1)} %get-tuple-element.34), channel_id=1, source_target_pairs={{0,1},{1,0},{2,3},{3,2},{4,5},{5,4},{6,7},{7,6},{8,9},{9,8},{10,11... | collective-permute-start | bytes 393224 | tf_op jit(solution)/shard_map/ppermute | solution.py:367
  11.3 6.2 %collective-permute-start.5 = (f32[128,256]{1,0:T(8,128)S(1)}, f32[128,256]{1,0:T(8,128)S(1)}, u32[]{:S(2)}, u32[]{:S(2)}) collective-permute-start(f32[128,256]{1,0:T(8,128)S(1)} %get-tuple-element.35), channel_id=1, source_target_pairs={{0,8},{1,2},{2,1},{3,4},{4,3},{5,6},{6,5},{7,15},{8,0},{9,10},{10,... | collective-permute-start | bytes 393224 | tf_op jit(solution)/shard_map/ppermute | solution.py:367
  13.6 3.9 %collective-permute-start.6 = (f32[32,256]{1,0:T(8,128)S(1)}, f32[32,256]{1,0:T(8,128)S(1)}, u32[]{:S(2)}, u32[]{:S(2)}) collective-permute-start(f32[32,256]{1,0:T(8,128)S(1)} %get-tuple-element.36), channel_id=1, source_target_pairs={{0,8},{1,9},{2,10},{3,11},{4,12},{5,13},{6,14},{7,15},{8,0},{9,1},... | collective-permute-start | bytes 98312 | tf_op jit(solution)/shard_map/ppermute | solution.py:367
  13.7 3.9 %collective-permute-start.7 = (f32[32,256]{1,0:T(8,128)S(1)}, f32[32,256]{1,0:T(8,128)S(1)}, u32[]{:S(2)}, u32[]{:S(2)}) collective-permute-start(f32[32,256]{1,0:T(8,128)S(1)} %get-tuple-element.37), channel_id=1, source_target_pairs={{0,1},{1,0},{2,3},{3,2},{4,5},{5,4},{6,7},{7,6},{8,16},{9,17},{10,... | collective-permute-start | bytes 98312 | tf_op jit(solution)/shard_map/ppermute | solution.py:367
  18.6 6.3 %collective-permute-start.8 = (f32[128,256]{1,0:T(8,128)S(1)}, f32[128,256]{1,0:T(8,128)S(1)}, u32[]{:S(2)}, u32[]{:S(2)}) collective-permute-start(f32[128,256]{1,0:T(8,128)S(1)} %get-tuple-element.42), channel_id=1, source_target_pairs={{0,1},{1,0},{2,3},{3,2},{4,5},{5,4},{6,7},{7,6},{8,9},{9,8},{10,11... | collective-permute-start | bytes 393224 | tf_op jit(solution)/shard_map/ppermute | solution.py:367
  19.0 5.9 %collective-permute-start.9 = (f32[128,256]{1,0:T(8,128)S(1)}, f32[128,256]{1,0:T(8,128)S(1)}, u32[]{:S(2)}, u32[]{:S(2)}) collective-permute-start(f32[128,256]{1,0:T(8,128)S(1)} %get-tuple-element.43), channel_id=1, source_target_pairs={{0,8},{1,2},{2,1},{3,4},{4,3},{5,6},{6,5},{7,15},{8,0},{9,10},{10,... | collective-permute-start | bytes 393224 | tf_op jit(solution)/shard_map/ppermute | solution.py:367
  21.0 3.9 %collective-permute-start.10 = (f32[32,256]{1,0:T(8,128)S(1)}, f32[32,256]{1,0:T(8,128)S(1)}, u32[]{:S(2)}, u32[]{:S(2)}) collective-permute-start(f32[32,256]{1,0:T(8,128)S(1)} %get-tuple-element.44), channel_id=1, source_target_pairs={{0,8},{1,9},{2,10},{3,11},{4,12},{5,13},{6,14},{7,15},{8,0},{9,1},... | collective-permute-start | bytes 98312 | tf_op jit(solution)/shard_map/ppermute | solution.py:367
  21.1 3.8 %collective-permute-start.11 = (f32[32,256]{1,0:T(8,128)S(1)}, f32[32,256]{1,0:T(8,128)S(1)}, u32[]{:S(2)}, u32[]{:S(2)}) collective-permute-start(f32[32,256]{1,0:T(8,128)S(1)} %get-tuple-element.45), channel_id=1, source_target_pairs={{0,1},{1,0},{2,3},{3,2},{4,5},{5,4},{6,7},{7,6},{8,16},{9,17},{10,... | collective-permute-start | bytes 98312 | tf_op jit(solution)/shard_map/ppermute | solution.py:367

commit v6 on v5

--- a/solution.py
+++ b/solution.py
@@ -12,7 +12,6 @@
 WELL_RATE = 4.0
 VMEM_BYTES = 24 * 1024 * 1024
 VMEM = pl.BlockSpec(memory_space=pltpu.VMEM)
-SMEM = pl.BlockSpec(memory_space=pltpu.SMEM)
 HBM = pl.BlockSpec(memory_space=pltpu.HBM)
 SCALE = 64.0
 AHEAD = 6
@@ -51,15 +50,19 @@
     return jnp.concatenate(parts, axis=1)
 
 
-def write_edges(sides_ref, cols, v_ref, coef_ref, edges):
+AXES = ("narrow", "wide")
+ORDER = (3, 1, 0, 2)
+
+
+def write_edges(cols, v_ref, coef_ref, edges):
     cols_x, cols_y = cols
     count = v_ref.shape[1]
-    for slot, ref in enumerate(edges):
-        odd = sides_ref[slot // 2]
+    for slot, ref in zip(ORDER, edges):
+        odd = lax.rem(lax.axis_index(AXES[slot // 2]), 2)
         at_low = odd if slot % 2 == 0 else 1 - odd
-        number = cols_y if slot < 2 else cols_x
+        number = cols_x if slot < 2 else cols_y
         for i in range(number):
-            if slot < 2:
+            if slot >= 2:
                 col = jnp.where(at_low == 1, 0, (cols_x - 1) * cols_y) + i
             else:
                 col = i * cols_y + jnp.where(at_low == 1, 0, cols_y - 1)
@@ -69,7 +72,7 @@
 
 
 def start_kernel(
-    cols, sides_ref, wells_hbm, active_hbm, sources_hbm, perm_hbm, storage_hbm, blocks_hbm,
+    cols, wells_hbm, active_hbm, sources_hbm, perm_hbm, storage_hbm, blocks_hbm,
     r_ref, v_ref, coef_ref, diag_ref, blocks_ref, *refs,
 ):
     edges = refs[:4]
@@ -116,20 +119,22 @@
             active = active_ref[x, y].astype(jnp.float32)
             coef_ref[col : col + 1, :] = active * perm_ref[col : col + 1, :]
             diag_ref[col : col + 1, :] = active * storage_ref[col : col + 1, :] + (1.0 - active)
+    grid_y = cols_y * lax.axis_size("narrow")
+    first_x, first_y = lax.axis_index("wide") * cols_x, lax.axis_index("narrow") * cols_y
     for x in range(cols_x):
         sources[x].wait()
         across = jnp.transpose(sources_ref[:, x], (1, 0, 2))
         blocks[x].wait()
         for y in range(cols_y):
             col = x * cols_y + y
-            column_id = sides_ref[6] + x * sides_ref[7] + y
+            column_id = (first_x + x) * grid_y + first_y + y
             r = across[y] + jnp.where(wells == column_id, WELL_RATE, 0.0)
             r_ref[col] = r
             v_ref[col] = apply_blocks(r, blocks_ref, col)
-    write_edges(sides_ref, cols, v_ref, coef_ref, edges)
-
-
-def neighbours(sides_ref, cols, count, got, got_coefs):
+    write_edges(cols, v_ref, coef_ref, edges)
+
+
+def neighbours(cols, count, got, got_coefs):
     cols_x, cols_y = cols
 
     def beyond(v_ref, coef_ref, x, y, step_x, step_y):
@@ -138,11 +143,13 @@
             col = nx * cols_y + ny
             return v_ref[col], coef_ref[col : col + 1, :]
         if step_x:
-            axis, i, number, low = 0, y, cols_y, step_x < 0
+            axis, i, number, low = 1, y, cols_y, step_x < 0
         else:
-            axis, i, number, low = 1, x, cols_x, step_y < 0
-        odd = sides_ref[axis] == 1
-        inside = sides_ref[2 + 2 * axis + (0 if low else 1)].astype(jnp.float32)
+            axis, i, number, low = 0, x, cols_x, step_y < 0
+        place = lax.axis_index(AXES[axis])
+        odd = lax.rem(place, 2) == 1
+        end = 0 if low else lax.axis_size(AXES[axis]) - 1
+        inside = (place != end).astype(jnp.float32)
         first, second = (
             ref[i * count : (i + 1) * count, :] for ref in got[2 * axis : 2 * axis + 2]
         )
@@ -174,17 +181,17 @@
     return (diag_ref[col : col + 1, :] * center + coef * total) * (1.0 / SCALE)
 
 
-def step_kernel(cols, sides_ref, v_ref, coef_ref, diag_ref, blocks_ref, *refs):
+def step_kernel(cols, v_ref, coef_ref, diag_ref, blocks_ref, *refs):
     got, got_coefs, (w_ref, next_ref), edges = refs[:4], refs[4:8], refs[8:10], refs[10:14]
     count = v_ref.shape[1]
-    beyond = neighbours(sides_ref, cols, count, got, got_coefs)
+    beyond = neighbours(cols, count, got, got_coefs)
     for x in range(cols[0]):
         for y in range(cols[1]):
             col = x * cols[1] + y
             w = operate(beyond, cols, v_ref, coef_ref, diag_ref, x, y)
             w_ref[col] = w
             next_ref[col] = apply_blocks(w, blocks_ref, col)
-    write_edges(sides_ref, cols, next_ref, None, edges)
+    write_edges(cols, next_ref, None, edges)
 
 
 def split_gram(left, right):
@@ -248,10 +255,10 @@
     return squares
 
 
-def last_kernel(cols, sides_ref, v_ref, coef_ref, diag_ref, early_ref, late_ref, *refs):
+def last_kernel(cols, v_ref, coef_ref, diag_ref, early_ref, late_ref, *refs):
     got, got_coefs, (w_ref, out_ref) = refs[:4], refs[4:8], refs[8:10]
     count = v_ref.shape[1]
-    beyond = neighbours(sides_ref, cols, count, got, got_coefs)
+    beyond = neighbours(cols, count, got, got_coefs)
     total = jnp.zeros((2 * count, 2 * count), jnp.float32)
     for x in range(cols[0]):
         for y in range(cols[1]):
@@ -360,11 +367,10 @@
 
 
 def exchange(edges):
-    axes = ("narrow", "wide")
-    sizes = tuple(lax.axis_size(axis) for axis in axes)
+    sizes = tuple(lax.axis_size(axis) for axis in AXES)
     out = [None] * len(edges)
-    for slot in (1, 3, 2, 0):
-        out[slot] = lax.ppermute(edges[slot], axes, pairing(sizes, 1 - slot // 2, slot % 2))
+    for slot, edge in zip(ORDER, edges):
+        out[slot] = lax.ppermute(edge, AXES, pairing(sizes, slot // 2, slot % 2))
     return out
 
 
@@ -372,35 +378,20 @@
     count, cols_x, cols_y, layers = sources.shape
     cols = (cols_x, cols_y)
     number = cols_x * cols_y
-    wide, narrow = lax.axis_index("wide"), lax.axis_index("narrow")
-    peers_x, peers_y = lax.axis_size("wide"), lax.axis_size("narrow")
-    grid_y = cols_y * peers_y
-    sides = jnp.stack(
-        [
-            wide % 2,
-            narrow % 2,
-            (wide > 0).astype(jnp.int32),
-            (wide < peers_x - 1).astype(jnp.int32),
-            (narrow > 0).astype(jnp.int32),
-            (narrow < peers_y - 1).astype(jnp.int32),
-            wide * cols_x * grid_y + narrow * cols_y,
-            jnp.full((), grid_y, jnp.int32),
-        ]
-    ).astype(jnp.int32)
+    devices = lax.axis_size("wide") * lax.axis_size("narrow")
     blocks = inverse_blocks.reshape((number,) + inverse_blocks.shape[2:])
     state, rows = (number, count, layers), (number, layers)
     apply_flops = 4 * count * number * layers * inverse_blocks.shape[-1]
     gram_flops = 8 * count * count * number * layers
 
-    numbers = (cols_y, cols_y, cols_x, cols_x)
+    numbers = [cols[slot // 2] for slot in ORDER]
     first_edges = [(n * (count + 1), layers) for n in numbers]
     later_edges = [(n * count, layers) for n in numbers]
     rhs, v, coef, diag_term, blocks, *edges = call(
         functools.partial(start_kernel, cols),
         [state, state, rows, rows, jax.ShapeDtypeStruct(blocks.shape, blocks.dtype)]
         + first_edges,
-        [SMEM] + [HBM] * 6,
-        sides,
+        [HBM] * 6,
         *(
             pltpu.with_memory_space_constraint(a, pltpu.HBM)
             for a in (
@@ -430,8 +421,8 @@
         w, v, *edges = call(
             functools.partial(step_kernel, cols),
             [state, state] + later_edges,
-            [SMEM] + [VMEM] * 12,
-            sides, vs[-1], coef, diag_term, blocks, *got, *got_coefs,
+            [VMEM] * 12,
+            vs[-1], coef, diag_term, blocks, *got, *got_coefs,
             flops=apply_flops,
         )
         vs.append(v)
@@ -448,9 +439,9 @@
         )
     w, joint = call(
         functools.partial(last_kernel, cols),
-        [state, (peers_x * peers_y, count // 2, 128)],
-        [SMEM] + [VMEM] * 13,
-        sides, vs[-1], coef, diag_term, *grams, *got, *got_coefs,
+        [state, (devices, count // 2, 128)],
+        [VMEM] * 13,
+        vs[-1], coef, diag_term, *grams, *got, *got_coefs,
         flops=gram_flops,
     )
     ws.append(w)

time: 42.8 us -> 40.5 us (0.946)
  Pallas kernels: 9.76 us -> 7.56 us
    pallas_call x7, Pallas kernels: 9.76 us -> 7.56 us  [call(): pl.pallas_call(kernel, out_shape=shapes, in_specs=in_specs, out_specs=out...]
where the time goes in v6:
time: 40.5 us; the launch traced here: 40.3 us
  blocking collectives  13.5 us (33%)
  starting transfers between devices  12.1 us (30%)
  Pallas kernels  7.56 us (19%)
  waiting for transfers between devices  6.44 us (16%)
  between operations  0.72 us (2%)
    all_to_all x1, blocking collectives, on_device(): joint = lax.all_to_all(joint, ('narrow', 'wide'), 0, 0)  13.5 us
    ppermute x12, starting transfers between devices, exchange(): out[slot] = lax.ppermute(edge, AXES, pairing(sizes, slot // 2, slot % 2))  12.1 us
    pallas_call x7, Pallas kernels, call(): pl.pallas_call(kernel, out_shape=shapes, in_specs=in_specs, out_specs=out...  7.56 us
    ppermute x12, waiting for transfers between devices, exchange(): out[slot] = lax.ppermute(edge, AXES, pairing(sizes, slot // 2, slot % 2))  6.44 us
  transfers between devices with their start and end apart: 12, of which 3 were waited for; matrix products, arithmetic and copies ran while one was open for 0% of the time, Pallas kernels for 3%

profile of v6, /device:TPU:0, one launch (start us, length us, event | category | flops | bytes accessed | tf_op | source)
XLA Modules:
  0.0 40.3 jit_solution(1125607075606283676)
XLA Ops:
  0.6 1.7 %shard_map.77 = (f32[16,16,256]{2,1,0:T(8,128)S(1)}, f32[16,16,256]{2,1,0:T(8,128)S(1)}, f32[16,256]{1,0:T(8,128)S(1)}, f32[16,256]{1,0:T(8,128)S(1)}, bf16[16,2...) custom-call(s32[16]{0:T(128)} %wells_hbm.1, ...), custom_call_target="tpu_custom_call" | custom-call | flops 33554432 | bytes 4345984 | tf_op jit(solution)/shard_map/pallas_call | solution.py:26
  2.4 0.5 %collective-permute-start.2 = (f32[136,256]{1,0:T(8,128)S(1)}, f32[136,256]{1,0:T(8,128)S(1)}, u32[]{:S(2)}, u32[]{:S(2)}) collective-permute-start(f32[136,256]{1,0:T(8,128)S(1)} %get-tuple-element.31), channel_id=1, source_target_pairs={{0,1},{1,0},{2,3},{3,2},{4,5},{5,4},{6,7},{7,6},{8,9},{9,8},{10,11... | collective-permute-start | bytes 417800 | tf_op jit(solution)/shard_map/ppermute | solution.py:373
  2.9 2.6 %collective-permute-start.3 = (f32[136,256]{1,0:T(8,128)S(1)}, f32[136,256]{1,0:T(8,128)S(1)}, u32[]{:S(2)}, u32[]{:S(2)}) collective-permute-start(f32[136,256]{1,0:T(8,128)S(1)} %get-tuple-element.32), channel_id=1, source_target_pairs={{0,8},{1,2},{2,1},{3,4},{4,3},{5,6},{6,5},{7,15},{8,0},{9,10},{10,... | collective-permute-start | bytes 417800 | tf_op jit(solution)/shard_map/ppermute | solution.py:373
  5.6 0.1 collective-permute-start
  5.6 1.2 %collective-permute-start.1 = (f32[34,256]{1,0:T(8,128)S(1)}, f32[34,256]{1,0:T(8,128)S(1)}, u32[]{:S(2)}, u32[]{:S(2)}) collective-permute-start(f32[34,256]{1,0:T(8,128)S(1)} %get-tuple-element.30), channel_id=1, source_target_pairs={{0,1},{1,0},{2,3},{3,2},{4,5},{5,4},{6,7},{7,6},{8,16},{9,17},{10,... | collective-permute-start | bytes 104456 | tf_op jit(solution)/shard_map/ppermute | solution.py:373
  6.9 2.7 %collective-permute-done.refs_0_.refs_4_ = f32[34,256]{1,0:T(8,128)S(1)} collective-permute-done((f32[34,256]{1,0:T(8,128)S(1)}, f32[34,256]{1,0:T(8,128)S(1)}, u32[]{:S(2)}, u32[]{:S(2)}) %collective-permute-start) | collective-permute-done | bytes 34848 | tf_op jit(solution)/shard_map/ppermute | solution.py:373
  9.6 0.0 collective-permute-done.2.refs_2_.refs_6_
  9.6 0.5 %shard_map.78 = (f32[16,16,256]{2,1,0:T(8,128)S(1)}, f32[16,16,256]{2,1,0:T(8,128)S(1)}, f32[128,256]{1,0:T(8,128)S(1)}, f32[32,256]{1,0:T(8,128)S(1)}, f32[32,256]{1,0:T(8,128)S(1)}, /*index=5*/f32[128,256]{1,0:T(8,128)S(1)}) custom-call(f32[16,16,256]{2,1,0:T(8,128)S(1)} %get-tuple-element.25.v_ref.refs_0_, f32[16,256]{1,0:T(8,128)S(1)} %get-tuple-element.26.coef_ref, ...), custom_call_target="tpu_custom_call" | custom-call | flops 33554432 | bytes 2891776 | tf_op jit(solution)/shard_map/pallas_call | solution.py:26
  10.1 0.1 collective-permute-start.6
  10.2 2.3 %collective-permute-start.7 = (f32[128,256]{1,0:T(8,128)S(1)}, f32[128,256]{1,0:T(8,128)S(1)}, u32[]{:S(2)}, u32[]{:S(2)}) collective-permute-start(f32[128,256]{1,0:T(8,128)S(1)} %get-tuple-element.37), channel_id=1, source_target_pairs={{0,8},{1,2},{2,1},{3,4},{4,3},{5,6},{6,5},{7,15},{8,0},{9,10},{10,... | collective-permute-start | bytes 393224 | tf_op jit(solution)/shard_map/ppermute | solution.py:373
  12.5 0.0 collective-permute-start.4
  12.5 1.7 %collective-permute-start.5 = (f32[32,256]{1,0:T(8,128)S(1)}, f32[32,256]{1,0:T(8,128)S(1)}, u32[]{:S(2)}, u32[]{:S(2)}) collective-permute-start(f32[32,256]{1,0:T(8,128)S(1)} %get-tuple-element.35), channel_id=1, source_target_pairs={{0,1},{1,0},{2,3},{3,2},{4,5},{5,4},{6,7},{7,6},{8,16},{9,17},{10,... | collective-permute-start | bytes 98312 | tf_op jit(solution)/shard_map/ppermute | solution.py:373
  14.2 2.2 %collective-permute-done.4.refs_0_ = f32[32,256]{1,0:T(8,128)S(1)} collective-permute-done((f32[32,256]{1,0:T(8,128)S(1)}, f32[32,256]{1,0:T(8,128)S(1)}, u32[]{:S(2)}, u32[]{:S(2)}) %collective-permute-start.4) | collective-permute-done | bytes 32800 | tf_op jit(solution)/shard_map/ppermute | solution.py:373
  16.4 0.5 %shard_map.79 = (f32[16,16,256]{2,1,0:T(8,128)S(1)}, f32[16,16,256]{2,1,0:T(8,128)S(1)}, f32[128,256]{1,0:T(8,128)S(1)}, f32[32,256]{1,0:T(8,128)S(1)}, f32[32,256]{1,0:T(8,128)S(1)}, /*index=5*/f32[128,256]{1,0:T(8,128)S(1)}) custom-call(f32[16,16,256]{2,1,0:T(8,128)S(1)} %get-tuple-element.33.v_ref.refs_1_.refs_0_, ...), custom_call_target="tpu_custom_call" | custom-call | flops 33554432 | bytes 2871296 | tf_op jit(solution)/shard_map/pallas_call | solution.py:26
  16.9 0.4 %collective-permute-start.10 = (f32[128,256]{1,0:T(8,128)S(1)}, f32[128,256]{1,0:T(8,128)S(1)}, u32[]{:S(2)}, u32[]{:S(2)}) collective-permute-start(f32[128,256]{1,0:T(8,128)S(1)} %get-tuple-element.44), channel_id=1, source_target_pairs={{0,1},{1,0},{2,3},{3,2},{4,5},{5,4},{6,7},{7,6},{8,9},{9,8},{10,11... | collective-permute-start | bytes 393224 | tf_op jit(solution)/shard_map/ppermute | solution.py:373
  17.3 1.9 %collective-permute-start.11 = (f32[128,256]{1,0:T(8,128)S(1)}, f32[128,256]{1,0:T(8,128)S(1)}, u32[]{:S(2)}, u32[]{:S(2)}) collective-permute-start(f32[128,256]{1,0:T(8,128)S(1)} %get-tuple-element.45), channel_id=1, source_target_pairs={{0,8},{1,2},{2,1},{3,4},{4,3},{5,6},{6,5},{7,15},{8,0},{9,10},{10,... | collective-permute-start | bytes 393224 | tf_op jit(solution)/shard_map/ppermute | solution.py:373
  19.3 0.1 collective-permute-start.8
  19.4 1.0 %collective-permute-start.9 = (f32[32,256]{1,0:T(8,128)S(1)}, f32[32,256]{1,0:T(8,128)S(1)}, u32[]{:S(2)}, u32[]{:S(2)}) collective-permute-start(f32[32,256]{1,0:T(8,128)S(1)} %get-tuple-element.43), channel_id=1, source_target_pairs={{0,1},{1,0},{2,3},{3,2},{4,5},{5,4},{6,7},{7,6},{8,16},{9,17},{10,... | collective-permute-start | bytes 98312 | tf_op jit(solution)/shard_map/ppermute | solution.py:373
  20.4 0.7 %shard_map.80.early_ref = f32[16,48]{1,0:T(8,128)S(1)} custom-call(f32[16,16,256]{2,1,0:T(8,128)S(1)} %get-tuple-element.25.v_ref.refs_0_, f32[16,16,256]{2,1,0:T(8,128)S(1)} %get-tuple-element.33.v_ref.refs_1_.refs_0_, f32[16,16,256]{2,1,0:T(8,128)S(1)} %get-tuple-element.39.refs_2_.refs_3_, f32[16,16,256]{2,1,0:T(8,128)S(1)} %get-tuple-element.40.refs_3_.r_ref), custom_call_target="tpu_custom_call" | custom-call | flops 25165824 | bytes 1051648 | tf_op jit(solution)/shard_map/pallas_call | solution.py:26
  21.1 0.5 %shard_map.81.late_ref = f32[16,32]{1,0:T(8,128)S(1)} custom-call(f32[16,16,256]{2,1,0:T(8,128)S(1)} %get-tuple-element.33.v_ref.refs_1_.refs_0_, f32[16,16,256]{2,1,0:T(8,128)S(1)} %get-tuple-element.38.refs_1_.v_ref.refs_2_, f32[16,16,256]{2,1,0:T(8,128)S(1)} %get-tuple-element.41.refs_2_.refs_4_), custom_call_target="tpu_custom_call" | custom-call | flops 16777216 | bytes 788480 | tf_op jit(solution)/shard_map/pallas_call | solution.py:26
  21.6 1.6 %collective-permute-done.8.refs_0_ = f32[32,256]{1,0:T(8,128)S(1)} collective-permute-done((f32[32,256]{1,0:T(8,128)S(1)}, f32[32,256]{1,0:T(8,128)S(1)}, u32[]{:S(2)}, u32[]{:S(2)}) %collective-permute-start.8) | collective-permute-done | bytes 32800 | tf_op jit(solution)/shard_map/ppermute | solution.py:373
  23.2 0.7 %shard_map.82 = (f32[16,16,256]{2,1,0:T(8,128)S(1)}, f32[32,8,128]{2,1,0:T(8,128)S(1)}) custom-call(f32[16,16,256]{2,1,0:T(8,128)S(1)} %get-tuple-element.38.refs_1_.v_ref.refs_2_, f32[16,256]{1,0:T(8,128)S(1)} %get-tuple-element.26.coef_ref, f32[16,256]{1,0:T(8,128)S(1)} %get-tuple-element.27.diag_ref, f32[16,48]{1,0:T(8,128)S(1)} %shard_map.80.early_ref, ...), custom_call_target="tpu_custom_call" | custom-call | flops 8388608 | bytes 1369088 | tf_op jit(solution)/shard_map/pallas_call | solution.py:26
  24.0 13.5 %all_to_all.5.sums_ref = f32[32,8,128]{2,1,0:T(8,128)S(1)} all-to-all(f32[32,8,128]{2,1,0:T(8,128)S(1)} %get-tuple-element.46), channel_id=1, replica_groups=mesh['narrow'=4,'wide'=8] {'narrow','wide'}, dimensions={0} | all-to-all | bytes 262144 | tf_op jit(solution)/shard_map/all_to_all | solution.py:448
  37.5 2.8 %shard_map.83 = (f32[16,2,8,256]{3,2,1,0:T(8,128)}, f32[16,2,8,256]{3,2,1,0:T(8,128)}) custom-call(f32[32,8,128]{2,1,0:T(8,128)S(1)} %all_to_all.5.sums_ref, f32[16,16,256]{2,1,0:T(8,128)S(1)} %get-tuple-element.40.refs_3_.r_ref, f32[16,16,256]{2,1,0:T(8,128)S(1)} %get-tuple-element.25.v_ref.refs_0_, ...), custom_call_target="tpu_custom_call" | custom-call | flops 75497472 | bytes 2490368 | tf_op jit(solution)/shard_map/pallas_call | solution.py:26
  (8 shorter events, 0.0 us)
Async XLA Ops:
  2.4 7.2 %collective-permute-start.2 = (f32[136,256]{1,0:T(8,128)S(1)}, f32[136,256]{1,0:T(8,128)S(1)}, u32[]{:S(2)}, u32[]{:S(2)}) collective-permute-start(f32[136,256]{1,0:T(8,128)S(1)} %get-tuple-element.31), channel_id=1, source_target_pairs={{0,1},{1,0},{2,3},{3,2},{4,5},{5,4},{6,7},{7,6},{8,9},{9,8},{10,11... | collective-permute-start | bytes 417800 | tf_op jit(solution)/shard_map/ppermute | solution.py:373
  2.9 6.7 %collective-permute-start.3 = (f32[136,256]{1,0:T(8,128)S(1)}, f32[136,256]{1,0:T(8,128)S(1)}, u32[]{:S(2)}, u32[]{:S(2)}) collective-permute-start(f32[136,256]{1,0:T(8,128)S(1)} %get-tuple-element.32), channel_id=1, source_target_pairs={{0,8},{1,2},{2,1},{3,4},{4,3},{5,6},{6,5},{7,15},{8,0},{9,10},{10,... | collective-permute-start | bytes 417800 | tf_op jit(solution)/shard_map/ppermute | solution.py:373
  5.6 4.0 %collective-permute-start = (f32[34,256]{1,0:T(8,128)S(1)}, f32[34,256]{1,0:T(8,128)S(1)}, u32[]{:S(2)}, u32[]{:S(2)}) collective-permute-start(f32[34,256]{1,0:T(8,128)S(1)} %get-tuple-element.29), channel_id=1, source_target_pairs={{0,8},{1,9},{2,10},{3,11},{4,12},{5,13},{6,14},{7,15},{8,0},{9,1},... | collective-permute-start | bytes 104456 | tf_op jit(solution)/shard_map/ppermute | solution.py:373
  5.6 3.9 %collective-permute-start.1 = (f32[34,256]{1,0:T(8,128)S(1)}, f32[34,256]{1,0:T(8,128)S(1)}, u32[]{:S(2)}, u32[]{:S(2)}) collective-permute-start(f32[34,256]{1,0:T(8,128)S(1)} %get-tuple-element.30), channel_id=1, source_target_pairs={{0,1},{1,0},{2,3},{3,2},{4,5},{5,4},{6,7},{7,6},{8,16},{9,17},{10,... | collective-permute-start | bytes 104456 | tf_op jit(solution)/shard_map/ppermute | solution.py:373
  10.1 6.3 %collective-permute-start.6 = (f32[128,256]{1,0:T(8,128)S(1)}, f32[128,256]{1,0:T(8,128)S(1)}, u32[]{:S(2)}, u32[]{:S(2)}) collective-permute-start(f32[128,256]{1,0:T(8,128)S(1)} %get-tuple-element.36), channel_id=1, source_target_pairs={{0,1},{1,0},{2,3},{3,2},{4,5},{5,4},{6,7},{7,6},{8,9},{9,8},{10,11... | collective-permute-start | bytes 393224 | tf_op jit(solution)/shard_map/ppermute | solution.py:373
  10.2 6.2 %collective-permute-start.7 = (f32[128,256]{1,0:T(8,128)S(1)}, f32[128,256]{1,0:T(8,128)S(1)}, u32[]{:S(2)}, u32[]{:S(2)}) collective-permute-start(f32[128,256]{1,0:T(8,128)S(1)} %get-tuple-element.37), channel_id=1, source_target_pairs={{0,8},{1,2},{2,1},{3,4},{4,3},{5,6},{6,5},{7,15},{8,0},{9,10},{10,... | collective-permute-start | bytes 393224 | tf_op jit(solution)/shard_map/ppermute | solution.py:373
  12.5 3.9 %collective-permute-start.4 = (f32[32,256]{1,0:T(8,128)S(1)}, f32[32,256]{1,0:T(8,128)S(1)}, u32[]{:S(2)}, u32[]{:S(2)}) collective-permute-start(f32[32,256]{1,0:T(8,128)S(1)} %get-tuple-element.34), channel_id=1, source_target_pairs={{0,8},{1,9},{2,10},{3,11},{4,12},{5,13},{6,14},{7,15},{8,0},{9,1},... | collective-permute-start | bytes 98312 | tf_op jit(solution)/shard_map/ppermute | solution.py:373
  12.5 3.9 %collective-permute-start.5 = (f32[32,256]{1,0:T(8,128)S(1)}, f32[32,256]{1,0:T(8,128)S(1)}, u32[]{:S(2)}, u32[]{:S(2)}) collective-permute-start(f32[32,256]{1,0:T(8,128)S(1)} %get-tuple-element.35), channel_id=1, source_target_pairs={{0,1},{1,0},{2,3},{3,2},{4,5},{5,4},{6,7},{7,6},{8,16},{9,17},{10,... | collective-permute-start | bytes 98312 | tf_op jit(solution)/shard_map/ppermute | solution.py:373
  16.9 6.3 %collective-permute-start.10 = (f32[128,256]{1,0:T(8,128)S(1)}, f32[128,256]{1,0:T(8,128)S(1)}, u32[]{:S(2)}, u32[]{:S(2)}) collective-permute-start(f32[128,256]{1,0:T(8,128)S(1)} %get-tuple-element.44), channel_id=1, source_target_pairs={{0,1},{1,0},{2,3},{3,2},{4,5},{5,4},{6,7},{7,6},{8,9},{9,8},{10,11... | collective-permute-start | bytes 393224 | tf_op jit(solution)/shard_map/ppermute | solution.py:373
  17.3 5.9 %collective-permute-start.11 = (f32[128,256]{1,0:T(8,128)S(1)}, f32[128,256]{1,0:T(8,128)S(1)}, u32[]{:S(2)}, u32[]{:S(2)}) collective-permute-start(f32[128,256]{1,0:T(8,128)S(1)} %get-tuple-element.45), channel_id=1, source_target_pairs={{0,8},{1,2},{2,1},{3,4},{4,3},{5,6},{6,5},{7,15},{8,0},{9,10},{10,... | collective-permute-start | bytes 393224 | tf_op jit(solution)/shard_map/ppermute | solution.py:373
  19.3 3.9 %collective-permute-start.8 = (f32[32,256]{1,0:T(8,128)S(1)}, f32[32,256]{1,0:T(8,128)S(1)}, u32[]{:S(2)}, u32[]{:S(2)}) collective-permute-start(f32[32,256]{1,0:T(8,128)S(1)} %get-tuple-element.42), channel_id=1, source_target_pairs={{0,8},{1,9},{2,10},{3,11},{4,12},{5,13},{6,14},{7,15},{8,0},{9,1},... | collective-permute-start | bytes 98312 | tf_op jit(solution)/shard_map/ppermute | solution.py:373
  19.4 3.8 %collective-permute-start.9 = (f32[32,256]{1,0:T(8,128)S(1)}, f32[32,256]{1,0:T(8,128)S(1)}, u32[]{:S(2)}, u32[]{:S(2)}) collective-permute-start(f32[32,256]{1,0:T(8,128)S(1)} %get-tuple-element.43), channel_id=1, source_target_pairs={{0,1},{1,0},{2,3},{3,2},{4,5},{5,4},{6,7},{7,6},{8,16},{9,17},{10,... | collective-permute-start | bytes 98312 | tf_op jit(solution)/shard_map/ppermute | solution.py:373

commit v7 on v6

v7 whole, which is shorter than its diff:
```python
import functools

import jax
import jax.numpy as jnp
import numpy as np
from jax import lax
from jax.experimental import pallas as pl
from jax.experimental.pallas import tpu as pltpu
from jax.sharding import PartitionSpec as P

ITERS = 3
WELL_RATE = 4.0
VMEM_BYTES = 24 * 1024 * 1024
VMEM = pl.BlockSpec(memory_space=pltpu.VMEM)
HBM = pl.BlockSpec(memory_space=pltpu.HBM)
SCALE = 64.0
AHEAD = 6


def call(kernel, out_shape, in_specs, *args, flops=0, out_specs=None, scratch=(), aliases=None):
    shapes = [
        s if isinstance(s, jax.ShapeDtypeStruct) else jax.ShapeDtypeStruct(s, jnp.float32)
        for s in out_shape
    ]
    size = sum(a.size * a.dtype.itemsize for a in args) + sum(s.size * 4 for s in shapes)
    out = pl.pallas_call(
        kernel,
        out_shape=shapes,
        in_specs=in_specs,
        out_specs=out_specs or [VMEM] * len(shapes),
        scratch_shapes=list(scratch),
        input_output_aliases=aliases or {},
        compiler_params=pltpu.CompilerParams(vmem_limit_bytes=VMEM_BYTES),
        cost_estimate=pl.CostEstimate(flops=flops, bytes_accessed=size, transcendentals=0),
    )(*args)
    return list(out)


def split(value):
    high = value.astype(jnp.bfloat16)
    return high, (value - high.astype(jnp.float32)).astype(jnp.bfloat16)


def apply_blocks(value, blocks_ref, col):
    count, layers = value.shape
    size = blocks_ref.shape[-1]
    number = layers // size
    terms = split(value)
    left = jnp.concatenate(
        [term[:, b * size : (b + 1) * size] for b in range(number) for term in terms], axis=0
    )
    right = jnp.concatenate([blocks_ref[col, b] for b in range(number)], axis=1)
    out = jnp.dot(left, right, preferred_element_type=jnp.float32)
    parts = []
    for b in range(number):
        piece = out[2 * b * count : 2 * (b + 1) * count, b * size : (b + 1) * size]
        parts.append(piece[:count] + piece[count:])
    return jnp.concatenate(parts, axis=1)


AXES = ("narrow", "wide")


def oriented(row, cols_x):
    odd = lax.rem(lax.axis_index("wide"), 2)
    return row + odd * (cols_x - 1 - 2 * row)


def partnered(slot):
    axis = AXES[slot // 2]
    place = lax.axis_index(axis)
    odd = lax.rem(place + slot, 2)
    partner = place + 1 - 2 * odd
    inside = jnp.logical_and(partner >= 0, partner < lax.axis_size(axis))
    return inside.astype(jnp.float32)


def write_edges(v_refs, coef_ref, edges):
    count = v_refs[0].shape[1]
    cols_y = v_refs[0].shape[0]
    odd = lax.rem(lax.axis_index("narrow"), 2)
    for ref, at_low in zip(edges, (odd, 1 - odd)):
        y = (1 - at_low) * (cols_y - 1)
        for row, v_ref in enumerate(v_refs):
            ref[row * count : (row + 1) * count, :] = v_ref[y]
            if coef_ref is not None:
                place = len(v_refs) * count + row
                ref[place : place + 1, :] = coef_ref[pl.ds(row * cols_y + y, 1), :]


def write_side(row, v_ref, coef_ref, edge):
    cols_y, count, _ = v_ref.shape
    for y in range(cols_y):
        edge[y * count : (y + 1) * count, :] = v_ref[y]
    if coef_ref is not None:
        edge[cols_y * count : cols_y * (count + 1), :] = coef_ref[
            row * cols_y : (row + 1) * cols_y, :
        ]


def start_kernel(
    wells_hbm, active_hbm, sources_hbm, perm_hbm, storage_hbm, blocks_hbm, *refs
):
    cols_x, cols_y = active_hbm.shape
    r_refs, v_refs, refs = refs[:cols_x], refs[cols_x : 2 * cols_x], refs[2 * cols_x :]
    coef_ref, diag_ref, blocks_ref, edge_0, edge_1, edge_2, edge_3 = refs[:7]
    wells_ref, active_ref, sources_ref, perm_ref, storage_ref, small_sem, big_sem, block_sem = refs[7:]
    _, count, layers = r_refs[0].shape
    small = [
        pltpu.make_async_copy(source, target, small_sem.at[i])
        for i, (source, target) in enumerate(
            (
                (wells_hbm, wells_ref),
                (active_hbm, active_ref),
                (perm_hbm, perm_ref),
                (storage_hbm, storage_ref),
            )
        )
    ]
    sources, blocks = [], []
    for row in range(cols_x):
        x = oriented(row, cols_x)
        sources.append(
            pltpu.make_async_copy(sources_hbm.at[:, x], sources_ref.at[row], big_sem.at[row])
        )
        blocks.append(
            pltpu.make_async_copy(
                blocks_hbm.at[pl.ds(x * cols_y, cols_y)],
                blocks_ref.at[pl.ds(row * cols_y, cols_y)],
                block_sem.at[row],
            )
        )
    for copy in small:
        copy.start()
    for pair in zip(sources, blocks):
        for copy in pair:
            copy.start()
    for copy in small:
        copy.wait()
    place = lax.broadcasted_iota(jnp.int32, (count, layers), 0)
    wells = jnp.zeros((count, layers), jnp.int32)
    for k in range(count):
        wells = jnp.where(place == k, wells_ref[k], wells)
    grid_y = cols_y * lax.axis_size("narrow")
    first_x, first_y = lax.axis_index("wide") * cols_x, lax.axis_index("narrow") * cols_y
    for row in range(cols_x):
        x = oriented(row, cols_x)
        for y in range(cols_y):
            col = row * cols_y + y
            active = active_ref[x, y].astype(jnp.float32)
            perm, storage = perm_ref[x, y : y + 1, :], storage_ref[x, y : y + 1, :]
            coef_ref[col : col + 1, :] = active * perm
            diag_ref[col : col + 1, :] = active * storage + (1.0 - active)
    for row in range(cols_x):
        sources[row].wait()
        across = jnp.transpose(sources_ref[row], (1, 0, 2))
        blocks[row].wait()
        for y in range(cols_y):
            column_id = (first_x + oriented(row, cols_x)) * grid_y + first_y + y
            r = across[y] + jnp.where(wells == column_id, WELL_RATE, 0.0)
            r_refs[row][y] = r
            v_refs[row][y] = apply_blocks(r, blocks_ref, row * cols_y + y)
    write_side(0, v_refs[0], coef_ref, edge_3)
    write_side(cols_x - 1, v_refs[-1], coef_ref, edge_2)
    write_edges(v_refs, coef_ref, (edge_0, edge_1))


def received(got, got_coefs, slot, i, number, count):
    place = number * count + i
    which = slot % 2
    value = got[which][i * count : (i + 1) * count, :]
    return value, got_coefs[which][place : place + 1, :] * partnered(slot)


def operate(v_refs, coef_ref, diag_ref, got, got_coefs, row, y):
    cols_x = len(v_refs)
    cols_y, count, layers = v_refs[row].shape
    col = row * cols_y + y
    center = v_refs[row][y]
    coef = coef_ref[col : col + 1, :]
    lane = lax.broadcasted_iota(jnp.int32, (1, layers), 1)
    upper_coef = jnp.where(lane == layers - 1, 0.0, pltpu.roll(coef, layers - 1, 1))
    lower_coef = jnp.where(lane == 0, 0.0, pltpu.roll(coef, 1, 1))
    total = upper_coef * (center - pltpu.roll(center, layers - 1, 1))
    total = total + lower_coef * (center - pltpu.roll(center, 1, 1))
    for step_row, step_y in ((1, 0), (-1, 0), (0, 1), (0, -1)):
        other, ny = row + step_row, y + step_y
        if not 0 <= ny < cols_y:
            continue
        if 0 <= other < cols_x:
            place = other * cols_y + ny
            value, other_coef = v_refs[other][ny], coef_ref[place : place + 1, :]
        else:
            slot = 3 if step_row < 0 else 2
            value, other_coef = received(got, got_coefs, slot, y, cols_y, count)
        total = total + other_coef * (center - value)
    return diag_ref[col : col + 1, :] * center + coef * total


def complete(part, v_refs, coef_ref, got, got_coefs, row, y):
    cols_x = len(v_refs)
    cols_y, count, _ = v_refs[row].shape
    col = row * cols_y + y
    odd = lax.rem(lax.axis_index("narrow"), 2) == 1
    first, c_first = received(got, got_coefs, 0, row, cols_x, count)
    second, c_second = received(got, got_coefs, 1, row, cols_x, count)
    for at_end, low in ((y == 0, True), (y == cols_y - 1, False)):
        if at_end:
            value = jnp.where(odd == low, first, second)
            face = coef_ref[col : col + 1, :] * jnp.where(odd == low, c_first, c_second)
            part = part + face * (v_refs[row][y] - value)
    return part


def columns(cols_x, cols_y, at_ends):
    return [
        (row, y)
        for row in range(cols_x)
        for y in range(cols_y)
        if (y in (0, cols_y - 1)) == at_ends
    ]


def middle_kernel(cols_x, last, *refs):
    v_refs, (coef_ref, diag_ref), refs = refs[:cols_x], refs[cols_x : cols_x + 2], refs[cols_x + 2 :]
    got, got_coefs, refs = refs[:2], refs[2:4], refs[4:]
    if last:
        w_refs, gram_ref = refs[:cols_x], refs[cols_x]
    else:
        blocks_ref, w_refs, next_refs = refs[0], refs[1 : 1 + cols_x], refs[1 + cols_x :]
    cols_y, count, _ = v_refs[0].shape
    total = jnp.zeros((2 * count, 2 * count), jnp.float32)
    for row, y in columns(cols_x, cols_y, True):
        w_refs[row][y] = operate(v_refs, coef_ref, diag_ref, got, got_coefs, row, y)
    for row, y in columns(cols_x, cols_y, False):
        w = operate(v_refs, coef_ref, diag_ref, got, got_coefs, row, y) * (1.0 / SCALE)
        w_refs[row][y] = w
        if last:
            total = total + split_gram(v_refs[row][y], w)
        else:
            next_refs[row][y] = apply_blocks(w, blocks_ref, row * cols_y + y)
    if last:
        gram_ref[...] = total


def end_kernel(cols_x, *refs):
    v_refs, refs = refs[:cols_x], refs[cols_x:]
    (coef_ref, blocks_ref), got, got_coefs, refs = refs[:2], refs[2:4], refs[4:6], refs[6:]
    part_refs, refs = refs[:cols_x], refs[2 * cols_x :]
    w_refs, next_refs, edges = refs[:cols_x], refs[cols_x : 2 * cols_x], refs[2 * cols_x :]
    cols_y = v_refs[0].shape[0]
    for row, y in columns(cols_x, cols_y, True):
        w = complete(part_refs[row][y], v_refs, coef_ref, got, got_coefs, row, y) * (1.0 / SCALE)
        w_refs[row][y] = w
        next_refs[row][y] = apply_blocks(w, blocks_ref, row * cols_y + y)
    write_edges(next_refs, None, edges[:2])
    write_side(0, next_refs[0], None, edges[2])


def split_gram(left, right):
    return lax.dot_general(
        jnp.concatenate(split(left), axis=0),
        jnp.concatenate(split(right), axis=0),
        (((1,), (1,)), ((), ())),
        preferred_element_type=jnp.float32,
    )


def fold(total):
    count = total.shape[0] // 2
    total = total[:count] + total[count:]
    total = total[:, :count] + total[:, count:]
    return 0.5 * (total + total.T)


def gram_kernel(cols_x, pairs, *refs):
    arrays, out_ref = refs[:-1], refs[-1]
    cols_y, count, _ = arrays[0].shape
    for slot, (left, right) in enumerate(pairs):
        total = jnp.zeros((2 * count, 2 * count), jnp.float32)
        for row in range(cols_x):
            for y in range(cols_y):
                total = total + split_gram(
                    arrays[left * cols_x + row][y], arrays[right * cols_x + row][y]
                )
        out_ref[:, slot * count : (slot + 1) * count] = fold(total)


def pack(squares):
    count = squares[0].shape[0]
    row = lax.broadcasted_iota(jnp.int32, (count, count), 0)
    lane = lax.broadcasted_iota(jnp.int32, (count, count), 1)
    halves = [
        jnp.where(row >= lane, first, second)
        for first, second in zip(squares[0::2], squares[1::2])
    ]
    diagonals = [
        jnp.sum(jnp.where(row == lane, second, 0.0), axis=1, keepdims=True)
        for second in squares[1::2]
    ]
    used = len(halves) * (count + 1)
    packed = jnp.concatenate(
        halves + diagonals + [jnp.zeros((count, 64 - used), jnp.float32)], axis=1
    )
    return jnp.concatenate([packed[: count // 2], packed[count // 2 :]], axis=1)


def unpack(packed, number):
    count = 2 * packed.shape[0]
    packed = jnp.concatenate([packed[:, :64], packed[:, 64:]], axis=0)
    row = lax.broadcasted_iota(jnp.int32, (count, count), 0)
    lane = lax.broadcasted_iota(jnp.int32, (count, count), 1)
    squares = []
    for i in range(number // 2):
        half = packed[:, i * count : (i + 1) * count]
        place = number // 2 * count + i
        turned = half.T
        squares.append(jnp.where(row >= lane, half, turned))
        second = jnp.where(row <= lane, half, turned)
        squares.append(jnp.where(row == lane, packed[:, place : place + 1], second))
    return squares


def last_kernel(cols_x, *refs):
    v_refs, refs = refs[:cols_x], refs[cols_x:]
    (coef_ref, early_ref, late_ref, gram_ref), got, got_coefs = refs[:4], refs[4:6], refs[6:8]
    part_refs, w_refs, out_ref = refs[8 : 8 + cols_x], refs[8 + cols_x : -1], refs[-1]
    cols_y, count, _ = v_refs[0].shape
    total = gram_ref[...]
    for row, y in columns(cols_x, cols_y, True):
        w = complete(part_refs[row][y], v_refs, coef_ref, got, got_coefs, row, y) * (1.0 / SCALE)
        w_refs[row][y] = w
        total = total + split_gram(v_refs[row][y], w)
    squares = [
        ref[:, i * count : (i + 1) * count]
        for ref in (early_ref, late_ref)
        for i in range(ref.shape[1] // count)
    ]
    packed = pack(squares + [fold(total)])
    for peer in range(out_ref.shape[0]):
        out_ref[peer] = packed


def solve_spd(matrix, target):
    size, width = matrix.shape[0], matrix.shape[1] + target.shape[1]
    lanes = 128
    work = jnp.concatenate(
        [matrix, target, jnp.zeros((size, lanes - width), jnp.float32)], axis=1
    )
    row = lax.broadcasted_iota(jnp.int32, (size, lanes), 0)

    def spread(p):
        return jnp.broadcast_to(work[:, p : p + 1], (size, lanes))

    ahead = {p: spread(p) for p in range(AHEAD)}
    inverses = jnp.zeros((size, lanes), jnp.float32)
    for p in range(size):
        column = ahead.pop(p)
        if p + AHEAD < size:
            ahead[p + AHEAD] = spread(p + AHEAD)
        inverse = 1.0 / column[p : p + 1, :]
        inverses = jnp.where(row == p, inverse, inverses)
        factor = jnp.where(row == p, 0.0, column)

        def eliminate(value):
            return value - factor * jnp.broadcast_to(value[p : p + 1, :] * inverse, value.shape)

        ahead = {q: eliminate(value) for q, value in ahead.items()}
        work = eliminate(work)
    return work[:, size:width] * inverses[:, size:width]


def finish_kernel(cols_x, blocks, sums_ref, *refs):
    r_refs, refs = refs[:cols_x], refs[cols_x:]
    v_refs, w_refs, refs = refs[: blocks * cols_x], refs[blocks * cols_x : 2 * blocks * cols_x], refs[2 * blocks * cols_x :]
    x_hbm, out_hbm, x_ref, out_ref, sem = refs
    cols_y = r_refs[0].shape[0]
    joint = sums_ref[0]
    for peer in range(1, sums_ref.shape[0]):
        joint = joint + sums_ref[peer]
    moments = unpack(joint, 2 * blocks)
    matrix = jnp.concatenate(
        [
            jnp.concatenate([moments[1 + i + j] for j in range(blocks)], axis=1)
            for i in range(blocks)
        ],
        axis=0,
    )
    target = jnp.concatenate(moments[:blocks], axis=0)
    coefs = solve_spd(matrix, target).T
    high = coefs.astype(jnp.bfloat16)
    middle, low = split(coefs - high.astype(jnp.float32))
    left = jnp.concatenate([high, high, middle, middle, low], axis=1)

    def combine(values, row, y):
        highs, lows = zip(*(split(values[j * cols_x + row][y]) for j in range(blocks)))
        right = jnp.concatenate(highs + lows + highs + lows + highs, axis=0)
        return jnp.dot(left, right, preferred_element_type=jnp.float32)

    copies = []

    def send(columns, ref, hbm, row):
        ref[row] = jnp.transpose(jnp.stack(columns), (1, 0, 2))
        target = hbm.at[:, oriented(row, cols_x)]
        copies.append(pltpu.make_async_copy(ref.at[row], target, sem.at[len(copies)]))
        copies[-1].start()

    for row in range(cols_x):
        send([r_refs[row][y] - combine(w_refs, row, y) for y in range(cols_y)], out_ref, out_hbm, row)
        send([combine(v_refs, row, y) * (1.0 / SCALE) for y in range(cols_y)], x_ref, x_hbm, row)
    for copy in copies:
        copy.wait()


def pairing(sizes, axis, phase):
    transfers = []
    for place in np.ndindex(*sizes):
        partner = list(place)
        partner[axis] += 1 if place[axis] % 2 == phase else -1
        if not 0 <= partner[axis] < sizes[axis]:
            partner = list(place)
            partner[1 - axis] ^= 1
            if partner[1 - axis] >= sizes[1 - axis]:
                continue
        transfers.append(tuple(int(np.ravel_multi_index(p, sizes)) for p in (place, partner)))
    return transfers


def exchange(slot, edge):
    sizes = tuple(lax.axis_size(axis) for axis in AXES)
    return lax.ppermute(edge, AXES, pairing(sizes, slot // 2, slot % 2))


def on_device(sources, well_columns, column_active, perm_root, storage_term, inverse_blocks):
    count, cols_x, cols_y, layers = sources.shape
    number = cols_x * cols_y
    devices = lax.axis_size("wide") * lax.axis_size("narrow")
    blocks = inverse_blocks.reshape((number,) + inverse_blocks.shape[2:])
    state, rows = (cols_y, count, layers), (number, layers)
    flat = (cols_y * count, layers)
    apply_flops = 4 * count * number * layers * inverse_blocks.shape[-1]
    gram_flops = 8 * count * count * number * layers

    ends = (cols_x * (count + 1), layers)
    side = (cols_y * (count + 1), layers)
    by_row = (cols_x, count, cols_y, layers)
    out = call(
        start_kernel,
        [state] * (2 * cols_x)
        + [rows, rows, jax.ShapeDtypeStruct(blocks.shape, blocks.dtype), ends, ends, side, (side[0] + 8, layers)],
        [HBM] * 6,
        *(
            pltpu.with_memory_space_constraint(a, pltpu.HBM)
            for a in (well_columns, column_active, sources, perm_root, storage_term, blocks)
        ),
        flops=apply_flops,
        scratch=[
            pltpu.SMEM(well_columns.shape, jnp.int32),
            pltpu.SMEM(column_active.shape, jnp.int32),
            pltpu.VMEM(by_row, jnp.float32),
            pltpu.VMEM(perm_root.shape, jnp.float32),
            pltpu.VMEM(storage_term.shape, jnp.float32),
            pltpu.SemaphoreType.DMA((4,)),
            pltpu.SemaphoreType.DMA((cols_x,)),
            pltpu.SemaphoreType.DMA((cols_x,)),
        ],
    )
    rhs, v = out[:cols_x], out[cols_x : 2 * cols_x]
    coef, diag_term, blocks, *edges = out[2 * cols_x :]
    got_coefs = got = [exchange(slot, edge) for slot, edge in enumerate(edges)]
    vs, ws, grams = [v], [], []
    later_ends, later_side = (cols_x * count, layers), (cols_y * count + 8, layers)

    for j in range(1, ITERS):
        parts = call(
            functools.partial(middle_kernel, cols_x, False),
            [state] * (2 * cols_x),
            [VMEM] * (cols_x + 7),
            *vs[-1], coef, diag_term, *got[2:], *got_coefs[2:], blocks,
            flops=apply_flops,
        )
        out = call(
            functools.partial(end_kernel, cols_x),
            [state] * (2 * cols_x) + [later_ends] * 2 + [later_side],
            [VMEM] * (3 * cols_x + 6),
            *vs[-1], coef, blocks, *got[:2], *got_coefs[:2], *parts,
            flops=apply_flops // 4,
            aliases={cols_x + 6 + i: i for i in range(2 * cols_x)},
        )
        w, v, edges = out[:cols_x], out[cols_x : 2 * cols_x], out[2 * cols_x :]
        edges.insert(2, v[-1].reshape(flat))
        got = [exchange(slot, edge) for slot, edge in enumerate(edges)]
        vs.append(v)
        ws.append(w)
        arrays = vs[-2] + v + w + (rhs if j == 1 else [])
        pairs = ([(0, 3)] if j == 1 else []) + [(0, 2), (1, 2)]
        grams += call(
            functools.partial(gram_kernel, cols_x, pairs),
            [(count, len(pairs) * count)],
            [VMEM] * len(arrays),
            *arrays,
            flops=len(pairs) * gram_flops,
        )
    *parts, gram = call(
        functools.partial(middle_kernel, cols_x, True),
        [state] * cols_x + [(2 * count, 2 * count)],
        [VMEM] * (cols_x + 6),
        *vs[-1], coef, diag_term, *got[2:], *got_coefs[2:],
        flops=gram_flops,
    )
    *w, joint = call(
        functools.partial(last_kernel, cols_x),
        [state] * cols_x + [(devices, count // 2, 128)],
        [VMEM] * (2 * cols_x + 8),
        *vs[-1], coef, *grams, gram, *got[:2], *got_coefs[:2], *parts,
        flops=gram_flops // 4,
        aliases={cols_x + 8 + i: i for i in range(cols_x)},
    )
    ws.append(w)
    joint = lax.all_to_all(joint, AXES, 0, 0)
    outs = call(
        functools.partial(finish_kernel, cols_x, ITERS),
        [sources.shape] * 2,
        [VMEM] * (1 + cols_x + 2 * ITERS * cols_x),
        joint, *rhs, *(a for v in vs for a in v), *(a for w in ws for a in w),
        flops=24 * ITERS * count * count * number * layers,
        out_specs=[HBM, HBM],
        scratch=[
            pltpu.VMEM(by_row, jnp.float32),
            pltpu.VMEM(by_row, jnp.float32),
            pltpu.SemaphoreType.DMA((2 * cols_x,)),
        ],
    )
    return tuple(outs)


def solution(mesh):
    in_specs = (
        P(None, "wide", "narrow", None),
        P(),
        P("wide", "narrow"),
        P("wide", "narrow", None),
        P("wide", "narrow", None),
        P("wide", "narrow", None, None, None),
    )
    out_specs = (P(None, "wide", "narrow", None), P(None, "wide", "narrow", None))
    return jax.shard_map(
        on_device, mesh=mesh, in_specs=in_specs, out_specs=out_specs, check_vma=False
    )
```

time: 40.5 us -> 40.1 us (level)
  waiting for transfers between devices: 6.44 us -> 4.18 us
  starting transfers between devices: 12.1 us -> 13.3 us
    ppermute x12, waiting for transfers between devices: 6.44 us -> 4.18 us  [exchange(): return lax.ppermute(edge, AXES, pairing(sizes, slot // 2, slot % 2))]
    ppermute x12, starting transfers between devices: 12.1 us -> 13.3 us  [exchange(): return lax.ppermute(edge, AXES, pairing(sizes, slot // 2, slot % 2))]
    all_to_all x1, blocking collectives: 13.5 us -> 13.9 us  [on_device(): joint = lax.all_to_all(joint, AXES, 0, 0)]
    pallas_call x7 -> x10, Pallas kernels: 7.56 us -> 7.8 us  [call(): pl.pallas_call(kernel, out_shape=shapes, in_specs=in_specs, out_specs=out...]
  transfers between devices with their start and end apart: 12 -> 12, of which waited for: 3 -> 6; matrix products, arithmetic and copies ran while one was open for 0% -> 0% of each run, Pallas kernels for 3% -> 6%
where the time goes in v7:
time: 40.1 us; the launch traced here: 39.9 us
  blocking collectives  13.9 us (35%)
  starting transfers between devices  13.3 us (33%)
  Pallas kernels  7.8 us (19%)
  waiting for transfers between devices  4.18 us (10%)
  between operations  0.74 us (2%)
    all_to_all x1, blocking collectives, on_device(): joint = lax.all_to_all(joint, AXES, 0, 0)  13.9 us
    ppermute x12, starting transfers between devices, exchange(): return lax.ppermute(edge, AXES, pairing(sizes, slot // 2, slot % 2))  13.3 us
    pallas_call x10, Pallas kernels, call(): pl.pallas_call(kernel, out_shape=shapes, in_specs=in_specs, out_specs=out...  7.8 us
    ppermute x12, waiting for transfers between devices, exchange(): return lax.ppermute(edge, AXES, pairing(sizes, slot // 2, slot % 2))  4.18 us
  transfers between devices with their start and end apart: 12, of which 6 were waited for; matrix products, arithmetic and copies ran while one was open for 0% of the time, Pallas kernels for 6%

profile of v7, /device:TPU:0, one launch (start us, length us, event | category | flops | bytes accessed | tf_op | source)
XLA Modules:
  0.0 39.9 jit_solution(9441000203185212107)
XLA Ops:
  0.6 1.7 %shard_map.77 = (f32[8,16,256]{2,1,0:T(8,128)S(1)}, f32[8,16,256]{2,1,0:T(8,128)S(1)}, f32[8,16,256]{2,1,0:T(8,128)S(1)}, f32[8,16,256]{2,1,0:T(8,128)S(1)}, f32...) custom-call(s32[16]{0:T(128)} %wells_hbm.1, ...), custom_call_target="tpu_custom_call" | custom-call | flops 33554432 | bytes 4354176 | tf_op jit(solution)/shard_map/pallas_call | solution.py:26
  2.4 3.1 %collective-permute-start.3 = (f32[144,256]{1,0:T(8,128)S(1)}, f32[144,256]{1,0:T(8,128)S(1)}, u32[]{:S(2)}, u32[]{:S(2)}) collective-permute-start(f32[144,256]{1,0:T(8,128)S(1)} %get-tuple-element.49), channel_id=1, source_target_pairs={{0,8},{1,2},{2,1},{3,4},{4,3},{5,6},{6,5},{7,15},{8,0},{9,10},{10,... | collective-permute-start | bytes 442376 | tf_op jit(solution)/shard_map/ppermute | solution.py:431
  5.5 0.0 collective-permute-start.2
  5.5 1.6 %collective-permute-start = (f32[34,256]{1,0:T(8,128)S(1)}, f32[34,256]{1,0:T(8,128)S(1)}, u32[]{:S(2)}, u32[]{:S(2)}) collective-permute-start(f32[34,256]{1,0:T(8,128)S(1)} %get-tuple-element.45), channel_id=1, source_target_pairs={{0,8},{1,9},{2,10},{3,11},{4,12},{5,13},{6,14},{7,15},{8,0},{9,1},... | collective-permute-start | bytes 104456 | tf_op jit(solution)/shard_map/ppermute | solution.py:431
  7.1 1.5 %collective-permute-done.3.refs_5_.refs_7_ = f32[144,256]{1,0:T(8,128)S(1)} collective-permute-done((f32[144,256]{1,0:T(8,128)S(1)}, f32[144,256]{1,0:T(8,128)S(1)}, u32[]{:S(2)}, u32[]{:S(2)}) %collective-permute-start.3) | collective-permute-done | bytes 147488 | tf_op jit(solution)/shard_map/ppermute | solution.py:431
  8.6 0.4 %shard_map.78 = (f32[8,16,256]{2,1,0:T(8,128)S(1)}, f32[8,16,256]{2,1,0:T(8,128)S(1)}, f32[8,16,256]{2,1,0:T(8,128)S(1)}, f32[8,16,256]{2,1,0:T(8,128)S(1)}) custom-call(f32[8,16,256]{2,1,0:T(8,128)S(1)} %get-tuple-element.41.refs_0_.refs_2_, f32[8,16,256]{2,1,0:T(8,128)S(1)} %get-tuple-element.42.refs_1_.refs_3_, f32[16,256]{1,0:T(8,128)S(1)} %get-tuple-element.43.refs_2_, ...), custom_call_target="tpu_custom_call" | custom-call | flops 33554432 | bytes 2441216 | tf_op jit(solution)/shard_map/pallas_call | solution.py:26
  9.0 0.5 %collective-permute-done.refs_4_.refs_6_.refs_8_ = f32[34,256]{1,0:T(8,128)S(1)} collective-permute-done((f32[34,256]{1,0:T(8,128)S(1)}, f32[34,256]{1,0:T(8,128)S(1)}, u32[]{:S(2)}, u32[]{:S(2)}) %collective-permute-start) | collective-permute-done | bytes 34848 | tf_op jit(solution)/shard_map/ppermute | solution.py:431
  9.5 0.2 shard_map.79
  9.7 2.8 %collective-permute-start.7 = (f32[136,256]{1,0:T(8,128)S(1)}, f32[136,256]{1,0:T(8,128)S(1)}, u32[]{:S(2)}, u32[]{:S(2)}) collective-permute-start(f32[136,256]{1,0:T(8,128)S(1)} %get-tuple-element.58), channel_id=1, source_target_pairs={{0,8},{1,2},{2,1},{3,4},{4,3},{5,6},{6,5},{7,15},{8,0},{9,10},{10,... | collective-permute-start | bytes 417800 | tf_op jit(solution)/shard_map/ppermute | solution.py:431
  12.5 1.6 %collective-permute-start.4 = (f32[32,256]{1,0:T(8,128)S(1)}, f32[32,256]{1,0:T(8,128)S(1)}, u32[]{:S(2)}, u32[]{:S(2)}) collective-permute-start(f32[32,256]{1,0:T(8,128)S(1)} %get-tuple-element.56), channel_id=1, source_target_pairs={{0,8},{1,9},{2,10},{3,11},{4,12},{5,13},{6,14},{7,15},{8,0},{9,1},... | collective-permute-start | bytes 98312 | tf_op jit(solution)/shard_map/ppermute | solution.py:431
  14.1 1.4 %collective-permute-done.7.refs_5_ = f32[136,256]{1,0:T(8,128)S(1)} collective-permute-done((f32[136,256]{1,0:T(8,128)S(1)}, f32[136,256]{1,0:T(8,128)S(1)}, u32[]{:S(2)}, u32[]{:S(2)}) %collective-permute-start.7) | collective-permute-done | bytes 139296 | tf_op jit(solution)/shard_map/ppermute | solution.py:431
  15.5 0.4 shard_map.80
  15.9 0.5 %collective-permute-done.4.refs_4_ = f32[32,256]{1,0:T(8,128)S(1)} collective-permute-done((f32[32,256]{1,0:T(8,128)S(1)}, f32[32,256]{1,0:T(8,128)S(1)}, u32[]{:S(2)}, u32[]{:S(2)}) %collective-permute-start.4) | collective-permute-done | bytes 32800 | tf_op jit(solution)/shard_map/ppermute | solution.py:431
  16.4 0.2 shard_map.81
  16.6 2.1 %collective-permute-start.9 = (f32[136,256]{1,0:T(8,128)S(1)}, f32[136,256]{1,0:T(8,128)S(1)}, u32[]{:S(2)}, u32[]{:S(2)}) collective-permute-start(f32[136,256]{1,0:T(8,128)S(1)} %get-tuple-element.71), channel_id=1, source_target_pairs={{0,8},{1,2},{2,1},{3,4},{4,3},{5,6},{6,5},{7,15},{8,0},{9,10},{10,... | collective-permute-start | bytes 417800 | tf_op jit(solution)/shard_map/ppermute | solution.py:431
  18.7 2.2 %collective-permute-start.10 = (f32[32,256]{1,0:T(8,128)S(1)}, f32[32,256]{1,0:T(8,128)S(1)}, u32[]{:S(2)}, u32[]{:S(2)}) collective-permute-start(f32[32,256]{1,0:T(8,128)S(1)} %get-tuple-element.73), channel_id=1, source_target_pairs={{0,8},{1,9},{2,10},{3,11},{4,12},{5,13},{6,14},{7,15},{8,0},{9,1},... | collective-permute-start | bytes 98312 | tf_op jit(solution)/shard_map/ppermute | solution.py:431
  20.8 0.7 %shard_map.82.refs_3_ = f32[16,48]{1,0:T(8,128)S(1)} custom-call(f32[8,16,256]{2,1,0:T(8,128)S(1)} %get-tuple-element.41.refs_0_.refs_2_, f32[8,16,256]{2,1,0:T(8,128)S(1)} %get-tuple-element.42.refs_1_.refs_3_, f32[8,16,256]{2,1,0:T(8,128)S(1)} %get-tuple-element.54.refs_0_.refs_2_.refs_4_, f32[8,16,256]{2,1,0:T(8,128)S(1)} %get-tuple-element.55.refs_1_.refs_3_.refs_5_, ...), custom_call_target="tpu_custom_call" | custom-call | flops 25165824 | bytes 1051648 | tf_op jit(solution)/shard_map/pallas_call | solution.py:26
  21.5 0.5 %shard_map.83.refs_4_ = f32[16,32]{1,0:T(8,128)S(1)} custom-call(f32[8,16,256]{2,1,0:T(8,128)S(1)} %get-tuple-element.54.refs_0_.refs_2_.refs_4_, f32[8,16,256]{2,1,0:T(8,128)S(1)} %get-tuple-element.55.refs_1_.refs_3_.refs_5_, f32[8,16,256]{2,1,0:T(8,128)S(1)} %get-tuple-element.63.refs_2_.refs_0_.refs_6_, ...), custom_call_target="tpu_custom_call" | custom-call | flops 16777216 | bytes 788480 | tf_op jit(solution)/shard_map/pallas_call | solution.py:26
  22.0 0.1 collective-permute-done.9.refs_5_
  22.1 0.4 shard_map.84
  22.5 0.2 collective-permute-done.10.refs_6_
  22.7 0.4 %shard_map.85 = (f32[8,16,256]{2,1,0:T(8,128)S(1)}, f32[8,16,256]{2,1,0:T(8,128)S(1)}, f32[32,8,128]{2,1,0:T(8,128)S(1)}) custom-call(f32[8,16,256]{2,1,0:T(8,128)S(1)} %get-tuple-element.63.refs_2_.refs_0_.refs_6_, f32[8,16,256]{2,1,0:T(8,128)S(1)} %get-tuple-element.64.refs_3_.refs_1_.refs_7_, ...), custom_call_target="tpu_custom_call", output_to_operand_aliasing={{0}: (10, {}), {1}: (11, {})} | custom-call | flops 2097152 | bytes 1078272 | tf_op jit(solution)/shard_map/pallas_call | solution.py:26
  23.2 13.9 %all_to_all.5.sums_ref = f32[32,8,128]{2,1,0:T(8,128)S(1)} all-to-all(f32[32,8,128]{2,1,0:T(8,128)S(1)} %get-tuple-element.77), channel_id=1, replica_groups=mesh['narrow'=4,'wide'=8] {'narrow','wide'}, dimensions={0} | all-to-all | bytes 262144 | tf_op jit(solution)/shard_map/all_to_all | solution.py:520
  37.1 2.9 %shard_map.86 = (f32[16,2,8,256]{3,2,1,0:T(8,128)}, f32[16,2,8,256]{3,2,1,0:T(8,128)}) custom-call(f32[32,8,128]{2,1,0:T(8,128)S(1)} %all_to_all.5.sums_ref, f32[8,16,256]{2,1,0:T(8,128)S(1)} %get-tuple-element.67.refs_6_.refs_0_, f32[8,16,256]{2,1,0:T(8,128)S(1)} %get-tuple-element.68.refs_7_.refs_1_, f32[8,16,256]{2,1,0:T(8,128)S(1)} %get-tuple-element.41.refs_0_.refs_2_, ...), custom_call_target="tpu_custom_call" | custom-call | flops 75497472 | bytes 2490368 | tf_op jit(solution)/shard_map/pallas_call | solution.py:26
  (11 shorter events, 0.0 us)
Async XLA Ops:
  2.4 6.2 %collective-permute-start.3 = (f32[144,256]{1,0:T(8,128)S(1)}, f32[144,256]{1,0:T(8,128)S(1)}, u32[]{:S(2)}, u32[]{:S(2)}) collective-permute-start(f32[144,256]{1,0:T(8,128)S(1)} %get-tuple-element.49), channel_id=1, source_target_pairs={{0,8},{1,2},{2,1},{3,4},{4,3},{5,6},{6,5},{7,15},{8,0},{9,10},{10,... | collective-permute-start | bytes 442376 | tf_op jit(solution)/shard_map/ppermute | solution.py:431
  5.5 1.6 %collective-permute-start.2 = (f32[136,256]{1,0:T(8,128)S(1)}, f32[136,256]{1,0:T(8,128)S(1)}, u32[]{:S(2)}, u32[]{:S(2)}) collective-permute-start(f32[136,256]{1,0:T(8,128)S(1)} %get-tuple-element.48), channel_id=1, source_target_pairs={{0,1},{1,0},{2,3},{3,2},{4,5},{5,4},{6,7},{7,6},{8,9},{9,8},{10,11... | collective-permute-start | bytes 417800 | tf_op jit(solution)/shard_map/ppermute | solution.py:431
  5.5 4.0 %collective-permute-start = (f32[34,256]{1,0:T(8,128)S(1)}, f32[34,256]{1,0:T(8,128)S(1)}, u32[]{:S(2)}, u32[]{:S(2)}) collective-permute-start(f32[34,256]{1,0:T(8,128)S(1)} %get-tuple-element.45), channel_id=1, source_target_pairs={{0,8},{1,9},{2,10},{3,11},{4,12},{5,13},{6,14},{7,15},{8,0},{9,1},... | collective-permute-start | bytes 104456 | tf_op jit(solution)/shard_map/ppermute | solution.py:431
  7.1 2.4 %collective-permute-start.1 = (f32[34,256]{1,0:T(8,128)S(1)}, f32[34,256]{1,0:T(8,128)S(1)}, u32[]{:S(2)}, u32[]{:S(2)}) collective-permute-start(f32[34,256]{1,0:T(8,128)S(1)} %get-tuple-element.46), channel_id=1, source_target_pairs={{0,1},{1,0},{2,3},{3,2},{4,5},{5,4},{6,7},{7,6},{8,16},{9,17},{10,... | collective-permute-start | bytes 104456 | tf_op jit(solution)/shard_map/ppermute | solution.py:431
  9.7 5.8 %collective-permute-start.7 = (f32[136,256]{1,0:T(8,128)S(1)}, f32[136,256]{1,0:T(8,128)S(1)}, u32[]{:S(2)}, u32[]{:S(2)}) collective-permute-start(f32[136,256]{1,0:T(8,128)S(1)} %get-tuple-element.58), channel_id=1, source_target_pairs={{0,8},{1,2},{2,1},{3,4},{4,3},{5,6},{6,5},{7,15},{8,0},{9,10},{10,... | collective-permute-start | bytes 417800 | tf_op jit(solution)/shard_map/ppermute | solution.py:431
  12.5 1.6 %collective-permute-start.6 = (f32[128,256]{1,0:T(8,128)S(1)}, f32[128,256]{1,0:T(8,128)S(1)}, u32[]{:S(2)}, u32[]{:S(2)}) collective-permute-start(f32[128,256]{1,0:T(8,128)S(1)} %bitcast.3), channel_id=1, source_target_pairs={{0,1},{1,0},{2,3},{3,2},{4,5},{5,4},{6,7},{7,6},{8,9},{9,8},{10,11... | collective-permute-start | bytes 393224 | tf_op jit(solution)/shard_map/ppermute | solution.py:431
  12.5 3.9 %collective-permute-start.4 = (f32[32,256]{1,0:T(8,128)S(1)}, f32[32,256]{1,0:T(8,128)S(1)}, u32[]{:S(2)}, u32[]{:S(2)}) collective-permute-start(f32[32,256]{1,0:T(8,128)S(1)} %get-tuple-element.56), channel_id=1, source_target_pairs={{0,8},{1,9},{2,10},{3,11},{4,12},{5,13},{6,14},{7,15},{8,0},{9,1},... | collective-permute-start | bytes 98312 | tf_op jit(solution)/shard_map/ppermute | solution.py:431
  14.1 2.3 %collective-permute-start.5 = (f32[32,256]{1,0:T(8,128)S(1)}, f32[32,256]{1,0:T(8,128)S(1)}, u32[]{:S(2)}, u32[]{:S(2)}) collective-permute-start(f32[32,256]{1,0:T(8,128)S(1)} %get-tuple-element.57), channel_id=1, source_target_pairs={{0,1},{1,0},{2,3},{3,2},{4,5},{5,4},{6,7},{7,6},{8,16},{9,17},{10,... | collective-permute-start | bytes 98312 | tf_op jit(solution)/shard_map/ppermute | solution.py:431
  16.6 5.5 %collective-permute-start.9 = (f32[136,256]{1,0:T(8,128)S(1)}, f32[136,256]{1,0:T(8,128)S(1)}, u32[]{:S(2)}, u32[]{:S(2)}) collective-permute-start(f32[136,256]{1,0:T(8,128)S(1)} %get-tuple-element.71), channel_id=1, source_target_pairs={{0,8},{1,2},{2,1},{3,4},{4,3},{5,6},{6,5},{7,15},{8,0},{9,10},{10,... | collective-permute-start | bytes 417800 | tf_op jit(solution)/shard_map/ppermute | solution.py:431
  18.7 3.4 %collective-permute-start.8 = (f32[128,256]{1,0:T(8,128)S(1)}, f32[128,256]{1,0:T(8,128)S(1)}, u32[]{:S(2)}, u32[]{:S(2)}) collective-permute-start(f32[128,256]{1,0:T(8,128)S(1)} %bitcast.4), channel_id=1, source_target_pairs={{0,1},{1,0},{2,3},{3,2},{4,5},{5,4},{6,7},{7,6},{8,9},{9,8},{10,11... | collective-permute-start | bytes 393224 | tf_op jit(solution)/shard_map/ppermute | solution.py:431
  18.7 4.0 %collective-permute-start.10 = (f32[32,256]{1,0:T(8,128)S(1)}, f32[32,256]{1,0:T(8,128)S(1)}, u32[]{:S(2)}, u32[]{:S(2)}) collective-permute-start(f32[32,256]{1,0:T(8,128)S(1)} %get-tuple-element.73), channel_id=1, source_target_pairs={{0,8},{1,9},{2,10},{3,11},{4,12},{5,13},{6,14},{7,15},{8,0},{9,1},... | collective-permute-start | bytes 98312 | tf_op jit(solution)/shard_map/ppermute | solution.py:431
  20.8 1.9 %collective-permute-start.11 = (f32[32,256]{1,0:T(8,128)S(1)}, f32[32,256]{1,0:T(8,128)S(1)}, u32[]{:S(2)}, u32[]{:S(2)}) collective-permute-start(f32[32,256]{1,0:T(8,128)S(1)} %get-tuple-element.74), channel_id=1, source_target_pairs={{0,1},{1,0},{2,3},{3,2},{4,5},{5,4},{6,7},{7,6},{8,16},{9,17},{10,... | collective-permute-start | bytes 98312 | tf_op jit(solution)/shard_map/ppermute | solution.py:431

commit v8 on v7

--- a/solution.py
+++ b/solution.py
@@ -167,9 +167,8 @@
 
 def received(got, got_coefs, slot, i, number, count):
     place = number * count + i
-    which = slot % 2
-    value = got[which][i * count : (i + 1) * count, :]
-    return value, got_coefs[which][place : place + 1, :] * partnered(slot)
+    value = got[slot][i * count : (i + 1) * count, :]
+    return value, got_coefs[slot][place : place + 1, :] * partnered(slot)
 
 
 def operate(v_refs, coef_ref, diag_ref, got, got_coefs, row, y):
@@ -212,27 +211,27 @@
     return part
 
 
-def columns(cols_x, cols_y, at_ends):
+def columns(rows, cols_y, at_ends):
     return [
-        (row, y)
-        for row in range(cols_x)
-        for y in range(cols_y)
-        if (y in (0, cols_y - 1)) == at_ends
+        (row, y) for row in rows for y in range(cols_y) if (y in (0, cols_y - 1)) == at_ends
     ]
 
 
-def middle_kernel(cols_x, last, *refs):
+def middle_kernel(cols_x, rows, slots, last, *refs):
     v_refs, (coef_ref, diag_ref), refs = refs[:cols_x], refs[cols_x : cols_x + 2], refs[cols_x + 2 :]
-    got, got_coefs, refs = refs[:2], refs[2:4], refs[4:]
+    number = len(slots)
+    got, got_coefs = dict(zip(slots, refs)), dict(zip(slots, refs[number:]))
+    refs = refs[2 * number :]
     if last:
-        w_refs, gram_ref = refs[:cols_x], refs[cols_x]
+        w_refs, gram_ref = dict(zip(rows, refs)), refs[-1]
     else:
-        blocks_ref, w_refs, next_refs = refs[0], refs[1 : 1 + cols_x], refs[1 + cols_x :]
+        blocks_ref, refs = refs[0], refs[1:]
+        w_refs, next_refs = dict(zip(rows, refs)), dict(zip(rows, refs[len(rows) :]))
     cols_y, count, _ = v_refs[0].shape
     total = jnp.zeros((2 * count, 2 * count), jnp.float32)
-    for row, y in columns(cols_x, cols_y, True):
+    for row, y in columns(rows, cols_y, True):
         w_refs[row][y] = operate(v_refs, coef_ref, diag_ref, got, got_coefs, row, y)
-    for row, y in columns(cols_x, cols_y, False):
+    for row, y in columns(rows, cols_y, False):
         w = operate(v_refs, coef_ref, diag_ref, got, got_coefs, row, y) * (1.0 / SCALE)
         w_refs[row][y] = w
         if last:
@@ -249,7 +248,7 @@
     part_refs, refs = refs[:cols_x], refs[2 * cols_x :]
     w_refs, next_refs, edges = refs[:cols_x], refs[cols_x : 2 * cols_x], refs[2 * cols_x :]
     cols_y = v_refs[0].shape[0]
-    for row, y in columns(cols_x, cols_y, True):
+    for row, y in columns(range(cols_x), cols_y, True):
         w = complete(part_refs[row][y], v_refs, coef_ref, got, got_coefs, row, y) * (1.0 / SCALE)
         w_refs[row][y] = w
         next_refs[row][y] = apply_blocks(w, blocks_ref, row * cols_y + y)
@@ -321,13 +320,16 @@
     return squares
 
 
-def last_kernel(cols_x, *refs):
+def last_kernel(cols_x, grams, *refs):
     v_refs, refs = refs[:cols_x], refs[cols_x:]
-    (coef_ref, early_ref, late_ref, gram_ref), got, got_coefs = refs[:4], refs[4:6], refs[6:8]
-    part_refs, w_refs, out_ref = refs[8 : 8 + cols_x], refs[8 + cols_x : -1], refs[-1]
+    (coef_ref, early_ref, late_ref), got, got_coefs = refs[:3], refs[3:5], refs[5:7]
+    gram_refs, refs, out_ref = refs[7 : 7 + grams], refs[7 + grams : -1], refs[-1]
+    part_refs, w_refs = refs[:cols_x], refs[cols_x:]
     cols_y, count, _ = v_refs[0].shape
-    total = gram_ref[...]
-    for row, y in columns(cols_x, cols_y, True):
+    total = gram_refs[0][...]
+    for ref in gram_refs[1:]:
+        total = total + ref[...]
+    for row, y in columns(range(cols_x), cols_y, True):
         w = complete(part_refs[row][y], v_refs, coef_ref, got, got_coefs, row, y) * (1.0 / SCALE)
         w_refs[row][y] = w
         total = total + split_gram(v_refs[row][y], w)
@@ -471,14 +473,31 @@
     vs, ws, grams = [v], [], []
     later_ends, later_side = (cols_x * count, layers), (cols_y * count + 8, layers)
 
+    if cols_x > 1:
+        shares = [(tuple(range(1, cols_x)), (2,)), ((0,), (3,))]
+    else:
+        shares = [((0,), (2, 3))]
+
+    def middle(last):
+        w, v, totals = [], [], []
+        for rows, slots in shares:
+            out = call(
+                functools.partial(middle_kernel, cols_x, rows, slots, last),
+                [state] * (len(rows) * (1 if last else 2)) + [(2 * count, 2 * count)] * last,
+                [VMEM] * (cols_x + 3 - last + 2 * len(slots)),
+                *vs[-1], coef, diag_term, *(got[i] for i in slots), *(got_coefs[i] for i in slots),
+                *([] if last else [blocks]),
+                flops=apply_flops // len(shares),
+            )
+            w = out[: len(rows)] + w
+            if last:
+                totals += out[len(rows) :]
+            else:
+                v = out[len(rows) :] + v
+        return w + v, totals
+
     for j in range(1, ITERS):
-        parts = call(
-            functools.partial(middle_kernel, cols_x, False),
-            [state] * (2 * cols_x),
-            [VMEM] * (cols_x + 7),
-            *vs[-1], coef, diag_term, *got[2:], *got_coefs[2:], blocks,
-            flops=apply_flops,
-        )
+        parts, _ = middle(False)
         out = call(
             functools.partial(end_kernel, cols_x),
             [state] * (2 * cols_x) + [later_ends] * 2 + [later_side],
@@ -501,20 +520,14 @@
             *arrays,
             flops=len(pairs) * gram_flops,
         )
-    *parts, gram = call(
-        functools.partial(middle_kernel, cols_x, True),
-        [state] * cols_x + [(2 * count, 2 * count)],
-        [VMEM] * (cols_x + 6),
-        *vs[-1], coef, diag_term, *got[2:], *got_coefs[2:],
-        flops=gram_flops,
-    )
+    parts, totals = middle(True)
     *w, joint = call(
-        functools.partial(last_kernel, cols_x),
+        functools.partial(last_kernel, cols_x, len(totals)),
         [state] * cols_x + [(devices, count // 2, 128)],
-        [VMEM] * (2 * cols_x + 8),
-        *vs[-1], coef, *grams, gram, *got[:2], *got_coefs[:2], *parts,
+        [VMEM] * (2 * cols_x + 7 + len(totals)),
+        *vs[-1], coef, *grams, *got[:2], *got_coefs[:2], *totals, *parts,
         flops=gram_flops // 4,
-        aliases={cols_x + 8 + i: i for i in range(cols_x)},
+        aliases={cols_x + 7 + len(totals) + i: i for i in range(cols_x)},
     )
     ws.append(w)
     joint = lax.all_to_all(joint, AXES, 0, 0)

time: 40.1 us -> 39.9 us (level)
  waiting for transfers between devices: 4.18 us -> 3.57 us
  Pallas kernels: 7.8 us -> 8.39 us
    ppermute x12, waiting for transfers between devices: 4.18 us -> 3.57 us  [exchange(): return lax.ppermute(edge, AXES, pairing(sizes, slot // 2, slot % 2))]
    pallas_call x10 -> x13, Pallas kernels: 7.8 us -> 8.39 us  [call(): pl.pallas_call(kernel, out_shape=shapes, in_specs=in_specs, out_specs=out...]
  transfers between devices with their start and end apart: 12 -> 12, of which waited for: 6 -> 4; matrix products, arithmetic and copies ran while one was open for 0% -> 0% of each run, Pallas kernels for 6% -> 8%
where the time goes in v8:
time: 39.9 us; the launch traced here: 39.7 us
  blocking collectives  13.8 us (35%)
  starting transfers between devices  13.2 us (33%)
  Pallas kernels  8.39 us (21%)
  waiting for transfers between devices  3.57 us (9%)
  between operations  0.77 us (2%)
    all_to_all x1, blocking collectives, on_device(): joint = lax.all_to_all(joint, AXES, 0, 0)  13.8 us
    ppermute x12, starting transfers between devices, exchange(): return lax.ppermute(edge, AXES, pairing(sizes, slot // 2, slot % 2))  13.2 us
    pallas_call x13, Pallas kernels, call(): pl.pallas_call(kernel, out_shape=shapes, in_specs=in_specs, out_specs=out...  8.39 us
    ppermute x12, waiting for transfers between devices, exchange(): return lax.ppermute(edge, AXES, pairing(sizes, slot // 2, slot % 2))  3.57 us
  transfers between devices with their start and end apart: 12, of which 4 were waited for; matrix products, arithmetic and copies ran while one was open for 0% of the time, Pallas kernels for 8%

profile of v8, /device:TPU:0, one launch (start us, length us, event | category | flops | bytes accessed | tf_op | source)
XLA Modules:
  0.0 39.7 jit_solution(17656751021468684206)
XLA Ops:
  0.6 1.7 %shard_map.77 = (f32[8,16,256]{2,1,0:T(8,128)S(1)}, f32[8,16,256]{2,1,0:T(8,128)S(1)}, f32[8,16,256]{2,1,0:T(8,128)S(1)}, f32[8,16,256]{2,1,0:T(8,128)S(1)}, f32...) custom-call(s32[16]{0:T(128)} %wells_hbm.1, ...), custom_call_target="tpu_custom_call" | custom-call | flops 33554432 | bytes 4354176 | tf_op jit(solution)/shard_map/pallas_call | solution.py:26
  2.4 3.1 %collective-permute-start.2 = (f32[144,256]{1,0:T(8,128)S(1)}, f32[144,256]{1,0:T(8,128)S(1)}, u32[]{:S(2)}, u32[]{:S(2)}) collective-permute-start(f32[144,256]{1,0:T(8,128)S(1)} %get-tuple-element.49), channel_id=1, source_target_pairs={{0,8},{1,2},{2,1},{3,4},{4,3},{5,6},{6,5},{7,15},{8,0},{9,10},{10,... | collective-permute-start | bytes 442376 | tf_op jit(solution)/shard_map/ppermute | solution.py:433
  5.5 1.6 %collective-permute-start = (f32[34,256]{1,0:T(8,128)S(1)}, f32[34,256]{1,0:T(8,128)S(1)}, u32[]{:S(2)}, u32[]{:S(2)}) collective-permute-start(f32[34,256]{1,0:T(8,128)S(1)} %get-tuple-element.46), channel_id=1, source_target_pairs={{0,8},{1,9},{2,10},{3,11},{4,12},{5,13},{6,14},{7,15},{8,0},{9,1},... | collective-permute-start | bytes 104456 | tf_op jit(solution)/shard_map/ppermute | solution.py:433
  7.1 0.3 shard_map.79
  7.4 1.2 %collective-permute-done.2.refs_4_.refs_5_ = f32[144,256]{1,0:T(8,128)S(1)} collective-permute-done((f32[144,256]{1,0:T(8,128)S(1)}, f32[144,256]{1,0:T(8,128)S(1)}, u32[]{:S(2)}, u32[]{:S(2)}) %collective-permute-start.2) | collective-permute-done | bytes 147488 | tf_op jit(solution)/shard_map/ppermute | solution.py:433
  8.6 0.3 shard_map.78
  8.9 0.6 %collective-permute-done.refs_4_.refs_6_.refs_7_ = f32[34,256]{1,0:T(8,128)S(1)} collective-permute-done((f32[34,256]{1,0:T(8,128)S(1)}, f32[34,256]{1,0:T(8,128)S(1)}, u32[]{:S(2)}, u32[]{:S(2)}) %collective-permute-start) | collective-permute-done | bytes 34848 | tf_op jit(solution)/shard_map/ppermute | solution.py:433
  9.5 0.2 shard_map.80
  9.7 2.8 %collective-permute-start.6 = (f32[136,256]{1,0:T(8,128)S(1)}, f32[136,256]{1,0:T(8,128)S(1)}, u32[]{:S(2)}, u32[]{:S(2)}) collective-permute-start(f32[136,256]{1,0:T(8,128)S(1)} %get-tuple-element.59), channel_id=1, source_target_pairs={{0,8},{1,2},{2,1},{3,4},{4,3},{5,6},{6,5},{7,15},{8,0},{9,10},{10,... | collective-permute-start | bytes 417800 | tf_op jit(solution)/shard_map/ppermute | solution.py:433
  12.5 1.6 %collective-permute-start.4 = (f32[32,256]{1,0:T(8,128)S(1)}, f32[32,256]{1,0:T(8,128)S(1)}, u32[]{:S(2)}, u32[]{:S(2)}) collective-permute-start(f32[32,256]{1,0:T(8,128)S(1)} %get-tuple-element.57), channel_id=1, source_target_pairs={{0,8},{1,9},{2,10},{3,11},{4,12},{5,13},{6,14},{7,15},{8,0},{9,1},... | collective-permute-start | bytes 98312 | tf_op jit(solution)/shard_map/ppermute | solution.py:433
  14.1 0.3 shard_map.82
  14.4 1.1 %collective-permute-done.6.refs_4_ = f32[136,256]{1,0:T(8,128)S(1)} collective-permute-done((f32[136,256]{1,0:T(8,128)S(1)}, f32[136,256]{1,0:T(8,128)S(1)}, u32[]{:S(2)}, u32[]{:S(2)}) %collective-permute-start.6) | collective-permute-done | bytes 139296 | tf_op jit(solution)/shard_map/ppermute | solution.py:433
  15.5 0.3 shard_map.81
  15.8 0.6 %collective-permute-done.4.refs_4_ = f32[32,256]{1,0:T(8,128)S(1)} collective-permute-done((f32[32,256]{1,0:T(8,128)S(1)}, f32[32,256]{1,0:T(8,128)S(1)}, u32[]{:S(2)}, u32[]{:S(2)}) %collective-permute-start.4) | collective-permute-done | bytes 32800 | tf_op jit(solution)/shard_map/ppermute | solution.py:433
  16.4 0.2 shard_map.83
  16.6 2.1 %collective-permute-start.11 = (f32[136,256]{1,0:T(8,128)S(1)}, f32[136,256]{1,0:T(8,128)S(1)}, u32[]{:S(2)}, u32[]{:S(2)}) collective-permute-start(f32[136,256]{1,0:T(8,128)S(1)} %get-tuple-element.75), channel_id=1, source_target_pairs={{0,8},{1,2},{2,1},{3,4},{4,3},{5,6},{6,5},{7,15},{8,0},{9,10},{10,... | collective-permute-start | bytes 417800 | tf_op jit(solution)/shard_map/ppermute | solution.py:433
  18.7 2.0 %collective-permute-start.8 = (f32[32,256]{1,0:T(8,128)S(1)}, f32[32,256]{1,0:T(8,128)S(1)}, u32[]{:S(2)}, u32[]{:S(2)}) collective-permute-start(f32[32,256]{1,0:T(8,128)S(1)} %get-tuple-element.72), channel_id=1, source_target_pairs={{0,8},{1,9},{2,10},{3,11},{4,12},{5,13},{6,14},{7,15},{8,0},{9,1},... | collective-permute-start | bytes 98312 | tf_op jit(solution)/shard_map/ppermute | solution.py:433
  20.7 0.7 %shard_map.84.refs_3_ = f32[16,48]{1,0:T(8,128)S(1)} custom-call(f32[8,16,256]{2,1,0:T(8,128)S(1)} %get-tuple-element.42.refs_0_.refs_2_, f32[8,16,256]{2,1,0:T(8,128)S(1)} %get-tuple-element.43.refs_1_.refs_3_, f32[8,16,256]{2,1,0:T(8,128)S(1)} %get-tuple-element.55.refs_0_.refs_2_.refs_4_, f32[8,16,256]{2,1,0:T(8,128)S(1)} %get-tuple-element.56.refs_1_.refs_3_.refs_5_, ...), custom_call_target="tpu_custom_call" | custom-call | flops 25165824 | bytes 1051648 | tf_op jit(solution)/shard_map/pallas_call | solution.py:26
  21.4 0.5 %shard_map.85.refs_4_ = f32[16,32]{1,0:T(8,128)S(1)} custom-call(f32[8,16,256]{2,1,0:T(8,128)S(1)} %get-tuple-element.55.refs_0_.refs_2_.refs_4_, f32[8,16,256]{2,1,0:T(8,128)S(1)} %get-tuple-element.56.refs_1_.refs_3_.refs_5_, f32[8,16,256]{2,1,0:T(8,128)S(1)} %get-tuple-element.64.refs_2_.refs_0_.refs_6_, ...), custom_call_target="tpu_custom_call" | custom-call | flops 16777216 | bytes 788480 | tf_op jit(solution)/shard_map/pallas_call | solution.py:26
  21.9 0.3 shard_map.86
  22.3 0.3 shard_map.87
  22.6 0.4 %shard_map.88 = (f32[8,16,256]{2,1,0:T(8,128)S(1)}, f32[8,16,256]{2,1,0:T(8,128)S(1)}, f32[32,8,128]{2,1,0:T(8,128)S(1)}) custom-call(f32[8,16,256]{2,1,0:T(8,128)S(1)} %get-tuple-element.64.refs_2_.refs_0_.refs_6_, f32[8,16,256]{2,1,0:T(8,128)S(1)} %get-tuple-element.65.refs_3_.refs_1_.refs_7_, ...), custom_call_target="tpu_custom_call", output_to_operand_aliasing={{0}: (11, {}), {1}: (12, {})} | custom-call | flops 2097152 | bytes 1082368 | tf_op jit(solution)/shard_map/pallas_call | solution.py:26
  23.1 13.8 %all_to_all.5.sums_ref = f32[32,8,128]{2,1,0:T(8,128)S(1)} all-to-all(f32[32,8,128]{2,1,0:T(8,128)S(1)} %get-tuple-element.79), channel_id=1, replica_groups=mesh['narrow'=4,'wide'=8] {'narrow','wide'}, dimensions={0} | all-to-all | bytes 262144 | tf_op jit(solution)/shard_map/all_to_all | solution.py:533
  36.9 2.9 %shard_map.89 = (f32[16,2,8,256]{3,2,1,0:T(8,128)}, f32[16,2,8,256]{3,2,1,0:T(8,128)}) custom-call(f32[32,8,128]{2,1,0:T(8,128)S(1)} %all_to_all.5.sums_ref, f32[8,16,256]{2,1,0:T(8,128)S(1)} %get-tuple-element.68.refs_6_.refs_0_, f32[8,16,256]{2,1,0:T(8,128)S(1)} %get-tuple-element.69.refs_7_.refs_1_, f32[8,16,256]{2,1,0:T(8,128)S(1)} %get-tuple-element.42.refs_0_.refs_2_, ...), custom_call_target="tpu_custom_call" | custom-call | flops 75497472 | bytes 2490368 | tf_op jit(solution)/shard_map/pallas_call | solution.py:26
  (14 shorter events, 0.1 us)
Async XLA Ops:
  2.4 6.2 %collective-permute-start.2 = (f32[144,256]{1,0:T(8,128)S(1)}, f32[144,256]{1,0:T(8,128)S(1)}, u32[]{:S(2)}, u32[]{:S(2)}) collective-permute-start(f32[144,256]{1,0:T(8,128)S(1)} %get-tuple-element.49), channel_id=1, source_target_pairs={{0,8},{1,2},{2,1},{3,4},{4,3},{5,6},{6,5},{7,15},{8,0},{9,10},{10,... | collective-permute-start | bytes 442376 | tf_op jit(solution)/shard_map/ppermute | solution.py:433
  5.5 1.6 %collective-permute-start.3 = (f32[136,256]{1,0:T(8,128)S(1)}, f32[136,256]{1,0:T(8,128)S(1)}, u32[]{:S(2)}, u32[]{:S(2)}) collective-permute-start(f32[136,256]{1,0:T(8,128)S(1)} %get-tuple-element.51), channel_id=1, source_target_pairs={{0,1},{1,0},{2,3},{3,2},{4,5},{5,4},{6,7},{7,6},{8,9},{9,8},{10,11... | collective-permute-start | bytes 417800 | tf_op jit(solution)/shard_map/ppermute | solution.py:433
  5.5 4.0 %collective-permute-start = (f32[34,256]{1,0:T(8,128)S(1)}, f32[34,256]{1,0:T(8,128)S(1)}, u32[]{:S(2)}, u32[]{:S(2)}) collective-permute-start(f32[34,256]{1,0:T(8,128)S(1)} %get-tuple-element.46), channel_id=1, source_target_pairs={{0,8},{1,9},{2,10},{3,11},{4,12},{5,13},{6,14},{7,15},{8,0},{9,1},... | collective-permute-start | bytes 104456 | tf_op jit(solution)/shard_map/ppermute | solution.py:433
  7.1 2.4 %collective-permute-start.1 = (f32[34,256]{1,0:T(8,128)S(1)}, f32[34,256]{1,0:T(8,128)S(1)}, u32[]{:S(2)}, u32[]{:S(2)}) collective-permute-start(f32[34,256]{1,0:T(8,128)S(1)} %get-tuple-element.47), channel_id=1, source_target_pairs={{0,1},{1,0},{2,3},{3,2},{4,5},{5,4},{6,7},{7,6},{8,16},{9,17},{10,... | collective-permute-start | bytes 104456 | tf_op jit(solution)/shard_map/ppermute | solution.py:433
  9.7 5.8 %collective-permute-start.6 = (f32[136,256]{1,0:T(8,128)S(1)}, f32[136,256]{1,0:T(8,128)S(1)}, u32[]{:S(2)}, u32[]{:S(2)}) collective-permute-start(f32[136,256]{1,0:T(8,128)S(1)} %get-tuple-element.59), channel_id=1, source_target_pairs={{0,8},{1,2},{2,1},{3,4},{4,3},{5,6},{6,5},{7,15},{8,0},{9,10},{10,... | collective-permute-start | bytes 417800 | tf_op jit(solution)/shard_map/ppermute | solution.py:433
  12.5 1.6 %collective-permute-start.7 = (f32[128,256]{1,0:T(8,128)S(1)}, f32[128,256]{1,0:T(8,128)S(1)}, u32[]{:S(2)}, u32[]{:S(2)}) collective-permute-start(f32[128,256]{1,0:T(8,128)S(1)} %bitcast.3), channel_id=1, source_target_pairs={{0,1},{1,0},{2,3},{3,2},{4,5},{5,4},{6,7},{7,6},{8,9},{9,8},{10,11... | collective-permute-start | bytes 393224 | tf_op jit(solution)/shard_map/ppermute | solution.py:433
  12.5 3.9 %collective-permute-start.4 = (f32[32,256]{1,0:T(8,128)S(1)}, f32[32,256]{1,0:T(8,128)S(1)}, u32[]{:S(2)}, u32[]{:S(2)}) collective-permute-start(f32[32,256]{1,0:T(8,128)S(1)} %get-tuple-element.57), channel_id=1, source_target_pairs={{0,8},{1,9},{2,10},{3,11},{4,12},{5,13},{6,14},{7,15},{8,0},{9,1},... | collective-permute-start | bytes 98312 | tf_op jit(solution)/shard_map/ppermute | solution.py:433
  14.1 2.3 %collective-permute-start.5 = (f32[32,256]{1,0:T(8,128)S(1)}, f32[32,256]{1,0:T(8,128)S(1)}, u32[]{:S(2)}, u32[]{:S(2)}) collective-permute-start(f32[32,256]{1,0:T(8,128)S(1)} %get-tuple-element.58), channel_id=1, source_target_pairs={{0,1},{1,0},{2,3},{3,2},{4,5},{5,4},{6,7},{7,6},{8,16},{9,17},{10,... | collective-permute-start | bytes 98312 | tf_op jit(solution)/shard_map/ppermute | solution.py:433
  16.6 5.7 %collective-permute-start.11 = (f32[136,256]{1,0:T(8,128)S(1)}, f32[136,256]{1,0:T(8,128)S(1)}, u32[]{:S(2)}, u32[]{:S(2)}) collective-permute-start(f32[136,256]{1,0:T(8,128)S(1)} %get-tuple-element.75), channel_id=1, source_target_pairs={{0,8},{1,2},{2,1},{3,4},{4,3},{5,6},{6,5},{7,15},{8,0},{9,10},{10,... | collective-permute-start | bytes 417800 | tf_op jit(solution)/shard_map/ppermute | solution.py:433
  18.7 3.3 %collective-permute-start.10 = (f32[128,256]{1,0:T(8,128)S(1)}, f32[128,256]{1,0:T(8,128)S(1)}, u32[]{:S(2)}, u32[]{:S(2)}) collective-permute-start(f32[128,256]{1,0:T(8,128)S(1)} %bitcast.4), channel_id=1, source_target_pairs={{0,1},{1,0},{2,3},{3,2},{4,5},{5,4},{6,7},{7,6},{8,9},{9,8},{10,11... | collective-permute-start | bytes 393224 | tf_op jit(solution)/shard_map/ppermute | solution.py:433
  18.7 3.9 %collective-permute-start.8 = (f32[32,256]{1,0:T(8,128)S(1)}, f32[32,256]{1,0:T(8,128)S(1)}, u32[]{:S(2)}, u32[]{:S(2)}) collective-permute-start(f32[32,256]{1,0:T(8,128)S(1)} %get-tuple-element.72), channel_id=1, source_target_pairs={{0,8},{1,9},{2,10},{3,11},{4,12},{5,13},{6,14},{7,15},{8,0},{9,1},... | collective-permute-start | bytes 98312 | tf_op jit(solution)/shard_map/ppermute | solution.py:433
  20.7 1.9 %collective-permute-start.9 = (f32[32,256]{1,0:T(8,128)S(1)}, f32[32,256]{1,0:T(8,128)S(1)}, u32[]{:S(2)}, u32[]{:S(2)}) collective-permute-start(f32[32,256]{1,0:T(8,128)S(1)} %get-tuple-element.73), channel_id=1, source_target_pairs={{0,1},{1,0},{2,3},{3,2},{4,5},{5,4},{6,7},{7,6},{8,16},{9,17},{10,... | collective-permute-start | bytes 98312 | tf_op jit(solution)/shard_map/ppermute | solution.py:433

commit v9 on v8

--- a/solution.py
+++ b/solution.py
@@ -17,7 +17,7 @@
 AHEAD = 6
 
 
-def call(kernel, out_shape, in_specs, *args, flops=0, out_specs=None, scratch=(), aliases=None):
+def call(kernel, out_shape, in_specs, *args, flops=0, out_specs=None, scratch=()):
     shapes = [
         s if isinstance(s, jax.ShapeDtypeStruct) else jax.ShapeDtypeStruct(s, jnp.float32)
         for s in out_shape
@@ -29,7 +29,6 @@
         in_specs=in_specs,
         out_specs=out_specs or [VMEM] * len(shapes),
         scratch_shapes=list(scratch),
-        input_output_aliases=aliases or {},
         compiler_params=pltpu.CompilerParams(vmem_limit_bytes=VMEM_BYTES),
         cost_estimate=pl.CostEstimate(flops=flops, bytes_accessed=size, transcendentals=0),
     )(*args)
@@ -184,81 +183,85 @@
     total = total + lower_coef * (center - pltpu.roll(center, 1, 1))
     for step_row, step_y in ((1, 0), (-1, 0), (0, 1), (0, -1)):
         other, ny = row + step_row, y + step_y
-        if not 0 <= ny < cols_y:
-            continue
-        if 0 <= other < cols_x:
+        if 0 <= ny < cols_y and 0 <= other < cols_x:
             place = other * cols_y + ny
             value, other_coef = v_refs[other][ny], coef_ref[place : place + 1, :]
-        else:
+        elif step_row:
             slot = 3 if step_row < 0 else 2
             value, other_coef = received(got, got_coefs, slot, y, cols_y, count)
+        else:
+            odd = lax.rem(lax.axis_index("narrow"), 2) == 1
+            first, c_first = received(got, got_coefs, 0, row, cols_x, count)
+            second, c_second = received(got, got_coefs, 1, row, cols_x, count)
+            low = step_y < 0
+            value = jnp.where(odd == low, first, second)
+            other_coef = jnp.where(odd == low, c_first, c_second)
         total = total + other_coef * (center - value)
-    return diag_ref[col : col + 1, :] * center + coef * total
-
-
-def complete(part, v_refs, coef_ref, got, got_coefs, row, y):
-    cols_x = len(v_refs)
-    cols_y, count, _ = v_refs[row].shape
-    col = row * cols_y + y
-    odd = lax.rem(lax.axis_index("narrow"), 2) == 1
-    first, c_first = received(got, got_coefs, 0, row, cols_x, count)
-    second, c_second = received(got, got_coefs, 1, row, cols_x, count)
-    for at_end, low in ((y == 0, True), (y == cols_y - 1, False)):
-        if at_end:
-            value = jnp.where(odd == low, first, second)
-            face = coef_ref[col : col + 1, :] * jnp.where(odd == low, c_first, c_second)
-            part = part + face * (v_refs[row][y] - value)
-    return part
-
-
-def columns(rows, cols_y, at_ends):
-    return [
-        (row, y) for row in rows for y in range(cols_y) if (y in (0, cols_y - 1)) == at_ends
-    ]
-
-
-def middle_kernel(cols_x, rows, slots, last, *refs):
+    return (diag_ref[col : col + 1, :] * center + coef * total) * (1.0 / SCALE)
+
+
+def row_kernel(cols_x, rows, slots, after, *refs):
+    v_refs, (coef_ref, diag_ref), refs = refs[:cols_x], refs[cols_x : cols_x + 2], refs[cols_x + 2 :]
+    number = len(slots)
+    got, got_coefs = dict(zip(slots, refs)), dict(zip(slots, refs[number:]))
+    blocks_ref, refs = refs[2 * number], refs[2 * number + 1 + after :]
+    others = cols_x - len(rows) if rows[0] == 0 else 0
+    done, refs = refs[:others], refs[others:]
+    w_refs, next_refs, edges = refs[: len(rows)], refs[len(rows) : 2 * len(rows)], refs[2 * len(rows) :]
+    cols_y = v_refs[0].shape[0]
+    for row, w_ref, next_ref in zip(rows, w_refs, next_refs):
+        for y in range(cols_y):
+            w = operate(v_refs, coef_ref, diag_ref, got, got_coefs, row, y)
+            w_ref[y] = w
+            next_ref[y] = apply_blocks(w, blocks_ref, row * cols_y + y)
+    if edges:
+        write_edges((*next_refs, *done), None, edges[:2])
+        write_side(0, next_refs[0], None, edges[2])
+
+
+def share_size(matrices, count):
+    return (matrices * (count + 1) + 1) // 2
+
+
+def lanes_of(used):
+    return -(-used // 64) * 64
+
+
+def last_kernel(cols_x, rows, slots, grams, *refs):
     v_refs, (coef_ref, diag_ref), refs = refs[:cols_x], refs[cols_x : cols_x + 2], refs[cols_x + 2 :]
     number = len(slots)
     got, got_coefs = dict(zip(slots, refs)), dict(zip(slots, refs[number:]))
     refs = refs[2 * number :]
-    if last:
-        w_refs, gram_ref = dict(zip(rows, refs)), refs[-1]
-    else:
-        blocks_ref, refs = refs[0], refs[1:]
-        w_refs, next_refs = dict(zip(rows, refs)), dict(zip(rows, refs[len(rows) :]))
+    gram_refs, w_refs, out_ref = refs[:grams], refs[grams:-1], refs[-1]
     cols_y, count, _ = v_refs[0].shape
     total = jnp.zeros((2 * count, 2 * count), jnp.float32)
-    for row, y in columns(rows, cols_y, True):
-        w_refs[row][y] = operate(v_refs, coef_ref, diag_ref, got, got_coefs, row, y)
-    for row, y in columns(rows, cols_y, False):
-        w = operate(v_refs, coef_ref, diag_ref, got, got_coefs, row, y) * (1.0 / SCALE)
-        w_refs[row][y] = w
-        if last:
-            total = total + split_gram(v_refs[row][y], w)
-        else:
-            next_refs[row][y] = apply_blocks(w, blocks_ref, row * cols_y + y)
-    if last:
-        gram_ref[...] = total
-
-
-def end_kernel(cols_x, *refs):
-    v_refs, refs = refs[:cols_x], refs[cols_x:]
-    (coef_ref, blocks_ref), got, got_coefs, refs = refs[:2], refs[2:4], refs[4:6], refs[6:]
-    part_refs, refs = refs[:cols_x], refs[2 * cols_x :]
-    w_refs, next_refs, edges = refs[:cols_x], refs[cols_x : 2 * cols_x], refs[2 * cols_x :]
-    cols_y = v_refs[0].shape[0]
-    for row, y in columns(range(cols_x), cols_y, True):
-        w = complete(part_refs[row][y], v_refs, coef_ref, got, got_coefs, row, y) * (1.0 / SCALE)
-        w_refs[row][y] = w
-        next_refs[row][y] = apply_blocks(w, blocks_ref, row * cols_y + y)
-    write_edges(next_refs, None, edges[:2])
-    write_side(0, next_refs[0], None, edges[2])
-
-
-def split_gram(left, right):
+    for ref in gram_refs[2:]:
+        total = total + ref[...]
+    for row, w_ref in zip(rows, w_refs):
+        for y in range(cols_y):
+            w = operate(v_refs, coef_ref, diag_ref, got, got_coefs, row, y)
+            w_ref[y] = w
+            total = total + split_gram([v_refs[row][y]], w)
+    if rows[0] != 0:
+        out_ref[...] = total
+        return
+    size = share_size(2 * ITERS - 1, count)
+    last = fold_square(fold(total))
+    used = size + last.shape[1]
+    rest = jnp.zeros((count // 2, lanes_of(used) - used), jnp.float32)
+    early = (gram_refs[0][...] + gram_refs[1][...])[:, :size]
+    packed = jnp.concatenate([early, last, rest], axis=1)
+    middle = count // 4
+    packed = jnp.concatenate(
+        [packed[:middle], packed[middle:]], axis=1
+    )
+    for peer in range(out_ref.shape[0]):
+        out_ref[peer] = packed
+
+
+def split_gram(lefts, right):
     return lax.dot_general(
-        jnp.concatenate(split(left), axis=0),
+        jnp.concatenate([term for left in lefts for term in split(left)], axis=0),
         jnp.concatenate(split(right), axis=0),
         (((1,), (1,)), ((), ())),
         preferred_element_type=jnp.float32,
@@ -272,75 +275,83 @@
     return 0.5 * (total + total.T)
 
 
-def gram_kernel(cols_x, pairs, *refs):
-    arrays, out_ref = refs[:-1], refs[-1]
+def grams_of(cols_x, groups, arrays):
     cols_y, count, _ = arrays[0].shape
-    for slot, (left, right) in enumerate(pairs):
-        total = jnp.zeros((2 * count, 2 * count), jnp.float32)
+    squares = []
+    for lefts, right in groups:
+        total = jnp.zeros((2 * count * len(lefts), 2 * count), jnp.float32)
         for row in range(cols_x):
             for y in range(cols_y):
                 total = total + split_gram(
-                    arrays[left * cols_x + row][y], arrays[right * cols_x + row][y]
+                    [arrays[left * cols_x + row][y] for left in lefts],
+                    arrays[right * cols_x + row][y],
                 )
-        out_ref[:, slot * count : (slot + 1) * count] = fold(total)
-
-
-def pack(squares):
-    count = squares[0].shape[0]
-    row = lax.broadcasted_iota(jnp.int32, (count, count), 0)
-    lane = lax.broadcasted_iota(jnp.int32, (count, count), 1)
-    halves = [
-        jnp.where(row >= lane, first, second)
-        for first, second in zip(squares[0::2], squares[1::2])
+        squares += [fold(total[2 * count * i : 2 * count * (i + 1)]) for i in range(len(lefts))]
+    return squares
+
+
+def gram_kernel(cols_x, groups, *refs):
+    refs[-1][...] = jnp.concatenate(grams_of(cols_x, groups, refs[:-1]), axis=1)
+
+
+def fold_square(square):
+    half = square.shape[0] // 2
+    bottom = jnp.concatenate([square[half:], jnp.zeros((half, 1), jnp.float32)], axis=1)
+    top = jnp.concatenate(
+        [jnp.zeros((half, half + 1), jnp.float32), square[:half, :half]], axis=1
+    )
+    row = lax.broadcasted_iota(jnp.int32, bottom.shape, 0)
+    lane = lax.broadcasted_iota(jnp.int32, bottom.shape, 1)
+    return jnp.where(lane <= half + row, bottom, top)
+
+
+def unfold_squares(folded):
+    half = folded.shape[0]
+    row = lax.broadcasted_iota(jnp.int32, (half, half), 0)
+    lane = lax.broadcasted_iota(jnp.int32, (half, half), 1)
+    diagonal = jnp.where(row == lane, 0.5, 1.0)
+    width = 2 * half + 1
+    parts = []
+    for i in range(folded.shape[1] // width):
+        one = folded[:, i * width : (i + 1) * width]
+        upper = jnp.where(row <= lane, one[:, half + 1 :] * diagonal, 0.0)
+        lower = jnp.where(row >= lane, one[:, half : 2 * half] * diagonal, 0.0)
+        parts.append(
+            jnp.concatenate(
+                [
+                    jnp.concatenate([upper, jnp.zeros_like(upper)], axis=1),
+                    jnp.concatenate([one[:, :half], lower], axis=1),
+                ],
+                axis=0,
+            )
+        )
+    turned = jnp.concatenate(parts, axis=1).T
+    return [
+        part + turned[2 * half * i : 2 * half * (i + 1)] for i, part in enumerate(parts)
     ]
-    diagonals = [
-        jnp.sum(jnp.where(row == lane, second, 0.0), axis=1, keepdims=True)
-        for second in squares[1::2]
-    ]
-    used = len(halves) * (count + 1)
-    packed = jnp.concatenate(
-        halves + diagonals + [jnp.zeros((count, 64 - used), jnp.float32)], axis=1
-    )
-    return jnp.concatenate([packed[: count // 2], packed[count // 2 :]], axis=1)
-
-
-def unpack(packed, number):
-    count = 2 * packed.shape[0]
-    packed = jnp.concatenate([packed[:, :64], packed[:, 64:]], axis=0)
-    row = lax.broadcasted_iota(jnp.int32, (count, count), 0)
-    lane = lax.broadcasted_iota(jnp.int32, (count, count), 1)
-    squares = []
-    for i in range(number // 2):
-        half = packed[:, i * count : (i + 1) * count]
-        place = number // 2 * count + i
-        turned = half.T
-        squares.append(jnp.where(row >= lane, half, turned))
-        second = jnp.where(row <= lane, half, turned)
-        squares.append(jnp.where(row == lane, packed[:, place : place + 1], second))
-    return squares
-
-
-def last_kernel(cols_x, grams, *refs):
-    v_refs, refs = refs[:cols_x], refs[cols_x:]
-    (coef_ref, early_ref, late_ref), got, got_coefs = refs[:3], refs[3:5], refs[5:7]
-    gram_refs, refs, out_ref = refs[7 : 7 + grams], refs[7 + grams : -1], refs[-1]
-    part_refs, w_refs = refs[:cols_x], refs[cols_x:]
-    cols_y, count, _ = v_refs[0].shape
-    total = gram_refs[0][...]
-    for ref in gram_refs[1:]:
-        total = total + ref[...]
-    for row, y in columns(range(cols_x), cols_y, True):
-        w = complete(part_refs[row][y], v_refs, coef_ref, got, got_coefs, row, y) * (1.0 / SCALE)
-        w_refs[row][y] = w
-        total = total + split_gram(v_refs[row][y], w)
+
+
+def share(folded, axis_odd):
+    lanes = folded.shape[1]
+    size = (lanes + 1) // 2
+    return jnp.where(axis_odd, folded[:, lanes - size :], folded[:, :size])
+
+
+def halves_kernel(cols_x, groups, *refs):
+    arrays, early_refs, (send_ref, keep_ref) = refs[:-3], refs[-3:-2], refs[-2:]
+    count = arrays[0].shape[1]
     squares = [
         ref[:, i * count : (i + 1) * count]
-        for ref in (early_ref, late_ref)
+        for ref in early_refs
         for i in range(ref.shape[1] // count)
     ]
-    packed = pack(squares + [fold(total)])
-    for peer in range(out_ref.shape[0]):
-        out_ref[peer] = packed
+    squares += grams_of(cols_x, groups, arrays)
+    folded = jnp.concatenate([fold_square(square) for square in squares], axis=1)
+    odd = lax.rem(lax.axis_index("wide"), 2) == 1
+    for ref, mine in ((send_ref, jnp.logical_not(odd)), (keep_ref, odd)):
+        half = share(folded, mine)
+        rest = jnp.zeros((half.shape[0], ref.shape[1] - half.shape[1]), jnp.float32)
+        ref[...] = jnp.concatenate([half, rest], axis=1)
 
 
 def solve_spd(matrix, target):
@@ -377,10 +388,27 @@
     v_refs, w_refs, refs = refs[: blocks * cols_x], refs[blocks * cols_x : 2 * blocks * cols_x], refs[2 * blocks * cols_x :]
     x_hbm, out_hbm, x_ref, out_ref, sem = refs
     cols_y = r_refs[0].shape[0]
-    joint = sums_ref[0]
-    for peer in range(1, sums_ref.shape[0]):
-        joint = joint + sums_ref[peer]
-    moments = unpack(joint, 2 * blocks)
+    count = r_refs[0].shape[1]
+    sums = []
+    for parity in range(2):
+        total = sums_ref[parity]
+        for peer in range(parity + 2, sums_ref.shape[0], 2):
+            total = total + sums_ref[peer]
+        middle = total.shape[1] // 2
+        sums.append(jnp.concatenate([total[:, :middle], total[:, middle:]], axis=0))
+    even, odd = sums
+    size, width = share_size(2 * blocks - 1, count), count + 1
+    early = (2 * blocks - 1) * width
+    moments = unfold_squares(
+        jnp.concatenate(
+            [
+                even[:, :size],
+                odd[:, 2 * size - early : size],
+                even[:, size : size + width] + odd[:, size : size + width],
+            ],
+            axis=1,
+        )
+    )
     matrix = jnp.concatenate(
         [
             jnp.concatenate([moments[1 + i + j] for j in range(blocks)], axis=1)
@@ -474,61 +502,69 @@
     later_ends, later_side = (cols_x * count, layers), (cols_y * count + 8, layers)
 
     if cols_x > 1:
-        shares = [(tuple(range(1, cols_x)), (2,)), ((0,), (3,))]
+        shares = [(tuple(range(1, cols_x)), (0, 1, 2)), ((0,), (0, 1, 3))]
     else:
-        shares = [((0,), (2, 3))]
-
-    def middle(last):
-        w, v, totals = [], [], []
+        shares = [((0,), (0, 1, 2, 3))]
+
+    def halo(slots):
+        return [*(got[i] for i in slots), *(got_coefs[i] for i in slots)]
+
+    for j in range(1, ITERS):
+        w, v = [], []
         for rows, slots in shares:
+            ahead = [] if v else grams
+            operands = [*vs[-1], coef, diag_term, *halo(slots), blocks, *ahead, *v]
             out = call(
-                functools.partial(middle_kernel, cols_x, rows, slots, last),
-                [state] * (len(rows) * (1 if last else 2)) + [(2 * count, 2 * count)] * last,
-                [VMEM] * (cols_x + 3 - last + 2 * len(slots)),
-                *vs[-1], coef, diag_term, *(got[i] for i in slots), *(got_coefs[i] for i in slots),
-                *([] if last else [blocks]),
+                functools.partial(row_kernel, cols_x, rows, slots, len(ahead)),
+                [state] * (2 * len(rows))
+                + ([later_ends] * 2 + [later_side] if rows[0] == 0 else []),
+                [VMEM] * len(operands),
+                *operands,
                 flops=apply_flops // len(shares),
             )
             w = out[: len(rows)] + w
-            if last:
-                totals += out[len(rows) :]
-            else:
-                v = out[len(rows) :] + v
-        return w + v, totals
-
-    for j in range(1, ITERS):
-        parts, _ = middle(False)
-        out = call(
-            functools.partial(end_kernel, cols_x),
-            [state] * (2 * cols_x) + [later_ends] * 2 + [later_side],
-            [VMEM] * (3 * cols_x + 6),
-            *vs[-1], coef, blocks, *got[:2], *got_coefs[:2], *parts,
-            flops=apply_flops // 4,
-            aliases={cols_x + 6 + i: i for i in range(2 * cols_x)},
-        )
-        w, v, edges = out[:cols_x], out[cols_x : 2 * cols_x], out[2 * cols_x :]
+            v = out[len(rows) : 2 * len(rows)] + v
+            edges = out[2 * len(rows) :]
         edges.insert(2, v[-1].reshape(flat))
         got = [exchange(slot, edge) for slot, edge in enumerate(edges)]
         vs.append(v)
         ws.append(w)
         arrays = vs[-2] + v + w + (rhs if j == 1 else [])
-        pairs = ([(0, 3)] if j == 1 else []) + [(0, 2), (1, 2)]
-        grams += call(
-            functools.partial(gram_kernel, cols_x, pairs),
-            [(count, len(pairs) * count)],
-            [VMEM] * len(arrays),
-            *arrays,
-            flops=len(pairs) * gram_flops,
+        groups = ([((0,), 3)] if j == 1 else []) + [((0, 1), 2)]
+        number_of = len(groups) + 1
+        if j < ITERS - 1:
+            grams += call(
+                functools.partial(gram_kernel, cols_x, groups),
+                [(count, number_of * count)],
+                [VMEM] * len(arrays),
+                *arrays,
+                flops=number_of * gram_flops,
+            )
+        else:
+            send, keep = call(
+                functools.partial(halves_kernel, cols_x, groups),
+                [(count // 2, 128)] * 2,
+                [VMEM] * (len(arrays) + 1),
+                *arrays, *grams,
+                flops=number_of * gram_flops,
+            )
+            grams = [keep, exchange(2, send)]
+    lanes = lanes_of(share_size(2 * ITERS - 1, count) + count + 1)
+    w, totals = [], []
+    for rows, slots in shares:
+        first = [] if rows[0] else [*grams, *totals]
+        operands = [*vs[-1], coef, diag_term, *halo(slots), *first]
+        out = call(
+            functools.partial(last_kernel, cols_x, rows, slots, len(first)),
+            [state] * len(rows)
+            + [(2 * count, 2 * count) if rows[0] else (devices, count // 4, 2 * lanes)],
+            [VMEM] * len(operands),
+            *operands,
+            flops=gram_flops // len(shares),
         )
-    parts, totals = middle(True)
-    *w, joint = call(
-        functools.partial(last_kernel, cols_x, len(totals)),
-        [state] * cols_x + [(devices, count // 2, 128)],
-        [VMEM] * (2 * cols_x + 7 + len(totals)),
-        *vs[-1], coef, *grams, *got[:2], *got_coefs[:2], *totals, *parts,
-        flops=gram_flops // 4,
-        aliases={cols_x + 7 + len(totals) + i: i for i in range(cols_x)},
-    )
+        w = out[:-1] + w
+        totals.append(out[-1])
+    joint = totals[-1]
     ws.append(w)
     joint = lax.all_to_all(joint, AXES, 0, 0)
     outs = call(

time: 39.9 us -> 39.4 us (0.987)
  blocking collectives: 13.8 us -> 11.6 us
  waiting for transfers between devices: 3.57 us -> 5.44 us
    all_to_all x1, blocking collectives: 13.8 us -> 11.6 us  [on_device(): joint = lax.all_to_all(joint, AXES, 0, 0)]
    ppermute x12 -> x13, waiting for transfers between devices: 3.57 us -> 5.44 us  [exchange(): return lax.ppermute(edge, AXES, pairing(sizes, slot // 2, slot % 2))]
    ppermute x12 -> x13, starting transfers between devices: 13.2 us -> 13 us  [exchange(): return lax.ppermute(edge, AXES, pairing(sizes, slot // 2, slot % 2))]
    pallas_call x13 -> x10, Pallas kernels: 8.39 us -> 8.35 us  [call(): pl.pallas_call(kernel, out_shape=shapes, in_specs=in_specs, out_specs=out...]
  transfers between devices with their start and end apart: 12 -> 13, of which waited for: 4 -> 3; matrix products, arithmetic and copies ran while one was open for 0% -> 0% of each run, Pallas kernels for 8% -> 6%
where the time goes in v9:
time: 39.4 us; the launch traced here: 39.2 us
  starting transfers between devices  13 us (33%)
  blocking collectives  11.6 us (29%)
  Pallas kernels  8.35 us (21%)
  waiting for transfers between devices  5.44 us (14%)
  between operations  0.74 us (2%)
    ppermute x13, starting transfers between devices, exchange(): return lax.ppermute(edge, AXES, pairing(sizes, slot // 2, slot % 2))  13 us
    all_to_all x1, blocking collectives, on_device(): joint = lax.all_to_all(joint, AXES, 0, 0)  11.6 us
    pallas_call x10, Pallas kernels, call(): pl.pallas_call(kernel, out_shape=shapes, in_specs=in_specs, out_specs=out...  8.35 us
    ppermute x13, waiting for transfers between devices, exchange(): return lax.ppermute(edge, AXES, pairing(sizes, slot // 2, slot % 2))  5.44 us
  transfers between devices with their start and end apart: 13, of which 3 were waited for; matrix products, arithmetic and copies ran while one was open for 0% of the time, Pallas kernels for 6%

profile of v9, /device:TPU:0, one launch (start us, length us, event | category | flops | bytes accessed | tf_op | source)
XLA Modules:
  0.0 39.2 jit_solution(12240236062126077042)
XLA Ops:
  0.6 1.7 %shard_map.77 = (f32[8,16,256]{2,1,0:T(8,128)S(1)}, f32[8,16,256]{2,1,0:T(8,128)S(1)}, f32[8,16,256]{2,1,0:T(8,128)S(1)}, f32[8,16,256]{2,1,0:T(8,128)S(1)}, f32...) custom-call(s32[16]{0:T(128)} %wells_hbm.1, ...), custom_call_target="tpu_custom_call" | custom-call | flops 33554432 | bytes 4354176 | tf_op jit(solution)/shard_map/pallas_call | solution.py:26
  2.4 3.1 %collective-permute-start.2 = (f32[144,256]{1,0:T(8,128)S(1)}, f32[144,256]{1,0:T(8,128)S(1)}, u32[]{:S(2)}, u32[]{:S(2)}) collective-permute-start(f32[144,256]{1,0:T(8,128)S(1)} %get-tuple-element.39), channel_id=1, source_target_pairs={{0,8},{1,2},{2,1},{3,4},{4,3},{5,6},{6,5},{7,15},{8,0},{9,10},{10,... | collective-permute-start | bytes 442376 | tf_op jit(solution)/shard_map/ppermute | solution.py:461
  5.5 0.0 collective-permute-start.3
  5.5 1.6 %collective-permute-start = (f32[34,256]{1,0:T(8,128)S(1)}, f32[34,256]{1,0:T(8,128)S(1)}, u32[]{:S(2)}, u32[]{:S(2)}) collective-permute-start(f32[34,256]{1,0:T(8,128)S(1)} %get-tuple-element.37), channel_id=1, source_target_pairs={{0,8},{1,9},{2,10},{3,11},{4,12},{5,13},{6,14},{7,15},{8,0},{9,1},... | collective-permute-start | bytes 104456 | tf_op jit(solution)/shard_map/ppermute | solution.py:461
  7.1 2.4 %collective-permute-done.refs_4_.refs_7_ = f32[34,256]{1,0:T(8,128)S(1)} collective-permute-done((f32[34,256]{1,0:T(8,128)S(1)}, f32[34,256]{1,0:T(8,128)S(1)}, u32[]{:S(2)}, u32[]{:S(2)}) %collective-permute-start) | collective-permute-done | bytes 34848 | tf_op jit(solution)/shard_map/ppermute | solution.py:461
  9.5 0.3 shard_map.78
  9.9 0.3 shard_map.79
  10.2 2.8 %collective-permute-start.6 = (f32[136,256]{1,0:T(8,128)S(1)}, f32[136,256]{1,0:T(8,128)S(1)}, u32[]{:S(2)}, u32[]{:S(2)}) collective-permute-start(f32[136,256]{1,0:T(8,128)S(1)} %get-tuple-element.46), channel_id=1, source_target_pairs={{0,8},{1,2},{2,1},{3,4},{4,3},{5,6},{6,5},{7,15},{8,0},{9,10},{10,... | collective-permute-start | bytes 417800 | tf_op jit(solution)/shard_map/ppermute | solution.py:461
  13.0 1.6 %collective-permute-start.4 = (f32[32,256]{1,0:T(8,128)S(1)}, f32[32,256]{1,0:T(8,128)S(1)}, u32[]{:S(2)}, u32[]{:S(2)}) collective-permute-start(f32[32,256]{1,0:T(8,128)S(1)} %get-tuple-element.44), channel_id=1, source_target_pairs={{0,8},{1,9},{2,10},{3,11},{4,12},{5,13},{6,14},{7,15},{8,0},{9,1},... | collective-permute-start | bytes 98312 | tf_op jit(solution)/shard_map/ppermute | solution.py:461
  14.6 0.7 %shard_map.80.refs_11_.refs_6_ = f32[16,48]{1,0:T(8,128)S(1)} custom-call(f32[8,16,256]{2,1,0:T(8,128)S(1)} %get-tuple-element.33.refs_0_.refs_2_, f32[8,16,256]{2,1,0:T(8,128)S(1)} %get-tuple-element.34.refs_1_.refs_3_, f32[8,16,256]{2,1,0:T(8,128)S(1)} %get-tuple-element.43.refs_2_.refs_0_.refs_4_, ...), custom_call_target="tpu_custom_call" | custom-call | flops 25165824 | bytes 1051648 | tf_op jit(solution)/shard_map/pallas_call | solution.py:26
  15.2 1.7 %collective-permute-done.4.refs_4_ = f32[32,256]{1,0:T(8,128)S(1)} collective-permute-done((f32[32,256]{1,0:T(8,128)S(1)}, f32[32,256]{1,0:T(8,128)S(1)}, u32[]{:S(2)}, u32[]{:S(2)}) %collective-permute-start.4) | collective-permute-done | bytes 32800 | tf_op jit(solution)/shard_map/ppermute | solution.py:461
  16.9 0.3 shard_map.81
  17.2 0.3 shard_map.82
  17.6 2.1 %collective-permute-start.10 = (f32[136,256]{1,0:T(8,128)S(1)}, f32[136,256]{1,0:T(8,128)S(1)}, u32[]{:S(2)}, u32[]{:S(2)}) collective-permute-start(f32[136,256]{1,0:T(8,128)S(1)} %get-tuple-element.55), channel_id=1, source_target_pairs={{0,8},{1,2},{2,1},{3,4},{4,3},{5,6},{6,5},{7,15},{8,0},{9,10},{10,... | collective-permute-start | bytes 417800 | tf_op jit(solution)/shard_map/ppermute | solution.py:461
  19.7 1.4 %collective-permute-start.8 = (f32[32,256]{1,0:T(8,128)S(1)}, f32[32,256]{1,0:T(8,128)S(1)}, u32[]{:S(2)}, u32[]{:S(2)}) collective-permute-start(f32[32,256]{1,0:T(8,128)S(1)} %get-tuple-element.53), channel_id=1, source_target_pairs={{0,8},{1,9},{2,10},{3,11},{4,12},{5,13},{6,14},{7,15},{8,0},{9,1},... | collective-permute-start | bytes 98312 | tf_op jit(solution)/shard_map/ppermute | solution.py:461
  21.0 0.7 %shard_map.83 = (f32[8,128]{1,0:T(8,128)S(1)}, f32[8,128]{1,0:T(8,128)S(1)}) custom-call(f32[8,16,256]{2,1,0:T(8,128)S(1)} %get-tuple-element.43.refs_2_.refs_0_.refs_4_, f32[8,16,256]{2,1,0:T(8,128)S(1)} %get-tuple-element.42.refs_11_.refs_3_.refs_1_.refs_5_, f32[8,16,256]{2,1,0:T(8,128)S(1)} %get-tuple-element.52.refs_2_.refs_0_.refs_6_, ...), custom_call_target="tpu_custom_call" | custom-call | flops 16777216 | bytes 797696 | tf_op jit(solution)/shard_map/pallas_call | solution.py:26
  21.7 0.5 %collective-permute-start.11 = (f32[8,128]{1,0:T(8,128)S(1)}, f32[8,128]{1,0:T(8,128)S(1)}, u32[]{:S(2)}, u32[]{:S(2)}) collective-permute-start(f32[8,128]{1,0:T(8,128)S(1)} %get-tuple-element.59), channel_id=1, source_target_pairs={{0,1},{1,0},{2,3},{3,2},{4,5},{5,4},{6,7},{7,6},{8,9},{9,8},{10,11... | collective-permute-start | bytes 12296 | tf_op jit(solution)/shard_map/ppermute | solution.py:461
  22.2 1.3 %collective-permute-done.8.refs_4_ = f32[32,256]{1,0:T(8,128)S(1)} collective-permute-done((f32[32,256]{1,0:T(8,128)S(1)}, f32[32,256]{1,0:T(8,128)S(1)}, u32[]{:S(2)}, u32[]{:S(2)}) %collective-permute-start.8) | collective-permute-done | bytes 32800 | tf_op jit(solution)/shard_map/ppermute | solution.py:461
  23.6 0.3 shard_map.84
  23.9 0.0 collective-permute-done.11.refs_11_
  23.9 0.0 collective-permute-done.10.refs_6_
  23.9 0.7 %shard_map.85 = (f32[8,16,256]{2,1,0:T(8,128)S(1)}, f32[32,4,128]{2,1,0:T(4,128)S(1)}) custom-call(f32[8,16,256]{2,1,0:T(8,128)S(1)} %get-tuple-element.52.refs_2_.refs_0_.refs_6_, f32[8,16,256]{2,1,0:T(8,128)S(1)} %get-tuple-element.51.refs_11_.refs_3_.refs_1_.refs_7_, f32[16,256]{1,0:T(8,128)S(1)} %get-tuple-element.35.refs_2_, ...), custom_call_target="tpu_custom_call" | custom-call | flops 4194304 | bytes 925696 | tf_op jit(solution)/shard_map/pallas_call | solution.py:26
  24.6 11.6 %all_to_all.5.sums_ref = f32[32,4,128]{2,1,0:T(4,128)S(1)} all-to-all(f32[32,4,128]{2,1,0:T(4,128)S(1)} %get-tuple-element.61), channel_id=1, replica_groups=mesh['narrow'=4,'wide'=8] {'narrow','wide'}, dimensions={0} | all-to-all | bytes 131072 | tf_op jit(solution)/shard_map/all_to_all | solution.py:569
  36.2 3.0 %shard_map.86 = (f32[16,2,8,256]{3,2,1,0:T(8,128)}, f32[16,2,8,256]{3,2,1,0:T(8,128)}) custom-call(f32[32,4,128]{2,1,0:T(4,128)S(1)} %all_to_all.5.sums_ref, f32[8,16,256]{2,1,0:T(8,128)S(1)} %get-tuple-element.49.refs_6_.refs_0_, f32[8,16,256]{2,1,0:T(8,128)S(1)} %get-tuple-element.50.refs_7_.refs_1_, f32[8,16,256]{2,1,0:T(8,128)S(1)} %get-tuple-element.33.refs_0_.refs_2_, ...), custom_call_target="tpu_custom_call" | custom-call | flops 75497472 | bytes 2424832 | tf_op jit(solution)/shard_map/pallas_call | solution.py:26
  (13 shorter events, 0.0 us)
Async XLA Ops:
  2.4 7.5 %collective-permute-start.2 = (f32[144,256]{1,0:T(8,128)S(1)}, f32[144,256]{1,0:T(8,128)S(1)}, u32[]{:S(2)}, u32[]{:S(2)}) collective-permute-start(f32[144,256]{1,0:T(8,128)S(1)} %get-tuple-element.39), channel_id=1, source_target_pairs={{0,8},{1,2},{2,1},{3,4},{4,3},{5,6},{6,5},{7,15},{8,0},{9,10},{10,... | collective-permute-start | bytes 442376 | tf_op jit(solution)/shard_map/ppermute | solution.py:461
  5.5 4.0 %collective-permute-start.3 = (f32[136,256]{1,0:T(8,128)S(1)}, f32[136,256]{1,0:T(8,128)S(1)}, u32[]{:S(2)}, u32[]{:S(2)}) collective-permute-start(f32[136,256]{1,0:T(8,128)S(1)} %get-tuple-element.41), channel_id=1, source_target_pairs={{0,1},{1,0},{2,3},{3,2},{4,5},{5,4},{6,7},{7,6},{8,9},{9,8},{10,11... | collective-permute-start | bytes 417800 | tf_op jit(solution)/shard_map/ppermute | solution.py:461
  5.5 4.0 %collective-permute-start = (f32[34,256]{1,0:T(8,128)S(1)}, f32[34,256]{1,0:T(8,128)S(1)}, u32[]{:S(2)}, u32[]{:S(2)}) collective-permute-start(f32[34,256]{1,0:T(8,128)S(1)} %get-tuple-element.37), channel_id=1, source_target_pairs={{0,8},{1,9},{2,10},{3,11},{4,12},{5,13},{6,14},{7,15},{8,0},{9,1},... | collective-permute-start | bytes 104456 | tf_op jit(solution)/shard_map/ppermute | solution.py:461
  7.1 2.4 %collective-permute-start.1 = (f32[34,256]{1,0:T(8,128)S(1)}, f32[34,256]{1,0:T(8,128)S(1)}, u32[]{:S(2)}, u32[]{:S(2)}) collective-permute-start(f32[34,256]{1,0:T(8,128)S(1)} %get-tuple-element.38), channel_id=1, source_target_pairs={{0,1},{1,0},{2,3},{3,2},{4,5},{5,4},{6,7},{7,6},{8,16},{9,17},{10,... | collective-permute-start | bytes 104456 | tf_op jit(solution)/shard_map/ppermute | solution.py:461
  10.2 7.0 %collective-permute-start.6 = (f32[136,256]{1,0:T(8,128)S(1)}, f32[136,256]{1,0:T(8,128)S(1)}, u32[]{:S(2)}, u32[]{:S(2)}) collective-permute-start(f32[136,256]{1,0:T(8,128)S(1)} %get-tuple-element.46), channel_id=1, source_target_pairs={{0,8},{1,2},{2,1},{3,4},{4,3},{5,6},{6,5},{7,15},{8,0},{9,10},{10,... | collective-permute-start | bytes 417800 | tf_op jit(solution)/shard_map/ppermute | solution.py:461
  13.0 3.9 %collective-permute-start.7 = (f32[128,256]{1,0:T(8,128)S(1)}, f32[128,256]{1,0:T(8,128)S(1)}, u32[]{:S(2)}, u32[]{:S(2)}) collective-permute-start(f32[128,256]{1,0:T(8,128)S(1)} %bitcast.3), channel_id=1, source_target_pairs={{0,1},{1,0},{2,3},{3,2},{4,5},{5,4},{6,7},{7,6},{8,9},{9,8},{10,11... | collective-permute-start | bytes 393224 | tf_op jit(solution)/shard_map/ppermute | solution.py:461
  13.0 3.9 %collective-permute-start.4 = (f32[32,256]{1,0:T(8,128)S(1)}, f32[32,256]{1,0:T(8,128)S(1)}, u32[]{:S(2)}, u32[]{:S(2)}) collective-permute-start(f32[32,256]{1,0:T(8,128)S(1)} %get-tuple-element.44), channel_id=1, source_target_pairs={{0,8},{1,9},{2,10},{3,11},{4,12},{5,13},{6,14},{7,15},{8,0},{9,1},... | collective-permute-start | bytes 98312 | tf_op jit(solution)/shard_map/ppermute | solution.py:461
  14.6 2.3 %collective-permute-start.5 = (f32[32,256]{1,0:T(8,128)S(1)}, f32[32,256]{1,0:T(8,128)S(1)}, u32[]{:S(2)}, u32[]{:S(2)}) collective-permute-start(f32[32,256]{1,0:T(8,128)S(1)} %get-tuple-element.45), channel_id=1, source_target_pairs={{0,1},{1,0},{2,3},{3,2},{4,5},{5,4},{6,7},{7,6},{8,16},{9,17},{10,... | collective-permute-start | bytes 98312 | tf_op jit(solution)/shard_map/ppermute | solution.py:461
  17.6 6.3 %collective-permute-start.10 = (f32[136,256]{1,0:T(8,128)S(1)}, f32[136,256]{1,0:T(8,128)S(1)}, u32[]{:S(2)}, u32[]{:S(2)}) collective-permute-start(f32[136,256]{1,0:T(8,128)S(1)} %get-tuple-element.55), channel_id=1, source_target_pairs={{0,8},{1,2},{2,1},{3,4},{4,3},{5,6},{6,5},{7,15},{8,0},{9,10},{10,... | collective-permute-start | bytes 417800 | tf_op jit(solution)/shard_map/ppermute | solution.py:461
  19.6 3.9 %collective-permute-start.12 = (f32[128,256]{1,0:T(8,128)S(1)}, f32[128,256]{1,0:T(8,128)S(1)}, u32[]{:S(2)}, u32[]{:S(2)}) collective-permute-start(f32[128,256]{1,0:T(8,128)S(1)} %bitcast.4), channel_id=1, source_target_pairs={{0,1},{1,0},{2,3},{3,2},{4,5},{5,4},{6,7},{7,6},{8,9},{9,8},{10,11... | collective-permute-start | bytes 393224 | tf_op jit(solution)/shard_map/ppermute | solution.py:461
  19.7 3.9 %collective-permute-start.8 = (f32[32,256]{1,0:T(8,128)S(1)}, f32[32,256]{1,0:T(8,128)S(1)}, u32[]{:S(2)}, u32[]{:S(2)}) collective-permute-start(f32[32,256]{1,0:T(8,128)S(1)} %get-tuple-element.53), channel_id=1, source_target_pairs={{0,8},{1,9},{2,10},{3,11},{4,12},{5,13},{6,14},{7,15},{8,0},{9,1},... | collective-permute-start | bytes 98312 | tf_op jit(solution)/shard_map/ppermute | solution.py:461
  21.0 2.6 %collective-permute-start.9 = (f32[32,256]{1,0:T(8,128)S(1)}, f32[32,256]{1,0:T(8,128)S(1)}, u32[]{:S(2)}, u32[]{:S(2)}) collective-permute-start(f32[32,256]{1,0:T(8,128)S(1)} %get-tuple-element.54), channel_id=1, source_target_pairs={{0,1},{1,0},{2,3},{3,2},{4,5},{5,4},{6,7},{7,6},{8,16},{9,17},{10,... | collective-permute-start | bytes 98312 | tf_op jit(solution)/shard_map/ppermute | solution.py:461
  21.7 2.2 %collective-permute-start.11 = (f32[8,128]{1,0:T(8,128)S(1)}, f32[8,128]{1,0:T(8,128)S(1)}, u32[]{:S(2)}, u32[]{:S(2)}) collective-permute-start(f32[8,128]{1,0:T(8,128)S(1)} %get-tuple-element.59), channel_id=1, source_target_pairs={{0,1},{1,0},{2,3},{3,2},{4,5},{5,4},{6,7},{7,6},{8,9},{9,8},{10,11... | collective-permute-start | bytes 12296 | tf_op jit(solution)/shard_map/ppermute | solution.py:461

commit v10 on v9

--- a/solution.py
+++ b/solution.py
@@ -91,10 +91,7 @@
     cols_y, count, _ = v_ref.shape
     for y in range(cols_y):
         edge[y * count : (y + 1) * count, :] = v_ref[y]
-    if coef_ref is not None:
-        edge[cols_y * count : cols_y * (count + 1), :] = coef_ref[
-            row * cols_y : (row + 1) * cols_y, :
-        ]
+    edge[cols_y * count :, :] = coef_ref[row * cols_y : (row + 1) * cols_y, :]
 
 
 def start_kernel(
@@ -215,8 +212,7 @@
             w_ref[y] = w
             next_ref[y] = apply_blocks(w, blocks_ref, row * cols_y + y)
     if edges:
-        write_edges((*next_refs, *done), None, edges[:2])
-        write_side(0, next_refs[0], None, edges[2])
+        write_edges((*next_refs, *done), None, edges)
 
 
 def share_size(matrices, count):
@@ -477,7 +473,7 @@
     out = call(
         start_kernel,
         [state] * (2 * cols_x)
-        + [rows, rows, jax.ShapeDtypeStruct(blocks.shape, blocks.dtype), ends, ends, side, (side[0] + 8, layers)],
+        + [rows, rows, jax.ShapeDtypeStruct(blocks.shape, blocks.dtype), ends, ends, side, side],
         [HBM] * 6,
         *(
             pltpu.with_memory_space_constraint(a, pltpu.HBM)
@@ -499,7 +495,7 @@
     coef, diag_term, blocks, *edges = out[2 * cols_x :]
     got_coefs = got = [exchange(slot, edge) for slot, edge in enumerate(edges)]
     vs, ws, grams = [v], [], []
-    later_ends, later_side = (cols_x * count, layers), (cols_y * count + 8, layers)
+    later_ends = (cols_x * count, layers)
 
     if cols_x > 1:
         shares = [(tuple(range(1, cols_x)), (0, 1, 2)), ((0,), (0, 1, 3))]
@@ -517,7 +513,7 @@
             out = call(
                 functools.partial(row_kernel, cols_x, rows, slots, len(ahead)),
                 [state] * (2 * len(rows))
-                + ([later_ends] * 2 + [later_side] if rows[0] == 0 else []),
+                + ([later_ends] * 2 if rows[0] == 0 else []),
                 [VMEM] * len(operands),
                 *operands,
                 flops=apply_flops // len(shares),
@@ -525,7 +521,7 @@
             w = out[: len(rows)] + w
             v = out[len(rows) : 2 * len(rows)] + v
             edges = out[2 * len(rows) :]
-        edges.insert(2, v[-1].reshape(flat))
+        edges += [v[-1].reshape(flat), v[0].reshape(flat)]
         got = [exchange(slot, edge) for slot, edge in enumerate(edges)]
         vs.append(v)
         ws.append(w)

time: 39.4 us -> 39.4 us (level)
  starting transfers between devices: 13 us -> 11.3 us
  waiting for transfers between devices: 5.44 us -> 6.82 us
  blocking collectives: 11.6 us -> 12 us
    ppermute x13, starting transfers between devices: 13 us -> 11.3 us  [exchange(): return lax.ppermute(edge, AXES, pairing(sizes, slot // 2, slot % 2))]
    ppermute x13, waiting for transfers between devices: 5.44 us -> 6.82 us  [exchange(): return lax.ppermute(edge, AXES, pairing(sizes, slot // 2, slot % 2))]
  transfers between devices with their start and end apart: 13 -> 13, of which waited for: 3 -> 3; matrix products, arithmetic and copies ran while one was open for 0% -> 0% of each run, Pallas kernels for 6% -> 8%
where the time goes in v10:
time: 39.4 us; the launch traced here: 39.2 us
  blocking collectives  12 us (30%)
  starting transfers between devices  11.3 us (29%)
  Pallas kernels  8.38 us (21%)
  waiting for transfers between devices  6.82 us (17%)
  between operations  0.76 us (2%)
    all_to_all x1, blocking collectives, on_device(): joint = lax.all_to_all(joint, AXES, 0, 0)  12 us
    ppermute x13, starting transfers between devices, exchange(): return lax.ppermute(edge, AXES, pairing(sizes, slot // 2, slot % 2))  11.3 us
    pallas_call x10, Pallas kernels, call(): pl.pallas_call(kernel, out_shape=shapes, in_specs=in_specs, out_specs=out...  8.38 us
    ppermute x13, waiting for transfers between devices, exchange(): return lax.ppermute(edge, AXES, pairing(sizes, slot // 2, slot % 2))  6.82 us
  transfers between devices with their start and end apart: 13, of which 3 were waited for; matrix products, arithmetic and copies ran while one was open for 0% of the time, Pallas kernels for 8%

profile of v10, /device:TPU:0, one launch (start us, length us, event | category | flops | bytes accessed | tf_op | source)
XLA Modules:
  0.0 39.2 jit_solution(4741258900243222016)
XLA Ops:
  0.6 1.7 %shard_map.77 = (f32[8,16,256]{2,1,0:T(8,128)S(1)}, f32[8,16,256]{2,1,0:T(8,128)S(1)}, f32[8,16,256]{2,1,0:T(8,128)S(1)}, f32[8,16,256]{2,1,0:T(8,128)S(1)}, f32...) custom-call(s32[16]{0:T(128)} %wells_hbm.1, ...), custom_call_target="tpu_custom_call" | custom-call | flops 33554432 | bytes 4345984 | tf_op jit(solution)/shard_map/pallas_call | solution.py:26
  2.4 0.5 %collective-permute-start.3 = (f32[136,256]{1,0:T(8,128)S(1)}, f32[136,256]{1,0:T(8,128)S(1)}, u32[]{:S(2)}, u32[]{:S(2)}) collective-permute-start(f32[136,256]{1,0:T(8,128)S(1)} %get-tuple-element.39), channel_id=1, source_target_pairs={{0,1},{1,0},{2,3},{3,2},{4,5},{5,4},{6,7},{7,6},{8,9},{9,8},{10,11... | collective-permute-start | bytes 417800 | tf_op jit(solution)/shard_map/ppermute | solution.py:457
  2.9 2.6 %collective-permute-start.2 = (f32[136,256]{1,0:T(8,128)S(1)}, f32[136,256]{1,0:T(8,128)S(1)}, u32[]{:S(2)}, u32[]{:S(2)}) collective-permute-start(f32[136,256]{1,0:T(8,128)S(1)} %get-tuple-element.37), channel_id=1, source_target_pairs={{0,8},{1,2},{2,1},{3,4},{4,3},{5,6},{6,5},{7,15},{8,0},{9,10},{10,... | collective-permute-start | bytes 417800 | tf_op jit(solution)/shard_map/ppermute | solution.py:457
  5.5 0.1 collective-permute-start
  5.6 1.2 %collective-permute-start.1 = (f32[34,256]{1,0:T(8,128)S(1)}, f32[34,256]{1,0:T(8,128)S(1)}, u32[]{:S(2)}, u32[]{:S(2)}) collective-permute-start(f32[34,256]{1,0:T(8,128)S(1)} %get-tuple-element.36), channel_id=1, source_target_pairs={{0,1},{1,0},{2,3},{3,2},{4,5},{5,4},{6,7},{7,6},{8,16},{9,17},{10,... | collective-permute-start | bytes 104456 | tf_op jit(solution)/shard_map/ppermute | solution.py:457
  6.9 2.7 %collective-permute-done.refs_4_.refs_7_ = f32[34,256]{1,0:T(8,128)S(1)} collective-permute-done((f32[34,256]{1,0:T(8,128)S(1)}, f32[34,256]{1,0:T(8,128)S(1)}, u32[]{:S(2)}, u32[]{:S(2)}) %collective-permute-start) | collective-permute-done | bytes 34848 | tf_op jit(solution)/shard_map/ppermute | solution.py:457
  9.6 0.3 shard_map.78
  10.0 0.3 shard_map.79
  10.3 2.3 %collective-permute-start.6 = (f32[128,256]{1,0:T(8,128)S(1)}, f32[128,256]{1,0:T(8,128)S(1)}, u32[]{:S(2)}, u32[]{:S(2)}) collective-permute-start(f32[128,256]{1,0:T(8,128)S(1)} %bitcast.6), channel_id=1, source_target_pairs={{0,8},{1,2},{2,1},{3,4},{4,3},{5,6},{6,5},{7,15},{8,0},{9,10},{10,... | collective-permute-start | bytes 393224 | tf_op jit(solution)/shard_map/ppermute | solution.py:457
  12.6 0.1 collective-permute-start.4
  12.7 1.2 %collective-permute-start.5 = (f32[32,256]{1,0:T(8,128)S(1)}, f32[32,256]{1,0:T(8,128)S(1)}, u32[]{:S(2)}, u32[]{:S(2)}) collective-permute-start(f32[32,256]{1,0:T(8,128)S(1)} %get-tuple-element.43), channel_id=1, source_target_pairs={{0,1},{1,0},{2,3},{3,2},{4,5},{5,4},{6,7},{7,6},{8,16},{9,17},{10,... | collective-permute-start | bytes 98312 | tf_op jit(solution)/shard_map/ppermute | solution.py:457
  13.9 0.7 %shard_map.80.refs_11_.refs_6_ = f32[16,48]{1,0:T(8,128)S(1)} custom-call(f32[8,16,256]{2,1,0:T(8,128)S(1)} %get-tuple-element.31.refs_0_.refs_2_, f32[8,16,256]{2,1,0:T(8,128)S(1)} %get-tuple-element.32.refs_1_.refs_3_, f32[8,16,256]{2,1,0:T(8,128)S(1)} %get-tuple-element.41.refs_2_.refs_0_.refs_4_, ...), custom_call_target="tpu_custom_call" | custom-call | flops 25165824 | bytes 1051648 | tf_op jit(solution)/shard_map/pallas_call | solution.py:26
  14.5 2.0 %collective-permute-done.4.refs_4_ = f32[32,256]{1,0:T(8,128)S(1)} collective-permute-done((f32[32,256]{1,0:T(8,128)S(1)}, f32[32,256]{1,0:T(8,128)S(1)}, u32[]{:S(2)}, u32[]{:S(2)}) %collective-permute-start.4) | collective-permute-done | bytes 32800 | tf_op jit(solution)/shard_map/ppermute | solution.py:457
  16.5 0.3 shard_map.81
  16.9 0.3 shard_map.82
  17.3 2.1 %collective-permute-start.10 = (f32[128,256]{1,0:T(8,128)S(1)}, f32[128,256]{1,0:T(8,128)S(1)}, u32[]{:S(2)}, u32[]{:S(2)}) collective-permute-start(f32[128,256]{1,0:T(8,128)S(1)} %bitcast.8), channel_id=1, source_target_pairs={{0,8},{1,2},{2,1},{3,4},{4,3},{5,6},{6,5},{7,15},{8,0},{9,10},{10,... | collective-permute-start | bytes 393224 | tf_op jit(solution)/shard_map/ppermute | solution.py:457
  19.4 0.1 collective-permute-start.8
  19.4 1.0 %collective-permute-start.9 = (f32[32,256]{1,0:T(8,128)S(1)}, f32[32,256]{1,0:T(8,128)S(1)}, u32[]{:S(2)}, u32[]{:S(2)}) collective-permute-start(f32[32,256]{1,0:T(8,128)S(1)} %get-tuple-element.51), channel_id=1, source_target_pairs={{0,1},{1,0},{2,3},{3,2},{4,5},{5,4},{6,7},{7,6},{8,16},{9,17},{10,... | collective-permute-start | bytes 98312 | tf_op jit(solution)/shard_map/ppermute | solution.py:457
  20.4 0.7 %shard_map.83 = (f32[8,128]{1,0:T(8,128)S(1)}, f32[8,128]{1,0:T(8,128)S(1)}) custom-call(f32[8,16,256]{2,1,0:T(8,128)S(1)} %get-tuple-element.41.refs_2_.refs_0_.refs_4_, f32[8,16,256]{2,1,0:T(8,128)S(1)} %get-tuple-element.40.refs_11_.refs_3_.refs_1_.refs_5_, f32[8,16,256]{2,1,0:T(8,128)S(1)} %get-tuple-element.49.refs_2_.refs_0_.refs_6_, ...), custom_call_target="tpu_custom_call" | custom-call | flops 16777216 | bytes 797696 | tf_op jit(solution)/shard_map/pallas_call | solution.py:26
  21.1 2.1 %collective-permute-done.8.refs_4_ = f32[32,256]{1,0:T(8,128)S(1)} collective-permute-done((f32[32,256]{1,0:T(8,128)S(1)}, f32[32,256]{1,0:T(8,128)S(1)}, u32[]{:S(2)}, u32[]{:S(2)}) %collective-permute-start.8) | collective-permute-done | bytes 32800 | tf_op jit(solution)/shard_map/ppermute | solution.py:457
  23.3 0.3 shard_map.84
  23.6 0.7 %shard_map.85 = (f32[8,16,256]{2,1,0:T(8,128)S(1)}, f32[32,4,128]{2,1,0:T(4,128)S(1)}) custom-call(f32[8,16,256]{2,1,0:T(8,128)S(1)} %get-tuple-element.49.refs_2_.refs_0_.refs_6_, f32[8,16,256]{2,1,0:T(8,128)S(1)} %get-tuple-element.48.refs_11_.refs_3_.refs_1_.refs_7_, f32[16,256]{1,0:T(8,128)S(1)} %get-tuple-element.33.refs_2_, ...), custom_call_target="tpu_custom_call" | custom-call | flops 4194304 | bytes 909312 | tf_op jit(solution)/shard_map/pallas_call | solution.py:26
  24.3 12.0 %all_to_all.5.sums_ref = f32[32,4,128]{2,1,0:T(4,128)S(1)} all-to-all(f32[32,4,128]{2,1,0:T(4,128)S(1)} %get-tuple-element.57), channel_id=1, replica_groups=mesh['narrow'=4,'wide'=8] {'narrow','wide'}, dimensions={0} | all-to-all | bytes 131072 | tf_op jit(solution)/shard_map/all_to_all | solution.py:565
  36.2 3.0 %shard_map.86 = (f32[16,2,8,256]{3,2,1,0:T(8,128)}, f32[16,2,8,256]{3,2,1,0:T(8,128)}) custom-call(f32[32,4,128]{2,1,0:T(4,128)S(1)} %all_to_all.5.sums_ref, f32[8,16,256]{2,1,0:T(8,128)S(1)} %get-tuple-element.46.refs_6_.refs_0_, f32[8,16,256]{2,1,0:T(8,128)S(1)} %get-tuple-element.47.refs_7_.refs_1_, f32[8,16,256]{2,1,0:T(8,128)S(1)} %get-tuple-element.31.refs_0_.refs_2_, ...), custom_call_target="tpu_custom_call" | custom-call | flops 75497472 | bytes 2424832 | tf_op jit(solution)/shard_map/pallas_call | solution.py:26
  (13 shorter events, 0.2 us)
Async XLA Ops:
  2.4 7.2 %collective-permute-start.3 = (f32[136,256]{1,0:T(8,128)S(1)}, f32[136,256]{1,0:T(8,128)S(1)}, u32[]{:S(2)}, u32[]{:S(2)}) collective-permute-start(f32[136,256]{1,0:T(8,128)S(1)} %get-tuple-element.39), channel_id=1, source_target_pairs={{0,1},{1,0},{2,3},{3,2},{4,5},{5,4},{6,7},{7,6},{8,9},{9,8},{10,11... | collective-permute-start | bytes 417800 | tf_op jit(solution)/shard_map/ppermute | solution.py:457
  2.9 7.1 %collective-permute-start.2 = (f32[136,256]{1,0:T(8,128)S(1)}, f32[136,256]{1,0:T(8,128)S(1)}, u32[]{:S(2)}, u32[]{:S(2)}) collective-permute-start(f32[136,256]{1,0:T(8,128)S(1)} %get-tuple-element.37), channel_id=1, source_target_pairs={{0,8},{1,2},{2,1},{3,4},{4,3},{5,6},{6,5},{7,15},{8,0},{9,10},{10,... | collective-permute-start | bytes 417800 | tf_op jit(solution)/shard_map/ppermute | solution.py:457
  5.5 4.0 %collective-permute-start = (f32[34,256]{1,0:T(8,128)S(1)}, f32[34,256]{1,0:T(8,128)S(1)}, u32[]{:S(2)}, u32[]{:S(2)}) collective-permute-start(f32[34,256]{1,0:T(8,128)S(1)} %get-tuple-element.35), channel_id=1, source_target_pairs={{0,8},{1,9},{2,10},{3,11},{4,12},{5,13},{6,14},{7,15},{8,0},{9,1},... | collective-permute-start | bytes 104456 | tf_op jit(solution)/shard_map/ppermute | solution.py:457
  5.6 3.9 %collective-permute-start.1 = (f32[34,256]{1,0:T(8,128)S(1)}, f32[34,256]{1,0:T(8,128)S(1)}, u32[]{:S(2)}, u32[]{:S(2)}) collective-permute-start(f32[34,256]{1,0:T(8,128)S(1)} %get-tuple-element.36), channel_id=1, source_target_pairs={{0,1},{1,0},{2,3},{3,2},{4,5},{5,4},{6,7},{7,6},{8,16},{9,17},{10,... | collective-permute-start | bytes 104456 | tf_op jit(solution)/shard_map/ppermute | solution.py:457
  9.9 6.6 %collective-permute-start.7 = (f32[128,256]{1,0:T(8,128)S(1)}, f32[128,256]{1,0:T(8,128)S(1)}, u32[]{:S(2)}, u32[]{:S(2)}) collective-permute-start(f32[128,256]{1,0:T(8,128)S(1)} %bitcast.5), channel_id=1, source_target_pairs={{0,1},{1,0},{2,3},{3,2},{4,5},{5,4},{6,7},{7,6},{8,9},{9,8},{10,11... | collective-permute-start | bytes 393224 | tf_op jit(solution)/shard_map/ppermute | solution.py:457
  10.3 6.6 %collective-permute-start.6 = (f32[128,256]{1,0:T(8,128)S(1)}, f32[128,256]{1,0:T(8,128)S(1)}, u32[]{:S(2)}, u32[]{:S(2)}) collective-permute-start(f32[128,256]{1,0:T(8,128)S(1)} %bitcast.6), channel_id=1, source_target_pairs={{0,8},{1,2},{2,1},{3,4},{4,3},{5,6},{6,5},{7,15},{8,0},{9,10},{10,... | collective-permute-start | bytes 393224 | tf_op jit(solution)/shard_map/ppermute | solution.py:457
  12.6 3.9 %collective-permute-start.4 = (f32[32,256]{1,0:T(8,128)S(1)}, f32[32,256]{1,0:T(8,128)S(1)}, u32[]{:S(2)}, u32[]{:S(2)}) collective-permute-start(f32[32,256]{1,0:T(8,128)S(1)} %get-tuple-element.42), channel_id=1, source_target_pairs={{0,8},{1,9},{2,10},{3,11},{4,12},{5,13},{6,14},{7,15},{8,0},{9,1},... | collective-permute-start | bytes 98312 | tf_op jit(solution)/shard_map/ppermute | solution.py:457
  12.7 3.8 %collective-permute-start.5 = (f32[32,256]{1,0:T(8,128)S(1)}, f32[32,256]{1,0:T(8,128)S(1)}, u32[]{:S(2)}, u32[]{:S(2)}) collective-permute-start(f32[32,256]{1,0:T(8,128)S(1)} %get-tuple-element.43), channel_id=1, source_target_pairs={{0,1},{1,0},{2,3},{3,2},{4,5},{5,4},{6,7},{7,6},{8,16},{9,17},{10,... | collective-permute-start | bytes 98312 | tf_op jit(solution)/shard_map/ppermute | solution.py:457
  16.8 6.4 %collective-permute-start.12 = (f32[128,256]{1,0:T(8,128)S(1)}, f32[128,256]{1,0:T(8,128)S(1)}, u32[]{:S(2)}, u32[]{:S(2)}) collective-permute-start(f32[128,256]{1,0:T(8,128)S(1)} %bitcast.7), channel_id=1, source_target_pairs={{0,1},{1,0},{2,3},{3,2},{4,5},{5,4},{6,7},{7,6},{8,9},{9,8},{10,11... | collective-permute-start | bytes 393224 | tf_op jit(solution)/shard_map/ppermute | solution.py:457
  17.3 6.3 %collective-permute-start.10 = (f32[128,256]{1,0:T(8,128)S(1)}, f32[128,256]{1,0:T(8,128)S(1)}, u32[]{:S(2)}, u32[]{:S(2)}) collective-permute-start(f32[128,256]{1,0:T(8,128)S(1)} %bitcast.8), channel_id=1, source_target_pairs={{0,8},{1,2},{2,1},{3,4},{4,3},{5,6},{6,5},{7,15},{8,0},{9,10},{10,... | collective-permute-start | bytes 393224 | tf_op jit(solution)/shard_map/ppermute | solution.py:457
  19.4 3.9 %collective-permute-start.8 = (f32[32,256]{1,0:T(8,128)S(1)}, f32[32,256]{1,0:T(8,128)S(1)}, u32[]{:S(2)}, u32[]{:S(2)}) collective-permute-start(f32[32,256]{1,0:T(8,128)S(1)} %get-tuple-element.50), channel_id=1, source_target_pairs={{0,8},{1,9},{2,10},{3,11},{4,12},{5,13},{6,14},{7,15},{8,0},{9,1},... | collective-permute-start | bytes 98312 | tf_op jit(solution)/shard_map/ppermute | solution.py:457
  19.4 3.8 %collective-permute-start.9 = (f32[32,256]{1,0:T(8,128)S(1)}, f32[32,256]{1,0:T(8,128)S(1)}, u32[]{:S(2)}, u32[]{:S(2)}) collective-permute-start(f32[32,256]{1,0:T(8,128)S(1)} %get-tuple-element.51), channel_id=1, source_target_pairs={{0,1},{1,0},{2,3},{3,2},{4,5},{5,4},{6,7},{7,6},{8,16},{9,17},{10,... | collective-permute-start | bytes 98312 | tf_op jit(solution)/shard_map/ppermute | solution.py:457
  21.1 2.5 %collective-permute-start.11 = (f32[8,128]{1,0:T(8,128)S(1)}, f32[8,128]{1,0:T(8,128)S(1)}, u32[]{:S(2)}, u32[]{:S(2)}) collective-permute-start(f32[8,128]{1,0:T(8,128)S(1)} %get-tuple-element.55), channel_id=1, source_target_pairs={{0,1},{1,0},{2,3},{3,2},{4,5},{5,4},{6,7},{7,6},{8,9},{9,8},{10,11... | collective-permute-start | bytes 12296 | tf_op jit(solution)/shard_map/ppermute | solution.py:457

commit v11 on v9

--- a/solution.py
+++ b/solution.py
@@ -129,11 +129,8 @@
                 block_sem.at[row],
             )
         )
-    for copy in small:
+    for copy in (sources[0], blocks[0], *small, *sources[1:], *blocks[1:]):
         copy.start()
-    for pair in zip(sources, blocks):
-        for copy in pair:
-            copy.start()
     for copy in small:
         copy.wait()
     place = lax.broadcasted_iota(jnp.int32, (count, layers), 0)
@@ -310,21 +307,17 @@
     row = lax.broadcasted_iota(jnp.int32, (half, half), 0)
     lane = lax.broadcasted_iota(jnp.int32, (half, half), 1)
     diagonal = jnp.where(row == lane, 0.5, 1.0)
+    across = lax.broadcasted_iota(jnp.int32, (half, 2 * half), 1)
+    end = half + lax.broadcasted_iota(jnp.int32, (half, 2 * half), 0)
+    below = jnp.where(across < end, 1.0, jnp.where(across == end, 0.5, 0.0))
     width = 2 * half + 1
     parts = []
     for i in range(folded.shape[1] // width):
         one = folded[:, i * width : (i + 1) * width]
         upper = jnp.where(row <= lane, one[:, half + 1 :] * diagonal, 0.0)
-        lower = jnp.where(row >= lane, one[:, half : 2 * half] * diagonal, 0.0)
-        parts.append(
-            jnp.concatenate(
-                [
-                    jnp.concatenate([upper, jnp.zeros_like(upper)], axis=1),
-                    jnp.concatenate([one[:, :half], lower], axis=1),
-                ],
-                axis=0,
-            )
-        )
+        lower = jnp.where(across <= end, one[:, : 2 * half] * below, 0.0)
+        upper = jnp.concatenate([upper, jnp.zeros_like(upper)], axis=1)
+        parts.append(jnp.concatenate([upper, lower], axis=0))
     turned = jnp.concatenate(parts, axis=1).T
     return [
         part + turned[2 * half * i : 2 * half * (i + 1)] for i, part in enumerate(parts)

time: 39.4 us -> 39.3 us (level)
  no operation moved by 1% of the time
where the time goes in v11:
time: 39.3 us; the launch traced here: 39.2 us
  starting transfers between devices  13 us (33%)
  blocking collectives  11.6 us (30%)
  Pallas kernels  8.31 us (21%)
  waiting for transfers between devices  5.44 us (14%)
  between operations  0.73 us (2%)
    ppermute x13, starting transfers between devices, exchange(): return lax.ppermute(edge, AXES, pairing(sizes, slot // 2, slot % 2))  13 us
    all_to_all x1, blocking collectives, on_device(): joint = lax.all_to_all(joint, AXES, 0, 0)  11.6 us
    pallas_call x10, Pallas kernels, call(): pl.pallas_call(kernel, out_shape=shapes, in_specs=in_specs, out_specs=out...  8.31 us
    ppermute x13, waiting for transfers between devices, exchange(): return lax.ppermute(edge, AXES, pairing(sizes, slot // 2, slot % 2))  5.44 us
  transfers between devices with their start and end apart: 13, of which 3 were waited for; matrix products, arithmetic and copies ran while one was open for 0% of the time, Pallas kernels for 6%

profile of v11, /device:TPU:0, one launch (start us, length us, event | category | flops | bytes accessed | tf_op | source)
XLA Modules:
  0.0 39.2 jit_solution(13643275397756691480)
XLA Ops:
  0.6 1.7 %shard_map.77 = (f32[8,16,256]{2,1,0:T(8,128)S(1)}, f32[8,16,256]{2,1,0:T(8,128)S(1)}, f32[8,16,256]{2,1,0:T(8,128)S(1)}, f32[8,16,256]{2,1,0:T(8,128)S(1)}, f32...) custom-call(s32[16]{0:T(128)} %wells_hbm.1, ...), custom_call_target="tpu_custom_call" | custom-call | flops 33554432 | bytes 4354176 | tf_op jit(solution)/shard_map/pallas_call | solution.py:26
  2.4 3.1 %collective-permute-start.2 = (f32[144,256]{1,0:T(8,128)S(1)}, f32[144,256]{1,0:T(8,128)S(1)}, u32[]{:S(2)}, u32[]{:S(2)}) collective-permute-start(f32[144,256]{1,0:T(8,128)S(1)} %get-tuple-element.39), channel_id=1, source_target_pairs={{0,8},{1,2},{2,1},{3,4},{4,3},{5,6},{6,5},{7,15},{8,0},{9,10},{10,... | collective-permute-start | bytes 442376 | tf_op jit(solution)/shard_map/ppermute | solution.py:454
  5.5 0.0 collective-permute-start.3
  5.5 1.6 %collective-permute-start = (f32[34,256]{1,0:T(8,128)S(1)}, f32[34,256]{1,0:T(8,128)S(1)}, u32[]{:S(2)}, u32[]{:S(2)}) collective-permute-start(f32[34,256]{1,0:T(8,128)S(1)} %get-tuple-element.37), channel_id=1, source_target_pairs={{0,8},{1,9},{2,10},{3,11},{4,12},{5,13},{6,14},{7,15},{8,0},{9,1},... | collective-permute-start | bytes 104456 | tf_op jit(solution)/shard_map/ppermute | solution.py:454
  7.1 2.4 %collective-permute-done.refs_4_.refs_7_ = f32[34,256]{1,0:T(8,128)S(1)} collective-permute-done((f32[34,256]{1,0:T(8,128)S(1)}, f32[34,256]{1,0:T(8,128)S(1)}, u32[]{:S(2)}, u32[]{:S(2)}) %collective-permute-start) | collective-permute-done | bytes 34848 | tf_op jit(solution)/shard_map/ppermute | solution.py:454
  9.5 0.3 shard_map.78
  9.8 0.0 collective-permute-done.2.refs_6_.refs_9_
  9.9 0.3 shard_map.79
  10.2 2.8 %collective-permute-start.6 = (f32[136,256]{1,0:T(8,128)S(1)}, f32[136,256]{1,0:T(8,128)S(1)}, u32[]{:S(2)}, u32[]{:S(2)}) collective-permute-start(f32[136,256]{1,0:T(8,128)S(1)} %get-tuple-element.46), channel_id=1, source_target_pairs={{0,8},{1,2},{2,1},{3,4},{4,3},{5,6},{6,5},{7,15},{8,0},{9,10},{10,... | collective-permute-start | bytes 417800 | tf_op jit(solution)/shard_map/ppermute | solution.py:454
  13.0 1.6 %collective-permute-start.4 = (f32[32,256]{1,0:T(8,128)S(1)}, f32[32,256]{1,0:T(8,128)S(1)}, u32[]{:S(2)}, u32[]{:S(2)}) collective-permute-start(f32[32,256]{1,0:T(8,128)S(1)} %get-tuple-element.44), channel_id=1, source_target_pairs={{0,8},{1,9},{2,10},{3,11},{4,12},{5,13},{6,14},{7,15},{8,0},{9,1},... | collective-permute-start | bytes 98312 | tf_op jit(solution)/shard_map/ppermute | solution.py:454
  14.6 0.7 %shard_map.80.refs_11_.refs_6_ = f32[16,48]{1,0:T(8,128)S(1)} custom-call(f32[8,16,256]{2,1,0:T(8,128)S(1)} %get-tuple-element.33.refs_0_.refs_2_, f32[8,16,256]{2,1,0:T(8,128)S(1)} %get-tuple-element.34.refs_1_.refs_3_, f32[8,16,256]{2,1,0:T(8,128)S(1)} %get-tuple-element.43.refs_2_.refs_0_.refs_4_, ...), custom_call_target="tpu_custom_call" | custom-call | flops 25165824 | bytes 1051648 | tf_op jit(solution)/shard_map/pallas_call | solution.py:26
  15.2 1.7 %collective-permute-done.4.refs_4_ = f32[32,256]{1,0:T(8,128)S(1)} collective-permute-done((f32[32,256]{1,0:T(8,128)S(1)}, f32[32,256]{1,0:T(8,128)S(1)}, u32[]{:S(2)}, u32[]{:S(2)}) %collective-permute-start.4) | collective-permute-done | bytes 32800 | tf_op jit(solution)/shard_map/ppermute | solution.py:454
  16.9 0.3 shard_map.81
  17.2 0.3 shard_map.82
  17.6 2.1 %collective-permute-start.10 = (f32[136,256]{1,0:T(8,128)S(1)}, f32[136,256]{1,0:T(8,128)S(1)}, u32[]{:S(2)}, u32[]{:S(2)}) collective-permute-start(f32[136,256]{1,0:T(8,128)S(1)} %get-tuple-element.55), channel_id=1, source_target_pairs={{0,8},{1,2},{2,1},{3,4},{4,3},{5,6},{6,5},{7,15},{8,0},{9,10},{10,... | collective-permute-start | bytes 417800 | tf_op jit(solution)/shard_map/ppermute | solution.py:454
  19.7 1.3 %collective-permute-start.8 = (f32[32,256]{1,0:T(8,128)S(1)}, f32[32,256]{1,0:T(8,128)S(1)}, u32[]{:S(2)}, u32[]{:S(2)}) collective-permute-start(f32[32,256]{1,0:T(8,128)S(1)} %get-tuple-element.53), channel_id=1, source_target_pairs={{0,8},{1,9},{2,10},{3,11},{4,12},{5,13},{6,14},{7,15},{8,0},{9,1},... | collective-permute-start | bytes 98312 | tf_op jit(solution)/shard_map/ppermute | solution.py:454
  21.0 0.7 %shard_map.83 = (f32[8,128]{1,0:T(8,128)S(1)}, f32[8,128]{1,0:T(8,128)S(1)}) custom-call(f32[8,16,256]{2,1,0:T(8,128)S(1)} %get-tuple-element.43.refs_2_.refs_0_.refs_4_, f32[8,16,256]{2,1,0:T(8,128)S(1)} %get-tuple-element.42.refs_11_.refs_3_.refs_1_.refs_5_, f32[8,16,256]{2,1,0:T(8,128)S(1)} %get-tuple-element.52.refs_2_.refs_0_.refs_6_, ...), custom_call_target="tpu_custom_call" | custom-call | flops 16777216 | bytes 797696 | tf_op jit(solution)/shard_map/pallas_call | solution.py:26
  21.7 0.5 %collective-permute-start.11 = (f32[8,128]{1,0:T(8,128)S(1)}, f32[8,128]{1,0:T(8,128)S(1)}, u32[]{:S(2)}, u32[]{:S(2)}) collective-permute-start(f32[8,128]{1,0:T(8,128)S(1)} %get-tuple-element.59), channel_id=1, source_target_pairs={{0,1},{1,0},{2,3},{3,2},{4,5},{5,4},{6,7},{7,6},{8,9},{9,8},{10,11... | collective-permute-start | bytes 12296 | tf_op jit(solution)/shard_map/ppermute | solution.py:454
  22.2 1.3 %collective-permute-done.8.refs_4_ = f32[32,256]{1,0:T(8,128)S(1)} collective-permute-done((f32[32,256]{1,0:T(8,128)S(1)}, f32[32,256]{1,0:T(8,128)S(1)}, u32[]{:S(2)}, u32[]{:S(2)}) %collective-permute-start.8) | collective-permute-done | bytes 32800 | tf_op jit(solution)/shard_map/ppermute | solution.py:454
  23.6 0.3 shard_map.84
  23.9 0.0 collective-permute-done.11.refs_11_
  23.9 0.7 %shard_map.85 = (f32[8,16,256]{2,1,0:T(8,128)S(1)}, f32[32,4,128]{2,1,0:T(4,128)S(1)}) custom-call(f32[8,16,256]{2,1,0:T(8,128)S(1)} %get-tuple-element.52.refs_2_.refs_0_.refs_6_, f32[8,16,256]{2,1,0:T(8,128)S(1)} %get-tuple-element.51.refs_11_.refs_3_.refs_1_.refs_7_, f32[16,256]{1,0:T(8,128)S(1)} %get-tuple-element.35.refs_2_, ...), custom_call_target="tpu_custom_call" | custom-call | flops 4194304 | bytes 925696 | tf_op jit(solution)/shard_map/pallas_call | solution.py:26
  24.6 11.6 %all_to_all.5.sums_ref = f32[32,4,128]{2,1,0:T(4,128)S(1)} all-to-all(f32[32,4,128]{2,1,0:T(4,128)S(1)} %get-tuple-element.61), channel_id=1, replica_groups=mesh['narrow'=4,'wide'=8] {'narrow','wide'}, dimensions={0} | all-to-all | bytes 131072 | tf_op jit(solution)/shard_map/all_to_all | solution.py:562
  36.2 2.9 %shard_map.86 = (f32[16,2,8,256]{3,2,1,0:T(8,128)}, f32[16,2,8,256]{3,2,1,0:T(8,128)}) custom-call(f32[32,4,128]{2,1,0:T(4,128)S(1)} %all_to_all.5.sums_ref, f32[8,16,256]{2,1,0:T(8,128)S(1)} %get-tuple-element.49.refs_6_.refs_0_, f32[8,16,256]{2,1,0:T(8,128)S(1)} %get-tuple-element.50.refs_7_.refs_1_, f32[8,16,256]{2,1,0:T(8,128)S(1)} %get-tuple-element.33.refs_0_.refs_2_, ...), custom_call_target="tpu_custom_call" | custom-call | flops 75497472 | bytes 2424832 | tf_op jit(solution)/shard_map/pallas_call | solution.py:26
  (13 shorter events, 0.0 us)
Async XLA Ops:
  2.4 7.5 %collective-permute-start.2 = (f32[144,256]{1,0:T(8,128)S(1)}, f32[144,256]{1,0:T(8,128)S(1)}, u32[]{:S(2)}, u32[]{:S(2)}) collective-permute-start(f32[144,256]{1,0:T(8,128)S(1)} %get-tuple-element.39), channel_id=1, source_target_pairs={{0,8},{1,2},{2,1},{3,4},{4,3},{5,6},{6,5},{7,15},{8,0},{9,10},{10,... | collective-permute-start | bytes 442376 | tf_op jit(solution)/shard_map/ppermute | solution.py:454
  5.5 4.0 %collective-permute-start.3 = (f32[136,256]{1,0:T(8,128)S(1)}, f32[136,256]{1,0:T(8,128)S(1)}, u32[]{:S(2)}, u32[]{:S(2)}) collective-permute-start(f32[136,256]{1,0:T(8,128)S(1)} %get-tuple-element.41), channel_id=1, source_target_pairs={{0,1},{1,0},{2,3},{3,2},{4,5},{5,4},{6,7},{7,6},{8,9},{9,8},{10,11... | collective-permute-start | bytes 417800 | tf_op jit(solution)/shard_map/ppermute | solution.py:454
  5.5 4.0 %collective-permute-start = (f32[34,256]{1,0:T(8,128)S(1)}, f32[34,256]{1,0:T(8,128)S(1)}, u32[]{:S(2)}, u32[]{:S(2)}) collective-permute-start(f32[34,256]{1,0:T(8,128)S(1)} %get-tuple-element.37), channel_id=1, source_target_pairs={{0,8},{1,9},{2,10},{3,11},{4,12},{5,13},{6,14},{7,15},{8,0},{9,1},... | collective-permute-start | bytes 104456 | tf_op jit(solution)/shard_map/ppermute | solution.py:454
  7.1 2.4 %collective-permute-start.1 = (f32[34,256]{1,0:T(8,128)S(1)}, f32[34,256]{1,0:T(8,128)S(1)}, u32[]{:S(2)}, u32[]{:S(2)}) collective-permute-start(f32[34,256]{1,0:T(8,128)S(1)} %get-tuple-element.38), channel_id=1, source_target_pairs={{0,1},{1,0},{2,3},{3,2},{4,5},{5,4},{6,7},{7,6},{8,16},{9,17},{10,... | collective-permute-start | bytes 104456 | tf_op jit(solution)/shard_map/ppermute | solution.py:454
  10.2 7.0 %collective-permute-start.6 = (f32[136,256]{1,0:T(8,128)S(1)}, f32[136,256]{1,0:T(8,128)S(1)}, u32[]{:S(2)}, u32[]{:S(2)}) collective-permute-start(f32[136,256]{1,0:T(8,128)S(1)} %get-tuple-element.46), channel_id=1, source_target_pairs={{0,8},{1,2},{2,1},{3,4},{4,3},{5,6},{6,5},{7,15},{8,0},{9,10},{10,... | collective-permute-start | bytes 417800 | tf_op jit(solution)/shard_map/ppermute | solution.py:454
  13.0 3.9 %collective-permute-start.7 = (f32[128,256]{1,0:T(8,128)S(1)}, f32[128,256]{1,0:T(8,128)S(1)}, u32[]{:S(2)}, u32[]{:S(2)}) collective-permute-start(f32[128,256]{1,0:T(8,128)S(1)} %bitcast.3), channel_id=1, source_target_pairs={{0,1},{1,0},{2,3},{3,2},{4,5},{5,4},{6,7},{7,6},{8,9},{9,8},{10,11... | collective-permute-start | bytes 393224 | tf_op jit(solution)/shard_map/ppermute | solution.py:454
  13.0 3.9 %collective-permute-start.4 = (f32[32,256]{1,0:T(8,128)S(1)}, f32[32,256]{1,0:T(8,128)S(1)}, u32[]{:S(2)}, u32[]{:S(2)}) collective-permute-start(f32[32,256]{1,0:T(8,128)S(1)} %get-tuple-element.44), channel_id=1, source_target_pairs={{0,8},{1,9},{2,10},{3,11},{4,12},{5,13},{6,14},{7,15},{8,0},{9,1},... | collective-permute-start | bytes 98312 | tf_op jit(solution)/shard_map/ppermute | solution.py:454
  14.6 2.3 %collective-permute-start.5 = (f32[32,256]{1,0:T(8,128)S(1)}, f32[32,256]{1,0:T(8,128)S(1)}, u32[]{:S(2)}, u32[]{:S(2)}) collective-permute-start(f32[32,256]{1,0:T(8,128)S(1)} %get-tuple-element.45), channel_id=1, source_target_pairs={{0,1},{1,0},{2,3},{3,2},{4,5},{5,4},{6,7},{7,6},{8,16},{9,17},{10,... | collective-permute-start | bytes 98312 | tf_op jit(solution)/shard_map/ppermute | solution.py:454
  17.6 6.3 %collective-permute-start.10 = (f32[136,256]{1,0:T(8,128)S(1)}, f32[136,256]{1,0:T(8,128)S(1)}, u32[]{:S(2)}, u32[]{:S(2)}) collective-permute-start(f32[136,256]{1,0:T(8,128)S(1)} %get-tuple-element.55), channel_id=1, source_target_pairs={{0,8},{1,2},{2,1},{3,4},{4,3},{5,6},{6,5},{7,15},{8,0},{9,10},{10,... | collective-permute-start | bytes 417800 | tf_op jit(solution)/shard_map/ppermute | solution.py:454
  19.7 3.9 %collective-permute-start.12 = (f32[128,256]{1,0:T(8,128)S(1)}, f32[128,256]{1,0:T(8,128)S(1)}, u32[]{:S(2)}, u32[]{:S(2)}) collective-permute-start(f32[128,256]{1,0:T(8,128)S(1)} %bitcast.4), channel_id=1, source_target_pairs={{0,1},{1,0},{2,3},{3,2},{4,5},{5,4},{6,7},{7,6},{8,9},{9,8},{10,11... | collective-permute-start | bytes 393224 | tf_op jit(solution)/shard_map/ppermute | solution.py:454
  19.7 3.9 %collective-permute-start.8 = (f32[32,256]{1,0:T(8,128)S(1)}, f32[32,256]{1,0:T(8,128)S(1)}, u32[]{:S(2)}, u32[]{:S(2)}) collective-permute-start(f32[32,256]{1,0:T(8,128)S(1)} %get-tuple-element.53), channel_id=1, source_target_pairs={{0,8},{1,9},{2,10},{3,11},{4,12},{5,13},{6,14},{7,15},{8,0},{9,1},... | collective-permute-start | bytes 98312 | tf_op jit(solution)/shard_map/ppermute | solution.py:454
  21.0 2.6 %collective-permute-start.9 = (f32[32,256]{1,0:T(8,128)S(1)}, f32[32,256]{1,0:T(8,128)S(1)}, u32[]{:S(2)}, u32[]{:S(2)}) collective-permute-start(f32[32,256]{1,0:T(8,128)S(1)} %get-tuple-element.54), channel_id=1, source_target_pairs={{0,1},{1,0},{2,3},{3,2},{4,5},{5,4},{6,7},{7,6},{8,16},{9,17},{10,... | collective-permute-start | bytes 98312 | tf_op jit(solution)/shard_map/ppermute | solution.py:454
  21.7 2.2 %collective-permute-start.11 = (f32[8,128]{1,0:T(8,128)S(1)}, f32[8,128]{1,0:T(8,128)S(1)}, u32[]{:S(2)}, u32[]{:S(2)}) collective-permute-start(f32[8,128]{1,0:T(8,128)S(1)} %get-tuple-element.59), channel_id=1, source_target_pairs={{0,1},{1,0},{2,3},{3,2},{4,5},{5,4},{6,7},{7,6},{8,9},{9,8},{10,11... | collective-permute-start | bytes 12296 | tf_op jit(solution)/shard_map/ppermute | solution.py:454

commit v12 on v11

--- a/solution.py
+++ b/solution.py
@@ -413,11 +413,11 @@
     coefs = solve_spd(matrix, target).T
     high = coefs.astype(jnp.bfloat16)
     middle, low = split(coefs - high.astype(jnp.float32))
-    left = jnp.concatenate([high, high, middle, middle, low], axis=1)
+    left = jnp.concatenate([high, high, middle, low], axis=1)
 
     def combine(values, row, y):
         highs, lows = zip(*(split(values[j * cols_x + row][y]) for j in range(blocks)))
-        right = jnp.concatenate(highs + lows + highs + lows + highs, axis=0)
+        right = jnp.concatenate(highs + lows + highs + highs, axis=0)
         return jnp.dot(left, right, preferred_element_type=jnp.float32)
 
     copies = []

time: 39.3 us -> 39.2 us (level)
  no operation moved by 1% of the time
where the time goes in v12:
time: 39.2 us; the launch traced here: 39.1 us
  starting transfers between devices  13 us (33%)
  blocking collectives  11.6 us (30%)
  Pallas kernels  8.22 us (21%)
  waiting for transfers between devices  5.44 us (14%)
  between operations  0.73 us (2%)
    ppermute x13, starting transfers between devices, exchange(): return lax.ppermute(edge, AXES, pairing(sizes, slot // 2, slot % 2))  13 us
    all_to_all x1, blocking collectives, on_device(): joint = lax.all_to_all(joint, AXES, 0, 0)  11.6 us
    pallas_call x10, Pallas kernels, call(): pl.pallas_call(kernel, out_shape=shapes, in_specs=in_specs, out_specs=out...  8.22 us
    ppermute x13, waiting for transfers between devices, exchange(): return lax.ppermute(edge, AXES, pairing(sizes, slot // 2, slot % 2))  5.44 us
  transfers between devices with their start and end apart: 13, of which 3 were waited for; matrix products, arithmetic and copies ran while one was open for 0% of the time, Pallas kernels for 6%

profile of v12, /device:TPU:0, one launch (start us, length us, event | category | flops | bytes accessed | tf_op | source)
XLA Modules:
  0.0 39.1 jit_solution(5654336537798841834)
XLA Ops:
  0.6 1.7 %shard_map.77 = (f32[8,16,256]{2,1,0:T(8,128)S(1)}, f32[8,16,256]{2,1,0:T(8,128)S(1)}, f32[8,16,256]{2,1,0:T(8,128)S(1)}, f32[8,16,256]{2,1,0:T(8,128)S(1)}, f32...) custom-call(s32[16]{0:T(128)} %wells_hbm.1, ...), custom_call_target="tpu_custom_call" | custom-call | flops 33554432 | bytes 4354176 | tf_op jit(solution)/shard_map/pallas_call | solution.py:26
  2.4 3.1 %collective-permute-start.2 = (f32[144,256]{1,0:T(8,128)S(1)}, f32[144,256]{1,0:T(8,128)S(1)}, u32[]{:S(2)}, u32[]{:S(2)}) collective-permute-start(f32[144,256]{1,0:T(8,128)S(1)} %get-tuple-element.39), channel_id=1, source_target_pairs={{0,8},{1,2},{2,1},{3,4},{4,3},{5,6},{6,5},{7,15},{8,0},{9,10},{10,... | collective-permute-start | bytes 442376 | tf_op jit(solution)/shard_map/ppermute | solution.py:454
  5.5 0.0 collective-permute-start.3
  5.5 1.6 %collective-permute-start = (f32[34,256]{1,0:T(8,128)S(1)}, f32[34,256]{1,0:T(8,128)S(1)}, u32[]{:S(2)}, u32[]{:S(2)}) collective-permute-start(f32[34,256]{1,0:T(8,128)S(1)} %get-tuple-element.37), channel_id=1, source_target_pairs={{0,8},{1,9},{2,10},{3,11},{4,12},{5,13},{6,14},{7,15},{8,0},{9,1},... | collective-permute-start | bytes 104456 | tf_op jit(solution)/shard_map/ppermute | solution.py:454
  7.1 2.4 %collective-permute-done.refs_4_.refs_7_ = f32[34,256]{1,0:T(8,128)S(1)} collective-permute-done((f32[34,256]{1,0:T(8,128)S(1)}, f32[34,256]{1,0:T(8,128)S(1)}, u32[]{:S(2)}, u32[]{:S(2)}) %collective-permute-start) | collective-permute-done | bytes 34848 | tf_op jit(solution)/shard_map/ppermute | solution.py:454
  9.5 0.3 shard_map.78
  9.8 0.0 collective-permute-done.2.refs_6_.refs_9_
  9.9 0.3 shard_map.79
  10.2 2.8 %collective-permute-start.6 = (f32[136,256]{1,0:T(8,128)S(1)}, f32[136,256]{1,0:T(8,128)S(1)}, u32[]{:S(2)}, u32[]{:S(2)}) collective-permute-start(f32[136,256]{1,0:T(8,128)S(1)} %get-tuple-element.46), channel_id=1, source_target_pairs={{0,8},{1,2},{2,1},{3,4},{4,3},{5,6},{6,5},{7,15},{8,0},{9,10},{10,... | collective-permute-start | bytes 417800 | tf_op jit(solution)/shard_map/ppermute | solution.py:454
  13.0 1.6 %collective-permute-start.4 = (f32[32,256]{1,0:T(8,128)S(1)}, f32[32,256]{1,0:T(8,128)S(1)}, u32[]{:S(2)}, u32[]{:S(2)}) collective-permute-start(f32[32,256]{1,0:T(8,128)S(1)} %get-tuple-element.44), channel_id=1, source_target_pairs={{0,8},{1,9},{2,10},{3,11},{4,12},{5,13},{6,14},{7,15},{8,0},{9,1},... | collective-permute-start | bytes 98312 | tf_op jit(solution)/shard_map/ppermute | solution.py:454
  14.6 0.7 %shard_map.80.refs_11_.refs_6_ = f32[16,48]{1,0:T(8,128)S(1)} custom-call(f32[8,16,256]{2,1,0:T(8,128)S(1)} %get-tuple-element.33.refs_0_.refs_2_, f32[8,16,256]{2,1,0:T(8,128)S(1)} %get-tuple-element.34.refs_1_.refs_3_, f32[8,16,256]{2,1,0:T(8,128)S(1)} %get-tuple-element.43.refs_2_.refs_0_.refs_4_, ...), custom_call_target="tpu_custom_call" | custom-call | flops 25165824 | bytes 1051648 | tf_op jit(solution)/shard_map/pallas_call | solution.py:26
  15.2 1.7 %collective-permute-done.4.refs_4_ = f32[32,256]{1,0:T(8,128)S(1)} collective-permute-done((f32[32,256]{1,0:T(8,128)S(1)}, f32[32,256]{1,0:T(8,128)S(1)}, u32[]{:S(2)}, u32[]{:S(2)}) %collective-permute-start.4) | collective-permute-done | bytes 32800 | tf_op jit(solution)/shard_map/ppermute | solution.py:454
  16.9 0.3 shard_map.81
  17.2 0.3 shard_map.82
  17.6 2.1 %collective-permute-start.10 = (f32[136,256]{1,0:T(8,128)S(1)}, f32[136,256]{1,0:T(8,128)S(1)}, u32[]{:S(2)}, u32[]{:S(2)}) collective-permute-start(f32[136,256]{1,0:T(8,128)S(1)} %get-tuple-element.55), channel_id=1, source_target_pairs={{0,8},{1,2},{2,1},{3,4},{4,3},{5,6},{6,5},{7,15},{8,0},{9,10},{10,... | collective-permute-start | bytes 417800 | tf_op jit(solution)/shard_map/ppermute | solution.py:454
  19.7 1.3 %collective-permute-start.8 = (f32[32,256]{1,0:T(8,128)S(1)}, f32[32,256]{1,0:T(8,128)S(1)}, u32[]{:S(2)}, u32[]{:S(2)}) collective-permute-start(f32[32,256]{1,0:T(8,128)S(1)} %get-tuple-element.53), channel_id=1, source_target_pairs={{0,8},{1,9},{2,10},{3,11},{4,12},{5,13},{6,14},{7,15},{8,0},{9,1},... | collective-permute-start | bytes 98312 | tf_op jit(solution)/shard_map/ppermute | solution.py:454
  21.0 0.7 %shard_map.83 = (f32[8,128]{1,0:T(8,128)S(1)}, f32[8,128]{1,0:T(8,128)S(1)}) custom-call(f32[8,16,256]{2,1,0:T(8,128)S(1)} %get-tuple-element.43.refs_2_.refs_0_.refs_4_, f32[8,16,256]{2,1,0:T(8,128)S(1)} %get-tuple-element.42.refs_11_.refs_3_.refs_1_.refs_5_, f32[8,16,256]{2,1,0:T(8,128)S(1)} %get-tuple-element.52.refs_2_.refs_0_.refs_6_, ...), custom_call_target="tpu_custom_call" | custom-call | flops 16777216 | bytes 797696 | tf_op jit(solution)/shard_map/pallas_call | solution.py:26
  21.7 0.5 %collective-permute-start.11 = (f32[8,128]{1,0:T(8,128)S(1)}, f32[8,128]{1,0:T(8,128)S(1)}, u32[]{:S(2)}, u32[]{:S(2)}) collective-permute-start(f32[8,128]{1,0:T(8,128)S(1)} %get-tuple-element.59), channel_id=1, source_target_pairs={{0,1},{1,0},{2,3},{3,2},{4,5},{5,4},{6,7},{7,6},{8,9},{9,8},{10,11... | collective-permute-start | bytes 12296 | tf_op jit(solution)/shard_map/ppermute | solution.py:454
  22.2 1.3 %collective-permute-done.8.refs_4_ = f32[32,256]{1,0:T(8,128)S(1)} collective-permute-done((f32[32,256]{1,0:T(8,128)S(1)}, f32[32,256]{1,0:T(8,128)S(1)}, u32[]{:S(2)}, u32[]{:S(2)}) %collective-permute-start.8) | collective-permute-done | bytes 32800 | tf_op jit(solution)/shard_map/ppermute | solution.py:454
  23.6 0.3 shard_map.84
  23.9 0.0 collective-permute-done.11.refs_11_
  23.9 0.7 %shard_map.85 = (f32[8,16,256]{2,1,0:T(8,128)S(1)}, f32[32,4,128]{2,1,0:T(4,128)S(1)}) custom-call(f32[8,16,256]{2,1,0:T(8,128)S(1)} %get-tuple-element.52.refs_2_.refs_0_.refs_6_, f32[8,16,256]{2,1,0:T(8,128)S(1)} %get-tuple-element.51.refs_11_.refs_3_.refs_1_.refs_7_, f32[16,256]{1,0:T(8,128)S(1)} %get-tuple-element.35.refs_2_, ...), custom_call_target="tpu_custom_call" | custom-call | flops 4194304 | bytes 925696 | tf_op jit(solution)/shard_map/pallas_call | solution.py:26
  24.6 11.6 %all_to_all.5.sums_ref = f32[32,4,128]{2,1,0:T(4,128)S(1)} all-to-all(f32[32,4,128]{2,1,0:T(4,128)S(1)} %get-tuple-element.61), channel_id=1, replica_groups=mesh['narrow'=4,'wide'=8] {'narrow','wide'}, dimensions={0} | all-to-all | bytes 131072 | tf_op jit(solution)/shard_map/all_to_all | solution.py:562
  36.2 2.8 %shard_map.86 = (f32[16,2,8,256]{3,2,1,0:T(8,128)}, f32[16,2,8,256]{3,2,1,0:T(8,128)}) custom-call(f32[32,4,128]{2,1,0:T(4,128)S(1)} %all_to_all.5.sums_ref, f32[8,16,256]{2,1,0:T(8,128)S(1)} %get-tuple-element.49.refs_6_.refs_0_, f32[8,16,256]{2,1,0:T(8,128)S(1)} %get-tuple-element.50.refs_7_.refs_1_, f32[8,16,256]{2,1,0:T(8,128)S(1)} %get-tuple-element.33.refs_0_.refs_2_, ...), custom_call_target="tpu_custom_call" | custom-call | flops 75497472 | bytes 2424832 | tf_op jit(solution)/shard_map/pallas_call | solution.py:26
  (13 shorter events, 0.0 us)
Async XLA Ops:
  2.4 7.5 %collective-permute-start.2 = (f32[144,256]{1,0:T(8,128)S(1)}, f32[144,256]{1,0:T(8,128)S(1)}, u32[]{:S(2)}, u32[]{:S(2)}) collective-permute-start(f32[144,256]{1,0:T(8,128)S(1)} %get-tuple-element.39), channel_id=1, source_target_pairs={{0,8},{1,2},{2,1},{3,4},{4,3},{5,6},{6,5},{7,15},{8,0},{9,10},{10,... | collective-permute-start | bytes 442376 | tf_op jit(solution)/shard_map/ppermute | solution.py:454
  5.5 4.0 %collective-permute-start.3 = (f32[136,256]{1,0:T(8,128)S(1)}, f32[136,256]{1,0:T(8,128)S(1)}, u32[]{:S(2)}, u32[]{:S(2)}) collective-permute-start(f32[136,256]{1,0:T(8,128)S(1)} %get-tuple-element.41), channel_id=1, source_target_pairs={{0,1},{1,0},{2,3},{3,2},{4,5},{5,4},{6,7},{7,6},{8,9},{9,8},{10,11... | collective-permute-start | bytes 417800 | tf_op jit(solution)/shard_map/ppermute | solution.py:454
  5.5 4.0 %collective-permute-start = (f32[34,256]{1,0:T(8,128)S(1)}, f32[34,256]{1,0:T(8,128)S(1)}, u32[]{:S(2)}, u32[]{:S(2)}) collective-permute-start(f32[34,256]{1,0:T(8,128)S(1)} %get-tuple-element.37), channel_id=1, source_target_pairs={{0,8},{1,9},{2,10},{3,11},{4,12},{5,13},{6,14},{7,15},{8,0},{9,1},... | collective-permute-start | bytes 104456 | tf_op jit(solution)/shard_map/ppermute | solution.py:454
  7.1 2.4 %collective-permute-start.1 = (f32[34,256]{1,0:T(8,128)S(1)}, f32[34,256]{1,0:T(8,128)S(1)}, u32[]{:S(2)}, u32[]{:S(2)}) collective-permute-start(f32[34,256]{1,0:T(8,128)S(1)} %get-tuple-element.38), channel_id=1, source_target_pairs={{0,1},{1,0},{2,3},{3,2},{4,5},{5,4},{6,7},{7,6},{8,16},{9,17},{10,... | collective-permute-start | bytes 104456 | tf_op jit(solution)/shard_map/ppermute | solution.py:454
  10.2 7.0 %collective-permute-start.6 = (f32[136,256]{1,0:T(8,128)S(1)}, f32[136,256]{1,0:T(8,128)S(1)}, u32[]{:S(2)}, u32[]{:S(2)}) collective-permute-start(f32[136,256]{1,0:T(8,128)S(1)} %get-tuple-element.46), channel_id=1, source_target_pairs={{0,8},{1,2},{2,1},{3,4},{4,3},{5,6},{6,5},{7,15},{8,0},{9,10},{10,... | collective-permute-start | bytes 417800 | tf_op jit(solution)/shard_map/ppermute | solution.py:454
  13.0 3.9 %collective-permute-start.7 = (f32[128,256]{1,0:T(8,128)S(1)}, f32[128,256]{1,0:T(8,128)S(1)}, u32[]{:S(2)}, u32[]{:S(2)}) collective-permute-start(f32[128,256]{1,0:T(8,128)S(1)} %bitcast.3), channel_id=1, source_target_pairs={{0,1},{1,0},{2,3},{3,2},{4,5},{5,4},{6,7},{7,6},{8,9},{9,8},{10,11... | collective-permute-start | bytes 393224 | tf_op jit(solution)/shard_map/ppermute | solution.py:454
  13.0 3.9 %collective-permute-start.4 = (f32[32,256]{1,0:T(8,128)S(1)}, f32[32,256]{1,0:T(8,128)S(1)}, u32[]{:S(2)}, u32[]{:S(2)}) collective-permute-start(f32[32,256]{1,0:T(8,128)S(1)} %get-tuple-element.44), channel_id=1, source_target_pairs={{0,8},{1,9},{2,10},{3,11},{4,12},{5,13},{6,14},{7,15},{8,0},{9,1},... | collective-permute-start | bytes 98312 | tf_op jit(solution)/shard_map/ppermute | solution.py:454
  14.6 2.3 %collective-permute-start.5 = (f32[32,256]{1,0:T(8,128)S(1)}, f32[32,256]{1,0:T(8,128)S(1)}, u32[]{:S(2)}, u32[]{:S(2)}) collective-permute-start(f32[32,256]{1,0:T(8,128)S(1)} %get-tuple-element.45), channel_id=1, source_target_pairs={{0,1},{1,0},{2,3},{3,2},{4,5},{5,4},{6,7},{7,6},{8,16},{9,17},{10,... | collective-permute-start | bytes 98312 | tf_op jit(solution)/shard_map/ppermute | solution.py:454
  17.6 6.3 %collective-permute-start.10 = (f32[136,256]{1,0:T(8,128)S(1)}, f32[136,256]{1,0:T(8,128)S(1)}, u32[]{:S(2)}, u32[]{:S(2)}) collective-permute-start(f32[136,256]{1,0:T(8,128)S(1)} %get-tuple-element.55), channel_id=1, source_target_pairs={{0,8},{1,2},{2,1},{3,4},{4,3},{5,6},{6,5},{7,15},{8,0},{9,10},{10,... | collective-permute-start | bytes 417800 | tf_op jit(solution)/shard_map/ppermute | solution.py:454
  19.7 3.9 %collective-permute-start.12 = (f32[128,256]{1,0:T(8,128)S(1)}, f32[128,256]{1,0:T(8,128)S(1)}, u32[]{:S(2)}, u32[]{:S(2)}) collective-permute-start(f32[128,256]{1,0:T(8,128)S(1)} %bitcast.4), channel_id=1, source_target_pairs={{0,1},{1,0},{2,3},{3,2},{4,5},{5,4},{6,7},{7,6},{8,9},{9,8},{10,11... | collective-permute-start | bytes 393224 | tf_op jit(solution)/shard_map/ppermute | solution.py:454
  19.7 3.9 %collective-permute-start.8 = (f32[32,256]{1,0:T(8,128)S(1)}, f32[32,256]{1,0:T(8,128)S(1)}, u32[]{:S(2)}, u32[]{:S(2)}) collective-permute-start(f32[32,256]{1,0:T(8,128)S(1)} %get-tuple-element.53), channel_id=1, source_target_pairs={{0,8},{1,9},{2,10},{3,11},{4,12},{5,13},{6,14},{7,15},{8,0},{9,1},... | collective-permute-start | bytes 98312 | tf_op jit(solution)/shard_map/ppermute | solution.py:454
  21.0 2.6 %collective-permute-start.9 = (f32[32,256]{1,0:T(8,128)S(1)}, f32[32,256]{1,0:T(8,128)S(1)}, u32[]{:S(2)}, u32[]{:S(2)}) collective-permute-start(f32[32,256]{1,0:T(8,128)S(1)} %get-tuple-element.54), channel_id=1, source_target_pairs={{0,1},{1,0},{2,3},{3,2},{4,5},{5,4},{6,7},{7,6},{8,16},{9,17},{10,... | collective-permute-start | bytes 98312 | tf_op jit(solution)/shard_map/ppermute | solution.py:454
  21.7 2.2 %collective-permute-start.11 = (f32[8,128]{1,0:T(8,128)S(1)}, f32[8,128]{1,0:T(8,128)S(1)}, u32[]{:S(2)}, u32[]{:S(2)}) collective-permute-start(f32[8,128]{1,0:T(8,128)S(1)} %get-tuple-element.59), channel_id=1, source_target_pairs={{0,1},{1,0},{2,3},{3,2},{4,5},{5,4},{6,7},{7,6},{8,9},{9,8},{10,11... | collective-permute-start | bytes 12296 | tf_op jit(solution)/shard_map/ppermute | solution.py:454

commit v13 on v9

--- a/solution.py
+++ b/solution.py
@@ -209,12 +209,18 @@
     done, refs = refs[:others], refs[others:]
     w_refs, next_refs, edges = refs[: len(rows)], refs[len(rows) : 2 * len(rows)], refs[2 * len(rows) :]
     cols_y = v_refs[0].shape[0]
+    total = 0.0
     for row, w_ref, next_ref in zip(rows, w_refs, next_refs):
         for y in range(cols_y):
             w = operate(v_refs, coef_ref, diag_ref, got, got_coefs, row, y)
             w_ref[y] = w
-            next_ref[y] = apply_blocks(w, blocks_ref, row * cols_y + y)
-    if edges:
+            following = apply_blocks(w, blocks_ref, row * cols_y + y)
+            next_ref[y] = following
+            if rows[0] and edges:
+                total = total + split_gram([v_refs[row][y], following], w)
+    if rows[0] and edges:
+        edges[0][...] = total
+    elif edges:
         write_edges((*next_refs, *done), None, edges[:2])
         write_side(0, next_refs[0], None, edges[2])
 
@@ -337,15 +343,21 @@
     return jnp.where(axis_odd, folded[:, lanes - size :], folded[:, :size])
 
 
-def halves_kernel(cols_x, groups, *refs):
-    arrays, early_refs, (send_ref, keep_ref) = refs[:-3], refs[-3:-2], refs[-2:]
+def halves_kernel(*refs):
+    arrays, part_refs, early_refs, (send_ref, keep_ref) = refs[:3], refs[3:-3], refs[-3:-2], refs[-2:]
     count = arrays[0].shape[1]
     squares = [
         ref[:, i * count : (i + 1) * count]
         for ref in early_refs
         for i in range(ref.shape[1] // count)
     ]
-    squares += grams_of(cols_x, groups, arrays)
+    late = grams_of(1, [((0, 1), 2)], arrays)
+    for ref in part_refs:
+        late = [
+            square + fold(ref[2 * count * i : 2 * count * (i + 1), :])
+            for i, square in enumerate(late)
+        ]
+    squares += late
     folded = jnp.concatenate([fold_square(square) for square in squares], axis=1)
     odd = lax.rem(lax.axis_index("wide"), 2) == 1
     for ref, mine in ((send_ref, jnp.logical_not(odd)), (keep_ref, odd)):
@@ -510,14 +522,18 @@
         return [*(got[i] for i in slots), *(got_coefs[i] for i in slots)]
 
     for j in range(1, ITERS):
-        w, v = [], []
+        w, v, parts = [], [], []
         for rows, slots in shares:
             ahead = [] if v else grams
             operands = [*vs[-1], coef, diag_term, *halo(slots), blocks, *ahead, *v]
             out = call(
                 functools.partial(row_kernel, cols_x, rows, slots, len(ahead)),
                 [state] * (2 * len(rows))
-                + ([later_ends] * 2 + [later_side] if rows[0] == 0 else []),
+                + (
+                    [later_ends] * 2 + [later_side]
+                    if rows[0] == 0
+                    else [(4 * count, 2 * count)] * (j == ITERS - 1)
+                ),
                 [VMEM] * len(operands),
                 *operands,
                 flops=apply_flops // len(shares),
@@ -525,6 +541,8 @@
             w = out[: len(rows)] + w
             v = out[len(rows) : 2 * len(rows)] + v
             edges = out[2 * len(rows) :]
+            if rows[0]:
+                parts += edges
         edges.insert(2, v[-1].reshape(flat))
         got = [exchange(slot, edge) for slot, edge in enumerate(edges)]
         vs.append(v)
@@ -542,11 +560,11 @@
             )
         else:
             send, keep = call(
-                functools.partial(halves_kernel, cols_x, groups),
+                halves_kernel,
                 [(count // 2, 128)] * 2,
-                [VMEM] * (len(arrays) + 1),
-                *arrays, *grams,
-                flops=number_of * gram_flops,
+                [VMEM] * (4 + len(parts)),
+                vs[-2][0], v[0], w[0], *parts, *grams,
+                flops=number_of * gram_flops // cols_x,
             )
             grams = [keep, exchange(2, send)]
     lanes = lanes_of(share_size(2 * ITERS - 1, count) + count + 1)

time: 39.4 us -> 39.4 us (level)
  no operation moved by 1% of the time
where the time goes in v13:
time: 39.4 us; the launch traced here: 39.2 us
  starting transfers between devices  13 us (33%)
  blocking collectives  11.5 us (29%)
  Pallas kernels  8.47 us (21%)
  waiting for transfers between devices  5.52 us (14%)
  between operations  0.73 us (2%)
    ppermute x13, starting transfers between devices, exchange(): return lax.ppermute(edge, AXES, pairing(sizes, slot // 2, slot % 2))  13 us
    all_to_all x1, blocking collectives, on_device(): joint = lax.all_to_all(joint, AXES, 0, 0)  11.5 us
    pallas_call x10, Pallas kernels, call(): pl.pallas_call(kernel, out_shape=shapes, in_specs=in_specs, out_specs=out...  8.47 us
    ppermute x13, waiting for transfers between devices, exchange(): return lax.ppermute(edge, AXES, pairing(sizes, slot // 2, slot % 2))  5.52 us
  transfers between devices with their start and end apart: 13, of which 3 were waited for; matrix products, arithmetic and copies ran while one was open for 0% of the time, Pallas kernels for 6%

profile of v13, /device:TPU:0, one launch (start us, length us, event | category | flops | bytes accessed | tf_op | source)
XLA Modules:
  0.0 39.2 jit_solution(7327844762702306275)
XLA Ops:
  0.6 1.7 %shard_map.77 = (f32[8,16,256]{2,1,0:T(8,128)S(1)}, f32[8,16,256]{2,1,0:T(8,128)S(1)}, f32[8,16,256]{2,1,0:T(8,128)S(1)}, f32[8,16,256]{2,1,0:T(8,128)S(1)}, f32...) custom-call(s32[16]{0:T(128)} %wells_hbm.1, ...), custom_call_target="tpu_custom_call" | custom-call | flops 33554432 | bytes 4354176 | tf_op jit(solution)/shard_map/pallas_call | solution.py:26
  2.4 3.1 %collective-permute-start.2 = (f32[144,256]{1,0:T(8,128)S(1)}, f32[144,256]{1,0:T(8,128)S(1)}, u32[]{:S(2)}, u32[]{:S(2)}) collective-permute-start(f32[144,256]{1,0:T(8,128)S(1)} %get-tuple-element.40), channel_id=1, source_target_pairs={{0,8},{1,2},{2,1},{3,4},{4,3},{5,6},{6,5},{7,15},{8,0},{9,10},{10,... | collective-permute-start | bytes 442376 | tf_op jit(solution)/shard_map/ppermute | solution.py:473
  5.5 0.0 collective-permute-start.3
  5.5 1.6 %collective-permute-start = (f32[34,256]{1,0:T(8,128)S(1)}, f32[34,256]{1,0:T(8,128)S(1)}, u32[]{:S(2)}, u32[]{:S(2)}) collective-permute-start(f32[34,256]{1,0:T(8,128)S(1)} %get-tuple-element.38), channel_id=1, source_target_pairs={{0,8},{1,9},{2,10},{3,11},{4,12},{5,13},{6,14},{7,15},{8,0},{9,1},... | collective-permute-start | bytes 104456 | tf_op jit(solution)/shard_map/ppermute | solution.py:473
  7.1 2.4 %collective-permute-done.refs_4_.refs_7_ = f32[34,256]{1,0:T(8,128)S(1)} collective-permute-done((f32[34,256]{1,0:T(8,128)S(1)}, f32[34,256]{1,0:T(8,128)S(1)}, u32[]{:S(2)}, u32[]{:S(2)}) %collective-permute-start) | collective-permute-done | bytes 34848 | tf_op jit(solution)/shard_map/ppermute | solution.py:473
  9.5 0.3 shard_map.78
  9.9 0.3 shard_map.79
  10.2 2.8 %collective-permute-start.6 = (f32[136,256]{1,0:T(8,128)S(1)}, f32[136,256]{1,0:T(8,128)S(1)}, u32[]{:S(2)}, u32[]{:S(2)}) collective-permute-start(f32[136,256]{1,0:T(8,128)S(1)} %get-tuple-element.47), channel_id=1, source_target_pairs={{0,8},{1,2},{2,1},{3,4},{4,3},{5,6},{6,5},{7,15},{8,0},{9,10},{10,... | collective-permute-start | bytes 417800 | tf_op jit(solution)/shard_map/ppermute | solution.py:473
  13.0 1.6 %collective-permute-start.4 = (f32[32,256]{1,0:T(8,128)S(1)}, f32[32,256]{1,0:T(8,128)S(1)}, u32[]{:S(2)}, u32[]{:S(2)}) collective-permute-start(f32[32,256]{1,0:T(8,128)S(1)} %get-tuple-element.45), channel_id=1, source_target_pairs={{0,8},{1,9},{2,10},{3,11},{4,12},{5,13},{6,14},{7,15},{8,0},{9,1},... | collective-permute-start | bytes 98312 | tf_op jit(solution)/shard_map/ppermute | solution.py:473
  14.6 0.7 %shard_map.80.refs_11_.refs_4_ = f32[16,48]{1,0:T(8,128)S(1)} custom-call(f32[8,16,256]{2,1,0:T(8,128)S(1)} %get-tuple-element.34.refs_0_.refs_2_, f32[8,16,256]{2,1,0:T(8,128)S(1)} %get-tuple-element.35.refs_1_.refs_3_, f32[8,16,256]{2,1,0:T(8,128)S(1)} %get-tuple-element.44.refs_2_.refs_0_.refs_4_, ...), custom_call_target="tpu_custom_call" | custom-call | flops 25165824 | bytes 1051648 | tf_op jit(solution)/shard_map/pallas_call | solution.py:26
  15.2 1.7 %collective-permute-done.4.refs_4_ = f32[32,256]{1,0:T(8,128)S(1)} collective-permute-done((f32[32,256]{1,0:T(8,128)S(1)}, f32[32,256]{1,0:T(8,128)S(1)}, u32[]{:S(2)}, u32[]{:S(2)}) %collective-permute-start.4) | collective-permute-done | bytes 32800 | tf_op jit(solution)/shard_map/ppermute | solution.py:473
  16.9 0.5 %shard_map.81 = (f32[8,16,256]{2,1,0:T(8,128)S(1)}, f32[8,16,256]{2,1,0:T(8,128)S(1)}, f32[64,32]{1,0:T(8,128)S(1)}) custom-call(f32[8,16,256]{2,1,0:T(8,128)S(1)} %get-tuple-element.44.refs_2_.refs_0_.refs_4_, f32[8,16,256]{2,1,0:T(8,128)S(1)} %get-tuple-element.43.refs_11_.refs_3_.refs_1_.refs_5_, f32[16,256]{1,0:T(8,128)S(1)} %get-tuple-element.36.refs_2_, ...), custom_call_target="tpu_custom_call" | custom-call | flops 16777216 | bytes 2022400 | tf_op jit(solution)/shard_map/pallas_call | solution.py:26
  17.4 0.0 collective-permute-done.6.refs_6_
  17.4 0.3 shard_map.82
  17.7 2.1 %collective-permute-start.10 = (f32[136,256]{1,0:T(8,128)S(1)}, f32[136,256]{1,0:T(8,128)S(1)}, u32[]{:S(2)}, u32[]{:S(2)}) collective-permute-start(f32[136,256]{1,0:T(8,128)S(1)} %get-tuple-element.56), channel_id=1, source_target_pairs={{0,8},{1,2},{2,1},{3,4},{4,3},{5,6},{6,5},{7,15},{8,0},{9,10},{10,... | collective-permute-start | bytes 417800 | tf_op jit(solution)/shard_map/ppermute | solution.py:473
  19.8 1.4 %collective-permute-start.8 = (f32[32,256]{1,0:T(8,128)S(1)}, f32[32,256]{1,0:T(8,128)S(1)}, u32[]{:S(2)}, u32[]{:S(2)}) collective-permute-start(f32[32,256]{1,0:T(8,128)S(1)} %get-tuple-element.54), channel_id=1, source_target_pairs={{0,8},{1,9},{2,10},{3,11},{4,12},{5,13},{6,14},{7,15},{8,0},{9,1},... | collective-permute-start | bytes 98312 | tf_op jit(solution)/shard_map/ppermute | solution.py:473
  21.2 0.6 %shard_map.83 = (f32[8,128]{1,0:T(8,128)S(1)}, f32[8,128]{1,0:T(8,128)S(1)}) custom-call(f32[8,16,256]{2,1,0:T(8,128)S(1)} %get-tuple-element.44.refs_2_.refs_0_.refs_4_, f32[8,16,256]{2,1,0:T(8,128)S(1)} %get-tuple-element.53.refs_1_.refs_0_.refs_6_, f32[8,16,256]{2,1,0:T(8,128)S(1)} %get-tuple-element.57.refs_2_.refs_10_, ...), custom_call_target="tpu_custom_call" | custom-call | flops 8388608 | bytes 412672 | tf_op jit(solution)/shard_map/pallas_call | solution.py:26
  21.8 0.5 %collective-permute-start.11 = (f32[8,128]{1,0:T(8,128)S(1)}, f32[8,128]{1,0:T(8,128)S(1)}, u32[]{:S(2)}, u32[]{:S(2)}) collective-permute-start(f32[8,128]{1,0:T(8,128)S(1)} %get-tuple-element.60), channel_id=1, source_target_pairs={{0,1},{1,0},{2,3},{3,2},{4,5},{5,4},{6,7},{7,6},{8,9},{9,8},{10,11... | collective-permute-start | bytes 12296 | tf_op jit(solution)/shard_map/ppermute | solution.py:473
  22.3 1.4 %collective-permute-done.8.refs_4_ = f32[32,256]{1,0:T(8,128)S(1)} collective-permute-done((f32[32,256]{1,0:T(8,128)S(1)}, f32[32,256]{1,0:T(8,128)S(1)}, u32[]{:S(2)}, u32[]{:S(2)}) %collective-permute-start.8) | collective-permute-done | bytes 32800 | tf_op jit(solution)/shard_map/ppermute | solution.py:473
  23.7 0.3 shard_map.84
  24.1 0.0 collective-permute-done.11.refs_11_
  24.1 0.7 %shard_map.85 = (f32[8,16,256]{2,1,0:T(8,128)S(1)}, f32[32,4,128]{2,1,0:T(4,128)S(1)}) custom-call(f32[8,16,256]{2,1,0:T(8,128)S(1)} %get-tuple-element.53.refs_1_.refs_0_.refs_6_, f32[8,16,256]{2,1,0:T(8,128)S(1)} %get-tuple-element.52.refs_11_.refs_1_.refs_7_, f32[16,256]{1,0:T(8,128)S(1)} %get-tuple-element.36.refs_2_, ...), custom_call_target="tpu_custom_call" | custom-call | flops 4194304 | bytes 925696 | tf_op jit(solution)/shard_map/pallas_call | solution.py:26
  24.8 11.5 %all_to_all.5.sums_ref = f32[32,4,128]{2,1,0:T(4,128)S(1)} all-to-all(f32[32,4,128]{2,1,0:T(4,128)S(1)} %get-tuple-element.62), channel_id=1, replica_groups=mesh['narrow'=4,'wide'=8] {'narrow','wide'}, dimensions={0} | all-to-all | bytes 131072 | tf_op jit(solution)/shard_map/all_to_all | solution.py:587
  36.2 3.0 %shard_map.86 = (f32[16,2,8,256]{3,2,1,0:T(8,128)}, f32[16,2,8,256]{3,2,1,0:T(8,128)}) custom-call(f32[32,4,128]{2,1,0:T(4,128)S(1)} %all_to_all.5.sums_ref, f32[8,16,256]{2,1,0:T(8,128)S(1)} %get-tuple-element.50.refs_6_.refs_0_, f32[8,16,256]{2,1,0:T(8,128)S(1)} %get-tuple-element.51.refs_7_.refs_1_, f32[8,16,256]{2,1,0:T(8,128)S(1)} %get-tuple-element.34.refs_0_.refs_2_, ...), custom_call_target="tpu_custom_call" | custom-call | flops 75497472 | bytes 2424832 | tf_op jit(solution)/shard_map/pallas_call | solution.py:26
  (13 shorter events, 0.0 us)
Async XLA Ops:
  2.4 7.5 %collective-permute-start.2 = (f32[144,256]{1,0:T(8,128)S(1)}, f32[144,256]{1,0:T(8,128)S(1)}, u32[]{:S(2)}, u32[]{:S(2)}) collective-permute-start(f32[144,256]{1,0:T(8,128)S(1)} %get-tuple-element.40), channel_id=1, source_target_pairs={{0,8},{1,2},{2,1},{3,4},{4,3},{5,6},{6,5},{7,15},{8,0},{9,10},{10,... | collective-permute-start | bytes 442376 | tf_op jit(solution)/shard_map/ppermute | solution.py:473
  5.5 4.0 %collective-permute-start.3 = (f32[136,256]{1,0:T(8,128)S(1)}, f32[136,256]{1,0:T(8,128)S(1)}, u32[]{:S(2)}, u32[]{:S(2)}) collective-permute-start(f32[136,256]{1,0:T(8,128)S(1)} %get-tuple-element.42), channel_id=1, source_target_pairs={{0,1},{1,0},{2,3},{3,2},{4,5},{5,4},{6,7},{7,6},{8,9},{9,8},{10,11... | collective-permute-start | bytes 417800 | tf_op jit(solution)/shard_map/ppermute | solution.py:473
  5.5 4.0 %collective-permute-start = (f32[34,256]{1,0:T(8,128)S(1)}, f32[34,256]{1,0:T(8,128)S(1)}, u32[]{:S(2)}, u32[]{:S(2)}) collective-permute-start(f32[34,256]{1,0:T(8,128)S(1)} %get-tuple-element.38), channel_id=1, source_target_pairs={{0,8},{1,9},{2,10},{3,11},{4,12},{5,13},{6,14},{7,15},{8,0},{9,1},... | collective-permute-start | bytes 104456 | tf_op jit(solution)/shard_map/ppermute | solution.py:473
  7.1 2.4 %collective-permute-start.1 = (f32[34,256]{1,0:T(8,128)S(1)}, f32[34,256]{1,0:T(8,128)S(1)}, u32[]{:S(2)}, u32[]{:S(2)}) collective-permute-start(f32[34,256]{1,0:T(8,128)S(1)} %get-tuple-element.39), channel_id=1, source_target_pairs={{0,1},{1,0},{2,3},{3,2},{4,5},{5,4},{6,7},{7,6},{8,16},{9,17},{10,... | collective-permute-start | bytes 104456 | tf_op jit(solution)/shard_map/ppermute | solution.py:473
  10.2 7.2 %collective-permute-start.6 = (f32[136,256]{1,0:T(8,128)S(1)}, f32[136,256]{1,0:T(8,128)S(1)}, u32[]{:S(2)}, u32[]{:S(2)}) collective-permute-start(f32[136,256]{1,0:T(8,128)S(1)} %get-tuple-element.47), channel_id=1, source_target_pairs={{0,8},{1,2},{2,1},{3,4},{4,3},{5,6},{6,5},{7,15},{8,0},{9,10},{10,... | collective-permute-start | bytes 417800 | tf_op jit(solution)/shard_map/ppermute | solution.py:473
  13.0 3.9 %collective-permute-start.7 = (f32[128,256]{1,0:T(8,128)S(1)}, f32[128,256]{1,0:T(8,128)S(1)}, u32[]{:S(2)}, u32[]{:S(2)}) collective-permute-start(f32[128,256]{1,0:T(8,128)S(1)} %bitcast.3), channel_id=1, source_target_pairs={{0,1},{1,0},{2,3},{3,2},{4,5},{5,4},{6,7},{7,6},{8,9},{9,8},{10,11... | collective-permute-start | bytes 393224 | tf_op jit(solution)/shard_map/ppermute | solution.py:473
  13.0 3.9 %collective-permute-start.4 = (f32[32,256]{1,0:T(8,128)S(1)}, f32[32,256]{1,0:T(8,128)S(1)}, u32[]{:S(2)}, u32[]{:S(2)}) collective-permute-start(f32[32,256]{1,0:T(8,128)S(1)} %get-tuple-element.45), channel_id=1, source_target_pairs={{0,8},{1,9},{2,10},{3,11},{4,12},{5,13},{6,14},{7,15},{8,0},{9,1},... | collective-permute-start | bytes 98312 | tf_op jit(solution)/shard_map/ppermute | solution.py:473
  14.6 2.3 %collective-permute-start.5 = (f32[32,256]{1,0:T(8,128)S(1)}, f32[32,256]{1,0:T(8,128)S(1)}, u32[]{:S(2)}, u32[]{:S(2)}) collective-permute-start(f32[32,256]{1,0:T(8,128)S(1)} %get-tuple-element.46), channel_id=1, source_target_pairs={{0,1},{1,0},{2,3},{3,2},{4,5},{5,4},{6,7},{7,6},{8,16},{9,17},{10,... | collective-permute-start | bytes 98312 | tf_op jit(solution)/shard_map/ppermute | solution.py:473
  17.7 6.3 %collective-permute-start.10 = (f32[136,256]{1,0:T(8,128)S(1)}, f32[136,256]{1,0:T(8,128)S(1)}, u32[]{:S(2)}, u32[]{:S(2)}) collective-permute-start(f32[136,256]{1,0:T(8,128)S(1)} %get-tuple-element.56), channel_id=1, source_target_pairs={{0,8},{1,2},{2,1},{3,4},{4,3},{5,6},{6,5},{7,15},{8,0},{9,10},{10,... | collective-permute-start | bytes 417800 | tf_op jit(solution)/shard_map/ppermute | solution.py:473
  19.8 3.9 %collective-permute-start.12 = (f32[128,256]{1,0:T(8,128)S(1)}, f32[128,256]{1,0:T(8,128)S(1)}, u32[]{:S(2)}, u32[]{:S(2)}) collective-permute-start(f32[128,256]{1,0:T(8,128)S(1)} %bitcast.4), channel_id=1, source_target_pairs={{0,1},{1,0},{2,3},{3,2},{4,5},{5,4},{6,7},{7,6},{8,9},{9,8},{10,11... | collective-permute-start | bytes 393224 | tf_op jit(solution)/shard_map/ppermute | solution.py:473
  19.8 3.9 %collective-permute-start.8 = (f32[32,256]{1,0:T(8,128)S(1)}, f32[32,256]{1,0:T(8,128)S(1)}, u32[]{:S(2)}, u32[]{:S(2)}) collective-permute-start(f32[32,256]{1,0:T(8,128)S(1)} %get-tuple-element.54), channel_id=1, source_target_pairs={{0,8},{1,9},{2,10},{3,11},{4,12},{5,13},{6,14},{7,15},{8,0},{9,1},... | collective-permute-start | bytes 98312 | tf_op jit(solution)/shard_map/ppermute | solution.py:473
  21.2 2.6 %collective-permute-start.9 = (f32[32,256]{1,0:T(8,128)S(1)}, f32[32,256]{1,0:T(8,128)S(1)}, u32[]{:S(2)}, u32[]{:S(2)}) collective-permute-start(f32[32,256]{1,0:T(8,128)S(1)} %get-tuple-element.55), channel_id=1, source_target_pairs={{0,1},{1,0},{2,3},{3,2},{4,5},{5,4},{6,7},{7,6},{8,16},{9,17},{10,... | collective-permute-start | bytes 98312 | tf_op jit(solution)/shard_map/ppermute | solution.py:473
  21.8 2.3 %collective-permute-start.11 = (f32[8,128]{1,0:T(8,128)S(1)}, f32[8,128]{1,0:T(8,128)S(1)}, u32[]{:S(2)}, u32[]{:S(2)}) collective-permute-start(f32[8,128]{1,0:T(8,128)S(1)} %get-tuple-element.60), channel_id=1, source_target_pairs={{0,1},{1,0},{2,3},{3,2},{4,5},{5,4},{6,7},{7,6},{8,9},{9,8},{10,11... | collective-permute-start | bytes 12296 | tf_op jit(solution)/shard_map/ppermute | solution.py:473
